TPU v7x, 32 devices: a whole 2x2x4 slice. The times are simulated.
32 devices in a mesh: rep: 4 (over x, core), shard: 8 (over z, y).
Axes of the slice: x: 2, y: 2, z: 4, core: 2. Of those that a mesh axis runs over, the one named last changes fastest.
Arguments:
- tokens: bfloat16 [1024, 8, 2048], P('rep', 'shard'), may hold values from -6 to 6
- cotangent: bfloat16 [1024, 8, 2048], P('rep', 'shard'), may hold values from -6 to 6
- seq_lengths: int32 [4, 16], P('rep'), may hold values from 16 to 464, as said below
- seq_order: int32 [4, 16], P('rep'), may hold values from 0 to 15, each once within a row
- ln1_gain: float32 [2048], replicated, may hold values from 0.1 to 1.9
- ln1_bias: float32 [2048], replicated, may hold values from -3 to 3
- ln2_gain: float32 [2048], replicated, may hold values from 0.1 to 1.9
- ln2_bias: float32 [2048], replicated, may hold values from -3 to 3
- w_qkv: bfloat16 [2048, 6144], P('shard'), may hold values from -0.125 to 0.125
- b_qkv: float32 [6144], replicated, may hold values from -3 to 3
- w_dense: bfloat16 [2048, 2048], P('shard'), may hold values from -0.75 to 0.75
- b_dense: float32 [2048], replicated, may hold values from -3 to 3
- w_up: bfloat16 [2048, 8192], P('shard'), may hold values from -0.125 to 0.125
- b_up: float32 [8192], replicated, may hold values from -3 to 3
- w_down: bfloat16 [8192, 2048], P('shard'), may hold values from -0.0625 to 0.0625
- b_down: float32 [2048], replicated, may hold values from -3 to 3
Outputs:
- output: bfloat16 [1024, 8, 2048], P('rep', 'shard')
- input_grad: float32 [1024, 8, 2048], P('rep', 'shard')
- ln1_gain_grad: float32 [2048], replicated
- ln1_bias_grad: float32 [2048], replicated
- ln2_gain_grad: float32 [2048], replicated
- ln2_bias_grad: float32 [2048], replicated
- w_qkv_grad: float32 [2048, 6144], P('shard')
- b_qkv_grad: float32 [6144], replicated
- w_dense_grad: float32 [2048, 2048], P('shard')
- b_dense_grad: float32 [2048], replicated
- w_up_grad: float32 [2048, 8192], P('shard')
- b_up_grad: float32 [8192], replicated
- w_down_grad: float32 [8192, 2048], P('shard')
- b_down_grad: float32 [2048], replicated
Inputs may be any that keep to these rules, and one draw needn't show every extreme that they name: `seq_lengths`: lengths are multiples of 8; the two sequences dealt to one device hold at most 480 tokens together, exactly 480 on some device of each group; a group's lengths sum to 2048. `seq_order`: each row holds every sequence number of its group once.
All inputs are finite; a program needn't handle non-finite values.
Results may differ from a plain program's by a relative error of at most 0.015.
Values may be sent and summed in bfloat16 or wider, within the bound.
No kernel may reach another device: no remote copies, remote signals or barrier semaphores. Data moves between devices by JAX's collectives and lax.ppermute only.
A program may use at most 640 MiB of HBM per device.

v0:
```python
import math

import jax
import jax.numpy as jnp
from jax import lax
from jax.sharding import PartitionSpec as P

HEADS = 8
HEAD = 256
ROT = 64


EPSILON = 1e-05
MASKED = -1e30


def layer_norm(vector, gain_vec, shift_vec):
    mean_val = jnp.mean(vector, axis=-1, keepdims=True)
    centered = vector - mean_val
    variance = jnp.mean(centered * centered, axis=-1, keepdims=True)
    return centered * lax.rsqrt(variance + EPSILON) * gain_vec + shift_vec


def gelu_exact(vector):
    return jax.nn.gelu(vector, approximate=False)


def rotary_tables(positions):
    half_rot = ROT // 2
    freq_index = jnp.arange(half_rot, dtype=jnp.float32)
    inverse_freq = jnp.exp(freq_index * (-2.0 * math.log(10000.0) / ROT))
    angles = positions[:, None] * inverse_freq[None, :]
    return (jnp.cos(angles), jnp.sin(angles))


def rotate(heads_in, cosine_table, sine_table):
    half_rot = ROT // 2
    first_half = heads_in[..., :half_rot]
    second_half = heads_in[..., half_rot:ROT]
    cos_wide = cosine_table[:, None, :]
    sin_wide = sine_table[:, None, :]
    return jnp.concatenate(
        [
            first_half * cos_wide - second_half * sin_wide,
            second_half * cos_wide + first_half * sin_wide,
            heads_in[..., ROT:],
        ],
        axis=-1,
    )


def stream_rows(lengths, seq_perm, shard_count):
    seq_range = jnp.arange(lengths.shape[0], dtype=jnp.int32)
    ranking = jnp.sum(
        jnp.where(seq_perm[:, None] == seq_range[None, :], seq_range[:, None], 0), axis=0
    )
    offsets = jnp.sum(jnp.where(ranking[None, :] < ranking[:, None], lengths[None, :], 0), axis=1)
    return (offsets // shard_count, lengths // shard_count)


def row_product(left, right):
    return jnp.dot(left.T, right, preferred_element_type=jnp.float32)


def block_mask(seq_flag, positions, live):
    return (
        live[:, None]
        & live[None, :]
        & (seq_flag[:, None] == seq_flag[None, :])
        & (positions[None, :] <= positions[:, None])
    )


def shards(
    tokens,
    cotangent,
    seq_lengths,
    seq_order,
    ln1_gain,
    ln1_bias,
    ln2_gain,
    ln2_bias,
    w_qkv,
    b_qkv,
    w_dense,
    b_dense,
    w_up,
    b_up,
    w_down,
    b_down,
):
    shard_count = lax.axis_size("shard")
    my_index = lax.axis_index("shard")
    inputs = tokens[:, 0, :].astype(jnp.float32)
    grad_out = cotangent[:, 0, :]
    local_rows, width = inputs.shape
    slot_rows = 2 * (local_rows // shard_count) - 4
    buffer_rows = slot_rows * shard_count
    row_offsets, row_counts = stream_rows(seq_lengths[0], seq_order[0], shard_count)
    first_count = row_counts[0::2]
    second_count = row_counts[1::2]
    first_start = row_offsets[0::2]
    second_start = row_offsets[1::2]
    slot_range = jnp.arange(slot_rows, dtype=jnp.int32)[None, :]
    in_first = slot_range < first_count[:, None]
    slot_live = slot_range < (first_count + second_count)[:, None]
    source_rows = jnp.where(
        in_first,
        first_start[:, None] + slot_range,
        second_start[:, None] + slot_range - first_count[:, None],
    )
    source_rows = jnp.where(slot_live, source_rows, 0)
    seq_range = jnp.arange(row_counts.shape[0], dtype=jnp.int32)
    parity = seq_range % 2
    slot_base = seq_range // 2 * slot_rows + parity * row_counts[seq_range - parity] - row_offsets
    token_range = jnp.arange(local_rows, dtype=jnp.int32)[:, None]
    member = (token_range >= row_offsets[None, :]) & (
        token_range < (row_offsets + row_counts)[None, :]
    )
    return_rows = token_range[:, 0] + jnp.sum(jnp.where(member, slot_base[None, :], 0), axis=1)
    own_first = first_count[my_index]
    own_second = second_count[my_index]
    buffer_range = jnp.arange(buffer_rows, dtype=jnp.int32)
    slot_index = buffer_range % slot_rows
    source_index = buffer_range // slot_rows
    seq_flag = (slot_index >= own_first).astype(jnp.int32)
    positions = (slot_index - seq_flag * own_first) * shard_count + source_index
    live = slot_index < own_first + own_second
    attn_full, dense_full = (
        lax.all_gather(w_qkv, "shard", axis=0, tiled=True),
        lax.all_gather(w_dense, "shard", axis=0, tiled=True),
    )
    up_full, down_full = (
        lax.all_gather(w_up, "shard", axis=0, tiled=True),
        lax.all_gather(w_down, "shard", axis=0, tiled=True),
    )
    normed_one_wide, pull_one = jax.vjp(layer_norm, inputs, ln1_gain, ln1_bias)
    normed_two_wide, pull_two = jax.vjp(layer_norm, inputs, ln2_gain, ln2_bias)
    normed_one = normed_one_wide.astype(jnp.bfloat16)
    normed_two = normed_two_wide.astype(jnp.bfloat16)
    qkv = (jnp.dot(normed_one, attn_full, preferred_element_type=jnp.float32) + b_qkv).astype(
        jnp.bfloat16
    )
    arrived = lax.all_to_all(
        jnp.take(qkv, source_rows, axis=0), "shard", split_axis=0, concat_axis=0, tiled=True
    )
    arrived = arrived.reshape(buffer_rows, 3 * width)
    heads_shape = (buffer_rows, HEADS, HEAD)
    cosine_table, sine_table = rotary_tables(positions.astype(jnp.float32))

    def rotate_here(heads_in):
        return rotate(heads_in, cosine_table, sine_table)

    query_wide, pull_query = jax.vjp(
        rotate_here, arrived[:, :width].astype(jnp.float32).reshape(heads_shape)
    )
    key_wide, pull_key = jax.vjp(
        rotate_here, arrived[:, width : 2 * width].astype(jnp.float32).reshape(heads_shape)
    )
    rotated_queries = query_wide.astype(jnp.bfloat16)
    rotated_keys = key_wide.astype(jnp.bfloat16)
    value_heads = arrived[:, 2 * width :].reshape(heads_shape)
    sources_per = shard_count
    while sources_per > 1 and sources_per * slot_rows > 1024:
        sources_per = sources_per // 2
    block_rows = sources_per * slot_rows
    block_total = buffer_rows // block_rows
    score_scale = HEAD ** (-0.5)

    def forward_block(block_index):
        allowed = block_mask(seq_flag, positions, live)
        scores = (
            jnp.einsum(
                "qhe,khe->hqk", rotated_queries, rotated_keys, preferred_element_type=jnp.float32
            )
            * score_scale
        )
        scores = jnp.where(allowed[None], scores, MASKED)
        row_max = jnp.max(scores, axis=-1, keepdims=True)
        exp_scores = jnp.exp(scores - row_max)
        exp_total = jnp.sum(exp_scores, axis=-1, keepdims=True)
        attn_probs = jnp.where(allowed[None], exp_scores / exp_total, 0.0)
        attended_blk = jnp.einsum(
            "hqk,khe->qhe",
            attn_probs.astype(jnp.bfloat16),
            value_heads,
            preferred_element_type=jnp.float32,
        )
        return (attended_blk.astype(jnp.bfloat16), row_max[..., 0] + jnp.log(exp_total[..., 0]))

    attended_blocks, log_totals = lax.map(forward_block, jnp.arange(block_total, dtype=jnp.int32))
    attended_slots = attended_blocks.reshape(shard_count, slot_rows, width)
    attn_back = lax.all_to_all(
        attended_slots, "shard", split_axis=0, concat_axis=0, tiled=True
    ).reshape(buffer_rows, width)
    attn_in = jnp.take(attn_back, return_rows, axis=0)
    attn_out = jnp.dot(attn_in, dense_full, preferred_element_type=jnp.float32) + b_dense
    pre_up = jnp.dot(normed_two, up_full, preferred_element_type=jnp.float32) + b_up
    activated_wide, pull_gelu = jax.vjp(gelu_exact, pre_up)
    activated = activated_wide.astype(jnp.bfloat16)
    mlp_out = jnp.dot(activated, down_full, preferred_element_type=jnp.float32) + b_down
    output = (inputs + attn_out + mlp_out).astype(jnp.bfloat16)
    attn_second, dense_second = (
        lax.all_gather(w_qkv, "shard", axis=0, tiled=True),
        lax.all_gather(w_dense, "shard", axis=0, tiled=True),
    )
    up_second, down_second = (
        lax.all_gather(w_up, "shard", axis=0, tiled=True),
        lax.all_gather(w_down, "shard", axis=0, tiled=True),
    )
    grad_attended = jnp.dot(grad_out, dense_second.T, preferred_element_type=jnp.float32).astype(
        jnp.bfloat16
    )
    grad_slots = jnp.where(
        slot_live[:, :, None],
        jnp.take(grad_attended, source_rows, axis=0),
        jnp.zeros((), jnp.bfloat16),
    )
    grad_heads = lax.all_to_all(
        grad_slots, "shard", split_axis=0, concat_axis=0, tiled=True
    ).reshape(heads_shape)

    def backward_block(carried, block_index):
        grad_keys, grad_values = carried
        allowed = block_mask(seq_flag, positions, live)
        scores = (
            jnp.einsum(
                "qhe,khe->hqk", rotated_queries, rotated_keys, preferred_element_type=jnp.float32
            )
            * score_scale
        )
        attn_probs = jnp.where(
            allowed[None], jnp.exp(scores - log_totals[block_index][..., None]), 0.0
        )
        grad_probs = jnp.einsum(
            "qhe,khe->hqk", grad_heads, value_heads, preferred_element_type=jnp.float32
        )
        row_delta = jnp.sum(attn_probs * grad_probs, axis=-1, keepdims=True)
        grad_scores = (attn_probs * (grad_probs - row_delta)).astype(jnp.bfloat16)
        grad_query = (
            jnp.einsum(
                "hqk,khe->qhe", grad_scores, rotated_keys, preferred_element_type=jnp.float32
            )
            * score_scale
        )
        grad_keys = (
            grad_keys
            + jnp.einsum(
                "hqk,qhe->khe", grad_scores, rotated_queries, preferred_element_type=jnp.float32
            )
            * score_scale
        )
        grad_values = grad_values + jnp.einsum(
            "hqk,qhe->khe",
            attn_probs.astype(jnp.bfloat16),
            grad_heads,
            preferred_element_type=jnp.float32,
        )
        return ((grad_keys, grad_values), grad_query)

    zero_heads = jnp.zeros(heads_shape, jnp.float32)
    (grad_keys, grad_values), grad_query_blocks = lax.scan(
        backward_block, (zero_heads, zero_heads), jnp.arange(block_total, dtype=jnp.int32)
    )
    grad_q_pre = pull_query(grad_query_blocks.reshape(heads_shape))[0]
    grad_k_pre = pull_key(grad_keys)[0]
    grad_qkv_slots = jnp.concatenate(
        [
            grad_q_pre.reshape(buffer_rows, width),
            grad_k_pre.reshape(buffer_rows, width),
            grad_values.reshape(buffer_rows, width),
        ],
        axis=1,
    ).astype(jnp.bfloat16)
    grad_qkv_slots = grad_qkv_slots.reshape(shard_count, slot_rows, 3 * width)
    grad_qkv_back = lax.all_to_all(grad_qkv_slots, "shard", split_axis=0, concat_axis=0, tiled=True)
    grad_qkv = jnp.take(grad_qkv_back.reshape(buffer_rows, 3 * width), return_rows, axis=0)
    grad_activated = jnp.dot(grad_out, down_second.T, preferred_element_type=jnp.float32)
    grad_pre = pull_gelu(grad_activated)[0].astype(jnp.bfloat16)
    grad_normed_one = jnp.dot(grad_qkv, attn_second.T, preferred_element_type=jnp.float32)
    grad_normed_two = jnp.dot(grad_pre, up_second.T, preferred_element_type=jnp.float32)
    grad_in_one, grad_gain_one, grad_bias_one = pull_one(grad_normed_one)
    grad_in_two, grad_gain_two, grad_bias_two = pull_two(grad_normed_two)
    input_grad = grad_out.astype(jnp.float32) + grad_in_one + grad_in_two
    qkv_rows = lax.psum_scatter(
        row_product(normed_one, grad_qkv).astype(jnp.bfloat16),
        "shard",
        scatter_dimension=0,
        tiled=True,
    ).astype(jnp.float32)
    dense_rows = lax.psum_scatter(
        row_product(attn_in, grad_out).astype(jnp.bfloat16),
        "shard",
        scatter_dimension=0,
        tiled=True,
    ).astype(jnp.float32)
    up_rows = lax.psum_scatter(
        row_product(normed_two, grad_pre).astype(jnp.bfloat16),
        "shard",
        scatter_dimension=0,
        tiled=True,
    ).astype(jnp.float32)
    down_rows = lax.psum_scatter(
        row_product(activated, grad_out).astype(jnp.bfloat16),
        "shard",
        scatter_dimension=0,
        tiled=True,
    ).astype(jnp.float32)
    qkv_rows, dense_rows, up_rows, down_rows = (
        lax.psum(qkv_rows.astype(jnp.bfloat16), "rep").astype(jnp.float32),
        lax.psum(dense_rows.astype(jnp.bfloat16), "rep").astype(jnp.float32),
        lax.psum(up_rows.astype(jnp.bfloat16), "rep").astype(jnp.float32),
        lax.psum(down_rows.astype(jnp.bfloat16), "rep").astype(jnp.float32),
    )
    out_column_sum = jnp.sum(grad_out, axis=0, dtype=jnp.float32)
    small_totals = lax.psum(
        (
            grad_gain_one,
            grad_bias_one,
            grad_gain_two,
            grad_bias_two,
            jnp.sum(grad_qkv, axis=0, dtype=jnp.float32),
            out_column_sum,
            jnp.sum(grad_pre, axis=0, dtype=jnp.float32),
        ),
        ("rep", "shard"),
    )
    return (
        output[:, None, :],
        input_grad[:, None, :],
        small_totals[0],
        small_totals[1],
        small_totals[2],
        small_totals[3],
        qkv_rows,
        small_totals[4],
        dense_rows,
        small_totals[5],
        up_rows,
        small_totals[6],
        down_rows,
        small_totals[5],
    )


def solution(mesh):
    in_specs = (
        P("rep", "shard", None),
        P("rep", "shard", None),
        P("rep", None),
        P("rep", None),
        P(),
        P(),
        P(),
        P(),
        P("shard", None),
        P(),
        P("shard", None),
        P(),
        P("shard", None),
        P(),
        P("shard", None),
        P(),
    )
    out_specs = (
        P("rep", "shard", None),
        P("rep", "shard", None),
        P(),
        P(),
        P(),
        P(),
        P("shard", None),
        P(),
        P("shard", None),
        P(),
        P("shard", None),
        P(),
        P("shard", None),
        P(),
    )
    return jax.shard_map(shards, mesh=mesh, in_specs=in_specs, out_specs=out_specs, check_vma=False)
```

profile of v0, /device:TPU:0, one launch (start us, length us, event | category | flops | bytes accessed | tf_op | source)
XLA Modules:
  0.0 4165.5 jit_solution(5597175099494450353)
XLA Ops:
  12.4 480.3 %all-gather.5.cloned.1.call-done = bf16[2048,6144]{1,0:T(8,128)(2,1)} async-done(((bf16[256,6144]{1,0:T(8,128)(2,1)}), bf16[2048,6144]{1,0:T(8,128)(2,1)}) %all-gather.5.cloned.1.call-update) | async-done | bytes 25165840 | tf_op jit(solution)/shard_map/all_gather | solution.py:130
  492.7 12.1 fusion.6
  534.1 206.0 %all-gather.7.cloned.1.call-done = bf16[2048,2048]{1,0:T(8,128)(2,1)} async-done(((bf16[256,2048]{1,0:T(8,128)(2,1)}), bf16[2048,2048]{1,0:T(8,128)(2,1)}) %all-gather.7.cloned.1.call-update) | async-done | bytes 8388624 | tf_op jit(solution)/shard_map/all_gather | solution.py:131
  781.1 14.1 convert_bitcast_fusion.2
  798.3 33.3 all-to-all-done.2
  831.6 36.4 all-to-all-start.1
  873.1 64.2 %all-to-all-done.1 = bf16[8,60,2048]{2,1,0:T(8,128)(2,1)} async-done(((bf16[8,60,2048]{2,1,0:T(8,128)(2,1)}), bf16[8,60,2048]{2,1,0:T(8,128)(2,1)}, u32[]{:S(2)}, u32[]{:S(2)}) %all-to-all-start.1) | async-done | bytes 1966112 | tf_op jit(solution)/shard_map/all_to_all | solution.py:193
  1000.5 210.8 %all_to_all.20 = bf16[8,60,6144]{2,1,0:T(8,128)(2,1)} all-to-all(bf16[8,60,6144]{2,1,0:T(8,128)(2,1)S(1)} %pad_maximum_fusion), channel_id=1, replica_groups=mesh['rep'=4,'shard'=8] {'shard'}, dimensions={0} | all-to-all | bytes 11796480 | tf_op jit(solution)/shard_map/all_to_all | solution.py:276
  1228.4 13.8 convolution_convert_fusion.2
  1242.3 246.7 %all-gather.9.cloned.1.call-done = bf16[2048,8192]{1,0:T(8,128)(2,1)} async-done(((bf16[256,8192]{1,0:T(8,128)(2,1)}), bf16[2048,8192]{1,0:T(8,128)(2,1)}) %all-gather.9.cloned.1.call-update) | async-done | bytes 33554448 | tf_op jit(solution)/shard_map/all_gather | solution.py:134
  1489.0 32.4 multiply_convert_fusion
  1521.4 606.7 %all-gather.11.cloned.1.call-done = bf16[8192,2048]{1,0:T(8,128)(2,1)} async-done(((bf16[1024,2048]{1,0:T(8,128)(2,1)}), bf16[8192,2048]{1,0:T(8,128)(2,1)}) %all-gather.11.cloned.1.call-update) | async-done | bytes 33554448 | tf_op jit(solution)/shard_map/all_gather | solution.py:135
  2128.1 34.0 convert_reduce_fusion
  2162.1 16.6 convolution_convert_fusion.1
  2178.8 16.1 convolution_convert_fusion
  2195.0 17.3 fusion.98
  2212.4 15.2 fusion.96
  2237.4 43.8 %reduce-scatter.7.cloned.1.call-done = bf16[256,2048]{1,0:T(8,128)(2,1)} async-done(((bf16[2048,2048]{1,0:T(8,128)(2,1)}), bf16[256,2048]{1,0:T(8,128)(2,1)}) %reduce-scatter.7.cloned.1.call-update) | async-done | bytes 1048592 | tf_op jit(solution)/shard_map/reduce_scatter | solution.py:291
  2281.2 407.1 %reduce-scatter.5.cloned.1.call-done = bf16[256,6144]{1,0:T(8,128)(2,1)} async-done(((bf16[2048,6144]{1,0:T(8,128)(2,1)}), bf16[256,6144]{1,0:T(8,128)(2,1)}) %reduce-scatter.5.cloned.1.call-update) | async-done | bytes 3145744 | tf_op jit(solution)/shard_map/reduce_scatter | solution.py:285
  2688.3 546.3 %reduce-scatter.9.cloned.1.call-done = bf16[256,8192]{1,0:T(8,128)(2,1)} async-done(((bf16[2048,8192]{1,0:T(8,128)(2,1)}), bf16[256,8192]{1,0:T(8,128)(2,1)}) %reduce-scatter.9.cloned.1.call-update) | async-done | bytes 4194320 | tf_op jit(solution)/shard_map/reduce_scatter | solution.py:297
  3234.6 546.6 %reduce-scatter.11.cloned.1.call-done = bf16[1024,2048]{1,0:T(8,128)(2,1)} async-done(((bf16[8192,2048]{1,0:T(8,128)(2,1)}), bf16[1024,2048]{1,0:T(8,128)(2,1)}) %reduce-scatter.11.cloned.1.call-update) | async-done | bytes 4194320 | tf_op jit(solution)/shard_map/reduce_scatter | solution.py:303
  3789.7 17.4 fusion.31
  3810.5 102.4 %all-reduce.11.cloned.1.call-done = (f32[2048]{0:T(1024)}, f32[2048]{0:T(1024)}, f32[2048]{0:T(1024)}, f32[2048]{0:T(1024)}, f32[6144]{0:T(1024)}, /*index=5*/f32[2048]{0:T(1024)}, f32[8192]{0:T(1024)}) async-done(((f32[2048]{0:T(1024)}, f32[2048]{0:T(1024)}, f32[2048]{0:T(1024)}, f32[2048]{0:T(1024)}, f32[6144]{0:T(1024)}, /*index=5*/f32[2048]{0:T(1024)}, f32[8192]{0:T(1024)}), (f32[2048]{0:T(1024)}, ...) | async-done | bytes 98320 | tf_op jit(solution)/shard_map/psum | solution.py:316
  3912.9 225.3 %all-reduce.13.cloned.1.call-done = (bf16[256,6144]{1,0:T(8,128)(2,1)}, bf16[256,2048]{1,0:T(8,128)(2,1)}, bf16[256,8192]{1,0:T(8,128)(2,1)}, bf16[1024,2048]{1,0:T(8,128)(2,1)}) async-done(((bf16[256,6144]{1,0:T(8,128)(2,1)}, bf16[256,2048]{1,0:T(8,128)(2,1)}, bf16[256,8192]{1,0:T(8,128)(2,1)}, bf16[1024,2048]{1,0:T(8,128)(2,1)}), (bf16[256,6144]{1,0:T(8,128)(2,1)}, bf16[256,2048]{1,0:T(8,128)(2,1)}, ...) | async-done | bytes 12582928 | tf_op jit(solution)/shard_map/psum | solution.py:310
  (232 shorter events, 204.2 us)
Async XLA Ops:
  7.2 485.5 %all-gather.5.cloned.1.call-start = ((), (), s32[]{:S(2)}) async-start(), calls=%async_computation.8 | async-start | bytes 28311552 | tf_op jit(solution)/shard_map/all_gather | solution.py:130
  7.9 732.2 %all-gather.7.cloned.1.call-start = ((), (), s32[]{:S(2)}) async-start(), calls=%async_computation.9 | async-start | bytes 9437184 | tf_op jit(solution)/shard_map/all_gather | solution.py:131
  8.7 1480.3 %all-gather.9.cloned.1.call-start = ((), (), s32[]{:S(2)}) async-start(), calls=%async_computation.10 | async-start | bytes 37748736 | tf_op jit(solution)/shard_map/all_gather | solution.py:134
  9.4 483.3 %copy-start.31 = (f32[2048]{0:T(1024)S(1)}, f32[2048]{0:T(1024)}, u32[]{:S(2)}) copy-start(f32[2048]{0:T(1024)} %param.20) | copy-start | bytes 24580
  9.4 483.3 %copy-start.38 = (f32[2048]{0:T(1024)S(1)}, f32[2048]{0:T(1024)}, u32[]{:S(2)}) copy-start(f32[2048]{0:T(1024)} %param.21) | copy-start | bytes 24580
  9.5 483.3 %copy-start.53 = (f32[6144]{0:T(1024)S(1)}, f32[6144]{0:T(1024)}, u32[]{:S(2)}) copy-start(f32[6144]{0:T(1024)} %param.25) | copy-start | bytes 73732
  9.5 2118.7 %all-gather.11.cloned.1.call-start = ((), (), s32[]{:S(2)}) async-start(), calls=%async_computation.11 | async-start | bytes 37748736 | tf_op jit(solution)/shard_map/all_gather | solution.py:135
  11.8 492.9 %copy-start.34 = (f32[256]{0:T(256)}, f32[256]{0:T(256)S(1)}, u32[]{:S(2)}) copy-start(f32[256]{0:T(256)S(1)} %broadcast_multiply_fusion) | copy-start | bytes 3076
  12.3 492.5 %copy-start.43 = (f32[256]{0:T(256)}, f32[256]{0:T(256)S(1)}, u32[]{:S(2)}) copy-start(f32[256]{0:T(256)S(1)} %fusion.38) | copy-start | bytes 3076
  12.3 492.5 %copy-start.36 = (f32[256]{0:T(256)}, f32[256]{0:T(256)S(1)}, u32[]{:S(2)}) copy-start(f32[256]{0:T(256)S(1)} %fusion.71) | copy-start | bytes 3076
  523.1 217.0 %copy-start.4 = (bf16[256,1,2048]{2,0,1:T(8,128)(2,1)S(1)}, bf16[256,1,2048]{2,0,1:T(8,128)(2,1)}, u32[]{:S(2)}) copy-start(bf16[256,1,2048]{2,0,1:T(8,128)(2,1)} %param.17) | copy-start | bytes 3145732
  523.1 232.0 %all-to-all-start = ((bf16[8,60,6144]{2,1,0:T(8,128)(2,1)}), bf16[8,60,6144]{2,1,0:T(8,128)(2,1)}, u32[]{:S(2)}, u32[]{:S(2)}) async-start(bf16[8,60,6144]{2,1,0:T(8,128)(2,1)} %broadcast_select_fusion), calls=%async_computation | async-start | bytes 12582912 | tf_op jit(solution)/shard_map/all_to_all | solution.py:144
  533.1 246.5 %copy-start.19 = (pred[480,480]{0,1:T(8,128)(4,1)}, pred[480,480]{0,1:T(8,128)(4,1)S(1)}, u32[]{:S(2)}) copy-start(pred[480,480]{0,1:T(8,128)(4,1)S(1)} %compare_and_fusion) | copy-start | bytes 691204
  755.1 76.4 %all-to-all-start.2 = ((bf16[8,60,2048]{2,1,0:T(8,128)(2,1)}), bf16[8,60,2048]{2,1,0:T(8,128)(2,1)}, u32[]{:S(2)}, u32[]{:S(2)}) async-start(bf16[8,60,2048]{2,1,0:T(8,128)(2,1)} %select_select_fusion), calls=%async_computation.2 | async-start | bytes 4194304 | tf_op jit(solution)/shard_map/all_to_all | solution.py:219
  831.6 105.7 %all-to-all-start.1 = ((bf16[8,60,2048]{2,1,0:T(8,128)(2,1)}), bf16[8,60,2048]{2,1,0:T(8,128)(2,1)}, u32[]{:S(2)}, u32[]{:S(2)}) async-start(bf16[8,60,2048]{2,1,0:T(8,128)(2,1)} %reshape.721), calls=%async_computation.1 | async-start | bytes 4194304 | tf_op jit(solution)/shard_map/all_to_all | solution.py:193
  867.9 1413.3 %reduce-scatter.7.cloned.1.call-start = ((), (), s32[]{:S(2)}) async-start(), calls=%async_computation.13 | async-start | bytes 9437184 | tf_op jit(solution)/shard_map/reduce_scatter | solution.py:291
  948.8 1739.5 %reduce-scatter.5.cloned.1.call-start = ((), (), s32[]{:S(2)}) async-start(), calls=%async_computation.12 | async-start | bytes 28311552 | tf_op jit(solution)/shard_map/reduce_scatter | solution.py:285
  1242.2 246.8 %copy-start.29 = (f32[2048]{0:T(1024)S(1)}, f32[2048]{0:T(1024)}, u32[]{:S(2)}) copy-start(f32[2048]{0:T(1024)} %param.22) | copy-start | bytes 24580
  1242.2 246.8 %copy-start.30 = (f32[2048]{0:T(1024)S(1)}, f32[2048]{0:T(1024)}, u32[]{:S(2)}) copy-start(f32[2048]{0:T(1024)} %param.23) | copy-start | bytes 24580
  1242.2 246.8 %copy-start.52 = (f32[8192]{0:T(1024)S(1)}, f32[8192]{0:T(1024)}, u32[]{:S(2)}) copy-start(f32[8192]{0:T(1024)} %param.29) | copy-start | bytes 98308
  1242.3 1992.3 %reduce-scatter.9.cloned.1.call-start = ((), (), s32[]{:S(2)}) async-start(), calls=%async_computation.14 | async-start | bytes 37748736 | tf_op jit(solution)/shard_map/reduce_scatter | solution.py:297
  2178.8 1602.4 %reduce-scatter.11.cloned.1.call-start = ((), (), s32[]{:S(2)}) async-start(), calls=%async_computation.15 | async-start | bytes 37748736 | tf_op jit(solution)/shard_map/reduce_scatter | solution.py:303
  2195.0 1718.0 %all-reduce.11.cloned.1.call-start = ((), (), s32[]{:S(2)}) async-start(), calls=%async_computation.16 | async-start | bytes 196608 | tf_op jit(solution)/shard_map/psum | solution.py:316
  2237.3 1900.9 %all-reduce.13.cloned.1.call-start = ((), (), s32[]{:S(2)}) async-start(), calls=%async_computation.17 | async-start | bytes 25165824 | tf_op jit(solution)/shard_map/psum | solution.py:310
  (46 other events, 284.0 us)
Sparse Core Ops, SparseCore 0:
  9.5 483.1 all-gather.4
  494.8 245.2 all-gather.6
  741.6 747.3 all-gather.8
  1490.4 637.6 all-gather.10
  2132.2 148.9 reduce-scatter.6
  2285.4 402.7 reduce-scatter.4
  2692.5 542.0 reduce-scatter.8
  3238.8 542.2 reduce-scatter.10
  3789.9 122.9 all-reduce.10
  3915.5 222.7 all-reduce.12
where the time goes:
time: 4170 us
  waiting for transfers between devices  3510 us (84%)
  matrix products  231 us (6%)
  blocking collectives  211 us (5%)
  local copies, waits for them, and re-layouts  87.9 us (2%)
  other arithmetic  61.4 us (1%)
  starting transfers between devices  46.6 us (1%)
    all_gather x1, waiting for transfers between devices, shards(): lax.all_gather(w_down, 'shard', axis=0, tiled=True)  607 us
    reduce_scatter x1, waiting for transfers between devices, shards(): lax.psum_scatter(row_product(activated, grad_out).astype(jnp.bfloat16), '...  547 us
    reduce_scatter x1, waiting for transfers between devices, shards(): lax.psum_scatter(row_product(normed_two, grad_pre).astype(jnp.bfloat16),...  546 us
    all_gather x1, waiting for transfers between devices, shards(): lax.all_gather(w_qkv, 'shard', axis=0, tiled=True)  480 us
    reduce_scatter x1, waiting for transfers between devices, shards(): lax.psum_scatter(row_product(normed_one, grad_qkv).astype(jnp.bfloat16),...  407 us
    all_gather x1, waiting for transfers between devices, shards(): lax.all_gather(w_up, 'shard', axis=0, tiled=True)  247 us
    psum x1, waiting for transfers between devices, shards(): lax.psum(qkv_rows.astype(jnp.bfloat16), 'rep').astype(jnp.float32)  225 us
    all_to_all x1, blocking collectives, shards(): lax.all_to_all(grad_qkv_slots, 'shard', split_axis=0, concat_axis=0, tile...  211 us
  transfers between devices with their start and end apart: 13, of which 12 were waited for; matrix products, arithmetic and copies ran while one was open for 9% of the time, Pallas kernels for 0%

commit v1 on v0

--- a/solution.py
+++ b/solution.py
@@ -1,8 +1,11 @@
+import functools
 import math
 
 import jax
 import jax.numpy as jnp
 from jax import lax
+from jax.experimental import pallas as pl
+from jax.experimental.pallas import tpu as pltpu
 from jax.sharding import PartitionSpec as P
 
 HEADS = 8
@@ -343,6 +346,524 @@
     )
 
 
+TILE_ROWS = 32
+F32 = jnp.float32
+BF16 = jnp.bfloat16
+
+
+def flip(value, axis, bit):
+    size = lax.axis_size(axis)
+    return lax.ppermute(value, axis, [(i, i ^ bit) for i in range(size)])
+
+
+def send(value, pairs):
+    return lax.ppermute(value, "shard", [(2 * a + y, 2 * b + y) for a, b in pairs for y in (0, 1)])
+
+
+MIDDLE = ((1, 2), (2, 1))
+OUTWARD = ((1, 0), (2, 3))
+INWARD = ((0, 1), (3, 2))
+
+
+def plus(*terms):
+    total = terms[0].astype(F32)
+    for term in terms[1:]:
+        total = total + term.astype(F32)
+    return total
+
+
+def gather_blocks(own, is_middle):
+    near = flip(own, "shard", 2)
+    across = send(own, MIDDLE)
+    across_near = send(near, MIDDLE)
+    two = jnp.where(is_middle, across_near, send(across, OUTWARD))
+    three = jnp.where(is_middle, across, send(across_near, OUTWARD))
+    mine = [own, near, two, three]
+    return mine + [flip(block, "shard", 1) for block in mine]
+
+
+def scatter_sum(blocks):
+    three = plus(blocks[3], flip(blocks[7], "shard", 1)).astype(BF16)
+    from_corner = send(three, INWARD)
+    two = plus(blocks[2], flip(blocks[6], "shard", 1), from_corner).astype(BF16)
+    across_near = send(two, MIDDLE)
+    across = send(two, INWARD)
+    one = plus(blocks[1], flip(blocks[5], "shard", 1), across_near).astype(BF16)
+    three = plus(three, across).astype(BF16)
+    return plus(
+        blocks[0], flip(blocks[4], "shard", 1), flip(one, "shard", 2), send(three, MIDDLE)
+    )
+
+
+def turn(heads_in, cosine, sine):
+    left = heads_in[:, :128]
+    lane = lax.broadcasted_iota(jnp.int32, left.shape, 1)
+    half = ROT // 2
+    partner = jnp.where(lane < half, pltpu.roll(left, 128 - half, 1), pltpu.roll(left, half, 1))
+    return jnp.concatenate([left * cosine + partner * sine, heads_in[:, 128:]], axis=1)
+
+
+def token_labels(my_index, shape, dim):
+    inner = lax.broadcasted_iota(jnp.int32, shape, dim)
+    block = inner // TILE_ROWS
+    apart = (block % 4) * 2 + block // 4
+    return (inner % TILE_ROWS) * HEADS + jnp.bitwise_xor(apart, my_index)
+
+
+def tile_weights(tile, seq_ref, query, key_tiles, count):
+    tile_tokens = TILE_ROWS * HEADS
+    my_index = seq_ref[count]
+    query_label = token_labels(my_index, (tile_tokens, 1), 0) + tile * tile_tokens
+    key_label = token_labels(my_index, (1, tile_tokens), 1)
+    scores = []
+    for place, key in key_tiles:
+        label = key_label + place * tile_tokens
+        last = jnp.full(label.shape, 1 << 30, jnp.int32)
+        for k in range(count):
+            last = jnp.minimum(last, jnp.where(label < seq_ref[k], seq_ref[k], 1 << 30))
+        allowed = query_label < last
+        if place == tile:
+            allowed = allowed & (label <= query_label)
+        product = lax.dot_general(query, key, (((1,), (1,)), ((), ())), preferred_element_type=F32)
+        scores.append(jnp.where(allowed, product * HEAD ** (-0.5), MASKED))
+    scores = jnp.concatenate(scores, axis=1)
+    exp_scores = jnp.exp(scores - jnp.max(scores, axis=1, keepdims=True))
+    return exp_scores * (1.0 / jnp.sum(exp_scores, axis=1, keepdims=True))
+
+
+def attend_kernel(seq_ref, qkv_ref, cos_ref, sin_ref, out_ref, query_ref, key_ref):
+    tiles = query_ref.shape[0]
+    tile_tokens = TILE_ROWS * HEADS
+
+    def part(tile, lane):
+        rows = qkv_ref[:, tile * TILE_ROWS : (tile + 1) * TILE_ROWS, lane : lane + HEAD]
+        return rows.reshape(tile_tokens, HEAD)
+
+    for tile in range(tiles):
+        cosine, sine = cos_ref[tile], sin_ref[tile]
+        query = turn(part(tile, 0).astype(F32), cosine, sine).astype(BF16)
+        query_ref[tile] = query
+        key_ref[tile] = turn(part(tile, HEAD).astype(F32), cosine, sine).astype(BF16)
+        near = list(range(max(tile - 2, 0), tile + 1))
+        probs = tile_weights(
+            tile, seq_ref, query, [(k, key_ref[k]) for k in near], seq_ref.shape[0] - 1
+        ).astype(BF16)
+        total = jnp.zeros((tile_tokens, HEAD), F32)
+        for at, k in enumerate(near):
+            total = total + jnp.dot(
+                probs[:, at * tile_tokens : (at + 1) * tile_tokens],
+                part(k, 2 * HEAD),
+                preferred_element_type=F32,
+            )
+        out_ref[:, tile * TILE_ROWS : (tile + 1) * TILE_ROWS, :] = total.astype(BF16).reshape(
+            HEADS, TILE_ROWS, HEAD
+        )
+
+
+def attend_back_kernel(
+    seq_ref, qkv_ref, grad_ref, cos_ref, sin_ref, query_ref, key_ref, out_ref, sum_ref, gk_ref, gv_ref
+):
+    tiles = query_ref.shape[0]
+    tile_tokens = TILE_ROWS * HEADS
+    scale = HEAD ** (-0.5)
+    over_rows = (((0,), (0,)), ((), ()))
+    over_lanes = (((1,), (1,)), ((), ()))
+
+    def rows_of(tile):
+        return slice(tile * TILE_ROWS, (tile + 1) * TILE_ROWS)
+
+    def put(tile, lane, value):
+        low = value.astype(BF16)
+        out_ref[:, rows_of(tile), lane : lane + HEAD] = low.reshape(HEADS, TILE_ROWS, HEAD)
+        columns = jnp.sum(low.astype(F32), axis=0, keepdims=True)
+        if tile == 0:
+            sum_ref[:, lane : lane + HEAD] = columns
+        else:
+            sum_ref[:, lane : lane + HEAD] += columns
+
+    def finish(tile):
+        put(tile, HEAD, turn(gk_ref[tile] * scale, cos_ref[tile], -sin_ref[tile]))
+        put(tile, 2 * HEAD, gv_ref[tile])
+
+    for tile in range(tiles):
+        query = query_ref[tile]
+        near = list(range(max(tile - 2, 0), tile + 1))
+        grad = grad_ref[:, rows_of(tile), :].reshape(tile_tokens, HEAD)
+        probs = tile_weights(
+            tile, seq_ref, query, [(k, key_ref[k]) for k in near], seq_ref.shape[0] - 1
+        )
+        grad_probs = jnp.concatenate(
+            [
+                lax.dot_general(
+                    grad,
+                    qkv_ref[:, rows_of(k), 2 * HEAD :].reshape(tile_tokens, HEAD),
+                    over_lanes,
+                    preferred_element_type=F32,
+                )
+                for k in near
+            ],
+            axis=1,
+        )
+        delta = jnp.sum(probs * grad_probs, axis=1, keepdims=True)
+        grad_scores = (probs * (grad_probs - delta)).astype(BF16)
+        probs = probs.astype(BF16)
+        grad_query = jnp.zeros((tile_tokens, HEAD), F32)
+        for at, k in enumerate(near):
+            span = slice(at * tile_tokens, (at + 1) * tile_tokens)
+            grad_query = grad_query + jnp.dot(
+                grad_scores[:, span], key_ref[k], preferred_element_type=F32
+            )
+            to_key = lax.dot_general(
+                grad_scores[:, span], query, over_rows, preferred_element_type=F32
+            )
+            to_value = lax.dot_general(probs[:, span], grad, over_rows, preferred_element_type=F32)
+            if k == tile:
+                gk_ref[k] = to_key
+                gv_ref[k] = to_value
+            else:
+                gk_ref[k] += to_key
+                gv_ref[k] += to_value
+        put(tile, 0, turn(grad_query * scale, cos_ref[tile], -sin_ref[tile]))
+        if tile >= 2:
+            finish(tile - 2)
+    for tile in range(max(tiles - 2, 0), tiles):
+        finish(tile)
+
+
+VMEM_SPEC = pl.BlockSpec(memory_space=pltpu.VMEM)
+SMEM_SPEC = pl.BlockSpec(memory_space=pltpu.SMEM)
+
+
+def attend(seq_scalars, qkv, cosine, sine):
+    blocks, rows, _ = qkv.shape
+    tiled = (rows // TILE_ROWS, blocks * TILE_ROWS, HEAD)
+    return pl.pallas_call(
+        attend_kernel,
+        out_shape=(
+            jax.ShapeDtypeStruct((blocks, rows, HEAD), BF16),
+            jax.ShapeDtypeStruct(tiled, BF16),
+            jax.ShapeDtypeStruct(tiled, BF16),
+        ),
+        in_specs=[SMEM_SPEC, VMEM_SPEC, VMEM_SPEC, VMEM_SPEC],
+        out_specs=(VMEM_SPEC, VMEM_SPEC, VMEM_SPEC),
+        compiler_params=pltpu.CompilerParams(vmem_limit_bytes=48 << 20),
+        cost_estimate=pl.CostEstimate(
+            flops=4 * blocks * rows * 768 * HEAD, bytes_accessed=10 << 20, transcendentals=0
+        ),
+    )(seq_scalars, qkv, cosine, sine)
+
+
+def attend_back(seq_scalars, qkv, grad, cosine, sine, query, key):
+    blocks, rows, wide = qkv.shape
+    return pl.pallas_call(
+        attend_back_kernel,
+        out_shape=(
+            jax.ShapeDtypeStruct((blocks, rows, wide), BF16),
+            jax.ShapeDtypeStruct((1, wide), F32),
+        ),
+        in_specs=[SMEM_SPEC] + [VMEM_SPEC] * 6,
+        out_specs=(VMEM_SPEC, VMEM_SPEC),
+        scratch_shapes=[pltpu.VMEM(query.shape, F32), pltpu.VMEM(query.shape, F32)],
+        compiler_params=pltpu.CompilerParams(vmem_limit_bytes=48 << 20),
+        cost_estimate=pl.CostEstimate(
+            flops=10 * blocks * rows * 768 * HEAD, bytes_accessed=12 << 20, transcendentals=0
+        ),
+    )(seq_scalars, qkv, grad, cosine, sine, query, key)
+
+
+def place_weights_kernel(order_ref, part_ref, gain_ref, shift_ref, raw_ref, scaled_ref, sum_ref, *, hidden):
+    raw = part_ref[0]
+    raw_ref[...] = raw
+    weight = raw.astype(F32)
+    lane = lax.broadcasted_iota(jnp.int32, weight.shape, 1)
+    gain = jnp.where(lane < hidden, gain_ref[:, 1:2], gain_ref[:, 0:1])
+    shift = jnp.where(lane < hidden, shift_ref[:, 1:2], shift_ref[:, 0:1])
+    scaled_ref[...] = (weight * gain).astype(BF16)
+    share = jnp.sum(weight * shift, axis=0, keepdims=True)
+
+    @pl.when(pl.program_id(0) == 0)
+    def _():
+        sum_ref[...] = share
+
+    @pl.when(pl.program_id(0) > 0)
+    def _():
+        sum_ref[...] += share
+
+
+def place_weights(order, parts, gains, shifts, hidden):
+    count, rows, wide = parts.shape
+    whole = jax.ShapeDtypeStruct((count * rows, wide), BF16)
+    by_row = pl.BlockSpec((rows, wide), lambda i, order_ref: (i, 0))
+    pair = pl.BlockSpec((rows, 2), lambda i, order_ref: (i, 0))
+    return pl.pallas_call(
+        functools.partial(place_weights_kernel, hidden=hidden),
+        out_shape=(whole, whole, jax.ShapeDtypeStruct((1, wide), F32)),
+        grid_spec=pltpu.PrefetchScalarGridSpec(
+            num_scalar_prefetch=1,
+            grid=(count,),
+            in_specs=[
+                pl.BlockSpec((1, rows, wide), lambda i, order_ref: (order_ref[i], 0, 0)),
+                pair,
+                pair,
+            ],
+            out_specs=(by_row, by_row, pl.BlockSpec((1, wide), lambda i, order_ref: (0, 0))),
+        ),
+        cost_estimate=pl.CostEstimate(
+            flops=4 * count * rows * wide, bytes_accessed=6 * count * rows * wide, transcendentals=0
+        ),
+    )(order, parts, gains, shifts)
+
+
+def place_grads_kernel(order_ref, part_ref, up_ref, qkv_ref, *, hidden):
+    values = part_ref[0].astype(F32)
+    up_ref[...] = values[:, :hidden]
+    third = qkv_ref.shape[1] // 3
+    for k in range(3):
+        start = pl.multiple_of(k * third + pl.program_id(1) * HEAD, HEAD)
+        qkv_ref[:, pl.ds(start, HEAD)] = values[:, hidden + k * HEAD : hidden + (k + 1) * HEAD]
+
+
+def place_grads(order, parts, hidden):
+    count, rows, wide = parts.shape
+    depth = count // HEADS * rows
+    return pl.pallas_call(
+        functools.partial(place_grads_kernel, hidden=hidden),
+        out_shape=(
+            jax.ShapeDtypeStruct((depth, HEADS * hidden), F32),
+            jax.ShapeDtypeStruct((depth, 3 * HEADS * HEAD), F32),
+        ),
+        grid_spec=pltpu.PrefetchScalarGridSpec(
+            num_scalar_prefetch=1,
+            grid=(count // HEADS, HEADS),
+            in_specs=[
+                pl.BlockSpec(
+                    (1, rows, wide), lambda q, s, order_ref: (order_ref[s * 4 + q], 0, 0)
+                )
+            ],
+            out_specs=(
+                pl.BlockSpec((rows, hidden), lambda q, s, order_ref: (q, s)),
+                pl.BlockSpec((rows, 3 * HEADS * HEAD), lambda q, s, order_ref: (q, 0)),
+            ),
+        ),
+        cost_estimate=pl.CostEstimate(
+            flops=0, bytes_accessed=6 * count * rows * wide, transcendentals=0
+        ),
+    )(order, parts)
+
+
+def dot32(left, right, left_dim=1, right_dim=0):
+    return lax.dot_general(
+        left, right, (((left_dim,), (right_dim,)), ((), ())), preferred_element_type=F32
+    )
+
+
+def split_shards(
+    tokens,
+    cotangent,
+    seq_lengths,
+    seq_order,
+    ln1_gain,
+    ln1_bias,
+    ln2_gain,
+    ln2_bias,
+    w_qkv,
+    b_qkv,
+    w_dense,
+    b_dense,
+    w_up,
+    b_up,
+    w_down,
+    b_down,
+):
+    me = lax.axis_index("shard")
+    rep = lax.axis_index("rep")
+    place = me // 2
+    is_middle = (place == 1) | (place == 2)
+    own = tokens[:, 0, :]
+    own_grad = cotangent[:, 0, :]
+    rows, width = own.shape
+    group_tokens = rows * HEADS
+    depth = w_up.shape[0]
+    hidden = w_down.shape[0]
+    wide = hidden + 3 * HEAD
+    quarter = depth // 4
+
+    up_rows = lax.dynamic_slice_in_dim(w_up, rep * quarter, quarter, 0)
+    qkv_rows = lax.dynamic_slice_in_dim(w_qkv, rep * quarter, quarter, 0)
+
+    def columns_for(target):
+        pieces = [lax.dynamic_slice_in_dim(up_rows, target * hidden, hidden, 1)]
+        for k in range(3):
+            pieces.append(
+                lax.dynamic_slice_in_dim(qkv_rows, k * width + target * HEAD, HEAD, 1)
+            )
+        return jnp.concatenate(pieces, axis=1)
+
+    keep = [columns_for(me ^ (2 * z)) for z in range(4)]
+    moved = flip(jnp.stack([columns_for(me ^ (2 * z + 1)) for z in range(4)]), "shard", 1)
+    pairs = [jnp.stack([keep[z], moved[z]]) for z in range(4)]
+    for z in range(1, 4):
+        pairs[z] = flip(pairs[z], "shard", 2 * z)
+    part = jnp.stack(pairs)
+    part = jnp.stack([part, flip(part, "rep", 2)])
+    part = jnp.stack([part, flip(part, "rep", 1)], axis=1)
+    from_shard = jnp.arange(HEADS, dtype=jnp.int32)[:, None] ^ me
+    from_rep = jnp.arange(4, dtype=jnp.int32)[None, :] ^ rep
+    order = (from_rep * HEADS + from_shard).reshape(-1)
+    gains = jnp.stack([ln1_gain, ln2_gain], axis=1)
+    shifts = jnp.stack([ln1_bias, ln2_bias], axis=1)
+    w_in, w_scaled, shifted = place_weights(
+        order, part.reshape(4 * HEADS, quarter, wide), gains, shifts, hidden
+    )
+    is_hidden = jnp.arange(wide, dtype=jnp.int32)[None, :] < hidden
+    gain = jnp.where(is_hidden, ln2_gain[:, None], ln1_gain[:, None])
+    shift = jnp.where(is_hidden, ln2_bias[:, None], ln1_bias[:, None])
+    b_in = jnp.concatenate(
+        [lax.dynamic_slice_in_dim(b_up, me * hidden, hidden, 0)]
+        + [lax.dynamic_slice_in_dim(b_qkv, k * width + me * HEAD, HEAD, 0) for k in range(3)]
+    )
+    b_in = b_in + shifted[0]
+    w_out = jnp.concatenate([w_down, w_dense], axis=0)
+
+    row_offsets, row_counts = stream_rows(seq_lengths[0], seq_order[0], HEADS)
+    ends = (row_offsets + row_counts) * HEADS
+    seq_scalars = jnp.concatenate([ends, me[None]]).astype(jnp.int32)
+    row_range = jnp.arange(rows, dtype=jnp.int32)
+    member = (row_range[:, None] >= row_offsets[None, :]) & (
+        row_range[:, None] < (row_offsets + row_counts)[None, :]
+    )
+    in_seq = row_range - jnp.sum(jnp.where(member, row_offsets[None, :], 0), axis=1)
+    block_range = jnp.arange(HEADS, dtype=jnp.int32)
+    apart = (block_range % 4) * 2 + block_range // 4
+    positions = (
+        in_seq.reshape(rows // TILE_ROWS, 1, TILE_ROWS) * HEADS + (apart ^ me)[None, :, None]
+    )
+    cosine, sine = rotary_tables(positions.reshape(-1).astype(F32))
+    rest = 128 - ROT
+    cosine = jnp.concatenate([cosine, cosine, jnp.ones((group_tokens, rest), F32)], axis=1)
+    sine = jnp.concatenate([-sine, sine, jnp.zeros((group_tokens, rest), F32)], axis=1)
+    tiled = (rows // TILE_ROWS, TILE_ROWS * HEADS, 128)
+    cosine = cosine.reshape(tiled)
+    sine = sine.reshape(tiled)
+
+    stream = jnp.concatenate(gather_blocks(own, is_middle), axis=0)
+    grad_out = jnp.concatenate(gather_blocks(own_grad, is_middle), axis=0)
+
+    def normalize(values):
+        values = values.astype(F32)
+        centered = values - jnp.mean(values, axis=-1, keepdims=True)
+        rstd = lax.rsqrt(jnp.mean(centered * centered, axis=-1, keepdims=True) + EPSILON)
+        return centered * rstd, rstd
+
+    normed = normalize(stream)[0].astype(BF16)
+    qkv = (dot32(normed, w_scaled[:, hidden:]) + b_in[hidden:]).astype(BF16)
+    qkv = qkv.reshape(HEADS, rows, 3 * HEAD)
+    attended, query, key = attend(seq_scalars, qkv, cosine, sine)
+    pre_up = dot32(normed, w_scaled[:, :hidden]) + b_in[:hidden]
+    normal = 0.5 * (1.0 + lax.erf(pre_up * (0.5**0.5)))
+    slope = normal + pre_up * jnp.exp(-0.5 * pre_up * pre_up) * ((2.0 * math.pi) ** -0.5)
+    slope = slope.astype(BF16)
+    activated = (pre_up * normal).astype(BF16)
+    mixed = jnp.concatenate([activated, attended.reshape(group_tokens, HEAD)], axis=1)
+    out_part = dot32(mixed, w_out).astype(BF16).reshape(HEADS, rows, width)
+    out_sum = scatter_sum([out_part[k] for k in range(HEADS)])
+    output = (own.astype(F32) + out_sum + (b_dense + b_down)).astype(BF16)
+
+    grad_mixed = dot32(grad_out, w_out, 1, 1)
+    grad_attended = grad_mixed[:, hidden:].astype(BF16).reshape(HEADS, rows, HEAD)
+    grad_pre = (grad_mixed[:, :hidden] * slope.astype(F32)).astype(BF16)
+    grad_qkv, qkv_columns = attend_back(
+        seq_scalars, qkv, grad_attended, cosine, sine, query, key
+    )
+    grad_in = jnp.concatenate([grad_pre, grad_qkv.reshape(group_tokens, 3 * HEAD)], axis=1)
+    columns = jnp.concatenate([jnp.sum(grad_pre, axis=0, dtype=F32), qkv_columns[0]])
+
+    gy_part = dot32(grad_in, w_scaled, 1, 1).astype(BF16).reshape(HEADS, rows, width)
+    gy = scatter_sum([gy_part[k] for k in range(HEADS)])
+    own_normed, own_rstd = normalize(own)
+    input_grad = own_grad.astype(F32) + own_rstd * (
+        gy
+        - jnp.mean(gy, axis=-1, keepdims=True)
+        - own_normed * jnp.mean(gy * own_normed, axis=-1, keepdims=True)
+    )
+
+    out_grads = dot32(mixed, grad_out, 0, 0).astype(BF16)
+    half_rows = out_grads.shape[0] // 2
+    my_core = rep % 2
+    my_side = rep // 2
+    halves = out_grads.reshape(2, half_rows, width)
+    half = plus(
+        lax.dynamic_index_in_dim(halves, my_core, 0, False),
+        flip(lax.dynamic_index_in_dim(halves, 1 - my_core, 0, False), "rep", 1),
+    ).astype(BF16)
+    half = plus(half, flip(half, "rep", 2)).astype(BF16)
+    other = flip(half, "rep", 1)
+    first = jnp.where(my_core == 0, half, other)
+    second = jnp.where(my_core == 0, other, half)
+    out_grads = jnp.concatenate([first, second], axis=0).astype(F32)
+
+    moments = dot32(normed, grad_in, 0, 0)
+    w_wide = w_in.astype(F32)
+    gain_terms = moments * w_wide
+    bias_terms = w_wide * columns[None, :]
+    in_grads = (moments * gain + shift * columns[None, :]).astype(BF16)
+    in_grads = in_grads.reshape(HEADS, 2, 2, quarter, wide)
+    summed = plus(
+        lax.dynamic_index_in_dim(in_grads, my_core, 2, False),
+        flip(lax.dynamic_index_in_dim(in_grads, 1 - my_core, 2, False), "rep", 1),
+    ).astype(BF16)
+    summed = plus(
+        lax.dynamic_index_in_dim(summed, my_side, 1, False),
+        flip(lax.dynamic_index_in_dim(summed, 1 - my_side, 1, False), "rep", 2),
+    ).astype(BF16)
+    summed = summed.reshape(4, 2, quarter, wide)
+    my_row = me % 2
+    keep_half = lax.dynamic_index_in_dim(summed, my_row, 1, False)
+    got_half = flip(lax.dynamic_index_in_dim(summed, 1 - my_row, 1, False), "shard", 1)
+    both = jnp.stack([keep_half, got_half], axis=1)
+    came = []
+    for z in range(4):
+        piece = lax.dynamic_index_in_dim(both, place ^ z, 0, False)
+        came.append(piece if z == 0 else flip(piece, "shard", 2 * z))
+    came = jnp.stack(came)
+    came = jnp.stack([came, flip(came, "rep", 2)])
+    came = jnp.stack([came, flip(came, "rep", 1)], axis=1)
+    up_grad, qkv_grad = place_grads(order, came.reshape(4 * HEADS, quarter, wide), hidden)
+
+    small = jnp.concatenate(
+        [
+            jnp.sum(gain_terms[:, hidden:], axis=1),
+            jnp.sum(bias_terms[:, hidden:], axis=1),
+            jnp.sum(gain_terms[:, :hidden], axis=1),
+            jnp.sum(bias_terms[:, :hidden], axis=1),
+            jnp.sum(own_grad, axis=0, dtype=F32),
+            jnp.where(block_range[:, None] == me, columns[None, :], 0.0).reshape(-1),
+        ]
+    )
+    for axis, bit in (("rep", 1), ("shard", 1), ("shard", 2), ("shard", 4), ("rep", 2)):
+        small = small + flip(small, axis, bit)
+    vectors = small[: 5 * width].reshape(5, width)
+    slots = small[5 * width :].reshape(HEADS, wide)
+    b_up_grad = slots[:, :hidden].reshape(-1)
+    b_qkv_grad = slots[:, hidden:].reshape(HEADS, 3, HEAD).transpose(1, 0, 2).reshape(-1)
+    return (
+        output[:, None, :],
+        input_grad[:, None, :],
+        vectors[0],
+        vectors[1],
+        vectors[2],
+        vectors[3],
+        qkv_grad,
+        b_qkv_grad,
+        out_grads[hidden:],
+        vectors[4],
+        up_grad,
+        b_up_grad,
+        out_grads[:hidden],
+        vectors[4],
+    )
+
+
 def solution(mesh):
     in_specs = (
         P("rep", "shard", None),
@@ -378,4 +899,7 @@
         P("shard", None),
         P(),
     )
-    return jax.shard_map(shards, mesh=mesh, in_specs=in_specs, out_specs=out_specs, check_vma=False)
+    body = split_shards if mesh.shape["shard"] == HEADS else shards
+    return jax.shard_map(
+        body, mesh=mesh, in_specs=in_specs, out_specs=out_specs, check_vma=False
+    )

time: 4170 us -> 820 us (0.20)
  waiting for transfers between devices: 3510 us -> 328 us
  blocking collectives: 211 us -> 0 us
  matrix products: 231 us -> 127 us
  Pallas kernels: 0 us -> 64.8 us
  starting transfers between devices: 46.6 us -> 99.6 us
    reduce_scatter x4 -> x0, waiting for transfers between devices: 1540 us -> none  [the longest x1 547 us: shards(): lax.psum_scatter(row_product(activated, grad_out).astype(jnp.bfloat16), '...]
    all_gather x4 -> x0, waiting for transfers between devices: 1540 us -> none  [the longest x1 607 us: shards(): lax.all_gather(w_down, 'shard', axis=0, tiled=True)]
    psum x2 -> x0, waiting for transfers between devices: 328 us -> none  [the longest x1 225 us: shards(): lax.psum(qkv_rows.astype(jnp.bfloat16), 'rep').astype(jnp.float32)]
    ppermute x0 -> x58, waiting for transfers between devices: none -> 328 us  [the longest x42 279 us: flip(): return lax.ppermute(value, axis, [(i, i ^ bit) for i in range(size)])]
    all_to_all x1 -> x0, blocking collectives: 211 us -> none  [shards(): lax.all_to_all(grad_qkv_slots, 'shard', split_axis=0, concat_axis=0, tile...]
    dot_general x18 -> x7, matrix products: 231 us -> 127 us  [dot32(): lax.dot_general(left, right, (((left_dim,), (right_dim,)), ((), ())), pre...]
    ppermute x0 -> x58, starting transfers between devices: none -> 99.6 us  [the longest x42 61.6 us: flip(): return lax.ppermute(value, axis, [(i, i ^ bit) for i in range(size)])]
    all_to_all x3 -> x0, waiting for transfers between devices: 97.4 us -> none  [the longest x1 64.2 us: shards(): lax.all_to_all(attended_slots, 'shard', split_axis=0, concat_axis=0, tile...]
  transfers between devices with their start and end apart: 13 -> 58, of which waited for: 12 -> 24; matrix products, arithmetic and copies ran while one was open for 9% -> 27% of each run, Pallas kernels for 0% -> 0%
where the time goes in v1:
time: 820 us; the launch traced here: 810 us
  waiting for transfers between devices  328 us (40%)
  matrix products  127 us (15%)
  other arithmetic  103 us (13%)
  starting transfers between devices  99.6 us (12%)
  local copies, waits for them, and re-layouts  86.1 us (10%)
  Pallas kernels  64.8 us (8%)
    ppermute x42, waiting for transfers between devices, flip(): return lax.ppermute(value, axis, [(i, i ^ bit) for i in range(size)])  279 us
    dot_general x7, matrix products, dot32(): lax.dot_general(left, right, (((left_dim,), (right_dim,)), ((), ())), pre...  127 us
    ppermute x42, starting transfers between devices, flip(): return lax.ppermute(value, axis, [(i, i ^ bit) for i in range(size)])  61.6 us
    ppermute x16, waiting for transfers between devices, send(): lax.ppermute(value, 'shard', [(2 * a + y, 2 * b + y) for a, b in pairs fo...  48.2 us
    unnamed x122, local copies, waits for them, and re-layouts  38.6 us
    ppermute x16, starting transfers between devices, send(): lax.ppermute(value, 'shard', [(2 * a + y, 2 * b + y) for a, b in pairs fo...  38 us
    pallas_call x1, Pallas kernels, place_weights(): pl.pallas_call(functools.partial(place_weights_kernel, hidden=hidden), ou...  23.9 us
    pallas_call x1, Pallas kernels, place_grads(): pl.pallas_call(functools.partial(place_grads_kernel, hidden=hidden), out_...  21.9 us
  transfers between devices with their start and end apart: 58, of which 24 were waited for; matrix products, arithmetic and copies ran while one was open for 27% of the time, Pallas kernels for 0%

profile of v1, /device:TPU:0, one launch (start us, length us, event | category | flops | bytes accessed | tf_op | source)
XLA Modules:
  0.0 810.5 jit_solution(8027684750215590612)
XLA Ops:
  65.2 43.5 %collective-permute-done.11 = bf16[2,64,1792]{2,1,0:T(8,128)(2,1)S(1)} collective-permute-done((bf16[2,64,1792]{2,1,0:T(8,128)(2,1)S(1)}, bf16[2,64,1792]{2,1,0:T(8,128)(2,1)S(1)}, u32[]{:S(2)}, u32[]{:S(2)}) %collective-permute-start.11) | collective-permute-done | bytes 458784 | tf_op jit(solution)/shard_map/ppermute | solution.py:356
  116.8 11.8 %collective-permute-done.3 = bf16[256,2048]{1,0:T(8,128)(2,1)S(1)} collective-permute-done((bf16[256,2048]{1,0:T(8,128)(2,1)}, bf16[256,2048]{1,0:T(8,128)(2,1)S(1)}, u32[]{:S(2)}, u32[]{:S(2)}) %collective-permute-start.3) | collective-permute-done | bytes 1048608 | tf_op jit(solution)/shard_map/ppermute | solution.py:360
  131.9 18.0 %collective-permute-done.28 = bf16[256,2048]{1,0:T(8,128)(2,1)S(1)} collective-permute-done((bf16[256,2048]{1,0:T(8,128)(2,1)S(1)}, bf16[256,2048]{1,0:T(8,128)(2,1)S(1)}, u32[]{:S(2)}, u32[]{:S(2)}) %collective-permute-start.28) | collective-permute-done | bytes 1048608 | tf_op jit(solution)/shard_map/ppermute | solution.py:360
  155.4 27.4 %collective-permute-done.30 = bf16[256,2048]{1,0:T(8,128)(2,1)S(1)} collective-permute-done((bf16[256,2048]{1,0:T(8,128)(2,1)}, bf16[256,2048]{1,0:T(8,128)(2,1)S(1)}, u32[]{:S(2)}, u32[]{:S(2)}) %collective-permute-start.30) | collective-permute-done | bytes 1048608 | tf_op jit(solution)/shard_map/ppermute | solution.py:356
  184.4 20.9 %collective-permute-done.31 = bf16[256,2048]{1,0:T(8,128)(2,1)S(1)} collective-permute-done((bf16[256,2048]{1,0:T(8,128)(2,1)S(1)}, bf16[256,2048]{1,0:T(8,128)(2,1)S(1)}, u32[]{:S(2)}, u32[]{:S(2)}) %collective-permute-start.31) | collective-permute-done | bytes 1048608 | tf_op jit(solution)/shard_map/ppermute | solution.py:356
  211.8 16.0 %collective-permute-done.6 = bf16[256,2048]{1,0:T(8,128)(2,1)S(1)} collective-permute-done((bf16[256,2048]{1,0:T(8,128)(2,1)}, bf16[256,2048]{1,0:T(8,128)(2,1)S(1)}, u32[]{:S(2)}, u32[]{:S(2)}) %collective-permute-start.6) | collective-permute-done | bytes 1048608 | tf_op jit(solution)/shard_map/ppermute | solution.py:356
  228.8 21.4 %collective-permute-done.7 = bf16[256,2048]{1,0:T(8,128)(2,1)S(1)} collective-permute-done((bf16[256,2048]{1,0:T(8,128)(2,1)S(1)}, bf16[256,2048]{1,0:T(8,128)(2,1)S(1)}, u32[]{:S(2)}, u32[]{:S(2)}) %collective-permute-start.7) | collective-permute-done | bytes 1048608 | tf_op jit(solution)/shard_map/ppermute | solution.py:356
  255.1 17.6 %collective-permute-done.32 = bf16[256,2048]{1,0:T(8,128)(2,1)S(1)} collective-permute-done((bf16[256,2048]{1,0:T(8,128)(2,1)S(1)}, bf16[256,2048]{1,0:T(8,128)(2,1)S(1)}, u32[]{:S(2)}, u32[]{:S(2)}) %collective-permute-start.32) | collective-permute-done | bytes 1048608 | tf_op jit(solution)/shard_map/ppermute | solution.py:356
  272.8 17.4 %fusion.64 = f32[2048,1280]{1,0:T(8,128)S(1)} fusion(bf16[2048,2048]{1,0:T(8,128)(2,1)S(1)} %constant_dynamic-update-slice_fusion.10, bf16[1280,2048]{1,0:T(8,128)(2,1)} %constant_dynamic-update-slice_fusion.8), kind=kOutput, calls=%fused_computation.218 | convolution fusion | flops 10737418240 | bytes 24117248 | tf_op jit(solution)/shard_map/dot_general | solution.py:655
  324.1 23.9 %shard_map.263 = (bf16[2048,1792]{1,0:T(8,128)(2,1)}, bf16[2048,1792]{1,0:T(8,128)(2,1)}, f32[1,1792]{1,0:T(1,128)}) custom-call(s32[32]{0:T(128)} %add.542.order_ref, bf16[32,64,1792]{2,1,0:T(8,128)(2,1)} %bitcast.123, f32[2048,2]{1,0:T(8,128)} %copy.58.gain_ref, f32[2048,2]{1,0:T(8,128)} %copy.59.shift_ref), custom_call_target="tpu_custom_call" | custom-call | flops 14680064 | bytes 22020096 | tf_op jit(solution)/shard_map/pallas_call | solution.py:598
  348.9 15.2 %fusion.13 = f32[2048,1024]{0,1:T(8,128)} fusion(bf16[2048,1792]{1,0:T(8,128)(2,1)} %get-tuple-element.24, bf16[2048,2048]{1,0:T(8,128)(2,1)} %constant_dynamic-update-slice_fusion, f32[2048]{0:T(1024)S(1)} %add_rsqrt_fusion, f32[2048]{0:T(1024)S(1)} %broadcast_multiply_fusion), kind=kOutput, calls=%fused_computation.39 | convolution fusion | flops 8606711808 | bytes 20987904 | tf_op jit(solution)/shard_map/dot_general | solution.py:655
  364.1 11.4 %add_convert_fusion.1 = bf16[2048,768]{1,0:T(8,128)(2,1)} fusion(f32[768]{0:T(1024)S(1)} %slice.194, bf16[2048,1792]{1,0:T(8,128)(2,1)} %get-tuple-element.24, bf16[2048,2048]{1,0:T(8,128)(2,1)} %constant_dynamic-update-slice_fusion, f32[2048]{0:T(1024)S(1)} %add_rsqrt_fusion, f32[2048]{0:T(1024)S(1)} %broadcast_multiply_fusion), kind=kOutput, calls=%fused_computation.31 | convolution fusion | flops 6462373888 | bytes 14699520 | tf_op jit(solution)/shard_map/dot_general | solution.py:655
  388.0 10.3 %convert_reduce_fusion.1 = (f32[1024]{0:T(1024)S(1)}, bf16[2048,1024]{0,1:T(8,128)(2,1)}, bf16[2048,1024]{0,1:T(8,128)(2,1)S(1)}) fusion(f32[2048,1024]{0,1:T(8,128)} %copy.67, f32[2048,1024]{0,1:T(8,128)} %fusion.13, f32[1024]{0:T(1024)S(1)} %slice-done.8), kind=kLoop, calls=%fused_computation.17 | loop fusion | flops 35650560 | bytes 25174016 | tf_op jit(solution)/shard_map/reduce_sum | solution.py:779
  398.3 15.3 %convolution_convert_fusion = bf16[1280,2048]{1,0:T(8,128)(2,1)} fusion(bf16[2048,2048]{1,0:T(8,128)(2,1)} %copy-done.21, bf16[2048,256]{0,1:T(8,128)(2,1)S(1)} %copy-done.14, bf16[2048,1024]{0,1:T(8,128)(2,1)S(1)} %get-tuple-element.106), kind=kOutput, calls=%fused_computation.21 | convolution fusion | flops 10750525440 | bytes 18874368 | tf_op jit(solution)/shard_map/dot_general | solution.py:655
  413.6 16.0 %convolution_convert_fusion.1 = bf16[2048,2048]{1,0:T(8,128)(2,1)} fusion(bf16[1280,2048]{1,0:T(8,128)(2,1)} %constant_dynamic-update-slice_fusion.8, bf16[2048,256]{0,1:T(8,128)(2,1)S(1)} %copy-done.14, bf16[2048,1024]{0,1:T(8,128)(2,1)S(1)} %get-tuple-element.106), kind=kOutput, calls=%fused_computation.22 | convolution fusion | flops 10752098304 | bytes 18874368 | tf_op jit(solution)/shard_map/dot_general | solution.py:655
  429.6 11.7 %shard_map.265 = (bf16[8,256,768]{2,1,0:T(8,128)(2,1)}, f32[1,768]{1,0:T(1,128)S(1)}) custom-call(s32[17]{0:T(128)S(1)} %pad_add_fusion.seq_ref, bf16[8,256,768]{2,1,0:T(8,128)(2,1)} %bitcast.164, bf16[8,256,256]{2,1,0:T(8,128)(2,1)S(1)} %bitcast.121, f32[8,256,128]{2,1,0:T(8,128)S(1)} %maximum_maximum_fusion.cos_ref, ...), custom_call_target="tpu_custom_call" | custom-call | flops 4026531840 | bytes 12582912 | tf_op jit(solution)/shard_map/pallas_call | solution.py:558
  456.3 29.5 %add_convert_fusion = (bf16[2048,1792]{1,0:T(8,128)(2,1)}, f32[2048,1792]{1,0:T(8,128)}, f32[2048,1792]{1,0:T(8,128)}) fusion(f32[2048]{0:T(1024)S(1)} %copy-done.37, f32[2048]{0:T(1024)S(1)} %copy-done.35, f32[2048]{0:T(1024)S(1)} %copy-done.33, f32[2048]{0:T(1024)S(1)} %copy-done.31, f32[1792]{0:T(1024)S(1)} %pad_maximum_fusion.19, ...), kind=kOutput, calls=%fused_computation.8 | convolution fusion | flops 15096872960 | bytes 59826944 | tf_op jit(solution)/shard_map/dot_general | solution.py:655
  490.0 22.0 %convolution_convert_fusion.2 = bf16[2048,2048]{1,0:T(8,128)(2,1)} fusion(bf16[2048,1792]{1,0:T(8,128)(2,1)} %get-tuple-element.24, bf16[2048,768]{0,1:T(8,128)(2,1)} %copy.62, bf16[2048,1024]{0,1:T(8,128)(2,1)} %get-tuple-element.93), kind=kOutput, calls=%fused_computation.23 | convolution fusion | flops 15051259904 | bytes 23068672 | tf_op jit(solution)/shard_map/dot_general | solution.py:655
  557.2 16.0 %collective-permute-done.48 = bf16[8,64,1792]{2,1,0:T(8,128)(2,1)S(1)} collective-permute-done((bf16[8,64,1792]{2,1,0:T(8,128)(2,1)S(1)}, bf16[8,64,1792]{2,1,0:T(8,128)(2,1)S(1)}, u32[]{:S(2)}, u32[]{:S(2)}) %collective-permute-start.48) | collective-permute-done | bytes 1835040 | tf_op jit(solution)/shard_map/ppermute | solution.py:356
  587.6 18.5 %collective-permute-done.19 = bf16[256,2048]{1,0:T(8,128)(2,1)S(1)} collective-permute-done((bf16[256,2048]{1,0:T(8,128)(2,1)S(1)}, bf16[256,2048]{1,0:T(8,128)(2,1)S(1)}, u32[]{:S(2)}, u32[]{:S(2)}) %collective-permute-start.19) | collective-permute-done | bytes 1048608 | tf_op jit(solution)/shard_map/ppermute | solution.py:360
  608.9 18.8 %collective-permute-done.49 = bf16[4,64,1792]{2,1,0:T(8,128)(2,1)S(1)} collective-permute-done((bf16[4,64,1792]{2,1,0:T(8,128)(2,1)S(1)}, bf16[4,64,1792]{2,1,0:T(8,128)(2,1)S(1)}, u32[]{:S(2)}, u32[]{:S(2)}) %collective-permute-start.49) | collective-permute-done | bytes 917536 | tf_op jit(solution)/shard_map/ppermute | solution.py:356
  642.4 43.2 %collective-permute-done.51 = bf16[2,64,1792]{2,1,0:T(8,128)(2,1)S(1)} collective-permute-done((bf16[2,64,1792]{2,1,0:T(8,128)(2,1)S(1)}, bf16[2,64,1792]{2,1,0:T(8,128)(2,1)S(1)}, u32[]{:S(2)}, u32[]{:S(2)}) %collective-permute-start.51) | collective-permute-done | bytes 458784 | tf_op jit(solution)/shard_map/ppermute | solution.py:356
  686.0 9.9 %collective-permute-done.52 = bf16[2,64,1792]{2,1,0:T(8,128)(2,1)S(1)} collective-permute-done((bf16[2,64,1792]{2,1,0:T(8,128)(2,1)S(1)}, bf16[2,64,1792]{2,1,0:T(8,128)(2,1)S(1)}, u32[]{:S(2)}, u32[]{:S(2)}) %collective-permute-start.52) | collective-permute-done | bytes 458784 | tf_op jit(solution)/shard_map/ppermute | solution.py:356
  787.5 21.9 %shard_map.266 = (f32[256,8192]{1,0:T(8,128)}, f32[256,6144]{1,0:T(8,128)}) custom-call(s32[32]{0:T(128)} %add.542.order_ref, bf16[32,64,1792]{2,1,0:T(8,128)(2,1)} %bitcast.124), custom_call_target="tpu_custom_call" | custom-call | bytes 22020096 | tf_op jit(solution)/shard_map/pallas_call | solution.py:629
  (355 shorter events, 330.9 us)
Async XLA Ops:
  0.7 46.8 %collective-permute-start.26 = (bf16[256,2048]{1,0:T(8,128)(2,1)}, bf16[256,2048]{1,0:T(8,128)(2,1)}, u32[]{:S(2)}, u32[]{:S(2)}) collective-permute-start(bf16[256,2048]{1,0:T(8,128)(2,1)} %bitcast.139), channel_id=1, source_target_pairs={{2,4},{3,5},{4,2},{5,3},{10,12},{11,13},{12,10},{13,11},{18,20},{1... | collective-permute-start | bytes 3145736 | tf_op jit(solution)/shard_map/ppermute | solution.py:360
  9.1 47.0 %collective-permute-start = (bf16[256,2048]{1,0:T(8,128)(2,1)}, bf16[256,2048]{1,0:T(8,128)(2,1)}, u32[]{:S(2)}, u32[]{:S(2)}) collective-permute-start(bf16[256,2048]{1,0:T(8,128)(2,1)} %bitcast.126), channel_id=1, source_target_pairs={{0,2},{1,3},{2,0},{3,1},{4,6},{5,7},{6,4},{7,5},{8,10},{9,11},{10,... | collective-permute-start | bytes 3145736 | tf_op jit(solution)/shard_map/ppermute | solution.py:356
  47.5 65.0 %collective-permute-start.27 = (bf16[256,2048]{1,0:T(8,128)(2,1)}, bf16[256,2048]{1,0:T(8,128)(2,1)S(1)}, u32[]{:S(2)}, u32[]{:S(2)}) collective-permute-start(bf16[256,2048]{1,0:T(8,128)(2,1)} %collective-permute-done.26), channel_id=1, source_target_pairs={{2,0},{3,1},{4,6},{5,7},{10,8},{11,9},{12,14},{13,15},{18,16},{19,... | collective-permute-start | bytes 3145736 | tf_op jit(solution)/shard_map/ppermute | solution.py:360
  48.8 65.3 %collective-permute-start.25 = (bf16[256,2048]{1,0:T(8,128)(2,1)}, bf16[256,2048]{1,0:T(8,128)(2,1)S(1)}, u32[]{:S(2)}, u32[]{:S(2)}) collective-permute-start(bf16[256,2048]{1,0:T(8,128)(2,1)} %collective-permute-done.24), channel_id=1, source_target_pairs={{2,4},{3,5},{4,2},{5,3},{10,12},{11,13},{12,10},{13,11},{18,20},{1... | collective-permute-start | bytes 3145736 | tf_op jit(solution)/shard_map/ppermute | solution.py:360
  50.6 58.1 %collective-permute-start.11 = (bf16[2,64,1792]{2,1,0:T(8,128)(2,1)S(1)}, bf16[2,64,1792]{2,1,0:T(8,128)(2,1)S(1)}, u32[]{:S(2)}, u32[]{:S(2)}) collective-permute-start(bf16[2,64,1792]{2,1,0:T(8,128)(2,1)S(1)} %pad_maximum_fusion.15), channel_id=1, source_target_pairs={{0,4},{1,5},{2,6},{3,7},{4,0},{5,1},{6,2},{7,3},{8,12},{9,13},{10,... | collective-permute-start | bytes 1376264 | tf_op jit(solution)/shard_map/ppermute | solution.py:356
  56.0 55.7 %collective-permute-start.12 = (bf16[2,64,1792]{2,1,0:T(8,128)(2,1)S(1)}, bf16[2,64,1792]{2,1,0:T(8,128)(2,1)S(1)}, u32[]{:S(2)}, u32[]{:S(2)}) collective-permute-start(bf16[2,64,1792]{2,1,0:T(8,128)(2,1)S(1)} %pad_maximum_fusion.16), channel_id=1, source_target_pairs={{0,6},{1,7},{2,4},{3,5},{4,2},{5,3},{6,0},{7,1},{8,14},{9,15},{10,... | collective-permute-start | bytes 1376264 | tf_op jit(solution)/shard_map/ppermute | solution.py:356
  63.9 64.6 %collective-permute-start.3 = (bf16[256,2048]{1,0:T(8,128)(2,1)}, bf16[256,2048]{1,0:T(8,128)(2,1)S(1)}, u32[]{:S(2)}, u32[]{:S(2)}) collective-permute-start(bf16[256,2048]{1,0:T(8,128)(2,1)} %collective-permute-done.2), channel_id=1, source_target_pairs={{2,0},{3,1},{4,6},{5,7},{10,8},{11,9},{12,14},{13,15},{18,16},{19,... | collective-permute-start | bytes 3145736 | tf_op jit(solution)/shard_map/ppermute | solution.py:360
  112.6 97.6 %collective-permute-start.5 = (bf16[256,2048]{1,0:T(8,128)(2,1)S(1)}, bf16[256,2048]{1,0:T(8,128)(2,1)S(1)}, u32[]{:S(2)}, u32[]{:S(2)}) collective-permute-start(bf16[256,2048]{1,0:T(8,128)(2,1)S(1)} %bitcast.127), channel_id=1, source_target_pairs={{0,1},{1,0},{2,3},{3,2},{4,5},{5,4},{6,7},{7,6},{8,9},{9,8},{10,11... | collective-permute-start | bytes 3145736 | tf_op jit(solution)/shard_map/ppermute | solution.py:356
  128.6 54.2 %collective-permute-start.30 = (bf16[256,2048]{1,0:T(8,128)(2,1)}, bf16[256,2048]{1,0:T(8,128)(2,1)S(1)}, u32[]{:S(2)}, u32[]{:S(2)}) collective-permute-start(bf16[256,2048]{1,0:T(8,128)(2,1)} %collective-permute-done.24), channel_id=1, source_target_pairs={{0,1},{1,0},{2,3},{3,2},{4,5},{5,4},{6,7},{7,6},{8,9},{9,8},{10,11... | collective-permute-start | bytes 3145736 | tf_op jit(solution)/shard_map/ppermute | solution.py:356
  130.1 75.2 %collective-permute-start.31 = (bf16[256,2048]{1,0:T(8,128)(2,1)S(1)}, bf16[256,2048]{1,0:T(8,128)(2,1)S(1)}, u32[]{:S(2)}, u32[]{:S(2)}) collective-permute-start(bf16[256,2048]{1,0:T(8,128)(2,1)S(1)} %get-tuple-element.97), channel_id=1, source_target_pairs={{0,1},{1,0},{2,3},{3,2},{4,5},{5,4},{6,7},{7,6},{8,9},{9,8},{10,11... | collective-permute-start | bytes 3145736 | tf_op jit(solution)/shard_map/ppermute | solution.py:356
  149.9 57.0 %collective-permute-start.4 = (bf16[256,2048]{1,0:T(8,128)(2,1)S(1)}, bf16[256,2048]{1,0:T(8,128)(2,1)S(1)}, u32[]{:S(2)}, u32[]{:S(2)}) collective-permute-start(bf16[256,2048]{1,0:T(8,128)(2,1)S(1)} %collective-permute-done.1), channel_id=1, source_target_pairs={{2,0},{3,1},{4,6},{5,7},{10,8},{11,9},{12,14},{13,15},{18,16},{19,... | collective-permute-start | bytes 3145736 | tf_op jit(solution)/shard_map/ppermute | solution.py:360
  152.8 98.4 %collective-permute-start.13 = (bf16[4,2,64,1792]{3,2,1,0:T(8,128)(2,1)S(1)}, bf16[4,2,64,1792]{3,2,1,0:T(8,128)(2,1)S(1)}, u32[]{:S(2)}, u32[]{:S(2)}) collective-permute-start(bf16[4,2,64,1792]{3,2,1,0:T(8,128)(2,1)S(1)} %get-tuple-element.163), channel_id=1, source_target_pairs={{0,16},{8,24},{16,0},{24,8},{1,17},{9,25},{17,1},{25,9},{2,18},{10... | collective-permute-start | bytes 5505032 | tf_op jit(solution)/shard_map/ppermute | solution.py:356
  206.9 65.8 %collective-permute-start.32 = (bf16[256,2048]{1,0:T(8,128)(2,1)S(1)}, bf16[256,2048]{1,0:T(8,128)(2,1)S(1)}, u32[]{:S(2)}, u32[]{:S(2)}) collective-permute-start(bf16[256,2048]{1,0:T(8,128)(2,1)S(1)} %get-tuple-element.95), channel_id=1, source_target_pairs={{0,1},{1,0},{2,3},{3,2},{4,5},{5,4},{6,7},{7,6},{8,9},{9,8},{10,11... | collective-permute-start | bytes 3145736 | tf_op jit(solution)/shard_map/ppermute | solution.py:356
  210.2 93.7 %collective-permute-start.8 = (bf16[256,2048]{1,0:T(8,128)(2,1)}, bf16[256,2048]{1,0:T(8,128)(2,1)}, u32[]{:S(2)}, u32[]{:S(2)}) collective-permute-start(bf16[256,2048]{1,0:T(8,128)(2,1)} %get-tuple-element.99), channel_id=1, source_target_pairs={{0,1},{1,0},{2,3},{3,2},{4,5},{5,4},{6,7},{7,6},{8,9},{9,8},{10,11... | collective-permute-start | bytes 3145736 | tf_op jit(solution)/shard_map/ppermute | solution.py:356
  255.1 61.3 %collective-permute-start.14 = (bf16[2,4,2,64,1792]{4,3,2,1,0:T(8,128)(2,1)}, bf16[2,4,2,64,1792]{4,3,2,1,0:T(8,128)(2,1)}, u32[]{:S(2)}, u32[]{:S(2)}) collective-permute-start(bf16[2,4,2,64,1792]{4,3,2,1,0:T(8,128)(2,1)} %get-tuple-element.129), channel_id=1, source_target_pairs={{0,8},{8,0},{16,24},{24,16},{1,9},{9,1},{17,25},{25,17},{2,10},{10... | collective-permute-start | bytes 11010056 | tf_op jit(solution)/shard_map/ppermute | solution.py:356
  449.8 178.3 %collective-permute-start.55 = (bf16[640,2048]{1,0:T(8,128)(2,1)}, bf16[640,2048]{1,0:T(8,128)(2,1)}, u32[]{:S(2)}, u32[]{:S(2)}) collective-permute-start(bf16[640,2048]{1,0:T(8,128)(2,1)} %dynamic-slice_bitcast_fusion.1), channel_id=1, source_target_pairs={{0,8},{8,0},{16,24},{24,16},{1,9},{9,1},{17,25},{25,17},{2,10},{10... | collective-permute-start | bytes 7864328 | tf_op jit(solution)/shard_map/ppermute | solution.py:356
  454.2 91.7 %collective-permute-start.18 = (bf16[256,2048]{1,0:T(8,128)(2,1)}, bf16[256,2048]{1,0:T(8,128)(2,1)}, u32[]{:S(2)}, u32[]{:S(2)}) collective-permute-start(bf16[256,2048]{1,0:T(8,128)(2,1)} %get-tuple-element.112), channel_id=1, source_target_pairs={{0,1},{1,0},{2,3},{3,2},{4,5},{5,4},{6,7},{7,6},{8,9},{9,8},{10,11... | collective-permute-start | bytes 3145736 | tf_op jit(solution)/shard_map/ppermute | solution.py:356
  454.7 131.3 %collective-permute-start.17 = (bf16[256,2048]{1,0:T(8,128)(2,1)}, bf16[256,2048]{1,0:T(8,128)(2,1)}, u32[]{:S(2)}, u32[]{:S(2)}) collective-permute-start(bf16[256,2048]{1,0:T(8,128)(2,1)} %get-tuple-element.113), channel_id=1, source_target_pairs={{0,1},{1,0},{2,3},{3,2},{4,5},{5,4},{6,7},{7,6},{8,9},{9,8},{10,11... | collective-permute-start | bytes 3145736 | tf_op jit(solution)/shard_map/ppermute | solution.py:356
  583.4 47.6 %collective-permute-start.34 = (bf16[256,2048]{1,0:T(8,128)(2,1)S(1)}, bf16[256,2048]{1,0:T(8,128)(2,1)S(1)}, u32[]{:S(2)}, u32[]{:S(2)}) collective-permute-start(bf16[256,2048]{1,0:T(8,128)(2,1)S(1)} %copy-done.18), channel_id=1, source_target_pairs={{0,1},{1,0},{2,3},{3,2},{4,5},{5,4},{6,7},{7,6},{8,9},{9,8},{10,11... | collective-permute-start | bytes 3145736 | tf_op jit(solution)/shard_map/ppermute | solution.py:356
  586.1 49.1 %collective-permute-start.40 = (bf16[256,2048]{1,0:T(8,128)(2,1)S(1)}, bf16[256,2048]{1,0:T(8,128)(2,1)S(1)}, u32[]{:S(2)}, u32[]{:S(2)}) collective-permute-start(bf16[256,2048]{1,0:T(8,128)(2,1)S(1)} %add_convert_fusion.5), channel_id=1, source_target_pairs={{0,2},{1,3},{6,4},{7,5},{8,10},{9,11},{14,12},{15,13},{16,18},{17,... | collective-permute-start | bytes 3145736 | tf_op jit(solution)/shard_map/ppermute | solution.py:360
  627.6 70.4 %collective-permute-start.16 = (bf16[256,2048]{1,0:T(8,128)(2,1)S(1)}, bf16[256,2048]{1,0:T(8,128)(2,1)S(1)}, u32[]{:S(2)}, u32[]{:S(2)}) collective-permute-start(bf16[256,2048]{1,0:T(8,128)(2,1)S(1)} %copy-done.16), channel_id=1, source_target_pairs={{0,1},{1,0},{2,3},{3,2},{4,5},{5,4},{6,7},{7,6},{8,9},{9,8},{10,11... | collective-permute-start | bytes 3145736 | tf_op jit(solution)/shard_map/ppermute | solution.py:356
  631.0 67.9 %collective-permute-start.22 = (bf16[256,2048]{1,0:T(8,128)(2,1)S(1)}, bf16[256,2048]{1,0:T(8,128)(2,1)S(1)}, u32[]{:S(2)}, u32[]{:S(2)}) collective-permute-start(bf16[256,2048]{1,0:T(8,128)(2,1)S(1)} %add_convert_fusion.9), channel_id=1, source_target_pairs={{0,2},{1,3},{6,4},{7,5},{8,10},{9,11},{14,12},{15,13},{16,18},{17,... | collective-permute-start | bytes 3145736 | tf_op jit(solution)/shard_map/ppermute | solution.py:360
  635.1 71.7 %collective-permute-start.20 = (bf16[256,2048]{1,0:T(8,128)(2,1)S(1)}, bf16[256,2048]{1,0:T(8,128)(2,1)S(1)}, u32[]{:S(2)}, u32[]{:S(2)}) collective-permute-start(bf16[256,2048]{1,0:T(8,128)(2,1)S(1)} %add_convert_fusion.9), channel_id=1, source_target_pairs={{2,4},{3,5},{4,2},{5,3},{10,12},{11,13},{12,10},{13,11},{18,20},{1... | collective-permute-start | bytes 3145736 | tf_op jit(solution)/shard_map/ppermute | solution.py:360
  635.9 97.4 %collective-permute-start.56 = (bf16[640,2048]{1,0:T(8,128)(2,1)S(1)}, bf16[640,2048]{1,0:T(8,128)(2,1)S(1)}, u32[]{:S(2)}, u32[]{:S(2)}) collective-permute-start(bf16[640,2048]{1,0:T(8,128)(2,1)S(1)} %fusion.10), channel_id=1, source_target_pairs={{0,16},{8,24},{16,0},{24,8},{1,17},{9,25},{17,1},{25,9},{2,18},{10... | collective-permute-start | bytes 7864328 | tf_op jit(solution)/shard_map/ppermute | solution.py:356
  (86 other events, 1884.4 us)

commit v2 on v1

--- a/solution.py
+++ b/solution.py
@@ -347,6 +347,8 @@
 
 
 TILE_ROWS = 32
+BIG_VMEM = 56 << 20
+SMALL_COST = pl.CostEstimate(flops=1 << 20, bytes_accessed=1 << 20, transcendentals=0)
 F32 = jnp.float32
 BF16 = jnp.bfloat16
 
@@ -372,27 +374,8 @@
     return total
 
 
-def gather_blocks(own, is_middle):
-    near = flip(own, "shard", 2)
-    across = send(own, MIDDLE)
-    across_near = send(near, MIDDLE)
-    two = jnp.where(is_middle, across_near, send(across, OUTWARD))
-    three = jnp.where(is_middle, across, send(across_near, OUTWARD))
-    mine = [own, near, two, three]
-    return mine + [flip(block, "shard", 1) for block in mine]
-
-
-def scatter_sum(blocks):
-    three = plus(blocks[3], flip(blocks[7], "shard", 1)).astype(BF16)
-    from_corner = send(three, INWARD)
-    two = plus(blocks[2], flip(blocks[6], "shard", 1), from_corner).astype(BF16)
-    across_near = send(two, MIDDLE)
-    across = send(two, INWARD)
-    one = plus(blocks[1], flip(blocks[5], "shard", 1), across_near).astype(BF16)
-    three = plus(three, across).astype(BF16)
-    return plus(
-        blocks[0], flip(blocks[4], "shard", 1), flip(one, "shard", 2), send(three, MIDDLE)
-    )
+def hold(values, gates):
+    return lax.optimization_barrier(tuple(values) + tuple(gates))[: len(values)]
 
 
 def turn(heads_in, cosine, sine):
@@ -547,9 +530,7 @@
         in_specs=[SMEM_SPEC, VMEM_SPEC, VMEM_SPEC, VMEM_SPEC],
         out_specs=(VMEM_SPEC, VMEM_SPEC, VMEM_SPEC),
         compiler_params=pltpu.CompilerParams(vmem_limit_bytes=48 << 20),
-        cost_estimate=pl.CostEstimate(
-            flops=4 * blocks * rows * 768 * HEAD, bytes_accessed=10 << 20, transcendentals=0
-        ),
+        cost_estimate=SMALL_COST,
     )(seq_scalars, qkv, cosine, sine)
 
 
@@ -565,96 +546,404 @@
         out_specs=(VMEM_SPEC, VMEM_SPEC),
         scratch_shapes=[pltpu.VMEM(query.shape, F32), pltpu.VMEM(query.shape, F32)],
         compiler_params=pltpu.CompilerParams(vmem_limit_bytes=48 << 20),
-        cost_estimate=pl.CostEstimate(
-            flops=10 * blocks * rows * 768 * HEAD, bytes_accessed=12 << 20, transcendentals=0
-        ),
+        cost_estimate=SMALL_COST,
     )(seq_scalars, qkv, grad, cosine, sine, query, key)
 
 
-def place_weights_kernel(order_ref, part_ref, gain_ref, shift_ref, raw_ref, scaled_ref, sum_ref, *, hidden):
-    raw = part_ref[0]
-    raw_ref[...] = raw
-    weight = raw.astype(F32)
-    lane = lax.broadcasted_iota(jnp.int32, weight.shape, 1)
-    gain = jnp.where(lane < hidden, gain_ref[:, 1:2], gain_ref[:, 0:1])
-    shift = jnp.where(lane < hidden, shift_ref[:, 1:2], shift_ref[:, 0:1])
-    scaled_ref[...] = (weight * gain).astype(BF16)
-    share = jnp.sum(weight * shift, axis=0, keepdims=True)
+def place_weights_kernel(
+    at_ref, p0_ref, p1_ref, p2_ref, p3_ref, gain_ref, shift_ref, *out_refs, hidden
+):
+    raw_refs, scaled_refs, sum_ref = out_refs[:2], out_refs[2:4], out_refs[4]
+    quarter, wide = p0_ref.shape[1:]
 
     @pl.when(pl.program_id(0) == 0)
     def _():
-        sum_ref[...] = share
-
-    @pl.when(pl.program_id(0) > 0)
-    def _():
-        sum_ref[...] += share
-
-
-def place_weights(order, parts, gains, shifts, hidden):
-    count, rows, wide = parts.shape
-    whole = jax.ShapeDtypeStruct((count * rows, wide), BF16)
-    by_row = pl.BlockSpec((rows, wide), lambda i, order_ref: (i, 0))
-    pair = pl.BlockSpec((rows, 2), lambda i, order_ref: (i, 0))
+        sum_ref[...] = jnp.zeros_like(sum_ref)
+
+    for k, part_ref in enumerate((p0_ref, p1_ref, p2_ref, p3_ref)):
+        rows = pl.ds(pl.multiple_of((at_ref[1] ^ k) * quarter, quarter), quarter)
+        for norm, columns in ((1, slice(0, hidden)), (0, slice(hidden, wide))):
+            raw = part_ref[0, :, columns]
+            raw_refs[1 - norm][rows, :] = raw
+            weight = raw.astype(F32)
+            gain, shift = gain_ref[rows, norm : norm + 1], shift_ref[rows, norm : norm + 1]
+            scaled_refs[1 - norm][rows, :] = (weight * gain).astype(BF16)
+            sum_ref[:, columns] += jnp.sum(weight * shift, axis=0, keepdims=True)
+
+
+def place_weights(me, rep, parts, gains, shifts, hidden):
+    count, rows, wide = parts[0].shape
+    widths = (hidden, wide - hidden) * 2
+    pair = pl.BlockSpec((4 * rows, 2), lambda i, at_ref: (i ^ at_ref[0], 0))
+    part = pl.BlockSpec((1, rows, wide), lambda i, at_ref: (i, 0, 0))
     return pl.pallas_call(
         functools.partial(place_weights_kernel, hidden=hidden),
-        out_shape=(whole, whole, jax.ShapeDtypeStruct((1, wide), F32)),
+        out_shape=tuple(jax.ShapeDtypeStruct((count * 4 * rows, n), BF16) for n in widths)
+        + (jax.ShapeDtypeStruct((1, wide), F32),),
         grid_spec=pltpu.PrefetchScalarGridSpec(
             num_scalar_prefetch=1,
             grid=(count,),
-            in_specs=[
-                pl.BlockSpec((1, rows, wide), lambda i, order_ref: (order_ref[i], 0, 0)),
-                pair,
-                pair,
-            ],
-            out_specs=(by_row, by_row, pl.BlockSpec((1, wide), lambda i, order_ref: (0, 0))),
+            in_specs=[part] * 4 + [pair, pair],
+            out_specs=tuple(
+                pl.BlockSpec((4 * rows, n), lambda i, at_ref: (i ^ at_ref[0], 0)) for n in widths
+            )
+            + (pl.BlockSpec((1, wide), lambda i, at_ref: (0, 0)),),
         ),
-        cost_estimate=pl.CostEstimate(
-            flops=4 * count * rows * wide, bytes_accessed=6 * count * rows * wide, transcendentals=0
+        compiler_params=pltpu.CompilerParams(vmem_limit_bytes=32 << 20),
+        cost_estimate=SMALL_COST,
+    )(jnp.stack([me, rep]).astype(jnp.int32), *parts, gains, shifts)
+
+
+def place_grads_kernel(at_ref, p0_ref, p1_ref, p2_ref, p3_ref, out_ref, *, pieces):
+    quarter, wide = p0_ref.shape[1:]
+    source = pl.program_id(0) ^ at_ref[0]
+    size = wide // pieces
+    for k, part_ref in enumerate((p0_ref, p1_ref, p2_ref, p3_ref)):
+        rows = pl.ds(pl.multiple_of((at_ref[1] ^ k) * quarter, quarter), quarter)
+        values = part_ref[0].astype(F32)
+        if pieces == 1:
+            out_ref[rows, :] = values
+        else:
+            for j in range(pieces):
+                start = pl.multiple_of((j * HEADS + source) * size, size)
+                out_ref[rows, pl.ds(start, size)] = values[:, j * size : (j + 1) * size]
+
+
+def place_grads(me, rep, parts, pieces):
+    count, rows, wide = parts[0].shape
+    part = pl.BlockSpec((1, rows, wide), lambda i, at_ref: (i, 0, 0))
+    if pieces == 1:
+        out = pl.BlockSpec((4 * rows, wide), lambda i, at_ref: (0, i ^ at_ref[0]))
+    else:
+        out = pl.BlockSpec((4 * rows, count * wide), lambda i, at_ref: (0, 0))
+    return pl.pallas_call(
+        functools.partial(place_grads_kernel, pieces=pieces),
+        out_shape=jax.ShapeDtypeStruct((4 * rows, count * wide), F32),
+        grid_spec=pltpu.PrefetchScalarGridSpec(
+            num_scalar_prefetch=1, grid=(count,), in_specs=[part] * 4, out_specs=out
         ),
-    )(order, parts, gains, shifts)
-
-
-def place_grads_kernel(order_ref, part_ref, up_ref, qkv_ref, *, hidden):
-    values = part_ref[0].astype(F32)
-    up_ref[...] = values[:, :hidden]
-    third = qkv_ref.shape[1] // 3
-    for k in range(3):
-        start = pl.multiple_of(k * third + pl.program_id(1) * HEAD, HEAD)
-        qkv_ref[:, pl.ds(start, HEAD)] = values[:, hidden + k * HEAD : hidden + (k + 1) * HEAD]
-
-
-def place_grads(order, parts, hidden):
-    count, rows, wide = parts.shape
-    depth = count // HEADS * rows
+        compiler_params=pltpu.CompilerParams(vmem_limit_bytes=40 << 20),
+        cost_estimate=SMALL_COST,
+    )(jnp.stack([me, rep]).astype(jnp.int32), *parts)
+
+
+def place_halves_kernel(core_ref, mine_ref, other_ref, down_ref, dense_ref, *, cut):
+    step = pl.program_id(0)
+    first = (step < pl.num_programs(0) // 2) == (core_ref[0] == 0)
+    values = jnp.where(first, mine_ref[...], other_ref[...]).astype(F32)
+    in_down = step < cut
+
+    @pl.when(in_down)
+    def _():
+        down_ref[...] = values
+
+    @pl.when(jnp.logical_not(in_down))
+    def _():
+        dense_ref[...] = values
+
+
+def place_halves(core, mine, other, hidden):
+    rows, width = mine.shape
+    tile = 128
+    half, cut = rows // tile, hidden // tile
+    part = pl.BlockSpec((tile, width), lambda i, core_ref: (i % half, 0))
     return pl.pallas_call(
-        functools.partial(place_grads_kernel, hidden=hidden),
+        functools.partial(place_halves_kernel, cut=cut),
         out_shape=(
-            jax.ShapeDtypeStruct((depth, HEADS * hidden), F32),
-            jax.ShapeDtypeStruct((depth, 3 * HEADS * HEAD), F32),
+            jax.ShapeDtypeStruct((hidden, width), F32),
+            jax.ShapeDtypeStruct((2 * rows - hidden, width), F32),
         ),
         grid_spec=pltpu.PrefetchScalarGridSpec(
             num_scalar_prefetch=1,
-            grid=(count // HEADS, HEADS),
-            in_specs=[
-                pl.BlockSpec(
-                    (1, rows, wide), lambda q, s, order_ref: (order_ref[s * 4 + q], 0, 0)
-                )
-            ],
+            grid=(2 * half,),
+            in_specs=[part, part],
             out_specs=(
-                pl.BlockSpec((rows, hidden), lambda q, s, order_ref: (q, s)),
-                pl.BlockSpec((rows, 3 * HEADS * HEAD), lambda q, s, order_ref: (q, 0)),
+                pl.BlockSpec((tile, width), lambda i, core_ref: (jnp.minimum(i, cut - 1), 0)),
+                pl.BlockSpec((tile, width), lambda i, core_ref: (jnp.maximum(i - cut, 0), 0)),
             ),
         ),
-        cost_estimate=pl.CostEstimate(
-            flops=0, bytes_accessed=6 * count * rows * wide, transcendentals=0
-        ),
-    )(order, parts)
+        compiler_params=pltpu.CompilerParams(vmem_limit_bytes=32 << 20),
+        cost_estimate=SMALL_COST,
+    )(core[None].astype(jnp.int32), mine, other)
+
+
+def normalize(values):
+    values = values.astype(F32)
+    centered = values - jnp.mean(values, axis=-1, keepdims=True)
+    rstd = lax.rsqrt(jnp.mean(centered * centered, axis=-1, keepdims=True) + EPSILON)
+    return centered * rstd, rstd
+
+
+def norm_kernel(*refs, count, steps):
+    blocks, out_ref = refs[:count], refs[-1]
+    for k in range(count):
+
+        @pl.when(pl.program_id(0) // steps == k)
+        def _(block_ref=blocks[k]):
+            out_ref[...] = normalize(block_ref[...])[0].astype(BF16)
+
+
+def norm_blocks(blocks, places, buffer):
+    rows, width = blocks[0].shape
+    steps = 2
+    tile = rows // steps
+    count = len(blocks)
+
+    def spec(k):
+        return pl.BlockSpec((tile, width), lambda i: (jnp.clip(i - steps * k, 0, steps - 1), 0))
+
+    def put(i):
+        place = places[0]
+        for k in range(1, count):
+            place = jnp.where(i // steps >= k, places[k], place)
+        return place * steps + i % steps, 0
+
+    extra = [] if buffer is None else [buffer]
+    return pl.pallas_call(
+        functools.partial(norm_kernel, count=count, steps=steps),
+        out_shape=jax.ShapeDtypeStruct((HEADS * rows, width), BF16),
+        grid=(count * steps,),
+        in_specs=[spec(k) for k in range(count)] + [pl.BlockSpec(memory_space=pl.ANY)] * len(extra),
+        out_specs=pl.BlockSpec((tile, width), put),
+        input_output_aliases={count: 0} if extra else {},
+        cost_estimate=SMALL_COST,
+    )(*blocks, *extra)
 
 
 def dot32(left, right, left_dim=1, right_dim=0):
     return lax.dot_general(
         left, right, (((left_dim,), (right_dim,)), ((), ())), preferred_element_type=F32
     )
+
+
+def tokens_spec(tile, width, first):
+    return pl.BlockSpec((tile, width), lambda i: (first + i, 0))
+
+
+def whole_spec(shape):
+    return pl.BlockSpec(shape, lambda i: (0, 0), pipeline_mode=pl.Buffered(1))
+
+
+def block_specs(count, tile, width):
+    return [pl.BlockSpec((tile, width), lambda i: (0, 0)) for _ in range(count)]
+
+
+def project_kernel(normed_ref, up_ref, qkv_w_ref, shift_ref, act_ref, slope_ref, qkv_ref):
+    hidden = act_ref.shape[1]
+    lanes = 256
+    for start in range(0, hidden, lanes):
+        columns = slice(start, start + lanes)
+        value = dot32(normed_ref[...], up_ref[:, columns]) + shift_ref[:, columns]
+        normal = 0.5 + 0.5 * lax.erf(value * (0.5**0.5))
+        bell = jnp.exp(value * value * -0.5) * ((2.0 * math.pi) ** -0.5)
+        act_ref[:, columns] = (value * normal).astype(BF16)
+        slope_ref[:, columns] = (normal + value * bell).astype(BF16)
+    for start in range(0, qkv_ref.shape[1], lanes):
+        columns = slice(start, start + lanes)
+        value = dot32(normed_ref[...], qkv_w_ref[:, columns])
+        value = value + shift_ref[:, hidden + start : hidden + start + lanes]
+        qkv_ref[:, columns] = value.astype(BF16)
+
+
+def project(normed, w_up, w_qkv, shift):
+    count, width = normed.shape
+    hidden, rest = w_up.shape[1], w_qkv.shape[1]
+    tile = 512
+    return pl.pallas_call(
+        project_kernel,
+        out_shape=(
+            jax.ShapeDtypeStruct((count, hidden), BF16),
+            jax.ShapeDtypeStruct((count, hidden), BF16),
+            jax.ShapeDtypeStruct((count, rest), BF16),
+        ),
+        grid=(count // tile,),
+        in_specs=[
+            tokens_spec(tile, width, 0),
+            whole_spec(w_up.shape),
+            whole_spec(w_qkv.shape),
+            whole_spec(shift.shape),
+        ],
+        out_specs=(
+            tokens_spec(tile, hidden, 0),
+            tokens_spec(tile, hidden, 0),
+            tokens_spec(tile, rest, 0),
+        ),
+        compiler_params=pltpu.CompilerParams(vmem_limit_bytes=BIG_VMEM),
+        cost_estimate=SMALL_COST,
+    )(normed, w_up, w_qkv, shift)
+
+
+def combine_kernel(one_ref, two_ref, w_one_ref, w_two_ref, *out_refs, right_dim):
+    lanes = 512
+    width = w_one_ref.shape[1 - right_dim]
+    for k, out_ref in enumerate(out_refs):
+
+        @pl.when(pl.program_id(0) == k)
+        def _(out_ref=out_ref):
+            for start in range(0, width, lanes):
+                columns = slice(start, start + lanes)
+                if right_dim:
+                    w_one, w_two = w_one_ref[columns, :], w_two_ref[columns, :]
+                else:
+                    w_one, w_two = w_one_ref[:, columns], w_two_ref[:, columns]
+                value = dot32(one_ref[...], w_one, 1, right_dim)
+                value = value + dot32(two_ref[...], w_two, 1, right_dim)
+                out_ref[:, columns] = value.astype(BF16)
+
+
+def combine(one, two, w_one, w_two, rows, first, right_dim):
+    width = w_one.shape[1 - right_dim]
+    return pl.pallas_call(
+        functools.partial(combine_kernel, right_dim=right_dim),
+        out_shape=tuple(jax.ShapeDtypeStruct((rows, width), BF16) for _ in range(4)),
+        grid=(4,),
+        in_specs=[
+            tokens_spec(rows, one.shape[1], first),
+            tokens_spec(rows, two.shape[1], first),
+            whole_spec(w_one.shape),
+            whole_spec(w_two.shape),
+        ],
+        out_specs=tuple(block_specs(4, rows, width)),
+        compiler_params=pltpu.CompilerParams(vmem_limit_bytes=BIG_VMEM),
+        cost_estimate=SMALL_COST,
+    )(one, two, w_one, w_two)
+
+
+def pull_kernel(*refs, extra):
+    blocks, (w_one_ref, w_two_ref, slope_ref) = refs[:4], refs[4:7]
+    pre_ref, att_ref, sum_ref = refs[7 + extra :]
+    hidden = w_one_ref.shape[0]
+    lanes = 256
+
+    @pl.when(pl.program_id(0) == 0)
+    def _():
+        sum_ref[...] = jnp.zeros_like(sum_ref)
+
+    for k, block_ref in enumerate(blocks):
+
+        @pl.when(pl.program_id(0) == k)
+        def _(block_ref=block_ref):
+            for start in range(0, hidden, lanes):
+                columns = slice(start, start + lanes)
+                value = dot32(block_ref[...], w_one_ref[columns, :], 1, 1)
+                value = (value * slope_ref[:, columns].astype(F32)).astype(BF16)
+                pre_ref[:, columns] = value
+                sum_ref[:, columns] += jnp.sum(value.astype(F32), axis=0, keepdims=True)
+            att_ref[...] = dot32(block_ref[...], w_two_ref[...], 1, 1).astype(BF16)
+
+
+def pull(blocks, w_down, w_dense, slope, half, buffers):
+    rows, width = blocks[0].shape
+    hidden, head = w_down.shape[0], w_dense.shape[0]
+    count = HEADS * rows
+    return pl.pallas_call(
+        functools.partial(pull_kernel, extra=len(buffers)),
+        out_shape=(
+            jax.ShapeDtypeStruct((count, hidden), BF16),
+            jax.ShapeDtypeStruct((count, head), BF16),
+            jax.ShapeDtypeStruct((1, hidden), F32),
+        ),
+        grid=(4,),
+        in_specs=block_specs(4, rows, width)
+        + [whole_spec(w_down.shape), whole_spec(w_dense.shape), tokens_spec(rows, hidden, 4 * half)]
+        + [pl.BlockSpec(memory_space=pl.ANY)] * len(buffers),
+        out_specs=(
+            tokens_spec(rows, hidden, 4 * half),
+            tokens_spec(rows, head, 4 * half),
+            pl.BlockSpec((1, hidden), lambda i: (0, 0)),
+        ),
+        input_output_aliases={7 + k: k for k in range(len(buffers))},
+        compiler_params=pltpu.CompilerParams(vmem_limit_bytes=BIG_VMEM),
+        cost_estimate=SMALL_COST,
+    )(*blocks, w_down, w_dense, slope, *buffers)
+
+
+def moments_kernel(normed_ref, right_ref, weight_ref, gain_ref, shift_ref, columns_ref, out_ref, sums_ref):
+    lanes = 256
+    turned = normed_ref[...].T
+    gain, shift = gain_ref[...], shift_ref[...]
+    gain_terms, bias_terms = None, None
+    for start in range(0, out_ref.shape[1], lanes):
+        columns = slice(start, start + lanes)
+        moment = dot32(turned, right_ref[:, columns])
+        weight = weight_ref[:, columns].astype(F32)
+        total = columns_ref[:, columns]
+        out_ref[:, columns] = (moment * gain + shift * total).astype(BF16)
+        one, two = moment * weight, weight * total
+        gain_terms = one if gain_terms is None else gain_terms + one
+        bias_terms = two if bias_terms is None else bias_terms + two
+    sums_ref[:, 0:1] = jnp.sum(gain_terms, axis=1, keepdims=True)
+    sums_ref[:, 1:2] = jnp.sum(bias_terms, axis=1, keepdims=True)
+
+
+def moments_of(normed, right, weight, gain, shift, columns):
+    count, width = normed.shape
+    wide = weight.shape[1]
+    tile = 256
+    return pl.pallas_call(
+        moments_kernel,
+        out_shape=(
+            jax.ShapeDtypeStruct((width, wide), BF16),
+            jax.ShapeDtypeStruct((width, 2), F32),
+        ),
+        grid=(width // tile,),
+        in_specs=[
+            pl.BlockSpec((count, tile), lambda i: (0, i)),
+            whole_spec(right.shape),
+            tokens_spec(tile, wide, 0),
+            tokens_spec(tile, 1, 0),
+            tokens_spec(tile, 1, 0),
+            whole_spec(columns.shape),
+        ],
+        out_specs=(tokens_spec(tile, wide, 0), tokens_spec(tile, 2, 0)),
+        compiler_params=pltpu.CompilerParams(vmem_limit_bytes=BIG_VMEM),
+        cost_estimate=SMALL_COST,
+    )(normed, right, weight, gain[:, None], shift[:, None], columns)
+
+
+def outer_kernel(act_ref, att_ref, *refs):
+    blocks, out_ref = refs[:HEADS], refs[HEADS]
+    rows = blocks[0].shape[0]
+    lanes = 512
+    last = pl.num_programs(0) - 1
+
+    def fill(left_ref):
+        turned = left_ref[...].T
+        for start in range(0, out_ref.shape[1], lanes):
+            columns = slice(start, start + lanes)
+            total = None
+            for k, block_ref in enumerate(blocks):
+                term = dot32(turned[:, k * rows : (k + 1) * rows], block_ref[:, columns])
+                total = term if total is None else total + term
+            out_ref[:, columns] = total.astype(BF16)
+
+    @pl.when(pl.program_id(0) < last)
+    def _():
+        fill(act_ref)
+
+    @pl.when(pl.program_id(0) == last)
+    def _():
+        fill(att_ref)
+
+
+def outer(activated, attended, blocks):
+    count, hidden = activated.shape
+    rows, width = blocks[0].shape
+    tile = attended.shape[1]
+    steps = hidden // tile
+    return pl.pallas_call(
+        outer_kernel,
+        out_shape=jax.ShapeDtypeStruct((hidden + tile, width), BF16),
+        grid=(steps + 1,),
+        in_specs=[
+            pl.BlockSpec((count, tile), lambda i: (0, jnp.minimum(i, steps - 1))),
+            whole_spec(attended.shape),
+        ]
+        + [whole_spec((rows, width)) for _ in blocks],
+        out_specs=tokens_spec(tile, width, 0),
+        compiler_params=pltpu.CompilerParams(vmem_limit_bytes=BIG_VMEM),
+        cost_estimate=SMALL_COST,
+    )(activated, attended, *blocks)
 
 
 def split_shards(
@@ -699,32 +988,11 @@
             )
         return jnp.concatenate(pieces, axis=1)
 
+    odd = jnp.stack([columns_for(me ^ (2 * z + 1)) for z in range(4)])
+    odd_came = flip(odd, "shard", 1)
+    x_near = flip(own, "shard", 2)
+    x_across = send(own, MIDDLE)
     keep = [columns_for(me ^ (2 * z)) for z in range(4)]
-    moved = flip(jnp.stack([columns_for(me ^ (2 * z + 1)) for z in range(4)]), "shard", 1)
-    pairs = [jnp.stack([keep[z], moved[z]]) for z in range(4)]
-    for z in range(1, 4):
-        pairs[z] = flip(pairs[z], "shard", 2 * z)
-    part = jnp.stack(pairs)
-    part = jnp.stack([part, flip(part, "rep", 2)])
-    part = jnp.stack([part, flip(part, "rep", 1)], axis=1)
-    from_shard = jnp.arange(HEADS, dtype=jnp.int32)[:, None] ^ me
-    from_rep = jnp.arange(4, dtype=jnp.int32)[None, :] ^ rep
-    order = (from_rep * HEADS + from_shard).reshape(-1)
-    gains = jnp.stack([ln1_gain, ln2_gain], axis=1)
-    shifts = jnp.stack([ln1_bias, ln2_bias], axis=1)
-    w_in, w_scaled, shifted = place_weights(
-        order, part.reshape(4 * HEADS, quarter, wide), gains, shifts, hidden
-    )
-    is_hidden = jnp.arange(wide, dtype=jnp.int32)[None, :] < hidden
-    gain = jnp.where(is_hidden, ln2_gain[:, None], ln1_gain[:, None])
-    shift = jnp.where(is_hidden, ln2_bias[:, None], ln1_bias[:, None])
-    b_in = jnp.concatenate(
-        [lax.dynamic_slice_in_dim(b_up, me * hidden, hidden, 0)]
-        + [lax.dynamic_slice_in_dim(b_qkv, k * width + me * HEAD, HEAD, 0) for k in range(3)]
-    )
-    b_in = b_in + shifted[0]
-    w_out = jnp.concatenate([w_down, w_dense], axis=0)
-
     row_offsets, row_counts = stream_rows(seq_lengths[0], seq_order[0], HEADS)
     ends = (row_offsets + row_counts) * HEADS
     seq_scalars = jnp.concatenate([ends, me[None]]).astype(jnp.int32)
@@ -746,102 +1014,249 @@
     cosine = cosine.reshape(tiled)
     sine = sine.reshape(tiled)
 
-    stream = jnp.concatenate(gather_blocks(own, is_middle), axis=0)
-    grad_out = jnp.concatenate(gather_blocks(own_grad, is_middle), axis=0)
-
-    def normalize(values):
-        values = values.astype(F32)
-        centered = values - jnp.mean(values, axis=-1, keepdims=True)
-        rstd = lax.rsqrt(jnp.mean(centered * centered, axis=-1, keepdims=True) + EPSILON)
-        return centered * rstd, rstd
-
-    normed = normalize(stream)[0].astype(BF16)
-    qkv = (dot32(normed, w_scaled[:, hidden:]) + b_in[hidden:]).astype(BF16)
+
+    own, own_grad, x_near, x_across, odd_came, *keep = hold(
+        (own, own_grad, x_near, x_across, odd_came, *keep), (cosine, sine)
+    )
+    pairs = [jnp.stack([keep[z], odd_came[z]]) for z in range(4)]
+    got = [flip(pairs[z], "shard", 2 * z) for z in range(1, 4)]
+    x_own_y = flip(own, "shard", 1)
+    x_near_y = flip(x_near, "shard", 1)
+    beside = [flip(pairs[0], "rep", 2)]
+    x_near, x_across, own_grad, x_near_y, *got = hold(
+        (x_near, x_across, own_grad, x_near_y, *got), (x_own_y, beside[0])
+    )
+    x_across_near = send(x_near, MIDDLE)
+    x_two = send(x_across, OUTWARD)
+    g_own_y = flip(own_grad, "shard", 1)
+    beside = beside + [flip(jnp.stack(got), "rep", 2)]
+    part = jnp.stack([pairs[0]] + got).reshape(HEADS, quarter, wide)
+    x_across_near, x_two, own_grad, *beside = hold(
+        (x_across_near, x_two, own_grad, *beside), (part, g_own_y)
+    )
+    two = jnp.where(is_middle, x_across_near, x_two)
+    x_three = send(x_across_near, OUTWARD)
+    g_across = send(own_grad, MIDDLE)
+    x_two_y = flip(two, "shard", 1)
+    beside = jnp.concatenate([beside[0][None], beside[1]]).reshape(HEADS, quarter, wide)
+    part_c = flip(part, "rep", 1)
+    beside_c = flip(beside, "rep", 1)
+    normed = norm_blocks([own, x_near, x_own_y, x_near_y, two], (0, 1, 4, 5, 2), None)
+    x_three, own_grad, g_across, beside_c, part_c, x_two_y = hold(
+        (x_three, own_grad, g_across, beside_c, part_c, x_two_y), (normed,)
+    )
+    three = jnp.where(is_middle, x_across, x_three)
+    g_near = flip(own_grad, "shard", 2)
+    x_three_y = flip(three, "shard", 1)
+    parts = (part, part_c, beside, beside_c)
+    gains = jnp.stack([ln1_gain, ln2_gain], axis=1)
+    shifts = jnp.stack([ln1_bias, ln2_bias], axis=1)
+    up_raw, qkv_raw, up_scaled, qkv_scaled, shifted = place_weights(
+        me, rep, parts, gains, shifts, hidden
+    )
+    b_in = jnp.concatenate(
+        [lax.dynamic_slice_in_dim(b_up, me * hidden, hidden, 0)]
+        + [lax.dynamic_slice_in_dim(b_qkv, k * width + me * HEAD, HEAD, 0) for k in range(3)]
+    )
+    b_in = b_in[None, :] + shifted
+    normed = norm_blocks([three, x_two_y], (3, 6), normed)
+    g_near, x_three_y, normed = hold((g_near, x_three_y, normed), (b_in,))
+    g_across_near = send(g_near, MIDDLE)
+    g_two = send(g_across, OUTWARD)
+    g_near_y = flip(g_near, "shard", 1)
+    normed = norm_blocks([x_three_y], (7,), normed)
+    activated, slope, qkv = project(normed, up_scaled, qkv_scaled, b_in)
+    g_across_near, g_two, qkv, g_near_y = hold((g_across_near, g_two, qkv, g_near_y), (activated,))
+    g_two = jnp.where(is_middle, g_across_near, g_two)
+    g_three = send(g_across_near, OUTWARD)
+    g_two_y = flip(g_two, "shard", 1)
     qkv = qkv.reshape(HEADS, rows, 3 * HEAD)
     attended, query, key = attend(seq_scalars, qkv, cosine, sine)
-    pre_up = dot32(normed, w_scaled[:, :hidden]) + b_in[:hidden]
-    normal = 0.5 * (1.0 + lax.erf(pre_up * (0.5**0.5)))
-    slope = normal + pre_up * jnp.exp(-0.5 * pre_up * pre_up) * ((2.0 * math.pi) ** -0.5)
-    slope = slope.astype(BF16)
-    activated = (pre_up * normal).astype(BF16)
-    mixed = jnp.concatenate([activated, attended.reshape(group_tokens, HEAD)], axis=1)
-    out_part = dot32(mixed, w_out).astype(BF16).reshape(HEADS, rows, width)
-    out_sum = scatter_sum([out_part[k] for k in range(HEADS)])
+    attended = attended.reshape(group_tokens, HEAD)
+    far = combine(activated, attended, w_down, w_dense, rows, 4, 0)
+    g_three, g_two_y, *far = hold((g_three, g_two_y, *far), ())
+    g_three = jnp.where(is_middle, g_across, g_three)
+    g_three_y = flip(g_three, "shard", 1)
+    close = combine(activated, attended, w_down, w_dense, rows, 0, 0)
+    grad_pre, grad_attended, pre_sums = pull(
+        [own_grad, g_near, g_two, g_three], w_down, w_dense, slope, 0, []
+    )
+    g_three_y, grad_pre, *far = hold((g_three_y, grad_pre, *far), close)
+    came_three = flip(far[3], "shard", 1)
+    grad_pre, grad_attended, more_sums = pull(
+        [g_own_y, g_near_y, g_two_y, g_three_y],
+        w_down,
+        w_dense,
+        slope,
+        1,
+        [grad_pre, grad_attended],
+    )
+    pre_sums = pre_sums + more_sums
+    my_core = rep % 2
+    my_side = rep // 2
+    my_row = me % 2
+
+    def split(values, index):
+        return (
+            lax.dynamic_index_in_dim(values, index, 1, False),
+            lax.dynamic_index_in_dim(values, 1 - index, 1, False),
+        )
+
+    def by_core(grads):
+        return split(grads.reshape(2 * HEADS, 2, quarter, grads.shape[1]), my_core)
+
+    def by_side(summed):
+        return split(summed.reshape(HEADS, 2, quarter, summed.shape[-1]), my_side)
+
+    def by_row(summed):
+        return split(summed.reshape(4, 2, quarter, summed.shape[-1]), my_row)
+
+    def joined(mine, came):
+        return plus(mine, came).astype(BF16)
+
+    def by_place(mine, came):
+        both = jnp.stack([mine, came], axis=1)
+        return [lax.dynamic_index_in_dim(both, place ^ z, 0, False) for z in range(4)]
+
+    def far_places(pieces):
+        return flip(jnp.stack(pieces[2:]), "shard", 4)
+
+    def near_place(pieces, far):
+        return flip(jnp.stack([pieces[1], far[1]]), "shard", 2)
+
+    def sources(pieces, far, near):
+        both = jnp.stack([pieces[0], near[0], far[0], near[1]])
+        return both.reshape(HEADS, quarter, both.shape[-1])
+
+    up_grads, up_sums = moments_of(normed, grad_pre, up_raw, ln2_gain, ln2_bias, pre_sums)
+    up_keep, up_give = by_core(up_grads)
+    came_three, grad_attended, up_give, *far = hold((came_three, grad_attended, up_give, *far), ())
+    came_two = flip(far[2], "shard", 1)
+    three = plus(close[3], came_three).astype(BF16)
+    from_corner = send(three, INWARD)
+    up_came = flip(up_give, "rep", 1)
+    grad_qkv, qkv_sums = attend_back(
+        seq_scalars,
+        qkv,
+        grad_attended.reshape(HEADS, rows, HEAD),
+        cosine,
+        sine,
+        query,
+        key,
+    )
+    grad_qkv = grad_qkv.reshape(group_tokens, 3 * HEAD)
+    qkv_grads, qkv_row_sums = moments_of(normed, grad_qkv, qkv_raw, ln1_gain, ln1_bias, qkv_sums)
+    qkv_keep, qkv_give = by_core(qkv_grads)
+    came_two, from_corner, up_came, qkv_give, grad_qkv, *far = hold(
+        (came_two, from_corner, up_came, qkv_give, grad_qkv, *far), ()
+    )
+    up_keep, up_give = by_side(joined(up_keep, up_came))
+    up_came = flip(up_give, "rep", 2)
+    came_one = flip(far[1], "shard", 1)
+    two = plus(close[2], came_two, from_corner).astype(BF16)
+    across_near = send(two, MIDDLE)
+    across = send(two, INWARD)
+    qkv_came = flip(qkv_give, "rep", 1)
+    gy_far = combine(grad_pre, grad_qkv, up_scaled, qkv_scaled, rows, 4, 1)
+    gy_close = combine(grad_pre, grad_qkv, up_scaled, qkv_scaled, rows, 0, 1)
+    up_came, came_one, across_near, across, qkv_came, own_grad, *both = hold(
+        (up_came, came_one, across_near, across, qkv_came, own_grad, *far, *gy_far, *gy_close), ()
+    )
+    far, gy_far, gy_close = both[:4], both[4:8], both[8:]
+    up_keep, up_give = by_row(joined(up_keep, up_came))
+    came_own = flip(far[0], "shard", 1)
+    up_came = flip(up_give, "shard", 1)
+    one = plus(close[1], came_one, across_near).astype(BF16)
+    three = plus(three, across).astype(BF16)
+    one_near = flip(one, "shard", 2)
+    three_across = send(three, MIDDLE)
+    qkv_keep, qkv_give = by_side(joined(qkv_keep, qkv_came))
+    qkv_came = flip(qkv_give, "rep", 2)
+    out_grads = outer(
+        activated,
+        attended,
+        [own_grad, g_near, g_two, g_three, g_own_y, g_near_y, g_two_y, g_three_y],
+    )
+    half_rows = out_grads.shape[0] // 2
+    half_keep, half_give = split(out_grads.reshape(1, 2, half_rows, width), my_core)
+    small = jnp.concatenate(
+        [
+            qkv_row_sums.T.reshape(-1),
+            up_sums.T.reshape(-1),
+            jnp.sum(own_grad, axis=0, dtype=F32),
+            jnp.where(
+                block_range[:, None] == me, jnp.concatenate([pre_sums, qkv_sums], axis=1), 0.0
+            ).reshape(-1),
+        ]
+    )
+    came_own, one_near, three_across, up_came, qkv_came, half_give, small, *gy_far = hold(
+        (came_own, one_near, three_across, up_came, qkv_came, half_give, small, *gy_far), ()
+    )
+    came_three = flip(gy_far[3], "shard", 1)
+    qkv_keep, qkv_give = by_row(joined(qkv_keep, qkv_came))
+    qkv_came = flip(qkv_give, "shard", 1)
+    up_pieces = by_place(up_keep, up_came)
+    up_far = far_places(up_pieces)
+    half_came = flip(half_give, "rep", 1)
+    small = small + flip(small, "rep", 1)
+    out_sum = plus(close[0], came_own, one_near, three_across)
     output = (own.astype(F32) + out_sum + (b_dense + b_down)).astype(BF16)
-
-    grad_mixed = dot32(grad_out, w_out, 1, 1)
-    grad_attended = grad_mixed[:, hidden:].astype(BF16).reshape(HEADS, rows, HEAD)
-    grad_pre = (grad_mixed[:, :hidden] * slope.astype(F32)).astype(BF16)
-    grad_qkv, qkv_columns = attend_back(
-        seq_scalars, qkv, grad_attended, cosine, sine, query, key
-    )
-    grad_in = jnp.concatenate([grad_pre, grad_qkv.reshape(group_tokens, 3 * HEAD)], axis=1)
-    columns = jnp.concatenate([jnp.sum(grad_pre, axis=0, dtype=F32), qkv_columns[0]])
-
-    gy_part = dot32(grad_in, w_scaled, 1, 1).astype(BF16).reshape(HEADS, rows, width)
-    gy = scatter_sum([gy_part[k] for k in range(HEADS)])
+    came_three, qkv_came, up_far, half_came, small, *gy_far = hold(
+        (came_three, qkv_came, up_far, half_came, small, *gy_far), (output,)
+    )
+    came_two = flip(gy_far[2], "shard", 1)
+    three = plus(gy_close[3], came_three).astype(BF16)
+    from_corner = send(three, INWARD)
+    up_near = near_place(up_pieces, up_far)
+    qkv_pieces = by_place(qkv_keep, qkv_came)
+    qkv_far = far_places(qkv_pieces)
+    half = joined(half_keep, half_came).reshape(half_rows, width)
+    half_far = flip(half, "rep", 2)
+    came_two, from_corner, up_near, qkv_far, *gy_far = hold(
+        (came_two, from_corner, up_near, qkv_far, *gy_far), ()
+    )
+    came_one = flip(gy_far[1], "shard", 1)
+    two = plus(gy_close[2], came_two, from_corner).astype(BF16)
+    across_near = send(two, MIDDLE)
+    across = send(two, INWARD)
+    qkv_near = near_place(qkv_pieces, qkv_far)
+    up_part = sources(up_pieces, up_far, up_near)
+    came_one, across_near, across, qkv_near, up_part, half_far, *gy_far = hold(
+        (came_one, across_near, across, qkv_near, up_part, half_far, *gy_far), ()
+    )
+    came_own = flip(gy_far[0], "shard", 1)
+    one = plus(gy_close[1], came_one, across_near).astype(BF16)
+    three = plus(three, across).astype(BF16)
+    one_near = flip(one, "shard", 2)
+    three_across = send(three, MIDDLE)
+    up_beside = flip(up_part, "rep", 2)
+    up_c = flip(up_part, "rep", 1)
+    half = joined(half, half_far)
+    qkv_part = sources(qkv_pieces, qkv_far, qkv_near)
+    came_own, one_near, three_across, up_beside, half, qkv_part, small = hold(
+        (came_own, one_near, three_across, up_beside, half, qkv_part, small), (up_c,)
+    )
+    qkv_beside = flip(qkv_part, "rep", 2)
+    qkv_c = flip(qkv_part, "rep", 1)
+    up_beside_c = flip(up_beside, "rep", 1)
+    other = flip(half, "rep", 1)
+    small = small + flip(small, "rep", 2)
+    gy = plus(gy_close[0], came_own, one_near, three_across)
     own_normed, own_rstd = normalize(own)
     input_grad = own_grad.astype(F32) + own_rstd * (
         gy
         - jnp.mean(gy, axis=-1, keepdims=True)
         - own_normed * jnp.mean(gy * own_normed, axis=-1, keepdims=True)
     )
-
-    out_grads = dot32(mixed, grad_out, 0, 0).astype(BF16)
-    half_rows = out_grads.shape[0] // 2
-    my_core = rep % 2
-    my_side = rep // 2
-    halves = out_grads.reshape(2, half_rows, width)
-    half = plus(
-        lax.dynamic_index_in_dim(halves, my_core, 0, False),
-        flip(lax.dynamic_index_in_dim(halves, 1 - my_core, 0, False), "rep", 1),
-    ).astype(BF16)
-    half = plus(half, flip(half, "rep", 2)).astype(BF16)
-    other = flip(half, "rep", 1)
-    first = jnp.where(my_core == 0, half, other)
-    second = jnp.where(my_core == 0, other, half)
-    out_grads = jnp.concatenate([first, second], axis=0).astype(F32)
-
-    moments = dot32(normed, grad_in, 0, 0)
-    w_wide = w_in.astype(F32)
-    gain_terms = moments * w_wide
-    bias_terms = w_wide * columns[None, :]
-    in_grads = (moments * gain + shift * columns[None, :]).astype(BF16)
-    in_grads = in_grads.reshape(HEADS, 2, 2, quarter, wide)
-    summed = plus(
-        lax.dynamic_index_in_dim(in_grads, my_core, 2, False),
-        flip(lax.dynamic_index_in_dim(in_grads, 1 - my_core, 2, False), "rep", 1),
-    ).astype(BF16)
-    summed = plus(
-        lax.dynamic_index_in_dim(summed, my_side, 1, False),
-        flip(lax.dynamic_index_in_dim(summed, 1 - my_side, 1, False), "rep", 2),
-    ).astype(BF16)
-    summed = summed.reshape(4, 2, quarter, wide)
-    my_row = me % 2
-    keep_half = lax.dynamic_index_in_dim(summed, my_row, 1, False)
-    got_half = flip(lax.dynamic_index_in_dim(summed, 1 - my_row, 1, False), "shard", 1)
-    both = jnp.stack([keep_half, got_half], axis=1)
-    came = []
-    for z in range(4):
-        piece = lax.dynamic_index_in_dim(both, place ^ z, 0, False)
-        came.append(piece if z == 0 else flip(piece, "shard", 2 * z))
-    came = jnp.stack(came)
-    came = jnp.stack([came, flip(came, "rep", 2)])
-    came = jnp.stack([came, flip(came, "rep", 1)], axis=1)
-    up_grad, qkv_grad = place_grads(order, came.reshape(4 * HEADS, quarter, wide), hidden)
-
-    small = jnp.concatenate(
-        [
-            jnp.sum(gain_terms[:, hidden:], axis=1),
-            jnp.sum(bias_terms[:, hidden:], axis=1),
-            jnp.sum(gain_terms[:, :hidden], axis=1),
-            jnp.sum(bias_terms[:, :hidden], axis=1),
-            jnp.sum(own_grad, axis=0, dtype=F32),
-            jnp.where(block_range[:, None] == me, columns[None, :], 0.0).reshape(-1),
-        ]
-    )
-    for axis, bit in (("rep", 1), ("shard", 1), ("shard", 2), ("shard", 4), ("rep", 2)):
-        small = small + flip(small, axis, bit)
+    qkv_beside, up_beside_c, other, small = hold(
+        (qkv_beside, up_beside_c, other, small), (input_grad, qkv_c)
+    )
+    qkv_beside_c = flip(qkv_beside, "rep", 1)
+    for bit in (1, 2, 4):
+        small = small + flip(small, "shard", bit)
+    up_grad = place_grads(me, rep, (up_part, up_c, up_beside, up_beside_c), 1)
+    down_grad, dense_grad = place_halves(my_core, half, other, hidden)
+    qkv_grad = place_grads(me, rep, (qkv_part, qkv_c, qkv_beside, qkv_beside_c), 3)
     vectors = small[: 5 * width].reshape(5, width)
     slots = small[5 * width :].reshape(HEADS, wide)
     b_up_grad = slots[:, :hidden].reshape(-1)
@@ -855,11 +1270,11 @@
         vectors[3],
         qkv_grad,
         b_qkv_grad,
-        out_grads[hidden:],
+        dense_grad,
         vectors[4],
         up_grad,
         b_up_grad,
-        out_grads[:hidden],
+        down_grad,
         vectors[4],
     )
 

time: 820 us -> 642 us (0.78)
  Pallas kernels: 64.8 us -> 205 us
  matrix products: 127 us -> 0 us
  waiting for transfers between devices: 328 us -> 227 us
  other arithmetic: 103 us -> 52 us
  local copies, waits for them, and re-layouts: 86.1 us -> 49.9 us
    pallas_call x1 -> x16, Pallas kernels: 21.9 us -> 176 us  [the longest x4 50.6 us: combine(): pl.pallas_call(functools.partial(combine_kernel, right_dim=right_dim), ou...]
    dot_general x7 -> x0, matrix products: 127 us -> none  [dot32(): lax.dot_general(left, right, (((left_dim,), (right_dim,)), ((), ())), pre...]
    ppermute x42 -> x52, waiting for transfers between devices: 279 us -> 203 us  [flip(): return lax.ppermute(value, axis, [(i, i ^ bit) for i in range(size)])]
    ppermute x16, waiting for transfers between devices: 48.2 us -> 24.4 us  [send(): lax.ppermute(value, 'shard', [(2 * a + y, 2 * b + y) for a, b in pairs fo...]
    unnamed x122 -> x117, local copies, waits for them, and re-layouts: 38.6 us -> 19 us
    reduce_sum x5 -> x0, other arithmetic: 19 us -> none  [the longest x1 10.3 us: split_shards(): jnp.sum(grad_pre, axis=0, dtype=F32)]
    another operation x18, other arithmetic: 22.9 us -> 4.67 us  [the longest x2 1.52 us: split_shards(): part = jnp.stack([pairs[0]] + got).reshape(HEADS, quarter, wide)]
    pallas_call x1, Pallas kernels: 23.9 us -> 9.87 us  [place_weights(): pl.pallas_call(functools.partial(place_weights_kernel, hidden=hidden), ou...]
  transfers between devices with their start and end apart: 58 -> 68, of which waited for: 24 -> 20; matrix products, arithmetic and copies ran while one was open for 27% -> 12% of each run, Pallas kernels for 0% -> 32%
where the time goes in v2:
time: 642 us; the launch traced here: 632 us
  waiting for transfers between devices  227 us (35%)
  Pallas kernels  205 us (32%)
  starting transfers between devices  95.1 us (15%)
  other arithmetic  52 us (8%)
  local copies, waits for them, and re-layouts  49.9 us (8%)
    ppermute x52, waiting for transfers between devices, flip(): return lax.ppermute(value, axis, [(i, i ^ bit) for i in range(size)])  203 us
    ppermute x52, starting transfers between devices, flip(): return lax.ppermute(value, axis, [(i, i ^ bit) for i in range(size)])  63.6 us
    pallas_call x4, Pallas kernels, combine(): pl.pallas_call(functools.partial(combine_kernel, right_dim=right_dim), ou...  50.6 us
    ppermute x16, starting transfers between devices, send(): lax.ppermute(value, 'shard', [(2 * a + y, 2 * b + y) for a, b in pairs fo...  31.5 us
    pallas_call x2, Pallas kernels, moments_of(): pl.pallas_call(moments_kernel, out_shape=(jax.ShapeDtypeStruct((width, wi...  30.2 us
    ppermute x16, waiting for transfers between devices, send(): lax.ppermute(value, 'shard', [(2 * a + y, 2 * b + y) for a, b in pairs fo...  24.4 us
    pallas_call x1, Pallas kernels, project(): pl.pallas_call(project_kernel, out_shape=(jax.ShapeDtypeStruct((count, hi...  23.2 us
    pallas_call x2, Pallas kernels, pull(): pl.pallas_call(functools.partial(pull_kernel, extra=len(buffers)), out_sh...  22.7 us
  transfers between devices with their start and end apart: 68, of which 20 were waited for; matrix products, arithmetic and copies ran while one was open for 12% of the time, Pallas kernels for 32%

profile of v2, /device:TPU:0, one launch (start us, length us, event | category | flops | bytes accessed | tf_op | source)
XLA Modules:
  0.0 632.2 jit_solution(8826362094270633245)
XLA Ops:
  17.8 15.3 %collective-permute-done.2 = bf16[4,64,1792]{2,1,0:T(8,128)(2,1)} collective-permute-done((bf16[4,64,1792]{2,1,0:T(8,128)(2,1)}, bf16[4,64,1792]{2,1,0:T(8,128)(2,1)}, u32[]{:S(2)}, u32[]{:S(2)}) %collective-permute-start.2) | collective-permute-done | bytes 917536 | tf_op jit(solution)/shard_map/ppermute | solution.py:358
  53.7 26.1 %collective-permute-done.5 = bf16[2,64,1792]{2,1,0:T(8,128)(2,1)S(1)} collective-permute-done((bf16[2,64,1792]{2,1,0:T(8,128)(2,1)S(1)}, bf16[2,64,1792]{2,1,0:T(8,128)(2,1)S(1)}, u32[]{:S(2)}, u32[]{:S(2)}) %collective-permute-start.5) | collective-permute-done | bytes 458784 | tf_op jit(solution)/shard_map/ppermute | solution.py:358
  89.3 20.2 %collective-permute-done.10 = bf16[256,2048]{1,0:T(8,128)(2,1)S(1)} collective-permute-done((bf16[256,2048]{1,0:T(8,128)(2,1)S(1)}, bf16[256,2048]{1,0:T(8,128)(2,1)S(1)}, u32[]{:S(2)}, u32[]{:S(2)}) %collective-permute-start.10) | collective-permute-done | bytes 1048608 | tf_op jit(solution)/shard_map/ppermute | solution.py:362
  121.0 9.9 %shard_map.263.refs_2_ = bf16[2048,2048]{1,0:T(8,128)(2,1)} custom-call(bf16[256,2048]{1,0:T(8,128)(2,1)} %bitcast.127, bf16[256,2048]{1,0:T(8,128)(2,1)} %collective-permute-done.refs_1_, bf16[256,2048]{1,0:T(8,128)(2,1)} %copy-done.37, bf16[256,2048]{1,0:T(8,128)(2,1)} %copy-done.36, bf16[256,2048]{1,0:T(8,128)(2,1)} %copy-done.23), custom_call_target="tpu_custom_call" | custom-call | flops 1048576 | bytes 1048576 | tf_op jit(solution)/shard_map/pallas_call | solution.py:702
  130.9 12.3 %collective-permute-done.17.refs_1_ = bf16[256,2048]{1,0:T(8,128)(2,1)} collective-permute-done((bf16[256,2048]{1,0:T(8,128)(2,1)S(1)}, bf16[256,2048]{1,0:T(8,128)(2,1)}, u32[]{:S(2)}, u32[]{:S(2)}) %collective-permute-start.17) | collective-permute-done | bytes 1048608 | tf_op jit(solution)/shard_map/ppermute | solution.py:358
  163.0 9.9 %shard_map.265 = (bf16[2048,1024]{1,0:T(8,128)(2,1)S(1)}, bf16[2048,768]{1,0:T(8,128)(2,1)S(1)}, bf16[2048,1024]{1,0:T(8,128)(2,1)}, bf16[2048,768]{1,0:T(8,128)(2,1)S(1)}, f32[1,1792]{1,0:T(1,128)S(1)}) custom-call(s32[2]{0:T(128)S(1)} %pad_add_fusion.at_ref, bf16[8,64,1792]{2,1,0:T(8,128)(2,1)} %bitcast.18.p0_ref, ...), custom_call_target="tpu_custom_call" | custom-call | flops 1048576 | bytes 1048576 | tf_op jit(solution)/shard_map/pallas_call | solution.py:579
  184.5 23.2 %shard_map.267 = (bf16[2048,1024]{1,0:T(8,128)(2,1)}, bf16[2048,1024]{1,0:T(8,128)(2,1)}, bf16[2048,768]{1,0:T(8,128)(2,1)}) custom-call(bf16[2048,2048]{1,0:T(8,128)(2,1)} %shard_map.266.normed_ref, bf16[2048,1024]{1,0:T(8,128)(2,1)} %get-tuple-element.201.up_ref.w_one_ref, bf16[2048,768]{1,0:T(8,128)(2,1)} %copy-done, f32[1,1792]{1,0:T(1,128)} %reshape_add_fusion.shift_ref), custom_call_target="tpu_custom_call" | custom-call | flops 1048576 | bytes 1048576 | tf_op jit(solution)/shard_map/pallas_call | solution.py:752
  211.4 7.3 %shard_map.268 = (bf16[8,256,256]{2,1,0:T(8,128)(2,1)S(1)}, bf16[8,256,256]{2,1,0:T(8,128)(2,1)S(1)}, bf16[8,256,256]{2,1,0:T(8,128)(2,1)S(1)}) custom-call(s32[17]{0:T(128)S(1)} %pad_add_fusion.1.seq_ref, bf16[8,256,768]{2,1,0:T(8,128)(2,1)} %bitcast.137, f32[8,256,128]{2,1,0:T(8,128)S(1)} %get-tuple-element.469.cos_ref, ...), custom_call_target="tpu_custom_call" | custom-call | flops 1048576 | bytes 1048576 | tf_op jit(solution)/shard_map/pallas_call | solution.py:523
  221.6 11.3 %shard_map.270 = (bf16[256,2048]{1,0:T(8,128)(2,1)}, bf16[256,2048]{1,0:T(8,128)(2,1)}, bf16[256,2048]{1,0:T(8,128)(2,1)}, bf16[256,2048]{1,0:T(8,128)(2,1)}) custom-call(bf16[2048,1024]{1,0:T(8,128)(2,1)} %get-tuple-element.203.one_ref.act_ref, bf16[2048,256]{1,0:T(8,128)(2,1)} %bitcast.112, bf16[1024,2048]{1,0:T(8,128)(2,1)} %refs_4_.3, ...), custom_call_target="tpu_custom_call" | custom-call | flops 1048576 | bytes 1048576 | tf_op jit(solution)/shard_map/pallas_call | solution.py:796
  240.3 10.9 %shard_map.269 = (bf16[256,2048]{1,0:T(8,128)(2,1)}, bf16[256,2048]{1,0:T(8,128)(2,1)}, bf16[256,2048]{1,0:T(8,128)(2,1)}, bf16[256,2048]{1,0:T(8,128)(2,1)}) custom-call(bf16[2048,1024]{1,0:T(8,128)(2,1)} %get-tuple-element.203.one_ref.act_ref, bf16[2048,256]{1,0:T(8,128)(2,1)} %bitcast.113, bf16[1024,2048]{1,0:T(8,128)(2,1)} %refs_4_.3, ...), custom_call_target="tpu_custom_call" | custom-call | flops 1048576 | bytes 1048576 | tf_op jit(solution)/shard_map/pallas_call | solution.py:796
  251.2 11.5 %shard_map.271 = (bf16[2048,1024]{1,0:T(8,128)(2,1)}, bf16[2048,256]{1,0:T(8,128)(2,1)}, f32[1,1024]{1,0:T(1,128)}) custom-call(bf16[256,2048]{1,0:T(8,128)(2,1)} %bitcast.1.refs_0_, bf16[256,2048]{1,0:T(8,128)(2,1)} %collective-permute-done.18.refs_1_, bf16[256,2048]{1,0:T(8,128)(2,1)} %copy-done.15, bf16[256,2048]{1,0:T(8,128)(2,1)} %copy-done.16, ...), custom_call_target="tpu_custom_call" | custom-call | flops 1048576 | bytes 1048576 | tf_op jit(solution)/shard_map/pallas_call | solution.py:839
  266.0 11.3 %shard_map.272 = (bf16[2048,1024]{1,0:T(8,128)(2,1)}, bf16[2048,256]{1,0:T(8,128)(2,1)}, f32[1,1024]{1,0:T(1,128)}) custom-call(bf16[256,2048]{1,0:T(8,128)(2,1)} %collective-permute-done.12.refs_0_.refs_4_, bf16[256,2048]{1,0:T(8,128)(2,1)} %copy-done.19, bf16[256,2048]{1,0:T(8,128)(2,1)} %copy-done.20, ...), custom_call_target="tpu_custom_call", output_to_operand_aliasing={{0}: (7, {}), {1}: (8, {})} | custom-call | flops 1048576 | bytes 1048576 | tf_op jit(solution)/shard_map/pallas_call | solution.py:839
  278.6 16.4 %shard_map.273 = (bf16[2048,1024]{1,0:T(8,128)(2,1)}, f32[2048,2]{1,0:T(8,128)}) custom-call(bf16[2048,2048]{1,0:T(8,128)(2,1)} %shard_map.266.normed_ref, bf16[2048,1024]{1,0:T(8,128)(2,1)} %get-tuple-element.231.right_ref.one_ref, bf16[2048,1024]{1,0:T(8,128)(2,1)} %copy-done.2, f32[2048,1]{1,0:T(8,128)} %copy.63.gain_ref, f32[2048,1]{1,0:T(8,128)} %copy.64.shift_ref, ...), custom_call_target="tpu_custom_call" | custom-call | flops 1048576 | bytes 1048576 | tf_op jit(solution)/shard_map/pallas_call | solution.py:883
  312.7 11.9 %shard_map.274 = (bf16[8,256,768]{2,1,0:T(8,128)(2,1)}, f32[1,768]{1,0:T(1,128)S(1)}) custom-call(s32[17]{0:T(128)S(1)} %pad_add_fusion.1.seq_ref, bf16[8,256,768]{2,1,0:T(8,128)(2,1)} %bitcast.138, bf16[8,256,256]{2,1,0:T(8,128)(2,1)S(1)} %bitcast.115, f32[8,256,128]{2,1,0:T(8,128)S(1)} %get-tuple-element.469.cos_ref, ...), custom_call_target="tpu_custom_call" | custom-call | flops 1048576 | bytes 1048576 | tf_op jit(solution)/shard_map/pallas_call | solution.py:539
  325.2 13.8 %shard_map.275 = (bf16[2048,768]{1,0:T(8,128)(2,1)}, f32[2048,2]{1,0:T(8,128)}) custom-call(bf16[2048,2048]{1,0:T(8,128)(2,1)} %shard_map.266.normed_ref, bf16[2048,768]{1,0:T(8,128)(2,1)} %bitcast.122, bf16[2048,768]{1,0:T(8,128)(2,1)} %copy-done.5, f32[2048,1]{1,0:T(8,128)} %copy.65.gain_ref, f32[2048,1]{1,0:T(8,128)} %copy.66.shift_ref, f32[1,768]{1,0:T(1,128)} %copy-done.10), custom_call_target="tpu_custom_call" | custom-call | flops 1048576 | bytes 1048576 | tf_op jit(solution)/shard_map/pallas_call | solution.py:883
  357.2 14.0 %shard_map.277 = (bf16[256,2048]{1,0:T(8,128)(2,1)}, bf16[256,2048]{1,0:T(8,128)(2,1)}, bf16[256,2048]{1,0:T(8,128)(2,1)}, bf16[256,2048]{1,0:T(8,128)(2,1)}) custom-call(bf16[2048,1024]{1,0:T(8,128)(2,1)} %get-tuple-element.231.right_ref.one_ref, bf16[2048,768]{1,0:T(8,128)(2,1)} %bitcast.123, bf16[2048,1024]{1,0:T(8,128)(2,1)} %get-tuple-element.201.up_ref.w_one_ref, ...), custom_call_target="tpu_custom_call" | custom-call | flops 1048576 | bytes 1048576 | tf_op jit(solution)/shard_map/pallas_call | solution.py:796
  371.3 14.3 %shard_map.276 = (bf16[256,2048]{1,0:T(8,128)(2,1)}, bf16[256,2048]{1,0:T(8,128)(2,1)}, bf16[256,2048]{1,0:T(8,128)(2,1)}, bf16[256,2048]{1,0:T(8,128)(2,1)}) custom-call(bf16[2048,1024]{1,0:T(8,128)(2,1)} %get-tuple-element.231.right_ref.one_ref, bf16[2048,768]{1,0:T(8,128)(2,1)} %bitcast.124, bf16[2048,1024]{1,0:T(8,128)(2,1)} %get-tuple-element.201.up_ref.w_one_ref, ...), custom_call_target="tpu_custom_call" | custom-call | flops 1048576 | bytes 1048576 | tf_op jit(solution)/shard_map/pallas_call | solution.py:796
  399.5 17.2 %shard_map.278 = bf16[1280,2048]{1,0:T(8,128)(2,1)} custom-call(bf16[2048,1024]{1,0:T(8,128)(2,1)} %get-tuple-element.203.one_ref.act_ref, bf16[2048,256]{1,0:T(8,128)(2,1)} %bitcast.114, bf16[256,2048]{1,0:T(8,128)(2,1)} %bitcast.1.refs_0_, bf16[256,2048]{1,0:T(8,128)(2,1)} %collective-permute-done.18.refs_1_, bf16[256,2048]{1,0:T(8,128)(2,1)} %copy-done.15, ...), custom_call_target="tpu_custom_call" | custom-call | flops 1048576 | bytes 1048576 | tf_op jit(solution)/shard_map/pallas_call | solution.py:934
  421.8 9.1 %collective-permute-done.38 = bf16[4,64,1024]{2,1,0:T(8,128)(2,1)S(1)} collective-permute-done((bf16[4,64,1024]{2,1,0:T(8,128)(2,1)S(1)}, bf16[4,64,1024]{2,1,0:T(8,128)(2,1)S(1)}, u32[]{:S(2)}, u32[]{:S(2)}) %collective-permute-start.38) | collective-permute-done | bytes 524320 | tf_op jit(solution)/shard_map/ppermute | solution.py:358
  442.2 23.4 %collective-permute-done.41 = bf16[4,64,768]{2,1,0:T(8,128)(2,1)S(1)} collective-permute-done((bf16[4,64,768]{2,1,0:T(8,128)(2,1)S(1)}, bf16[4,64,768]{2,1,0:T(8,128)(2,1)S(1)}, u32[]{:S(2)}, u32[]{:S(2)}) %collective-permute-start.41) | collective-permute-done | bytes 393248 | tf_op jit(solution)/shard_map/ppermute | solution.py:358
  477.1 33.2 %collective-permute-done.48 = bf16[2,2,64,768]{3,2,1,0:T(8,128)(2,1)S(1)} collective-permute-done((bf16[2,2,64,768]{3,2,1,0:T(8,128)(2,1)S(1)}, bf16[2,2,64,768]{3,2,1,0:T(8,128)(2,1)S(1)}, u32[]{:S(2)}, u32[]{:S(2)}) %collective-permute-start.48) | collective-permute-done | bytes 393248 | tf_op jit(solution)/shard_map/ppermute | solution.py:358
  520.7 27.0 %collective-permute-done.52 = bf16[2,2,64,768]{3,2,1,0:T(8,128)(2,1)S(1)} collective-permute-done((bf16[2,2,64,768]{3,2,1,0:T(8,128)(2,1)S(1)}, bf16[2,2,64,768]{3,2,1,0:T(8,128)(2,1)S(1)}, u32[]{:S(2)}, u32[]{:S(2)}) %collective-permute-start.52) | collective-permute-done | bytes 393248 | tf_op jit(solution)/shard_map/ppermute | solution.py:358
  558.5 16.3 %collective-permute-done.55 = bf16[256,2048]{1,0:T(8,128)(2,1)S(1)} collective-permute-done((bf16[256,2048]{1,0:T(8,128)(2,1)S(1)}, bf16[256,2048]{1,0:T(8,128)(2,1)S(1)}, u32[]{:S(2)}, u32[]{:S(2)}) %collective-permute-start.55) | collective-permute-done | bytes 1048608 | tf_op jit(solution)/shard_map/ppermute | solution.py:358
  583.3 16.3 %collective-permute-done.62 = f32[24576]{0:T(1024)S(1)} collective-permute-done((f32[24576]{0:T(1024)S(1)}, f32[24576]{0:T(1024)S(1)}, u32[]{:S(2)}, u32[]{:S(2)}) %collective-permute-start.62) | collective-permute-done | bytes 98336 | tf_op jit(solution)/shard_map/ppermute | solution.py:358
  (364 shorter events, 247.7 us)
Async XLA Ops:
  36.3 43.5 %collective-permute-start.3 = (bf16[256,2048]{1,0:T(8,128)(2,1)}, bf16[256,2048]{1,0:T(8,128)(2,1)S(1)}, u32[]{:S(2)}, u32[]{:S(2)}) collective-permute-start(bf16[256,2048]{1,0:T(8,128)(2,1)} %collective-permute-done.refs_1_), channel_id=1, source_target_pairs={{0,1},{1,0},{2,3},{3,2},{4,5},{5,4},{6,7},{7,6},{8,9},{9,8},{10,11... | collective-permute-start | bytes 3145736 | tf_op jit(solution)/shard_map/ppermute | solution.py:358
  37.8 44.4 %collective-permute-start.7 = (bf16[256,2048]{1,0:T(8,128)(2,1)S(1)}, bf16[256,2048]{1,0:T(8,128)(2,1)S(1)}, u32[]{:S(2)}, u32[]{:S(2)}) collective-permute-start(bf16[256,2048]{1,0:T(8,128)(2,1)S(1)} %bitcast.128), channel_id=1, source_target_pairs={{0,1},{1,0},{2,3},{3,2},{4,5},{5,4},{6,7},{7,6},{8,9},{9,8},{10,11... | collective-permute-start | bytes 3145736 | tf_op jit(solution)/shard_map/ppermute | solution.py:358
  40.9 38.8 %collective-permute-start.5 = (bf16[2,64,1792]{2,1,0:T(8,128)(2,1)S(1)}, bf16[2,64,1792]{2,1,0:T(8,128)(2,1)S(1)}, u32[]{:S(2)}, u32[]{:S(2)}) collective-permute-start(bf16[2,64,1792]{2,1,0:T(8,128)(2,1)S(1)} %pad_maximum_fusion.9), channel_id=1, source_target_pairs={{0,4},{1,5},{2,6},{3,7},{4,0},{5,1},{6,2},{7,3},{8,12},{9,13},{10,... | collective-permute-start | bytes 1376264 | tf_op jit(solution)/shard_map/ppermute | solution.py:358
  89.3 41.7 %collective-permute-start.16 = (bf16[8,64,1792]{2,1,0:T(8,128)(2,1)}, bf16[8,64,1792]{2,1,0:T(8,128)(2,1)}, u32[]{:S(2)}, u32[]{:S(2)}) collective-permute-start(bf16[8,64,1792]{2,1,0:T(8,128)(2,1)} %bitcast.18.p0_ref), channel_id=1, source_target_pairs={{0,8},{8,0},{16,24},{24,16},{1,9},{9,1},{17,25},{25,17},{2,10},{10... | collective-permute-start | bytes 5505032 | tf_op jit(solution)/shard_map/ppermute | solution.py:358
  155.9 51.8 %collective-permute-start.21 = (bf16[256,2048]{1,0:T(8,128)(2,1)}, bf16[256,2048]{1,0:T(8,128)(2,1)}, u32[]{:S(2)}, u32[]{:S(2)}) collective-permute-start(bf16[256,2048]{1,0:T(8,128)(2,1)} %collective-permute-done.14), channel_id=1, source_target_pairs={{2,0},{3,1},{4,6},{5,7},{10,8},{11,9},{12,14},{13,15},{18,16},{19,... | collective-permute-start | bytes 3145736 | tf_op jit(solution)/shard_map/ppermute | solution.py:362
  262.7 35.5 %collective-permute-start.26 = (bf16[256,2048]{1,0:T(8,128)(2,1)}, bf16[256,2048]{1,0:T(8,128)(2,1)}, u32[]{:S(2)}, u32[]{:S(2)}) collective-permute-start(bf16[256,2048]{1,0:T(8,128)(2,1)} %get-tuple-element.236), channel_id=1, source_target_pairs={{0,1},{1,0},{2,3},{3,2},{4,5},{5,4},{6,7},{7,6},{8,9},{9,8},{10,11... | collective-permute-start | bytes 3145736 | tf_op jit(solution)/shard_map/ppermute | solution.py:358
  298.2 43.5 %collective-permute-start.29 = (bf16[16,64,1024]{2,1,0:T(8,128)(2,1)}, bf16[16,64,1024]{2,1,0:T(8,128)(2,1)}, u32[]{:S(2)}, u32[]{:S(2)}) collective-permute-start(bf16[16,64,1024]{2,1,0:T(8,128)(2,1)} %dynamic-slice_bitcast_fusion.1), channel_id=1, source_target_pairs={{0,8},{8,0},{16,24},{24,16},{1,9},{9,1},{17,25},{25,17},{2,10},{10... | collective-permute-start | bytes 6291464 | tf_op jit(solution)/shard_map/ppermute | solution.py:358
  301.0 40.8 %collective-permute-start.28 = (bf16[256,2048]{1,0:T(8,128)(2,1)}, bf16[256,2048]{1,0:T(8,128)(2,1)}, u32[]{:S(2)}, u32[]{:S(2)}) collective-permute-start(bf16[256,2048]{1,0:T(8,128)(2,1)} %add_convert_fusion.8), channel_id=1, source_target_pairs={{0,2},{1,3},{6,4},{7,5},{8,10},{9,11},{14,12},{15,13},{16,18},{17,... | collective-permute-start | bytes 3145736 | tf_op jit(solution)/shard_map/ppermute | solution.py:362
  306.0 35.8 %collective-permute-start.27 = (bf16[256,2048]{1,0:T(8,128)(2,1)}, bf16[256,2048]{1,0:T(8,128)(2,1)}, u32[]{:S(2)}, u32[]{:S(2)}) collective-permute-start(bf16[256,2048]{1,0:T(8,128)(2,1)} %get-tuple-element.241), channel_id=1, source_target_pairs={{0,1},{1,0},{2,3},{3,2},{4,5},{5,4},{6,7},{7,6},{8,9},{9,8},{10,11... | collective-permute-start | bytes 3145736 | tf_op jit(solution)/shard_map/ppermute | solution.py:358
  341.8 43.8 %collective-permute-start.34 = (bf16[16,64,768]{2,1,0:T(8,128)(2,1)}, bf16[16,64,768]{2,1,0:T(8,128)(2,1)}, u32[]{:S(2)}, u32[]{:S(2)}) collective-permute-start(bf16[16,64,768]{2,1,0:T(8,128)(2,1)} %dynamic-slice_bitcast_fusion.2), channel_id=1, source_target_pairs={{0,8},{8,0},{16,24},{24,16},{1,9},{9,1},{17,25},{25,17},{2,10},{10... | collective-permute-start | bytes 4718600 | tf_op jit(solution)/shard_map/ppermute | solution.py:358
  345.1 40.4 %collective-permute-start.32 = (bf16[256,2048]{1,0:T(8,128)(2,1)}, bf16[256,2048]{1,0:T(8,128)(2,1)}, u32[]{:S(2)}, u32[]{:S(2)}) collective-permute-start(bf16[256,2048]{1,0:T(8,128)(2,1)} %add_convert_fusion.7), channel_id=1, source_target_pairs={{2,4},{3,5},{4,2},{5,3},{10,12},{11,13},{12,10},{13,11},{18,20},{1... | collective-permute-start | bytes 3145736 | tf_op jit(solution)/shard_map/ppermute | solution.py:362
  346.7 38.8 %collective-permute-start.33 = (bf16[256,2048]{1,0:T(8,128)(2,1)}, bf16[256,2048]{1,0:T(8,128)(2,1)S(1)}, u32[]{:S(2)}, u32[]{:S(2)}) collective-permute-start(bf16[256,2048]{1,0:T(8,128)(2,1)} %add_convert_fusion.7), channel_id=1, source_target_pairs={{0,2},{1,3},{6,4},{7,5},{8,10},{9,11},{14,12},{15,13},{16,18},{17,... | collective-permute-start | bytes 3145736 | tf_op jit(solution)/shard_map/ppermute | solution.py:362
  388.4 42.5 %collective-permute-start.39 = (bf16[8,64,768]{2,1,0:T(8,128)(2,1)}, bf16[8,64,768]{2,1,0:T(8,128)(2,1)}, u32[]{:S(2)}, u32[]{:S(2)}) collective-permute-start(bf16[8,64,768]{2,1,0:T(8,128)(2,1)} %dynamic-slice_bitcast_fusion.4), channel_id=1, source_target_pairs={{0,16},{8,24},{16,0},{24,8},{1,17},{9,25},{17,1},{25,9},{2,18},{10... | collective-permute-start | bytes 2359304 | tf_op jit(solution)/shard_map/ppermute | solution.py:358
  391.1 39.8 %collective-permute-start.37 = (bf16[256,2048]{1,0:T(8,128)(2,1)S(1)}, bf16[256,2048]{1,0:T(8,128)(2,1)S(1)}, u32[]{:S(2)}, u32[]{:S(2)}) collective-permute-start(bf16[256,2048]{1,0:T(8,128)(2,1)S(1)} %add_convert_fusion.5), channel_id=1, source_target_pairs={{2,4},{3,5},{4,2},{5,3},{10,12},{11,13},{12,10},{13,11},{18,20},{1... | collective-permute-start | bytes 3145736 | tf_op jit(solution)/shard_map/ppermute | solution.py:362
  394.0 36.9 %collective-permute-start.36 = (bf16[256,2048]{1,0:T(8,128)(2,1)S(1)}, bf16[256,2048]{1,0:T(8,128)(2,1)}, u32[]{:S(2)}, u32[]{:S(2)}) collective-permute-start(bf16[256,2048]{1,0:T(8,128)(2,1)S(1)} %add_convert_fusion.6), channel_id=1, source_target_pairs={{0,2},{1,3},{2,0},{3,1},{4,6},{5,7},{6,4},{7,5},{8,10},{9,11},{10,... | collective-permute-start | bytes 3145736 | tf_op jit(solution)/shard_map/ppermute | solution.py:358
  395.6 35.3 %collective-permute-start.35 = (bf16[256,2048]{1,0:T(8,128)(2,1)}, bf16[256,2048]{1,0:T(8,128)(2,1)}, u32[]{:S(2)}, u32[]{:S(2)}) collective-permute-start(bf16[256,2048]{1,0:T(8,128)(2,1)} %get-tuple-element.268), channel_id=1, source_target_pairs={{0,1},{1,0},{2,3},{3,2},{4,5},{5,4},{6,7},{7,6},{8,9},{9,8},{10,11... | collective-permute-start | bytes 3145736 | tf_op jit(solution)/shard_map/ppermute | solution.py:358
  430.9 34.7 %collective-permute-start.43 = (bf16[1,640,2048]{2,1,0:T(8,128)(2,1)}, bf16[1,640,2048]{2,1,0:T(8,128)(2,1)}, u32[]{:S(2)}, u32[]{:S(2)}) collective-permute-start(bf16[1,640,2048]{2,1,0:T(8,128)(2,1)} %dynamic-slice_bitcast_fusion), channel_id=1, source_target_pairs={{0,8},{8,0},{16,24},{24,16},{1,9},{9,1},{17,25},{25,17},{2,10},{10... | collective-permute-start | bytes 7864328 | tf_op jit(solution)/shard_map/ppermute | solution.py:358
  466.0 44.3 %collective-permute-start.46 = (bf16[256,2048]{1,0:T(8,128)(2,1)S(1)}, bf16[256,2048]{1,0:T(8,128)(2,1)S(1)}, u32[]{:S(2)}, u32[]{:S(2)}) collective-permute-start(bf16[256,2048]{1,0:T(8,128)(2,1)S(1)} %add_convert_fusion.4), channel_id=1, source_target_pairs={{0,2},{1,3},{6,4},{7,5},{8,10},{9,11},{14,12},{15,13},{16,18},{17,... | collective-permute-start | bytes 3145736 | tf_op jit(solution)/shard_map/ppermute | solution.py:362
  468.9 41.4 %collective-permute-start.45 = (bf16[256,2048]{1,0:T(8,128)(2,1)S(1)}, bf16[256,2048]{1,0:T(8,128)(2,1)S(1)}, u32[]{:S(2)}, u32[]{:S(2)}) collective-permute-start(bf16[256,2048]{1,0:T(8,128)(2,1)S(1)} %copy-done.51), channel_id=1, source_target_pairs={{0,1},{1,0},{2,3},{3,2},{4,5},{5,4},{6,7},{7,6},{8,9},{9,8},{10,11... | collective-permute-start | bytes 3145736 | tf_op jit(solution)/shard_map/ppermute | solution.py:358
  473.3 74.4 %collective-permute-start.53 = (bf16[640,2048]{1,0:T(8,128)(2,1)S(1)}, bf16[640,2048]{1,0:T(8,128)(2,1)S(1)}, u32[]{:S(2)}, u32[]{:S(2)}) collective-permute-start(bf16[640,2048]{1,0:T(8,128)(2,1)S(1)} %fusion.3), channel_id=1, source_target_pairs={{0,16},{8,24},{16,0},{24,8},{1,17},{9,25},{17,1},{25,9},{2,18},{10... | collective-permute-start | bytes 7864328 | tf_op jit(solution)/shard_map/ppermute | solution.py:358
  474.3 36.0 %collective-permute-start.47 = (bf16[2,2,64,1024]{3,2,1,0:T(8,128)(2,1)S(1)}, bf16[2,2,64,1024]{3,2,1,0:T(8,128)(2,1)S(1)}, u32[]{:S(2)}, u32[]{:S(2)}) collective-permute-start(bf16[2,2,64,1024]{3,2,1,0:T(8,128)(2,1)S(1)} %pad_maximum_fusion.7), channel_id=1, source_target_pairs={{0,2},{1,3},{2,0},{3,1},{4,6},{5,7},{6,4},{7,5},{8,10},{9,11},{10,... | collective-permute-start | bytes 1572872 | tf_op jit(solution)/shard_map/ppermute | solution.py:358
  474.6 35.8 %collective-permute-start.48 = (bf16[2,2,64,768]{3,2,1,0:T(8,128)(2,1)S(1)}, bf16[2,2,64,768]{3,2,1,0:T(8,128)(2,1)S(1)}, u32[]{:S(2)}, u32[]{:S(2)}) collective-permute-start(bf16[2,2,64,768]{3,2,1,0:T(8,128)(2,1)S(1)} %pad_maximum_fusion.12), channel_id=1, source_target_pairs={{0,4},{1,5},{2,6},{3,7},{4,0},{5,1},{6,2},{7,3},{8,12},{9,13},{10,... | collective-permute-start | bytes 1179656 | tf_op jit(solution)/shard_map/ppermute | solution.py:358
  510.9 36.8 %collective-permute-start.50 = (bf16[256,2048]{1,0:T(8,128)(2,1)S(1)}, bf16[256,2048]{1,0:T(8,128)(2,1)S(1)}, u32[]{:S(2)}, u32[]{:S(2)}) collective-permute-start(bf16[256,2048]{1,0:T(8,128)(2,1)S(1)} %add_convert_fusion.3), channel_id=1, source_target_pairs={{2,4},{3,5},{4,2},{5,3},{10,12},{11,13},{12,10},{13,11},{18,20},{1... | collective-permute-start | bytes 3145736 | tf_op jit(solution)/shard_map/ppermute | solution.py:362
  511.7 36.1 %collective-permute-start.51 = (bf16[256,2048]{1,0:T(8,128)(2,1)S(1)}, bf16[256,2048]{1,0:T(8,128)(2,1)S(1)}, u32[]{:S(2)}, u32[]{:S(2)}) collective-permute-start(bf16[256,2048]{1,0:T(8,128)(2,1)S(1)} %add_convert_fusion.3), channel_id=1, source_target_pairs={{0,2},{1,3},{6,4},{7,5},{8,10},{9,11},{14,12},{15,13},{16,18},{17,... | collective-permute-start | bytes 3145736 | tf_op jit(solution)/shard_map/ppermute | solution.py:362
  (100 other events, 1746.8 us)

commit v3 on v2

--- a/solution.py
+++ b/solution.py
@@ -389,7 +389,7 @@
 def token_labels(my_index, shape, dim):
     inner = lax.broadcasted_iota(jnp.int32, shape, dim)
     block = inner // TILE_ROWS
-    apart = (block % 4) * 2 + block // 4
+    apart = block // 4 * 4 + block % 2 * 2 + block // 2 % 2
     return (inner % TILE_ROWS) * HEADS + jnp.bitwise_xor(apart, my_index)
 
 
@@ -628,38 +628,40 @@
 
 
 def place_halves_kernel(core_ref, mine_ref, other_ref, down_ref, dense_ref, *, cut):
-    step = pl.program_id(0)
-    first = (step < pl.num_programs(0) // 2) == (core_ref[0] == 0)
-    values = jnp.where(first, mine_ref[...], other_ref[...]).astype(F32)
-    in_down = step < cut
-
-    @pl.when(in_down)
+    half = mine_ref.shape[1]
+
+    def fill(out_ref):
+        for part_ref, core in ((mine_ref, core_ref[0]), (other_ref, 1 - core_ref[0])):
+            start = pl.multiple_of(core * half, half)
+            out_ref[:, pl.ds(start, half)] = part_ref[...].astype(F32)
+
+    @pl.when(pl.program_id(0) < cut)
     def _():
-        down_ref[...] = values
-
-    @pl.when(jnp.logical_not(in_down))
+        fill(down_ref)
+
+    @pl.when(pl.program_id(0) >= cut)
     def _():
-        dense_ref[...] = values
+        fill(dense_ref)
 
 
 def place_halves(core, mine, other, hidden):
-    rows, width = mine.shape
-    tile = 128
-    half, cut = rows // tile, hidden // tile
-    part = pl.BlockSpec((tile, width), lambda i, core_ref: (i % half, 0))
+    rows, half = mine.shape
+    tile = 256
+    cut = hidden // tile
+    part = pl.BlockSpec((tile, half), lambda i, core_ref: (i, 0))
     return pl.pallas_call(
         functools.partial(place_halves_kernel, cut=cut),
         out_shape=(
-            jax.ShapeDtypeStruct((hidden, width), F32),
-            jax.ShapeDtypeStruct((2 * rows - hidden, width), F32),
+            jax.ShapeDtypeStruct((hidden, 2 * half), F32),
+            jax.ShapeDtypeStruct((rows - hidden, 2 * half), F32),
         ),
         grid_spec=pltpu.PrefetchScalarGridSpec(
             num_scalar_prefetch=1,
-            grid=(2 * half,),
+            grid=(rows // tile,),
             in_specs=[part, part],
             out_specs=(
-                pl.BlockSpec((tile, width), lambda i, core_ref: (jnp.minimum(i, cut - 1), 0)),
-                pl.BlockSpec((tile, width), lambda i, core_ref: (jnp.maximum(i - cut, 0), 0)),
+                pl.BlockSpec((tile, 2 * half), lambda i, core_ref: (jnp.minimum(i, cut - 1), 0)),
+                pl.BlockSpec((tile, 2 * half), lambda i, core_ref: (jnp.maximum(i - cut, 0), 0)),
             ),
         ),
         compiler_params=pltpu.CompilerParams(vmem_limit_bytes=32 << 20),
@@ -728,7 +730,8 @@
     return [pl.BlockSpec((tile, width), lambda i: (0, 0)) for _ in range(count)]
 
 
-def project_kernel(normed_ref, up_ref, qkv_w_ref, shift_ref, act_ref, slope_ref, qkv_ref):
+def project_kernel(normed_ref, up_ref, qkv_w_ref, shift_ref, *refs):
+    act_ref, slope_ref, qkv_ref = refs[-3:]
     hidden = act_ref.shape[1]
     lanes = 256
     for start in range(0, hidden, lanes):
@@ -745,149 +748,188 @@
         qkv_ref[:, columns] = value.astype(BF16)
 
 
-def project(normed, w_up, w_qkv, shift):
+def project(normed, w_up, w_qkv, shift, first, last, buffers):
     count, width = normed.shape
-    hidden, rest = w_up.shape[1], w_qkv.shape[1]
-    tile = 512
+    tile = 2 * count // HEADS
+    widths = (w_up.shape[1], w_up.shape[1], w_qkv.shape[1])
     return pl.pallas_call(
         project_kernel,
-        out_shape=(
-            jax.ShapeDtypeStruct((count, hidden), BF16),
-            jax.ShapeDtypeStruct((count, hidden), BF16),
-            jax.ShapeDtypeStruct((count, rest), BF16),
-        ),
-        grid=(count // tile,),
+        out_shape=tuple(jax.ShapeDtypeStruct((count, n), BF16) for n in widths),
+        grid=(last - first,),
         in_specs=[
-            tokens_spec(tile, width, 0),
+            tokens_spec(tile, width, first),
             whole_spec(w_up.shape),
             whole_spec(w_qkv.shape),
             whole_spec(shift.shape),
-        ],
-        out_specs=(
-            tokens_spec(tile, hidden, 0),
-            tokens_spec(tile, hidden, 0),
-            tokens_spec(tile, rest, 0),
-        ),
+        ]
+        + [pl.BlockSpec(memory_space=pl.ANY)] * len(buffers),
+        out_specs=tuple(tokens_spec(tile, n, first) for n in widths),
+        input_output_aliases={4 + k: k for k in range(len(buffers))},
         compiler_params=pltpu.CompilerParams(vmem_limit_bytes=BIG_VMEM),
         cost_estimate=SMALL_COST,
-    )(normed, w_up, w_qkv, shift)
-
-
-def combine_kernel(one_ref, two_ref, w_one_ref, w_two_ref, *out_refs, right_dim):
-    lanes = 512
-    width = w_one_ref.shape[1 - right_dim]
-    for k, out_ref in enumerate(out_refs):
-
-        @pl.when(pl.program_id(0) == k)
-        def _(out_ref=out_ref):
-            for start in range(0, width, lanes):
-                columns = slice(start, start + lanes)
-                if right_dim:
-                    w_one, w_two = w_one_ref[columns, :], w_two_ref[columns, :]
-                else:
-                    w_one, w_two = w_one_ref[:, columns], w_two_ref[:, columns]
-                value = dot32(one_ref[...], w_one, 1, right_dim)
-                value = value + dot32(two_ref[...], w_two, 1, right_dim)
-                out_ref[:, columns] = value.astype(BF16)
-
-
-def combine(one, two, w_one, w_two, rows, first, right_dim):
+    )(normed, w_up, w_qkv, shift, *buffers)
+
+
+def combine_kernel(one_a_ref, one_b_ref, two_a_ref, two_b_ref, w_one_ref, w_two_ref, *out_refs, right_dim):
+    rows = out_refs[0].shape[0]
+    for pair, (one_ref, two_ref) in enumerate(((one_a_ref, two_a_ref), (one_b_ref, two_b_ref))):
+        value = dot32(one_ref[...], w_one_ref[...], 1, right_dim)
+        value = value + dot32(two_ref[...], w_two_ref[...], 1, right_dim)
+        out_refs[2 * pair][...] = value[:rows].astype(BF16)
+        out_refs[2 * pair + 1][...] = value[rows:].astype(BF16)
+
+
+def combine(one, two, w_one, w_two, rows, side, right_dim):
     width = w_one.shape[1 - right_dim]
+    lanes = 256
+
+    def weight_spec(weight):
+        if right_dim:
+            return pl.BlockSpec((lanes, weight.shape[1]), lambda i: (i, 0))
+        return pl.BlockSpec((weight.shape[0], lanes), lambda i: (0, i))
+
+    def left_spec(left, pair):
+        return pl.BlockSpec(
+            (2 * rows, left.shape[1]),
+            lambda i: (2 * pair + side, 0),
+            pipeline_mode=pl.Buffered(1),
+        )
+
     return pl.pallas_call(
         functools.partial(combine_kernel, right_dim=right_dim),
         out_shape=tuple(jax.ShapeDtypeStruct((rows, width), BF16) for _ in range(4)),
-        grid=(4,),
-        in_specs=[
-            tokens_spec(rows, one.shape[1], first),
-            tokens_spec(rows, two.shape[1], first),
-            whole_spec(w_one.shape),
-            whole_spec(w_two.shape),
-        ],
-        out_specs=tuple(block_specs(4, rows, width)),
+        grid=(width // lanes,),
+        in_specs=[left_spec(left, pair) for left in (one, two) for pair in (0, 1)]
+        + [weight_spec(w_one), weight_spec(w_two)],
+        out_specs=tuple(pl.BlockSpec((rows, lanes), lambda i: (0, i)) for _ in range(4)),
         compiler_params=pltpu.CompilerParams(vmem_limit_bytes=BIG_VMEM),
         cost_estimate=SMALL_COST,
-    )(one, two, w_one, w_two)
-
-
-def pull_kernel(*refs, extra):
-    blocks, (w_one_ref, w_two_ref, slope_ref) = refs[:4], refs[4:7]
-    pre_ref, att_ref, sum_ref = refs[7 + extra :]
-    hidden = w_one_ref.shape[0]
-    lanes = 256
+    )(one, one, two, two, w_one, w_two)
+
+
+def pull_kernel(*refs, count):
+    blocks, (w_one_ref, w_two_ref, slope_ref) = refs[:count], refs[count : count + 3]
+    pre_ref, att_ref, sum_ref, left_ref, sems = refs[-5:]
+    rows = blocks[0].shape[0]
+    last = pl.num_programs(0) - 1
 
     @pl.when(pl.program_id(0) == 0)
     def _():
-        sum_ref[...] = jnp.zeros_like(sum_ref)
-
-    for k, block_ref in enumerate(blocks):
-
-        @pl.when(pl.program_id(0) == k)
-        def _(block_ref=block_ref):
-            for start in range(0, hidden, lanes):
-                columns = slice(start, start + lanes)
-                value = dot32(block_ref[...], w_one_ref[columns, :], 1, 1)
-                value = (value * slope_ref[:, columns].astype(F32)).astype(BF16)
-                pre_ref[:, columns] = value
-                sum_ref[:, columns] += jnp.sum(value.astype(F32), axis=0, keepdims=True)
-            att_ref[...] = dot32(block_ref[...], w_two_ref[...], 1, 1).astype(BF16)
-
-
-def pull(blocks, w_down, w_dense, slope, half, buffers):
+        copies = [
+            pltpu.make_async_copy(block, left_ref.at[pl.ds(k * rows, rows)], sems.at[k])
+            for k, block in enumerate(blocks)
+        ]
+        for copy in copies:
+            copy.start()
+        for copy in copies:
+            copy.wait()
+
+    @pl.when(pl.program_id(0) < last)
+    def _():
+        value = dot32(left_ref[...], w_one_ref[...], 1, 1)
+        value = (value * slope_ref[...].astype(F32)).astype(BF16)
+        pre_ref[...] = value
+        sum_ref[...] = jnp.sum(value.astype(F32), axis=0, keepdims=True)
+
+    @pl.when(pl.program_id(0) == last)
+    def _():
+        att_ref[...] = dot32(left_ref[...], w_two_ref[...], 1, 1).astype(BF16)
+
+
+def pull(blocks, w_down, w_dense, slope, part, buffers):
     rows, width = blocks[0].shape
     hidden, head = w_down.shape[0], w_dense.shape[0]
-    count = HEADS * rows
+    tokens = HEADS * rows
+    count = len(blocks)
+    lanes = 256
+    steps = hidden // lanes
+
+    def at(i):
+        return jnp.minimum(i, steps - 1)
+
+    anywhere = pl.BlockSpec(memory_space=pl.ANY)
     return pl.pallas_call(
-        functools.partial(pull_kernel, extra=len(buffers)),
+        functools.partial(pull_kernel, count=count),
         out_shape=(
-            jax.ShapeDtypeStruct((count, hidden), BF16),
-            jax.ShapeDtypeStruct((count, head), BF16),
+            jax.ShapeDtypeStruct((tokens, hidden), BF16),
+            jax.ShapeDtypeStruct((tokens, head), BF16),
             jax.ShapeDtypeStruct((1, hidden), F32),
         ),
-        grid=(4,),
-        in_specs=block_specs(4, rows, width)
-        + [whole_spec(w_down.shape), whole_spec(w_dense.shape), tokens_spec(rows, hidden, 4 * half)]
-        + [pl.BlockSpec(memory_space=pl.ANY)] * len(buffers),
+        grid=(steps + 1,),
+        in_specs=[anywhere] * count
+        + [
+            pl.BlockSpec((lanes, width), lambda i: (at(i), 0)),
+            whole_spec(w_dense.shape),
+            pl.BlockSpec((count * rows, lanes), lambda i: (part, at(i))),
+        ]
+        + [anywhere] * len(buffers),
         out_specs=(
-            tokens_spec(rows, hidden, 4 * half),
-            tokens_spec(rows, head, 4 * half),
-            pl.BlockSpec((1, hidden), lambda i: (0, 0)),
+            pl.BlockSpec((count * rows, lanes), lambda i: (part, at(i))),
+            pl.BlockSpec((count * rows, head), lambda i: (part, 0)),
+            pl.BlockSpec((1, lanes), lambda i: (0, at(i))),
         ),
-        input_output_aliases={7 + k: k for k in range(len(buffers))},
+        scratch_shapes=[pltpu.VMEM((count * rows, width), BF16), pltpu.SemaphoreType.DMA((count,))],
+        input_output_aliases={count + 3 + k: k for k in range(len(buffers))},
         compiler_params=pltpu.CompilerParams(vmem_limit_bytes=BIG_VMEM),
         cost_estimate=SMALL_COST,
     )(*blocks, w_down, w_dense, slope, *buffers)
 
 
-def moments_kernel(normed_ref, right_ref, weight_ref, gain_ref, shift_ref, columns_ref, out_ref, sums_ref):
+def moments_kernel(
+    core_ref,
+    normed_ref,
+    right_ref,
+    weight_ref,
+    gain_ref,
+    shift_ref,
+    columns_ref,
+    keep_ref,
+    give_ref,
+    sums_ref,
+    low_ref,
+    *,
+    quarter,
+):
     lanes = 256
     turned = normed_ref[...].T
     gain, shift = gain_ref[...], shift_ref[...]
     gain_terms, bias_terms = None, None
-    for start in range(0, out_ref.shape[1], lanes):
+    for start in range(0, low_ref.shape[1], lanes):
         columns = slice(start, start + lanes)
         moment = dot32(turned, right_ref[:, columns])
         weight = weight_ref[:, columns].astype(F32)
         total = columns_ref[:, columns]
-        out_ref[:, columns] = (moment * gain + shift * total).astype(BF16)
+        low_ref[:, columns] = (moment * gain + shift * total).astype(BF16)
         one, two = moment * weight, weight * total
         gain_terms = one if gain_terms is None else gain_terms + one
         bias_terms = two if bias_terms is None else bias_terms + two
     sums_ref[:, 0:1] = jnp.sum(gain_terms, axis=1, keepdims=True)
     sums_ref[:, 1:2] = jnp.sum(bias_terms, axis=1, keepdims=True)
-
-
-def moments_of(normed, right, weight, gain, shift, columns):
+    for core in (0, 1):
+
+        @pl.when(core_ref[0] == core)
+        def _(core=core):
+            for k in range(low_ref.shape[0] // quarter):
+                target = keep_ref if k % 2 == core else give_ref
+                target[k // 2 * quarter : (k // 2 + 1) * quarter, :] = low_ref[
+                    k * quarter : (k + 1) * quarter, :
+                ]
+
+
+def moments_of(core, normed, right, weight, gain, shift, columns, quarter):
     count, width = normed.shape
     wide = weight.shape[1]
-    tile = 256
+    tile = 8 * quarter
     return pl.pallas_call(
-        moments_kernel,
+        functools.partial(moments_kernel, quarter=quarter),
         out_shape=(
-            jax.ShapeDtypeStruct((width, wide), BF16),
+            jax.ShapeDtypeStruct((width // 2, wide), BF16),
+            jax.ShapeDtypeStruct((width // 2, wide), BF16),
             jax.ShapeDtypeStruct((width, 2), F32),
         ),
         grid=(width // tile,),
         in_specs=[
+            SMEM_SPEC,
             pl.BlockSpec((count, tile), lambda i: (0, i)),
             whole_spec(right.shape),
             tokens_spec(tile, wide, 0),
@@ -895,19 +937,24 @@
             tokens_spec(tile, 1, 0),
             whole_spec(columns.shape),
         ],
-        out_specs=(tokens_spec(tile, wide, 0), tokens_spec(tile, 2, 0)),
+        out_specs=(
+            tokens_spec(tile // 2, wide, 0),
+            tokens_spec(tile // 2, wide, 0),
+            tokens_spec(tile, 2, 0),
+        ),
+        scratch_shapes=[pltpu.VMEM((tile, wide), BF16)],
         compiler_params=pltpu.CompilerParams(vmem_limit_bytes=BIG_VMEM),
         cost_estimate=SMALL_COST,
-    )(normed, right, weight, gain[:, None], shift[:, None], columns)
-
-
-def outer_kernel(act_ref, att_ref, *refs):
-    blocks, out_ref = refs[:HEADS], refs[HEADS]
+    )(core[None].astype(jnp.int32), normed, right, weight, gain, shift, columns)
+
+
+def outer_kernel(core_ref, act_ref, att_ref, *refs):
+    blocks, out_refs = refs[:HEADS], refs[HEADS:]
     rows = blocks[0].shape[0]
     lanes = 512
-    last = pl.num_programs(0) - 1
-
-    def fill(left_ref):
+    last = pl.num_programs(1) - 1
+
+    def fill(left_ref, out_ref):
         turned = left_ref[...].T
         for start in range(0, out_ref.shape[1], lanes):
             columns = slice(start, start + lanes)
@@ -917,33 +964,49 @@
                 total = term if total is None else total + term
             out_ref[:, columns] = total.astype(BF16)
 
-    @pl.when(pl.program_id(0) < last)
-    def _():
-        fill(act_ref)
-
-    @pl.when(pl.program_id(0) == last)
-    def _():
-        fill(att_ref)
-
-
-def outer(activated, attended, blocks):
+    for side in (0, 1):
+        for left_ref, chosen in (
+            (act_ref, pl.program_id(1) < last),
+            (att_ref, pl.program_id(1) == last),
+        ):
+
+            @pl.when((pl.program_id(0) == side) & chosen)
+            def _(left_ref=left_ref, side=side):
+                fill(left_ref, out_refs[side])
+
+
+def outer(core, activated, attended, blocks):
     count, hidden = activated.shape
     rows, width = blocks[0].shape
     tile = attended.shape[1]
     steps = hidden // tile
+    half = jax.ShapeDtypeStruct((hidden + tile, width // 2), BF16)
     return pl.pallas_call(
         outer_kernel,
-        out_shape=jax.ShapeDtypeStruct((hidden + tile, width), BF16),
-        grid=(steps + 1,),
-        in_specs=[
-            pl.BlockSpec((count, tile), lambda i: (0, jnp.minimum(i, steps - 1))),
-            whole_spec(attended.shape),
-        ]
-        + [whole_spec((rows, width)) for _ in blocks],
-        out_specs=tokens_spec(tile, width, 0),
+        out_shape=(half, half),
+        grid_spec=pltpu.PrefetchScalarGridSpec(
+            num_scalar_prefetch=1,
+            grid=(2, steps + 1),
+            in_specs=[
+                pl.BlockSpec((count, tile), lambda j, i, core_ref: (0, jnp.minimum(i, steps - 1))),
+                pl.BlockSpec((count, tile), lambda j, i, core_ref: (0, 0)),
+            ]
+            + [
+                pl.BlockSpec((rows, width // 2), lambda j, i, core_ref: (0, j ^ core_ref[0]))
+                for _ in blocks
+            ],
+            out_specs=(
+                pl.BlockSpec(
+                    (tile, width // 2), lambda j, i, core_ref: (jnp.where(j == 0, i, steps), 0)
+                ),
+                pl.BlockSpec(
+                    (tile, width // 2), lambda j, i, core_ref: (jnp.where(j == 0, 0, i), 0)
+                ),
+            ),
+        ),
         compiler_params=pltpu.CompilerParams(vmem_limit_bytes=BIG_VMEM),
         cost_estimate=SMALL_COST,
-    )(activated, attended, *blocks)
+    )(core[None].astype(jnp.int32), activated, attended, *blocks)
 
 
 def split_shards(
@@ -1002,7 +1065,7 @@
     )
     in_seq = row_range - jnp.sum(jnp.where(member, row_offsets[None, :], 0), axis=1)
     block_range = jnp.arange(HEADS, dtype=jnp.int32)
-    apart = (block_range % 4) * 2 + block_range // 4
+    apart = block_range // 4 * 4 + block_range % 2 * 2 + block_range // 2 % 2
     positions = (
         in_seq.reshape(rows // TILE_ROWS, 1, TILE_ROWS) * HEADS + (apart ^ me)[None, :, None]
     )
@@ -1015,9 +1078,18 @@
     sine = sine.reshape(tiled)
 
 
-    own, own_grad, x_near, x_across, odd_came, *keep = hold(
-        (own, own_grad, x_near, x_across, odd_came, *keep), (cosine, sine)
-    )
+    gains = jnp.stack([ln1_gain, ln2_gain], axis=1)
+    shifts = jnp.stack([ln1_bias, ln2_bias], axis=1)
+    tall = [vector[:, None] for vector in (ln1_gain, ln1_bias, ln2_gain, ln2_bias)]
+    b_in = jnp.concatenate(
+        [lax.dynamic_slice_in_dim(b_up, me * hidden, hidden, 0)]
+        + [lax.dynamic_slice_in_dim(b_qkv, k * width + me * HEAD, HEAD, 0) for k in range(3)]
+    )
+    own, own_grad, x_near, x_across, odd_came, gains, shifts, b_in, *both = hold(
+        (own, own_grad, x_near, x_across, odd_came, gains, shifts, b_in, *keep, *tall),
+        (cosine, sine),
+    )
+    keep, tall = both[:4], both[4:]
     pairs = [jnp.stack([keep[z], odd_came[z]]) for z in range(4)]
     got = [flip(pairs[z], "shard", 2 * z) for z in range(1, 4)]
     x_own_y = flip(own, "shard", 1)
@@ -1031,8 +1103,9 @@
     g_own_y = flip(own_grad, "shard", 1)
     beside = beside + [flip(jnp.stack(got), "rep", 2)]
     part = jnp.stack([pairs[0]] + got).reshape(HEADS, quarter, wide)
-    x_across_near, x_two, own_grad, *beside = hold(
-        (x_across_near, x_two, own_grad, *beside), (part, g_own_y)
+    normed = norm_blocks([own, x_near, x_own_y, x_near_y], (0, 1, 2, 3), None)
+    x_across_near, x_two, own_grad, normed, *beside = hold(
+        (x_across_near, x_two, own_grad, normed, *beside), (part, g_own_y)
     )
     two = jnp.where(is_middle, x_across_near, x_two)
     x_three = send(x_across_near, OUTWARD)
@@ -1041,57 +1114,48 @@
     beside = jnp.concatenate([beside[0][None], beside[1]]).reshape(HEADS, quarter, wide)
     part_c = flip(part, "rep", 1)
     beside_c = flip(beside, "rep", 1)
-    normed = norm_blocks([own, x_near, x_own_y, x_near_y, two], (0, 1, 4, 5, 2), None)
-    x_three, own_grad, g_across, beside_c, part_c, x_two_y = hold(
-        (x_three, own_grad, g_across, beside_c, part_c, x_two_y), (normed,)
+    normed = norm_blocks([two], (4,), normed)
+    parts = (part, part_c, beside, beside_c)
+    up_raw, qkv_raw, up_scaled, qkv_scaled, shifted = place_weights(
+        me, rep, parts, gains, shifts, hidden
+    )
+    b_in = b_in[None, :] + shifted
+    x_three, own_grad, g_across, x_two_y, normed, b_in = hold(
+        (x_three, own_grad, g_across, x_two_y, normed, b_in), ()
     )
     three = jnp.where(is_middle, x_across, x_three)
     g_near = flip(own_grad, "shard", 2)
     x_three_y = flip(three, "shard", 1)
-    parts = (part, part_c, beside, beside_c)
-    gains = jnp.stack([ln1_gain, ln2_gain], axis=1)
-    shifts = jnp.stack([ln1_bias, ln2_bias], axis=1)
-    up_raw, qkv_raw, up_scaled, qkv_scaled, shifted = place_weights(
-        me, rep, parts, gains, shifts, hidden
-    )
-    b_in = jnp.concatenate(
-        [lax.dynamic_slice_in_dim(b_up, me * hidden, hidden, 0)]
-        + [lax.dynamic_slice_in_dim(b_qkv, k * width + me * HEAD, HEAD, 0) for k in range(3)]
-    )
-    b_in = b_in[None, :] + shifted
-    normed = norm_blocks([three, x_two_y], (3, 6), normed)
-    g_near, x_three_y, normed = hold((g_near, x_three_y, normed), (b_in,))
+    normed = norm_blocks([three, x_two_y], (5, 6), normed)
+    halfway = project(normed, up_scaled, qkv_scaled, b_in, 0, 3, [])
+    g_near, x_three_y, *halfway = hold((g_near, x_three_y, *halfway), ())
     g_across_near = send(g_near, MIDDLE)
     g_two = send(g_across, OUTWARD)
     g_near_y = flip(g_near, "shard", 1)
     normed = norm_blocks([x_three_y], (7,), normed)
-    activated, slope, qkv = project(normed, up_scaled, qkv_scaled, b_in)
-    g_across_near, g_two, qkv, g_near_y = hold((g_across_near, g_two, qkv, g_near_y), (activated,))
+    activated, slope, qkv = project(normed, up_scaled, qkv_scaled, b_in, 3, 4, halfway)
+    qkv = qkv.reshape(HEADS, rows, 3 * HEAD)
+    attended, query, key = attend(seq_scalars, qkv, cosine, sine)
+    attended = attended.reshape(group_tokens, HEAD)
+    g_across_near, g_two, attended, g_near_y = hold((g_across_near, g_two, attended, g_near_y), ())
     g_two = jnp.where(is_middle, g_across_near, g_two)
     g_three = send(g_across_near, OUTWARD)
     g_two_y = flip(g_two, "shard", 1)
-    qkv = qkv.reshape(HEADS, rows, 3 * HEAD)
-    attended, query, key = attend(seq_scalars, qkv, cosine, sine)
-    attended = attended.reshape(group_tokens, HEAD)
-    far = combine(activated, attended, w_down, w_dense, rows, 4, 0)
-    g_three, g_two_y, *far = hold((g_three, g_two_y, *far), ())
+    far = combine(activated, attended, w_down, w_dense, rows, 1, 0)
+    close = combine(activated, attended, w_down, w_dense, rows, 0, 0)
+    g_three, g_near_y, g_two_y, *both = hold((g_three, g_near_y, g_two_y, *far, *close), ())
+    far, close = both[:4], both[4:]
     g_three = jnp.where(is_middle, g_across, g_three)
     g_three_y = flip(g_three, "shard", 1)
-    close = combine(activated, attended, w_down, w_dense, rows, 0, 0)
-    grad_pre, grad_attended, pre_sums = pull(
-        [own_grad, g_near, g_two, g_three], w_down, w_dense, slope, 0, []
-    )
-    g_three_y, grad_pre, *far = hold((g_three_y, grad_pre, *far), close)
+    *grads, sums_one = pull([own_grad, g_near, g_own_y, g_near_y], w_down, w_dense, slope, 0, [])
+    *grads, sums_two = pull([g_two, g_three], w_down, w_dense, slope, 2, grads)
+    g_three_y, *both = hold((g_three_y, *far, *grads), ())
+    far, grads = both[:4], both[4:]
     came_three = flip(far[3], "shard", 1)
-    grad_pre, grad_attended, more_sums = pull(
-        [g_own_y, g_near_y, g_two_y, g_three_y],
-        w_down,
-        w_dense,
-        slope,
-        1,
-        [grad_pre, grad_attended],
-    )
-    pre_sums = pre_sums + more_sums
+    grad_pre, grad_attended, sums_three = pull(
+        [g_two_y, g_three_y], w_down, w_dense, slope, 3, grads
+    )
+    pre_sums = sums_one + sums_two + sums_three
     my_core = rep % 2
     my_side = rep // 2
     my_row = me % 2
@@ -1102,9 +1166,6 @@
             lax.dynamic_index_in_dim(values, 1 - index, 1, False),
         )
 
-    def by_core(grads):
-        return split(grads.reshape(2 * HEADS, 2, quarter, grads.shape[1]), my_core)
-
     def by_side(summed):
         return split(summed.reshape(HEADS, 2, quarter, summed.shape[-1]), my_side)
 
@@ -1128,11 +1189,12 @@
         both = jnp.stack([pieces[0], near[0], far[0], near[1]])
         return both.reshape(HEADS, quarter, both.shape[-1])
 
-    up_grads, up_sums = moments_of(normed, grad_pre, up_raw, ln2_gain, ln2_bias, pre_sums)
-    up_keep, up_give = by_core(up_grads)
-    came_three, grad_attended, up_give, *far = hold((came_three, grad_attended, up_give, *far), ())
+    up_keep, up_give, up_sums = moments_of(
+        my_core, normed, grad_pre, up_raw, tall[2], tall[3], pre_sums, quarter
+    )
+    three = joined(close[3], came_three)
+    grad_attended, up_give, three, *far = hold((grad_attended, up_give, three, *far), ())
     came_two = flip(far[2], "shard", 1)
-    three = plus(close[3], came_three).astype(BF16)
     from_corner = send(three, INWARD)
     up_came = flip(up_give, "rep", 1)
     grad_qkv, qkv_sums = attend_back(
@@ -1145,40 +1207,76 @@
         key,
     )
     grad_qkv = grad_qkv.reshape(group_tokens, 3 * HEAD)
-    qkv_grads, qkv_row_sums = moments_of(normed, grad_qkv, qkv_raw, ln1_gain, ln1_bias, qkv_sums)
-    qkv_keep, qkv_give = by_core(qkv_grads)
-    came_two, from_corner, up_came, qkv_give, grad_qkv, *far = hold(
-        (came_two, from_corner, up_came, qkv_give, grad_qkv, *far), ()
-    )
+    qkv_keep, qkv_give, qkv_row_sums = moments_of(
+        my_core, normed, grad_qkv, qkv_raw, tall[0], tall[1], qkv_sums, quarter
+    )
+    two = joined(close[2], came_two)
     up_keep, up_give = by_side(joined(up_keep, up_came))
+    from_corner, up_give, qkv_give, grad_qkv, two, *far = hold(
+        (from_corner, up_give, qkv_give, grad_qkv, two, *far), (up_keep,)
+    )
     up_came = flip(up_give, "rep", 2)
     came_one = flip(far[1], "shard", 1)
-    two = plus(close[2], came_two, from_corner).astype(BF16)
+    two = joined(two, from_corner)
     across_near = send(two, MIDDLE)
     across = send(two, INWARD)
     qkv_came = flip(qkv_give, "rep", 1)
-    gy_far = combine(grad_pre, grad_qkv, up_scaled, qkv_scaled, rows, 4, 1)
-    gy_close = combine(grad_pre, grad_qkv, up_scaled, qkv_scaled, rows, 0, 1)
-    up_came, came_one, across_near, across, qkv_came, own_grad, *both = hold(
-        (up_came, came_one, across_near, across, qkv_came, own_grad, *far, *gy_far, *gy_close), ()
-    )
-    far, gy_far, gy_close = both[:4], both[4:8], both[8:]
+    gy_far = combine(grad_pre, grad_qkv, up_scaled, qkv_scaled, rows, 1, 1)
+    one = joined(close[1], came_one)
     up_keep, up_give = by_row(joined(up_keep, up_came))
+    qkv_keep, qkv_give = by_side(joined(qkv_keep, qkv_came))
+    up_give, across_near, across, qkv_give, own_grad, one, *both = hold(
+        (up_give, across_near, across, qkv_give, own_grad, one, *far, *gy_far),
+        (up_keep, qkv_keep),
+    )
+    far, gy_far = both[:4], both[4:]
     came_own = flip(far[0], "shard", 1)
     up_came = flip(up_give, "shard", 1)
-    one = plus(close[1], came_one, across_near).astype(BF16)
+    one = joined(one, across_near)
     three = plus(three, across).astype(BF16)
     one_near = flip(one, "shard", 2)
     three_across = send(three, MIDDLE)
-    qkv_keep, qkv_give = by_side(joined(qkv_keep, qkv_came))
     qkv_came = flip(qkv_give, "rep", 2)
-    out_grads = outer(
+    half_keep, half_give = outer(
+        my_core,
         activated,
         attended,
-        [own_grad, g_near, g_two, g_three, g_own_y, g_near_y, g_two_y, g_three_y],
-    )
-    half_rows = out_grads.shape[0] // 2
-    half_keep, half_give = split(out_grads.reshape(1, 2, half_rows, width), my_core)
+        [own_grad, g_near, g_own_y, g_near_y, g_two, g_three, g_two_y, g_three_y],
+    )
+    out_sum = plus(close[0], came_own)
+    up_pieces = by_place(up_keep, up_came)
+    qkv_keep, qkv_give = by_row(joined(qkv_keep, qkv_came))
+    (
+        one_near,
+        three_across,
+        qkv_keep,
+        qkv_give,
+        half_give,
+        up_sums,
+        qkv_row_sums,
+        out_sum,
+        *both,
+    ) = hold(
+        (
+            one_near,
+            three_across,
+            qkv_keep,
+            qkv_give,
+            half_give,
+            up_sums,
+            qkv_row_sums,
+            out_sum,
+            *up_pieces,
+            *gy_far,
+            grad_pre,
+        ),
+        (),
+    )
+    up_pieces, gy_far, grad_pre = both[:4], both[4:8], both[8]
+    came_three = flip(gy_far[3], "shard", 1)
+    qkv_came = flip(qkv_give, "shard", 1)
+    up_far = far_places(up_pieces)
+    half_came = flip(half_give, "rep", 1)
     small = jnp.concatenate(
         [
             qkv_row_sums.T.reshape(-1),
@@ -1189,81 +1287,79 @@
             ).reshape(-1),
         ]
     )
-    came_own, one_near, three_across, up_came, qkv_came, half_give, small, *gy_far = hold(
-        (came_own, one_near, three_across, up_came, qkv_came, half_give, small, *gy_far), ()
-    )
-    came_three = flip(gy_far[3], "shard", 1)
-    qkv_keep, qkv_give = by_row(joined(qkv_keep, qkv_came))
-    qkv_came = flip(qkv_give, "shard", 1)
-    up_pieces = by_place(up_keep, up_came)
-    up_far = far_places(up_pieces)
-    half_came = flip(half_give, "rep", 1)
+    small = small + flip(small, "rep", 2)
+    out_sum = plus(out_sum, one_near, three_across)
+    output = (own.astype(F32) + out_sum + (b_dense + b_down)).astype(BF16)
+    gy_close = combine(grad_pre, grad_qkv, up_scaled, qkv_scaled, rows, 0, 1)
+    qkv_pieces = by_place(qkv_keep, qkv_came)
+    three = joined(gy_close[3], came_three)
+    half = joined(half_keep, half_came)
+    output, up_far, half, small, three, *both = hold(
+        (output, up_far, half, small, three, *qkv_pieces, *gy_far, *gy_close), ()
+    )
+    qkv_pieces, gy_far, gy_close = both[:4], both[4:8], both[8:]
+    came_two = flip(gy_far[2], "shard", 1)
+    from_corner = send(three, INWARD)
+    qkv_far = far_places(qkv_pieces)
+    half_far = flip(half, "rep", 2)
     small = small + flip(small, "rep", 1)
-    out_sum = plus(close[0], came_own, one_near, three_across)
-    output = (own.astype(F32) + out_sum + (b_dense + b_down)).astype(BF16)
-    came_three, qkv_came, up_far, half_came, small, *gy_far = hold(
-        (came_three, qkv_came, up_far, half_came, small, *gy_far), (output,)
-    )
-    came_two = flip(gy_far[2], "shard", 1)
-    three = plus(gy_close[3], came_three).astype(BF16)
-    from_corner = send(three, INWARD)
-    up_near = near_place(up_pieces, up_far)
-    qkv_pieces = by_place(qkv_keep, qkv_came)
-    qkv_far = far_places(qkv_pieces)
-    half = joined(half_keep, half_came).reshape(half_rows, width)
-    half_far = flip(half, "rep", 2)
-    came_two, from_corner, up_near, qkv_far, *gy_far = hold(
-        (came_two, from_corner, up_near, qkv_far, *gy_far), ()
+    two = joined(gy_close[2], came_two)
+    from_corner, qkv_far, small, two, *gy_far = hold(
+        (from_corner, qkv_far, small, two, *gy_far), ()
     )
     came_one = flip(gy_far[1], "shard", 1)
-    two = plus(gy_close[2], came_two, from_corner).astype(BF16)
+    two = joined(two, from_corner)
     across_near = send(two, MIDDLE)
     across = send(two, INWARD)
-    qkv_near = near_place(qkv_pieces, qkv_far)
+    up_near = near_place(up_pieces, up_far)
+    one = joined(gy_close[1], came_one)
     up_part = sources(up_pieces, up_far, up_near)
-    came_one, across_near, across, qkv_near, up_part, half_far, *gy_far = hold(
-        (came_one, across_near, across, qkv_near, up_part, half_far, *gy_far), ()
+    across_near, across, up_part, half_far, one, *gy_far = hold(
+        (across_near, across, up_part, half_far, one, *gy_far), ()
     )
     came_own = flip(gy_far[0], "shard", 1)
-    one = plus(gy_close[1], came_one, across_near).astype(BF16)
+    one = joined(one, across_near)
     three = plus(three, across).astype(BF16)
     one_near = flip(one, "shard", 2)
     three_across = send(three, MIDDLE)
     up_beside = flip(up_part, "rep", 2)
-    up_c = flip(up_part, "rep", 1)
+    qkv_near = near_place(qkv_pieces, qkv_far)
     half = joined(half, half_far)
+    gy = plus(gy_close[0], came_own)
     qkv_part = sources(qkv_pieces, qkv_far, qkv_near)
-    came_own, one_near, three_across, up_beside, half, qkv_part, small = hold(
-        (came_own, one_near, three_across, up_beside, half, qkv_part, small), (up_c,)
+    one_near, three_across, qkv_part, up_beside, half, small, gy = hold(
+        (one_near, three_across, qkv_part, up_beside, half, small, gy), ()
     )
     qkv_beside = flip(qkv_part, "rep", 2)
-    qkv_c = flip(qkv_part, "rep", 1)
-    up_beside_c = flip(up_beside, "rep", 1)
+    up_c = flip(jnp.stack([up_part, up_beside]), "rep", 1)
     other = flip(half, "rep", 1)
-    small = small + flip(small, "rep", 2)
-    gy = plus(gy_close[0], came_own, one_near, three_across)
+    small = small + flip(small, "shard", 1)
+    gy = plus(gy, one_near, three_across)
     own_normed, own_rstd = normalize(own)
     input_grad = own_grad.astype(F32) + own_rstd * (
         gy
         - jnp.mean(gy, axis=-1, keepdims=True)
         - own_normed * jnp.mean(gy * own_normed, axis=-1, keepdims=True)
     )
-    qkv_beside, up_beside_c, other, small = hold(
-        (qkv_beside, up_beside_c, other, small), (input_grad, qkv_c)
+    input_grad = input_grad[:, None, :]
+    up_grad = place_grads(me, rep, (up_part, up_c[0], up_beside, up_c[1]), 1)
+    down_grad, dense_grad = place_halves(my_core, half, other, hidden)
+    qkv_c = flip(qkv_part, "rep", 1)
+    input_grad, up_grad, down_grad, qkv_beside, qkv_c, small = hold(
+        (input_grad, up_grad, down_grad, qkv_beside, qkv_c, small), ()
     )
     qkv_beside_c = flip(qkv_beside, "rep", 1)
-    for bit in (1, 2, 4):
-        small = small + flip(small, "shard", bit)
-    up_grad = place_grads(me, rep, (up_part, up_c, up_beside, up_beside_c), 1)
-    down_grad, dense_grad = place_halves(my_core, half, other, hidden)
+    one, two, three = [flip(small, "shard", bit) for bit in (2, 4, 6)]
     qkv_grad = place_grads(me, rep, (qkv_part, qkv_c, qkv_beside, qkv_beside_c), 3)
+    small, one, two, three = hold((small, one, two, three), (qkv_grad,))
+    small = (small + one) + (two + three)
     vectors = small[: 5 * width].reshape(5, width)
     slots = small[5 * width :].reshape(HEADS, wide)
     b_up_grad = slots[:, :hidden].reshape(-1)
     b_qkv_grad = slots[:, hidden:].reshape(HEADS, 3, HEAD).transpose(1, 0, 2).reshape(-1)
     return (
         output[:, None, :],
-        input_grad[:, None, :],
+        input_grad,
         vectors[0],
         vectors[1],
         vectors[2],

time: 642 us -> 603 us (0.939)
  waiting for transfers between devices: 227 us -> 158 us
  starting transfers between devices: 95.1 us -> 109 us
  Pallas kernels: 205 us -> 214 us
  other arithmetic: 52 us -> 60.8 us
    ppermute x52, waiting for transfers between devices: 203 us -> 123 us  [flip(): return lax.ppermute(value, axis, [(i, i ^ bit) for i in range(size)])]
    convert_element_type x5 -> x16, other arithmetic: 8.6 us -> 22.9 us  [joined(): return plus(mine, came).astype(BF16)]
    pallas_call x6 -> x8, Pallas kernels: 93.3 us -> 106 us  [the longest x3 29.4 us: pull(): pl.pallas_call(functools.partial(pull_kernel, count=count), out_shape=(ja...]
    ppermute x52, starting transfers between devices: 63.6 us -> 74.5 us  [flip(): return lax.ppermute(value, axis, [(i, i ^ bit) for i in range(size)])]
    squeeze x5 -> x1, local copies, waits for them, and re-layouts: 11.7 us -> 0.82 us  [split(): lax.dynamic_index_in_dim(values, 1 - index, 1, False)]
    ppermute x16, waiting for transfers between devices: 24.4 us -> 34.6 us  [send(): lax.ppermute(value, 'shard', [(2 * a + y, 2 * b + y) for a, b in pairs fo...]
    convert_element_type x6 -> x0, other arithmetic: 9.53 us -> none  [the longest x1 3.21 us: split_shards(): two = plus(close[2], came_two, from_corner).astype(BF16)]
    another operation x6 -> x0, local copies, waits for them, and re-layouts: 7.13 us -> none  [the longest x3 4.08 us: split_shards(): shifts = jnp.stack([ln1_bias, ln2_bias], axis=1)]
  transfers between devices with their start and end apart: 68 -> 68, of which waited for: 20 -> 26; matrix products, arithmetic and copies ran while one was open for 12% -> 14% of each run, Pallas kernels for 32% -> 36%
where the time goes in v3:
time: 603 us; the launch traced here: 592 us
  Pallas kernels  214 us (35%)
  waiting for transfers between devices  158 us (26%)
  starting transfers between devices  109 us (18%)
  other arithmetic  60.8 us (10%)
  local copies, waits for them, and re-layouts  47.9 us (8%)
    ppermute x52, waiting for transfers between devices, flip(): return lax.ppermute(value, axis, [(i, i ^ bit) for i in range(size)])  123 us
    ppermute x52, starting transfers between devices, flip(): return lax.ppermute(value, axis, [(i, i ^ bit) for i in range(size)])  74.5 us
    pallas_call x4, Pallas kernels, combine(): pl.pallas_call(functools.partial(combine_kernel, right_dim=right_dim), ou...  47.2 us
    ppermute x16, waiting for transfers between devices, send(): lax.ppermute(value, 'shard', [(2 * a + y, 2 * b + y) for a, b in pairs fo...  34.6 us
    ppermute x16, starting transfers between devices, send(): lax.ppermute(value, 'shard', [(2 * a + y, 2 * b + y) for a, b in pairs fo...  34.4 us
    pallas_call x3, Pallas kernels, pull(): pl.pallas_call(functools.partial(pull_kernel, count=count), out_shape=(ja...  29.4 us
    pallas_call x2, Pallas kernels, moments_of(): pl.pallas_call(functools.partial(moments_kernel, quarter=quarter), out_sh...  29.2 us
    pallas_call x2, Pallas kernels, project(): pl.pallas_call(project_kernel, out_shape=tuple((jax.ShapeDtypeStruct((cou...  27.8 us
  transfers between devices with their start and end apart: 68, of which 26 were waited for; matrix products, arithmetic and copies ran while one was open for 14% of the time, Pallas kernels for 36%

profile of v3, /device:TPU:0, one launch (start us, length us, event | category | flops | bytes accessed | tf_op | source)
XLA Modules:
  0.0 592.2 jit_solution(4134642382687189537)
XLA Ops:
  19.4 14.4 %collective-permute-done.2 = bf16[4,64,1792]{2,1,0:T(8,128)(2,1)} collective-permute-done((bf16[4,64,1792]{2,1,0:T(8,128)(2,1)}, bf16[4,64,1792]{2,1,0:T(8,128)(2,1)}, u32[]{:S(2)}, u32[]{:S(2)}) %collective-permute-start.2) | collective-permute-done | bytes 917536 | tf_op jit(solution)/shard_map/ppermute | solution.py:358
  54.4 26.1 %collective-permute-done.5 = bf16[2,64,1792]{2,1,0:T(8,128)(2,1)S(1)} collective-permute-done((bf16[2,64,1792]{2,1,0:T(8,128)(2,1)S(1)}, bf16[2,64,1792]{2,1,0:T(8,128)(2,1)S(1)}, u32[]{:S(2)}, u32[]{:S(2)}) %collective-permute-start.5) | collective-permute-done | bytes 458784 | tf_op jit(solution)/shard_map/ppermute | solution.py:358
  91.7 8.1 %shard_map.263.refs_1_ = bf16[2048,2048]{1,0:T(8,128)(2,1)} custom-call(bf16[256,2048]{1,0:T(8,128)(2,1)} %bitcast.142, bf16[256,2048]{1,0:T(8,128)(2,1)} %copy-done.25, bf16[256,2048]{1,0:T(8,128)(2,1)} %copy-done.32, bf16[256,2048]{1,0:T(8,128)(2,1)} %copy-done.31), custom_call_target="tpu_custom_call" | custom-call | flops 1048576 | bytes 1048576 | tf_op jit(solution)/shard_map/pallas_call | solution.py:704
  99.8 11.7 %collective-permute-done.10 = bf16[256,2048]{1,0:T(8,128)(2,1)} collective-permute-done((bf16[256,2048]{1,0:T(8,128)(2,1)}, bf16[256,2048]{1,0:T(8,128)(2,1)}, u32[]{:S(2)}, u32[]{:S(2)}) %collective-permute-start.10) | collective-permute-done | bytes 1048608 | tf_op jit(solution)/shard_map/ppermute | solution.py:362
  131.4 9.9 %shard_map.265 = (bf16[2048,1024]{1,0:T(8,128)(2,1)S(1)}, bf16[2048,768]{1,0:T(8,128)(2,1)S(1)}, bf16[2048,1024]{1,0:T(8,128)(2,1)}, bf16[2048,768]{1,0:T(8,128)(2,1)S(1)}, f32[1,1792]{1,0:T(1,128)S(1)}) custom-call(s32[2]{0:T(128)S(1)} %pad_add_fusion.at_ref, bf16[8,64,1792]{2,1,0:T(8,128)(2,1)} %bitcast.23.p0_ref, ...), custom_call_target="tpu_custom_call" | custom-call | flops 1048576 | bytes 1048576 | tf_op jit(solution)/shard_map/pallas_call | solution.py:579
  162.7 18.5 %shard_map.267 = (bf16[2048,1024]{1,0:T(8,128)(2,1)}, bf16[2048,1024]{1,0:T(8,128)(2,1)}, bf16[2048,768]{1,0:T(8,128)(2,1)}) custom-call(bf16[2048,2048]{1,0:T(8,128)(2,1)} %shard_map.266.normed_ref.refs_1_, bf16[2048,1024]{1,0:T(8,128)(2,1)} %get-tuple-element.242.up_ref.w_one_ref, bf16[2048,768]{1,0:T(8,128)(2,1)} %copy-done, ...), custom_call_target="tpu_custom_call" | custom-call | flops 1048576 | bytes 1048576 | tf_op jit(solution)/shard_map/pallas_call | solution.py:755
  187.1 9.3 %shard_map.269 = (bf16[2048,1024]{1,0:T(8,128)(2,1)}, bf16[2048,1024]{1,0:T(8,128)(2,1)}, bf16[2048,768]{1,0:T(8,128)(2,1)}) custom-call(bf16[2048,2048]{1,0:T(8,128)(2,1)} %shard_map.268.normed_ref, bf16[2048,1024]{1,0:T(8,128)(2,1)} %get-tuple-element.242.up_ref.w_one_ref, ...), custom_call_target="tpu_custom_call", output_to_operand_aliasing={{0}: (4, {}), {1}: (5, {}), {2}: (6, {})} | custom-call | flops 1048576 | bytes 1048576 | tf_op jit(solution)/shard_map/pallas_call | solution.py:755
  196.4 7.3 %shard_map.270 = (bf16[8,256,256]{2,1,0:T(8,128)(2,1)S(1)}, bf16[8,256,256]{2,1,0:T(8,128)(2,1)S(1)}, bf16[8,256,256]{2,1,0:T(8,128)(2,1)S(1)}) custom-call(s32[17]{0:T(128)S(1)} %pad_add_fusion.1.seq_ref, bf16[8,256,768]{2,1,0:T(8,128)(2,1)} %bitcast.138, f32[8,256,128]{2,1,0:T(8,128)S(1)} %get-tuple-element.555.cos_ref, ...), custom_call_target="tpu_custom_call" | custom-call | flops 1048576 | bytes 1048576 | tf_op jit(solution)/shard_map/pallas_call | solution.py:523
  212.2 10.8 %shard_map.272 = (bf16[256,2048]{1,0:T(8,128)(2,1)}, bf16[256,2048]{1,0:T(8,128)(2,1)}, bf16[256,2048]{1,0:T(8,128)(2,1)}, bf16[256,2048]{1,0:T(8,128)(2,1)}) custom-call(bf16[2048,1024]{1,0:T(8,128)(2,1)} %get-tuple-element.259.one_a_ref.one_b_ref.act_ref, bf16[2048,1024]{1,0:T(8,128)(2,1)} %get-tuple-element.259.one_a_ref.one_b_ref.act_ref, ...), custom_call_target="tpu_custom_call" | custom-call | flops 1048576 | bytes 1048576 | tf_op jit(solution)/shard_map/pallas_call | solution.py:798
  223.0 10.8 %shard_map.271 = (bf16[256,2048]{1,0:T(8,128)(2,1)}, bf16[256,2048]{1,0:T(8,128)(2,1)}, bf16[256,2048]{1,0:T(8,128)(2,1)}, bf16[256,2048]{1,0:T(8,128)(2,1)}) custom-call(bf16[2048,1024]{1,0:T(8,128)(2,1)} %get-tuple-element.259.one_a_ref.one_b_ref.act_ref, bf16[2048,1024]{1,0:T(8,128)(2,1)} %get-tuple-element.259.one_a_ref.one_b_ref.act_ref, ...), custom_call_target="tpu_custom_call" | custom-call | flops 1048576 | bytes 1048576 | tf_op jit(solution)/shard_map/pallas_call | solution.py:798
  238.7 12.0 %shard_map.273 = (bf16[2048,1024]{1,0:T(8,128)(2,1)}, bf16[2048,256]{1,0:T(8,128)(2,1)}, f32[1,1024]{1,0:T(1,128)}) custom-call(bf16[256,2048]{1,0:T(8,128)(2,1)} %bitcast.1.refs_0_, bf16[256,2048]{1,0:T(8,128)(2,1)} %collective-permute-done.18.refs_1_, bf16[256,2048]{1,0:T(8,128)(2,1)} %copy-done.20, bf16[256,2048]{1,0:T(8,128)(2,1)} %copy-done.21, ...), custom_call_target="tpu_custom_call" | custom-call | flops 1048576 | bytes 1048576 | tf_op jit(solution)/shard_map/pallas_call | solution.py:851
  250.7 8.7 %shard_map.274 = (bf16[2048,1024]{1,0:T(8,128)(2,1)}, bf16[2048,256]{1,0:T(8,128)(2,1)}, f32[1,1024]{1,0:T(1,128)}) custom-call(bf16[256,2048]{1,0:T(8,128)(2,1)} %copy-done.14, bf16[256,2048]{1,0:T(8,128)(2,1)} %copy-done.15, bf16[1024,2048]{1,0:T(8,128)(2,1)} %refs_2_.3, bf16[256,2048]{1,0:T(8,128)(2,1)} %refs_3_.3, ...), custom_call_target="tpu_custom_call", output_to_operand_aliasing={{0}: (5, {}), {1}: (6, {})} | custom-call | flops 1048576 | bytes 1048576 | tf_op jit(solution)/shard_map/pallas_call | solution.py:851
  264.2 8.7 %shard_map.275 = (bf16[2048,1024]{1,0:T(8,128)(2,1)}, bf16[2048,256]{1,0:T(8,128)(2,1)}, f32[1,1024]{1,0:T(1,128)}) custom-call(bf16[256,2048]{1,0:T(8,128)(2,1)} %copy-done.18, bf16[256,2048]{1,0:T(8,128)(2,1)} %copy-done.19, bf16[1024,2048]{1,0:T(8,128)(2,1)} %refs_2_.3, bf16[256,2048]{1,0:T(8,128)(2,1)} %refs_3_.3, ...), custom_call_target="tpu_custom_call", output_to_operand_aliasing={{0}: (5, {}), {1}: (6, {})} | custom-call | flops 1048576 | bytes 1048576 | tf_op jit(solution)/shard_map/pallas_call | solution.py:851
  274.3 16.2 %shard_map.276 = (bf16[1024,1024]{1,0:T(8,128)(2,1)}, bf16[1024,1024]{1,0:T(8,128)(2,1)}, f32[2048,2]{1,0:T(8,128)}) custom-call(s32[1]{0:T(128)} %bitcast.14.core_ref, bf16[2048,2048]{1,0:T(8,128)(2,1)} %shard_map.268.normed_ref, bf16[2048,1024]{1,0:T(8,128)(2,1)} %get-tuple-element.351.right_ref.one_a_ref.one_b_ref, bf16[2048,1024]{1,0:T(8,128)(2,1)} %copy-done.4, ...), custom_call_target="tpu_custom_call" | custom-call | flops 1048576 | bytes 1048576 | tf_op jit(solution)/shard_map/pallas_call | solution.py:923
  296.8 6.0 %collective-permute-start.28 = (bf16[256,2048]{1,0:T(8,128)(2,1)}, bf16[256,2048]{1,0:T(8,128)(2,1)}, u32[]{:S(2)}, u32[]{:S(2)}) collective-permute-start(bf16[256,2048]{1,0:T(8,128)(2,1)} %add_convert_fusion.16), channel_id=1, source_target_pairs={{0,2},{1,3},{6,4},{7,5},{8,10},{9,11},{14,12},{15,13},{16,18},{17,... | collective-permute-start | bytes 3145736 | tf_op jit(solution)/shard_map/ppermute | solution.py:362
  305.3 12.0 %shard_map.277 = (bf16[8,256,768]{2,1,0:T(8,128)(2,1)}, f32[1,768]{1,0:T(1,128)S(1)}) custom-call(s32[17]{0:T(128)S(1)} %pad_add_fusion.1.seq_ref, bf16[8,256,768]{2,1,0:T(8,128)(2,1)} %bitcast.139, bf16[8,256,256]{2,1,0:T(8,128)(2,1)S(1)} %bitcast.125, f32[8,256,128]{2,1,0:T(8,128)S(1)} %get-tuple-element.555.cos_ref, ...), custom_call_target="tpu_custom_call" | custom-call | flops 1048576 | bytes 1048576 | tf_op jit(solution)/shard_map/pallas_call | solution.py:539
  317.9 13.0 %shard_map.278 = (bf16[1024,768]{1,0:T(8,128)(2,1)}, bf16[1024,768]{1,0:T(8,128)(2,1)}, f32[2048,2]{1,0:T(8,128)}) custom-call(s32[1]{0:T(128)} %bitcast.14.core_ref, bf16[2048,2048]{1,0:T(8,128)(2,1)} %shard_map.268.normed_ref, bf16[2048,768]{1,0:T(8,128)(2,1)} %bitcast.133, bf16[2048,768]{1,0:T(8,128)(2,1)} %copy-done.5, f32[2048,1]{1,0:T(8,128)} %copy.65.gain_ref, ...), custom_call_target="tpu_custom_call" | custom-call | flops 1048576 | bytes 1048576 | tf_op jit(solution)/shard_map/pallas_call | solution.py:923
  346.4 12.8 %shard_map.279 = (bf16[256,2048]{1,0:T(8,128)(2,1)}, bf16[256,2048]{1,0:T(8,128)(2,1)}, bf16[256,2048]{1,0:T(8,128)(2,1)}, bf16[256,2048]{1,0:T(8,128)(2,1)}) custom-call(bf16[2048,1024]{1,0:T(8,128)(2,1)} %get-tuple-element.351.right_ref.one_a_ref.one_b_ref, bf16[2048,1024]{1,0:T(8,128)(2,1)} %get-tuple-element.351.right_ref.one_a_ref.one_b_ref, ...), custom_call_target="tpu_custom_call" | custom-call | flops 1048576 | bytes 1048576 | tf_op jit(solution)/shard_map/pallas_call | solution.py:798
  379.6 19.7 %shard_map.280 = (bf16[1280,1024]{1,0:T(8,128)(2,1)}, bf16[1280,1024]{1,0:T(8,128)(2,1)}) custom-call(s32[1]{0:T(128)} %bitcast.14.core_ref, bf16[2048,1024]{1,0:T(8,128)(2,1)} %get-tuple-element.259.one_a_ref.one_b_ref.act_ref, bf16[2048,256]{1,0:T(8,128)(2,1)} %bitcast.124, bf16[256,2048]{1,0:T(8,128)(2,1)} %bitcast.1.refs_0_, ...), custom_call_target="tpu_custom_call" | custom-call | flops 1048576 | bytes 1048576 | tf_op jit(solution)/shard_map/pallas_call | solution.py:984
  428.0 12.8 %shard_map.281 = (bf16[256,2048]{1,0:T(8,128)(2,1)}, bf16[256,2048]{1,0:T(8,128)(2,1)}, bf16[256,2048]{1,0:T(8,128)(2,1)}, bf16[256,2048]{1,0:T(8,128)(2,1)}) custom-call(bf16[2048,1024]{1,0:T(8,128)(2,1)} %get-tuple-element.351.right_ref.one_a_ref.one_b_ref, bf16[2048,1024]{1,0:T(8,128)(2,1)} %get-tuple-element.351.right_ref.one_a_ref.one_b_ref, ...), custom_call_target="tpu_custom_call" | custom-call | flops 1048576 | bytes 1048576 | tf_op jit(solution)/shard_map/pallas_call | solution.py:798
  458.4 15.4 %collective-permute-done.48 = bf16[256,2048]{1,0:T(8,128)(2,1)S(1)} collective-permute-done((bf16[256,2048]{1,0:T(8,128)(2,1)S(1)}, bf16[256,2048]{1,0:T(8,128)(2,1)S(1)}, u32[]{:S(2)}, u32[]{:S(2)}) %collective-permute-start.48) | collective-permute-done | bytes 1048608 | tf_op jit(solution)/shard_map/ppermute | solution.py:358
  474.1 11.8 %collective-permute-done.46 = bf16[2,2,64,768]{3,2,1,0:T(8,128)(2,1)S(1)} collective-permute-done((bf16[2,2,64,768]{3,2,1,0:T(8,128)(2,1)S(1)}, bf16[2,2,64,768]{3,2,1,0:T(8,128)(2,1)S(1)}, u32[]{:S(2)}, u32[]{:S(2)}) %collective-permute-start.46) | collective-permute-done | bytes 393248 | tf_op jit(solution)/shard_map/ppermute | solution.py:358
  508.3 18.1 %collective-permute-done.50 = bf16[256,2048]{1,0:T(8,128)(2,1)S(1)} collective-permute-done((bf16[256,2048]{1,0:T(8,128)(2,1)S(1)}, bf16[256,2048]{1,0:T(8,128)(2,1)S(1)}, u32[]{:S(2)}, u32[]{:S(2)}) %collective-permute-start.50) | collective-permute-done | bytes 1048608 | tf_op jit(solution)/shard_map/ppermute | solution.py:362
  537.1 12.9 %collective-permute-done.58 = bf16[256,2048]{1,0:T(8,128)(2,1)S(1)} collective-permute-done((bf16[256,2048]{1,0:T(8,128)(2,1)S(1)}, bf16[256,2048]{1,0:T(8,128)(2,1)S(1)}, u32[]{:S(2)}, u32[]{:S(2)}) %collective-permute-start.58) | collective-permute-done | bytes 1048608 | tf_op jit(solution)/shard_map/ppermute | solution.py:358
  (371 shorter events, 283.0 us)
Async XLA Ops:
  0.6 33.1 %collective-permute-start = (bf16[256,2048]{1,0:T(8,128)(2,1)}, bf16[256,2048]{1,0:T(8,128)(2,1)S(1)}, u32[]{:S(2)}, u32[]{:S(2)}) collective-permute-start(bf16[256,2048]{1,0:T(8,128)(2,1)} %bitcast.140), channel_id=1, source_target_pairs={{0,2},{1,3},{2,0},{3,1},{4,6},{5,7},{6,4},{7,5},{8,10},{9,11},{10,... | collective-permute-start | bytes 3145736 | tf_op jit(solution)/shard_map/ppermute | solution.py:358
  36.9 43.5 %collective-permute-start.3 = (bf16[256,2048]{1,0:T(8,128)(2,1)S(1)}, bf16[256,2048]{1,0:T(8,128)(2,1)S(1)}, u32[]{:S(2)}, u32[]{:S(2)}) collective-permute-start(bf16[256,2048]{1,0:T(8,128)(2,1)S(1)} %collective-permute-done.refs_1_), channel_id=1, source_target_pairs={{0,1},{1,0},{2,3},{3,2},{4,5},{5,4},{6,7},{7,6},{8,9},{9,8},{10,11... | collective-permute-start | bytes 3145736 | tf_op jit(solution)/shard_map/ppermute | solution.py:358
  38.5 44.2 %collective-permute-start.7 = (bf16[256,2048]{1,0:T(8,128)(2,1)S(1)}, bf16[256,2048]{1,0:T(8,128)(2,1)S(1)}, u32[]{:S(2)}, u32[]{:S(2)}) collective-permute-start(bf16[256,2048]{1,0:T(8,128)(2,1)S(1)} %bitcast.143), channel_id=1, source_target_pairs={{0,1},{1,0},{2,3},{3,2},{4,5},{5,4},{6,7},{7,6},{8,9},{9,8},{10,11... | collective-permute-start | bytes 3145736 | tf_op jit(solution)/shard_map/ppermute | solution.py:358
  41.6 38.8 %collective-permute-start.5 = (bf16[2,64,1792]{2,1,0:T(8,128)(2,1)S(1)}, bf16[2,64,1792]{2,1,0:T(8,128)(2,1)S(1)}, u32[]{:S(2)}, u32[]{:S(2)}) collective-permute-start(bf16[2,64,1792]{2,1,0:T(8,128)(2,1)S(1)} %pad_maximum_fusion.10), channel_id=1, source_target_pairs={{0,4},{1,5},{2,6},{3,7},{4,0},{5,1},{6,2},{7,3},{8,12},{9,13},{10,... | collective-permute-start | bytes 1376264 | tf_op jit(solution)/shard_map/ppermute | solution.py:358
  46.7 33.8 %collective-permute-start.4 = (bf16[2,64,1792]{2,1,0:T(8,128)(2,1)S(1)}, bf16[2,64,1792]{2,1,0:T(8,128)(2,1)S(1)}, u32[]{:S(2)}, u32[]{:S(2)}) collective-permute-start(bf16[2,64,1792]{2,1,0:T(8,128)(2,1)S(1)} %pad_maximum_fusion.9), channel_id=1, source_target_pairs={{0,2},{1,3},{2,0},{3,1},{4,6},{5,7},{6,4},{7,5},{8,10},{9,11},{10,... | collective-permute-start | bytes 1376264 | tf_op jit(solution)/shard_map/ppermute | solution.py:358
  84.9 31.2 %collective-permute-start.11 = (bf16[3,2,64,1792]{3,2,1,0:T(8,128)(2,1)}, bf16[3,2,64,1792]{3,2,1,0:T(8,128)(2,1)}, u32[]{:S(2)}, u32[]{:S(2)}) collective-permute-start(bf16[3,2,64,1792]{3,2,1,0:T(8,128)(2,1)} %pad_maximum_fusion.3), channel_id=1, source_target_pairs={{0,16},{8,24},{16,0},{24,8},{1,17},{9,25},{17,1},{25,9},{2,18},{10... | collective-permute-start | bytes 4128776 | tf_op jit(solution)/shard_map/ppermute | solution.py:358
  91.7 38.5 %collective-permute-start.16 = (bf16[8,64,1792]{2,1,0:T(8,128)(2,1)}, bf16[8,64,1792]{2,1,0:T(8,128)(2,1)}, u32[]{:S(2)}, u32[]{:S(2)}) collective-permute-start(bf16[8,64,1792]{2,1,0:T(8,128)(2,1)} %bitcast.23.p0_ref), channel_id=1, source_target_pairs={{0,8},{8,0},{16,24},{24,16},{1,9},{9,1},{17,25},{25,17},{2,10},{10... | collective-permute-start | bytes 5505032 | tf_op jit(solution)/shard_map/ppermute | solution.py:358
  149.7 31.5 %collective-permute-start.19 = (bf16[256,2048]{1,0:T(8,128)(2,1)S(1)}, bf16[256,2048]{1,0:T(8,128)(2,1)}, u32[]{:S(2)}, u32[]{:S(2)}) collective-permute-start(bf16[256,2048]{1,0:T(8,128)(2,1)S(1)} %broadcast_select_fusion.2.refs_0_), channel_id=1, source_target_pairs={{0,1},{1,0},{2,3},{3,2},{4,5},{5,4},{6,7},{7,6},{8,9},{9,8},{10,11... | collective-permute-start | bytes 3145736 | tf_op jit(solution)/shard_map/ppermute | solution.py:358
  156.8 49.7 %collective-permute-start.21 = (bf16[256,2048]{1,0:T(8,128)(2,1)}, bf16[256,2048]{1,0:T(8,128)(2,1)}, u32[]{:S(2)}, u32[]{:S(2)}) collective-permute-start(bf16[256,2048]{1,0:T(8,128)(2,1)} %collective-permute-done.14), channel_id=1, source_target_pairs={{2,0},{3,1},{4,6},{5,7},{10,8},{11,9},{12,14},{13,15},{18,16},{19,... | collective-permute-start | bytes 3145736 | tf_op jit(solution)/shard_map/ppermute | solution.py:362
  293.3 39.4 %collective-permute-start.27 = (bf16[1024,1024]{1,0:T(8,128)(2,1)}, bf16[1024,1024]{1,0:T(8,128)(2,1)}, u32[]{:S(2)}, u32[]{:S(2)}) collective-permute-start(bf16[1024,1024]{1,0:T(8,128)(2,1)} %get-tuple-element.299), channel_id=1, source_target_pairs={{0,8},{8,0},{16,24},{24,16},{1,9},{9,1},{17,25},{25,17},{2,10},{10... | collective-permute-start | bytes 6291464 | tf_op jit(solution)/shard_map/ppermute | solution.py:358
  293.3 37.6 %collective-permute-start.29 = (bf16[256,2048]{1,0:T(8,128)(2,1)}, bf16[256,2048]{1,0:T(8,128)(2,1)}, u32[]{:S(2)}, u32[]{:S(2)}) collective-permute-start(bf16[256,2048]{1,0:T(8,128)(2,1)} %get-tuple-element.311), channel_id=1, source_target_pairs={{0,1},{1,0},{2,3},{3,2},{4,5},{5,4},{6,7},{7,6},{8,9},{9,8},{10,11... | collective-permute-start | bytes 3145736 | tf_op jit(solution)/shard_map/ppermute | solution.py:358
  296.8 39.9 %collective-permute-start.28 = (bf16[256,2048]{1,0:T(8,128)(2,1)}, bf16[256,2048]{1,0:T(8,128)(2,1)}, u32[]{:S(2)}, u32[]{:S(2)}) collective-permute-start(bf16[256,2048]{1,0:T(8,128)(2,1)} %add_convert_fusion.16), channel_id=1, source_target_pairs={{0,2},{1,3},{6,4},{7,5},{8,10},{9,11},{14,12},{15,13},{16,18},{17,... | collective-permute-start | bytes 3145736 | tf_op jit(solution)/shard_map/ppermute | solution.py:362
  368.5 30.8 %collective-permute-start.39 = (bf16[4,64,1024]{2,1,0:T(8,128)(2,1)}, bf16[4,64,1024]{2,1,0:T(8,128)(2,1)}, u32[]{:S(2)}, u32[]{:S(2)}) collective-permute-start(bf16[4,64,1024]{2,1,0:T(8,128)(2,1)} %get-tuple-element.337), channel_id=1, source_target_pairs={{0,1},{1,0},{2,3},{3,2},{4,5},{5,4},{6,7},{7,6},{8,9},{9,8},{10,11... | collective-permute-start | bytes 1572872 | tf_op jit(solution)/shard_map/ppermute | solution.py:358
  369.0 35.5 %collective-permute-start.38 = (bf16[256,2048]{1,0:T(8,128)(2,1)}, bf16[256,2048]{1,0:T(8,128)(2,1)}, u32[]{:S(2)}, u32[]{:S(2)}) collective-permute-start(bf16[256,2048]{1,0:T(8,128)(2,1)} %get-tuple-element.336), channel_id=1, source_target_pairs={{0,1},{1,0},{2,3},{3,2},{4,5},{5,4},{6,7},{7,6},{8,9},{9,8},{10,11... | collective-permute-start | bytes 3145736 | tf_op jit(solution)/shard_map/ppermute | solution.py:358
  370.5 30.8 %collective-permute-start.37 = (bf16[8,64,768]{2,1,0:T(8,128)(2,1)S(1)}, bf16[8,64,768]{2,1,0:T(8,128)(2,1)}, u32[]{:S(2)}, u32[]{:S(2)}) collective-permute-start(bf16[8,64,768]{2,1,0:T(8,128)(2,1)S(1)} %get-tuple-element.330), channel_id=1, source_target_pairs={{0,16},{8,24},{16,0},{24,8},{1,17},{9,25},{17,1},{25,9},{2,18},{10... | collective-permute-start | bytes 2359304 | tf_op jit(solution)/shard_map/ppermute | solution.py:358
  373.4 32.7 %collective-permute-start.36 = (bf16[256,2048]{1,0:T(8,128)(2,1)S(1)}, bf16[256,2048]{1,0:T(8,128)(2,1)}, u32[]{:S(2)}, u32[]{:S(2)}) collective-permute-start(bf16[256,2048]{1,0:T(8,128)(2,1)S(1)} %add_convert_fusion.10), channel_id=1, source_target_pairs={{2,4},{3,5},{4,2},{5,3},{10,12},{11,13},{12,10},{13,11},{18,20},{1... | collective-permute-start | bytes 3145736 | tf_op jit(solution)/shard_map/ppermute | solution.py:362
  375.5 30.6 %collective-permute-start.35 = (bf16[256,2048]{1,0:T(8,128)(2,1)S(1)}, bf16[256,2048]{1,0:T(8,128)(2,1)}, u32[]{:S(2)}, u32[]{:S(2)}) collective-permute-start(bf16[256,2048]{1,0:T(8,128)(2,1)S(1)} %add_convert_fusion.11), channel_id=1, source_target_pairs={{0,2},{1,3},{2,0},{3,1},{4,6},{5,7},{6,4},{7,5},{8,10},{9,11},{10,... | collective-permute-start | bytes 3145736 | tf_op jit(solution)/shard_map/ppermute | solution.py:358
  406.1 39.6 %collective-permute-start.41 = (bf16[1280,1024]{1,0:T(8,128)(2,1)}, bf16[1280,1024]{1,0:T(8,128)(2,1)}, u32[]{:S(2)}, u32[]{:S(2)}) collective-permute-start(bf16[1280,1024]{1,0:T(8,128)(2,1)} %get-tuple-element.348), channel_id=1, source_target_pairs={{0,8},{8,0},{16,24},{24,16},{1,9},{9,1},{17,25},{25,17},{2,10},{10... | collective-permute-start | bytes 7864328 | tf_op jit(solution)/shard_map/ppermute | solution.py:358
  409.7 31.2 %collective-permute-start.44 = (bf16[4,64,768]{2,1,0:T(8,128)(2,1)}, bf16[4,64,768]{2,1,0:T(8,128)(2,1)}, u32[]{:S(2)}, u32[]{:S(2)}) collective-permute-start(bf16[4,64,768]{2,1,0:T(8,128)(2,1)} %get-tuple-element.355), channel_id=1, source_target_pairs={{0,1},{1,0},{2,3},{3,2},{4,5},{5,4},{6,7},{7,6},{8,9},{9,8},{10,11... | collective-permute-start | bytes 1179656 | tf_op jit(solution)/shard_map/ppermute | solution.py:358
  410.3 33.8 %collective-permute-start.43 = (bf16[256,2048]{1,0:T(8,128)(2,1)}, bf16[256,2048]{1,0:T(8,128)(2,1)}, u32[]{:S(2)}, u32[]{:S(2)}) collective-permute-start(bf16[256,2048]{1,0:T(8,128)(2,1)} %get-tuple-element.353), channel_id=1, source_target_pairs={{0,1},{1,0},{2,3},{3,2},{4,5},{5,4},{6,7},{7,6},{8,9},{9,8},{10,11... | collective-permute-start | bytes 3145736 | tf_op jit(solution)/shard_map/ppermute | solution.py:358
  449.5 36.4 %collective-permute-start.45 = (bf16[256,2048]{1,0:T(8,128)(2,1)S(1)}, bf16[256,2048]{1,0:T(8,128)(2,1)S(1)}, u32[]{:S(2)}, u32[]{:S(2)}) collective-permute-start(bf16[256,2048]{1,0:T(8,128)(2,1)S(1)} %add_convert_fusion.9), channel_id=1, source_target_pairs={{0,2},{1,3},{6,4},{7,5},{8,10},{9,11},{14,12},{15,13},{16,18},{17,... | collective-permute-start | bytes 3145736 | tf_op jit(solution)/shard_map/ppermute | solution.py:362
  454.1 31.8 %collective-permute-start.46 = (bf16[2,2,64,768]{3,2,1,0:T(8,128)(2,1)S(1)}, bf16[2,2,64,768]{3,2,1,0:T(8,128)(2,1)S(1)}, u32[]{:S(2)}, u32[]{:S(2)}) collective-permute-start(bf16[2,2,64,768]{3,2,1,0:T(8,128)(2,1)S(1)} %pad_maximum_fusion.13), channel_id=1, source_target_pairs={{0,4},{1,5},{2,6},{3,7},{4,0},{5,1},{6,2},{7,3},{8,12},{9,13},{10,... | collective-permute-start | bytes 1179656 | tf_op jit(solution)/shard_map/ppermute | solution.py:358
  454.3 42.9 %collective-permute-start.51 = (bf16[2,2,64,1024]{3,2,1,0:T(8,128)(2,1)S(1)}, bf16[2,2,64,1024]{3,2,1,0:T(8,128)(2,1)S(1)}, u32[]{:S(2)}, u32[]{:S(2)}) collective-permute-start(bf16[2,2,64,1024]{3,2,1,0:T(8,128)(2,1)S(1)} %pad_maximum_fusion.8), channel_id=1, source_target_pairs={{0,2},{1,3},{2,0},{3,1},{4,6},{5,7},{6,4},{7,5},{8,10},{9,11},{10,... | collective-permute-start | bytes 1572872 | tf_op jit(solution)/shard_map/ppermute | solution.py:358
  457.0 69.5 %collective-permute-start.52 = (bf16[1280,1024]{1,0:T(8,128)(2,1)S(1)}, bf16[1280,1024]{1,0:T(8,128)(2,1)S(1)}, u32[]{:S(2)}, u32[]{:S(2)}) collective-permute-start(bf16[1280,1024]{1,0:T(8,128)(2,1)S(1)} %add_convert_fusion.1), channel_id=1, source_target_pairs={{0,16},{8,24},{16,0},{24,8},{1,17},{9,25},{17,1},{25,9},{2,18},{10... | collective-permute-start | bytes 7864328 | tf_op jit(solution)/shard_map/ppermute | solution.py:358
  (101 other events, 1386.5 us)

commit v4 on v3

--- a/solution.py
+++ b/solution.py
@@ -347,7 +347,7 @@
 
 
 TILE_ROWS = 32
-BIG_VMEM = 56 << 20
+BIG_VMEM = 60 << 20
 SMALL_COST = pl.CostEstimate(flops=1 << 20, bytes_accessed=1 << 20, transcendentals=0)
 F32 = jnp.float32
 BF16 = jnp.bfloat16
@@ -513,7 +513,10 @@
         finish(tile)
 
 
-VMEM_SPEC = pl.BlockSpec(memory_space=pltpu.VMEM)
+def one_spec(shape):
+    return pl.BlockSpec(shape, lambda i: (0,) * len(shape), pipeline_mode=pl.Buffered(1))
+
+
 SMEM_SPEC = pl.BlockSpec(memory_space=pltpu.SMEM)
 
 
@@ -527,9 +530,10 @@
             jax.ShapeDtypeStruct(tiled, BF16),
             jax.ShapeDtypeStruct(tiled, BF16),
         ),
-        in_specs=[SMEM_SPEC, VMEM_SPEC, VMEM_SPEC, VMEM_SPEC],
-        out_specs=(VMEM_SPEC, VMEM_SPEC, VMEM_SPEC),
-        compiler_params=pltpu.CompilerParams(vmem_limit_bytes=48 << 20),
+        grid=(1,),
+        in_specs=[SMEM_SPEC] + [one_spec(array.shape) for array in (qkv, cosine, sine)],
+        out_specs=(one_spec((blocks, rows, HEAD)), one_spec(tiled), one_spec(tiled)),
+        compiler_params=pltpu.CompilerParams(vmem_limit_bytes=BIG_VMEM),
         cost_estimate=SMALL_COST,
     )(seq_scalars, qkv, cosine, sine)
 
@@ -542,16 +546,69 @@
             jax.ShapeDtypeStruct((blocks, rows, wide), BF16),
             jax.ShapeDtypeStruct((1, wide), F32),
         ),
-        in_specs=[SMEM_SPEC] + [VMEM_SPEC] * 6,
-        out_specs=(VMEM_SPEC, VMEM_SPEC),
+        grid=(1,),
+        in_specs=[SMEM_SPEC]
+        + [one_spec(array.shape) for array in (qkv, grad, cosine, sine, query, key)],
+        out_specs=(one_spec((blocks, rows, wide)), one_spec((1, wide))),
         scratch_shapes=[pltpu.VMEM(query.shape, F32), pltpu.VMEM(query.shape, F32)],
-        compiler_params=pltpu.CompilerParams(vmem_limit_bytes=48 << 20),
+        compiler_params=pltpu.CompilerParams(vmem_limit_bytes=BIG_VMEM),
         cost_estimate=SMALL_COST,
     )(seq_scalars, qkv, grad, cosine, sine, query, key)
 
 
+def copy_kernel(in_ref, out_ref):
+    out_ref[...] = in_ref[...]
+
+
+def settled(values):
+    return pl.pallas_call(
+        copy_kernel,
+        out_shape=jax.ShapeDtypeStruct(values.shape, values.dtype),
+        grid=(1,),
+        in_specs=[pl.BlockSpec(values.shape, lambda i: (0, 0))],
+        out_specs=pl.BlockSpec(values.shape, lambda i: (0, 0)),
+        cost_estimate=SMALL_COST,
+    )(values)
+
+
+def pack_kernel(at_ref, up_ref, qkv_ref, odd_ref, even_ref):
+    third = qkv_ref.shape[1] // 3
+    hidden = up_ref.shape[1] // HEADS
+    for k in range(HEADS):
+        out_ref = even_ref if k % 2 == 0 else odd_ref
+        target = at_ref[0] ^ k
+        start = pl.multiple_of(target * hidden, hidden)
+        out_ref[k // 2, :, :hidden] = up_ref[:, pl.ds(start, hidden)]
+        for j in range(3):
+            start = pl.multiple_of(j * third + target * HEAD, HEAD)
+            out_ref[k // 2, :, hidden + j * HEAD : hidden + (j + 1) * HEAD] = qkv_ref[
+                :, pl.ds(start, HEAD)
+            ]
+
+
+def pack(me, rep, w_up, w_qkv, hidden):
+    quarter = w_up.shape[0] // 4
+    shape = (HEADS // 2, quarter, hidden + 3 * HEAD)
+    packed = jax.ShapeDtypeStruct(shape, BF16)
+    return pl.pallas_call(
+        pack_kernel,
+        out_shape=(packed, packed),
+        grid_spec=pltpu.PrefetchScalarGridSpec(
+            num_scalar_prefetch=1,
+            grid=(1,),
+            in_specs=[
+                pl.BlockSpec((quarter, weight.shape[1]), lambda i, at_ref: (at_ref[1], 0))
+                for weight in (w_up, w_qkv)
+            ],
+            out_specs=tuple(pl.BlockSpec(shape, lambda i, at_ref: (0, 0, 0)) for _ in range(2)),
+        ),
+        compiler_params=pltpu.CompilerParams(vmem_limit_bytes=24 << 20),
+        cost_estimate=SMALL_COST,
+    )(jnp.stack([me, rep]).astype(jnp.int32), w_up, w_qkv)
+
+
 def place_weights_kernel(
-    at_ref, p0_ref, p1_ref, p2_ref, p3_ref, gain_ref, shift_ref, *out_refs, hidden
+    at_ref, p0_ref, p1_ref, p2_ref, p3_ref, norms_ref, *out_refs, hidden
 ):
     raw_refs, scaled_refs, sum_ref = out_refs[:2], out_refs[2:4], out_refs[4]
     quarter, wide = p0_ref.shape[1:]
@@ -566,15 +623,16 @@
             raw = part_ref[0, :, columns]
             raw_refs[1 - norm][rows, :] = raw
             weight = raw.astype(F32)
-            gain, shift = gain_ref[rows, norm : norm + 1], shift_ref[rows, norm : norm + 1]
+            gain = norms_ref[rows, 2 * norm : 2 * norm + 1]
+            shift = norms_ref[rows, 2 * norm + 1 : 2 * norm + 2]
             scaled_refs[1 - norm][rows, :] = (weight * gain).astype(BF16)
             sum_ref[:, columns] += jnp.sum(weight * shift, axis=0, keepdims=True)
 
 
-def place_weights(me, rep, parts, gains, shifts, hidden):
+def place_weights(me, rep, parts, norms, hidden):
     count, rows, wide = parts[0].shape
     widths = (hidden, wide - hidden) * 2
-    pair = pl.BlockSpec((4 * rows, 2), lambda i, at_ref: (i ^ at_ref[0], 0))
+    four = pl.BlockSpec((4 * rows, 4), lambda i, at_ref: (i ^ at_ref[0], 0))
     part = pl.BlockSpec((1, rows, wide), lambda i, at_ref: (i, 0, 0))
     return pl.pallas_call(
         functools.partial(place_weights_kernel, hidden=hidden),
@@ -583,15 +641,15 @@
         grid_spec=pltpu.PrefetchScalarGridSpec(
             num_scalar_prefetch=1,
             grid=(count,),
-            in_specs=[part] * 4 + [pair, pair],
+            in_specs=[part] * 4 + [four],
             out_specs=tuple(
                 pl.BlockSpec((4 * rows, n), lambda i, at_ref: (i ^ at_ref[0], 0)) for n in widths
             )
             + (pl.BlockSpec((1, wide), lambda i, at_ref: (0, 0)),),
         ),
-        compiler_params=pltpu.CompilerParams(vmem_limit_bytes=32 << 20),
+        compiler_params=pltpu.CompilerParams(vmem_limit_bytes=BIG_VMEM),
         cost_estimate=SMALL_COST,
-    )(jnp.stack([me, rep]).astype(jnp.int32), *parts, gains, shifts)
+    )(jnp.stack([me, rep]).astype(jnp.int32), *parts, norms)
 
 
 def place_grads_kernel(at_ref, p0_ref, p1_ref, p2_ref, p3_ref, out_ref, *, pieces):
@@ -880,19 +938,21 @@
     normed_ref,
     right_ref,
     weight_ref,
-    gain_ref,
-    shift_ref,
+    norms_ref,
     columns_ref,
     keep_ref,
     give_ref,
-    sums_ref,
+    gain_sum_ref,
+    bias_sum_ref,
     low_ref,
     *,
     quarter,
+    norm,
 ):
     lanes = 256
     turned = normed_ref[...].T
-    gain, shift = gain_ref[...], shift_ref[...]
+    gain = norms_ref[:, 2 * norm : 2 * norm + 1]
+    shift = norms_ref[:, 2 * norm + 1 : 2 * norm + 2]
     gain_terms, bias_terms = None, None
     for start in range(0, low_ref.shape[1], lanes):
         columns = slice(start, start + lanes)
@@ -903,8 +963,8 @@
         one, two = moment * weight, weight * total
         gain_terms = one if gain_terms is None else gain_terms + one
         bias_terms = two if bias_terms is None else bias_terms + two
-    sums_ref[:, 0:1] = jnp.sum(gain_terms, axis=1, keepdims=True)
-    sums_ref[:, 1:2] = jnp.sum(bias_terms, axis=1, keepdims=True)
+    for terms, sum_ref in ((gain_terms, gain_sum_ref), (bias_terms, bias_sum_ref)):
+        sum_ref[...] = jnp.sum(terms.T, axis=0, keepdims=True)
     for core in (0, 1):
 
         @pl.when(core_ref[0] == core)
@@ -916,16 +976,17 @@
                 ]
 
 
-def moments_of(core, normed, right, weight, gain, shift, columns, quarter):
+def moments_of(core, normed, right, weight, norms, norm, columns, quarter):
     count, width = normed.shape
     wide = weight.shape[1]
     tile = 8 * quarter
     return pl.pallas_call(
-        functools.partial(moments_kernel, quarter=quarter),
+        functools.partial(moments_kernel, quarter=quarter, norm=norm),
         out_shape=(
             jax.ShapeDtypeStruct((width // 2, wide), BF16),
             jax.ShapeDtypeStruct((width // 2, wide), BF16),
-            jax.ShapeDtypeStruct((width, 2), F32),
+            jax.ShapeDtypeStruct((1, width), F32),
+            jax.ShapeDtypeStruct((1, width), F32),
         ),
         grid=(width // tile,),
         in_specs=[
@@ -933,19 +994,19 @@
             pl.BlockSpec((count, tile), lambda i: (0, i)),
             whole_spec(right.shape),
             tokens_spec(tile, wide, 0),
-            tokens_spec(tile, 1, 0),
-            tokens_spec(tile, 1, 0),
+            tokens_spec(tile, 4, 0),
             whole_spec(columns.shape),
         ],
         out_specs=(
             tokens_spec(tile // 2, wide, 0),
             tokens_spec(tile // 2, wide, 0),
-            tokens_spec(tile, 2, 0),
+            pl.BlockSpec((1, tile), lambda i: (0, i)),
+            pl.BlockSpec((1, tile), lambda i: (0, i)),
         ),
         scratch_shapes=[pltpu.VMEM((tile, wide), BF16)],
         compiler_params=pltpu.CompilerParams(vmem_limit_bytes=BIG_VMEM),
         cost_estimate=SMALL_COST,
-    )(core[None].astype(jnp.int32), normed, right, weight, gain, shift, columns)
+    )(core[None].astype(jnp.int32), normed, right, weight, norms, columns)
 
 
 def outer_kernel(core_ref, act_ref, att_ref, *refs):
@@ -1040,22 +1101,10 @@
     wide = hidden + 3 * HEAD
     quarter = depth // 4
 
-    up_rows = lax.dynamic_slice_in_dim(w_up, rep * quarter, quarter, 0)
-    qkv_rows = lax.dynamic_slice_in_dim(w_qkv, rep * quarter, quarter, 0)
-
-    def columns_for(target):
-        pieces = [lax.dynamic_slice_in_dim(up_rows, target * hidden, hidden, 1)]
-        for k in range(3):
-            pieces.append(
-                lax.dynamic_slice_in_dim(qkv_rows, k * width + target * HEAD, HEAD, 1)
-            )
-        return jnp.concatenate(pieces, axis=1)
-
-    odd = jnp.stack([columns_for(me ^ (2 * z + 1)) for z in range(4)])
+    odd, keep = pack(me, rep, w_up, w_qkv, hidden)
     odd_came = flip(odd, "shard", 1)
     x_near = flip(own, "shard", 2)
     x_across = send(own, MIDDLE)
-    keep = [columns_for(me ^ (2 * z)) for z in range(4)]
     row_offsets, row_counts = stream_rows(seq_lengths[0], seq_order[0], HEADS)
     ends = (row_offsets + row_counts) * HEADS
     seq_scalars = jnp.concatenate([ends, me[None]]).astype(jnp.int32)
@@ -1078,31 +1127,30 @@
     sine = sine.reshape(tiled)
 
 
-    gains = jnp.stack([ln1_gain, ln2_gain], axis=1)
-    shifts = jnp.stack([ln1_bias, ln2_bias], axis=1)
-    tall = [vector[:, None] for vector in (ln1_gain, ln1_bias, ln2_gain, ln2_bias)]
+    norms = settled(jnp.stack([ln1_gain, ln1_bias, ln2_gain, ln2_bias], axis=1))
+    out_columns = jnp.sum(own_grad, axis=0, dtype=F32)
     b_in = jnp.concatenate(
         [lax.dynamic_slice_in_dim(b_up, me * hidden, hidden, 0)]
         + [lax.dynamic_slice_in_dim(b_qkv, k * width + me * HEAD, HEAD, 0) for k in range(3)]
     )
-    own, own_grad, x_near, x_across, odd_came, gains, shifts, b_in, *both = hold(
-        (own, own_grad, x_near, x_across, odd_came, gains, shifts, b_in, *keep, *tall),
+    pairs = jnp.stack([keep, odd_came], axis=1)
+    own, own_grad, x_near, x_across, norms, b_in, out_columns, *pairs = hold(
+        (own, own_grad, x_near, x_across, norms, b_in, out_columns, *[pairs[z] for z in range(4)]),
         (cosine, sine),
     )
-    keep, tall = both[:4], both[4:]
-    pairs = [jnp.stack([keep[z], odd_came[z]]) for z in range(4)]
     got = [flip(pairs[z], "shard", 2 * z) for z in range(1, 4)]
     x_own_y = flip(own, "shard", 1)
     x_near_y = flip(x_near, "shard", 1)
     beside = [flip(pairs[0], "rep", 2)]
-    x_near, x_across, own_grad, x_near_y, *got = hold(
-        (x_near, x_across, own_grad, x_near_y, *got), (x_own_y, beside[0])
+    got = jnp.stack(got)
+    x_near, x_across, own_grad, x_near_y, got = hold(
+        (x_near, x_across, own_grad, x_near_y, got), (x_own_y, beside[0])
     )
     x_across_near = send(x_near, MIDDLE)
     x_two = send(x_across, OUTWARD)
     g_own_y = flip(own_grad, "shard", 1)
-    beside = beside + [flip(jnp.stack(got), "rep", 2)]
-    part = jnp.stack([pairs[0]] + got).reshape(HEADS, quarter, wide)
+    beside = beside + [flip(got, "rep", 2)]
+    part = jnp.concatenate([pairs[0][None], got]).reshape(HEADS, quarter, wide)
     normed = norm_blocks([own, x_near, x_own_y, x_near_y], (0, 1, 2, 3), None)
     x_across_near, x_two, own_grad, normed, *beside = hold(
         (x_across_near, x_two, own_grad, normed, *beside), (part, g_own_y)
@@ -1117,16 +1165,18 @@
     normed = norm_blocks([two], (4,), normed)
     parts = (part, part_c, beside, beside_c)
     up_raw, qkv_raw, up_scaled, qkv_scaled, shifted = place_weights(
-        me, rep, parts, gains, shifts, hidden
+        me, rep, parts, norms, hidden
     )
     b_in = b_in[None, :] + shifted
-    x_three, own_grad, g_across, x_two_y, normed, b_in = hold(
-        (x_three, own_grad, g_across, x_two_y, normed, b_in), ()
+    (x_two_y,) = hold((x_two_y,), (b_in,))
+    normed = norm_blocks([x_two_y], (6,), normed)
+    x_three, own_grad, g_across, normed, b_in = hold(
+        (x_three, own_grad, g_across, normed, b_in), ()
     )
     three = jnp.where(is_middle, x_across, x_three)
     g_near = flip(own_grad, "shard", 2)
     x_three_y = flip(three, "shard", 1)
-    normed = norm_blocks([three, x_two_y], (5, 6), normed)
+    normed = norm_blocks([three], (5,), normed)
     halfway = project(normed, up_scaled, qkv_scaled, b_in, 0, 3, [])
     g_near, x_three_y, *halfway = hold((g_near, x_three_y, *halfway), ())
     g_across_near = send(g_near, MIDDLE)
@@ -1189,8 +1239,8 @@
         both = jnp.stack([pieces[0], near[0], far[0], near[1]])
         return both.reshape(HEADS, quarter, both.shape[-1])
 
-    up_keep, up_give, up_sums = moments_of(
-        my_core, normed, grad_pre, up_raw, tall[2], tall[3], pre_sums, quarter
+    up_keep, up_give, *up_sums = moments_of(
+        my_core, normed, grad_pre, up_raw, norms, 1, pre_sums, quarter
     )
     three = joined(close[3], came_three)
     grad_attended, up_give, three, *far = hold((grad_attended, up_give, three, *far), ())
@@ -1207,8 +1257,8 @@
         key,
     )
     grad_qkv = grad_qkv.reshape(group_tokens, 3 * HEAD)
-    qkv_keep, qkv_give, qkv_row_sums = moments_of(
-        my_core, normed, grad_qkv, qkv_raw, tall[0], tall[1], qkv_sums, quarter
+    qkv_keep, qkv_give, *qkv_row_sums = moments_of(
+        my_core, normed, grad_qkv, qkv_raw, norms, 0, qkv_sums, quarter
     )
     two = joined(close[2], came_two)
     up_keep, up_give = by_side(joined(up_keep, up_came))
@@ -1225,8 +1275,17 @@
     one = joined(close[1], came_one)
     up_keep, up_give = by_row(joined(up_keep, up_came))
     qkv_keep, qkv_give = by_side(joined(qkv_keep, qkv_came))
-    up_give, across_near, across, qkv_give, own_grad, one, *both = hold(
-        (up_give, across_near, across, qkv_give, own_grad, one, *far, *gy_far),
+    small = jnp.concatenate(
+        [vector[0] for vector in (*qkv_row_sums, *up_sums)]
+        + [
+            out_columns,
+            jnp.where(
+                block_range[:, None] == me, jnp.concatenate([pre_sums, qkv_sums], axis=1), 0.0
+            ).reshape(-1),
+        ]
+    )
+    up_give, across_near, across, qkv_give, own_grad, one, small, *both = hold(
+        (up_give, across_near, across, qkv_give, own_grad, one, small, *far, *gy_far),
         (up_keep, qkv_keep),
     )
     far, gy_far = both[:4], both[4:]
@@ -1252,8 +1311,6 @@
         qkv_keep,
         qkv_give,
         half_give,
-        up_sums,
-        qkv_row_sums,
         out_sum,
         *both,
     ) = hold(
@@ -1263,8 +1320,6 @@
             qkv_keep,
             qkv_give,
             half_give,
-            up_sums,
-            qkv_row_sums,
             out_sum,
             *up_pieces,
             *gy_far,
@@ -1277,35 +1332,26 @@
     qkv_came = flip(qkv_give, "shard", 1)
     up_far = far_places(up_pieces)
     half_came = flip(half_give, "rep", 1)
-    small = jnp.concatenate(
-        [
-            qkv_row_sums.T.reshape(-1),
-            up_sums.T.reshape(-1),
-            jnp.sum(own_grad, axis=0, dtype=F32),
-            jnp.where(
-                block_range[:, None] == me, jnp.concatenate([pre_sums, qkv_sums], axis=1), 0.0
-            ).reshape(-1),
-        ]
-    )
-    small = small + flip(small, "rep", 2)
+    small_side = flip(small, "rep", 2)
     out_sum = plus(out_sum, one_near, three_across)
     output = (own.astype(F32) + out_sum + (b_dense + b_down)).astype(BF16)
     gy_close = combine(grad_pre, grad_qkv, up_scaled, qkv_scaled, rows, 0, 1)
     qkv_pieces = by_place(qkv_keep, qkv_came)
     three = joined(gy_close[3], came_three)
-    half = joined(half_keep, half_came)
-    output, up_far, half, small, three, *both = hold(
-        (output, up_far, half, small, three, *qkv_pieces, *gy_far, *gy_close), ()
+    output, up_far, half_came, small, small_side, three, *both = hold(
+        (output, up_far, half_came, small, small_side, three, *qkv_pieces, *gy_far, *gy_close), ()
     )
     qkv_pieces, gy_far, gy_close = both[:4], both[4:8], both[8:]
     came_two = flip(gy_far[2], "shard", 1)
     from_corner = send(three, INWARD)
     qkv_far = far_places(qkv_pieces)
+    half = joined(half_keep, half_came)
     half_far = flip(half, "rep", 2)
-    small = small + flip(small, "rep", 1)
+    small = small + small_side
+    small_side = flip(small, "rep", 1)
     two = joined(gy_close[2], came_two)
-    from_corner, qkv_far, small, two, *gy_far = hold(
-        (from_corner, qkv_far, small, two, *gy_far), ()
+    from_corner, qkv_far, small, small_side, two, *gy_far = hold(
+        (from_corner, qkv_far, small, small_side, two, *gy_far), ()
     )
     came_one = flip(gy_far[1], "shard", 1)
     two = joined(two, from_corner)
@@ -1314,8 +1360,8 @@
     up_near = near_place(up_pieces, up_far)
     one = joined(gy_close[1], came_one)
     up_part = sources(up_pieces, up_far, up_near)
-    across_near, across, up_part, half_far, one, *gy_far = hold(
-        (across_near, across, up_part, half_far, one, *gy_far), ()
+    across_near, across, up_part, half_far, one, qkv_far, *gy_far = hold(
+        (across_near, across, up_part, half_far, one, qkv_far, *gy_far), ()
     )
     came_own = flip(gy_far[0], "shard", 1)
     one = joined(one, across_near)
@@ -1333,6 +1379,7 @@
     qkv_beside = flip(qkv_part, "rep", 2)
     up_c = flip(jnp.stack([up_part, up_beside]), "rep", 1)
     other = flip(half, "rep", 1)
+    small = small + small_side
     small = small + flip(small, "shard", 1)
     gy = plus(gy, one_near, three_across)
     own_normed, own_rstd = normalize(own)

time: 603 us -> 580 us (0.962)
  local copies, waits for them, and re-layouts: 47.9 us -> 25.1 us
  Pallas kernels: 214 us -> 224 us
  starting transfers between devices: 109 us -> 99.2 us
    ppermute x52, starting transfers between devices: 74.5 us -> 61.3 us  [flip(): return lax.ppermute(value, axis, [(i, i ^ bit) for i in range(size)])]
    ppermute x52, waiting for transfers between devices: 123 us -> 135 us  [flip(): return lax.ppermute(value, axis, [(i, i ^ bit) for i in range(size)])]
    ppermute x16, waiting for transfers between devices: 34.6 us -> 24.1 us  [send(): lax.ppermute(value, 'shard', [(2 * a + y, 2 * b + y) for a, b in pairs fo...]
    unnamed x119 -> x102, local copies, waits for them, and re-layouts: 23.1 us -> 15.1 us
    optimization_barrier x6 -> x0, local copies, waits for them, and re-layouts: 7.01 us -> none  [hold(): return lax.optimization_barrier(tuple(values) + tuple(gates))[:len(values)]]
    pallas_call x2 -> x4, Pallas kernels: 29.2 us -> 32.2 us  [the longest x2 29.2 us: moments_of(): pl.pallas_call(functools.partial(moments_kernel, quarter=quarter, norm=no...]
    pallas_call x4 -> x5, Pallas kernels: 17.8 us -> 19 us  [norm_blocks(): pl.pallas_call(functools.partial(norm_kernel, count=count, steps=steps),...]
  transfers between devices with their start and end apart: 68 -> 68, of which waited for: 26 -> 28; matrix products, arithmetic and copies ran while one was open for 14% -> 13% of each run, Pallas kernels for 36% -> 39%
where the time goes in v4:
time: 580 us; the launch traced here: 569 us
  Pallas kernels  224 us (39%)
  waiting for transfers between devices  159 us (27%)
  starting transfers between devices  99.2 us (17%)
  other arithmetic  58.9 us (10%)
  local copies, waits for them, and re-layouts  25.1 us (4%)
    ppermute x52, waiting for transfers between devices, flip(): return lax.ppermute(value, axis, [(i, i ^ bit) for i in range(size)])  135 us
    ppermute x52, starting transfers between devices, flip(): return lax.ppermute(value, axis, [(i, i ^ bit) for i in range(size)])  61.3 us
    pallas_call x4, Pallas kernels, combine(): pl.pallas_call(functools.partial(combine_kernel, right_dim=right_dim), ou...  47.3 us
    ppermute x16, starting transfers between devices, send(): lax.ppermute(value, 'shard', [(2 * a + y, 2 * b + y) for a, b in pairs fo...  37.9 us
    pallas_call x3, Pallas kernels, pull(): pl.pallas_call(functools.partial(pull_kernel, count=count), out_shape=(ja...  29.4 us
    pallas_call x2, Pallas kernels, moments_of(): pl.pallas_call(functools.partial(moments_kernel, quarter=quarter, norm=no...  29.2 us
    pallas_call x2, Pallas kernels, project(): pl.pallas_call(project_kernel, out_shape=tuple((jax.ShapeDtypeStruct((cou...  27.9 us
    ppermute x16, waiting for transfers between devices, send(): lax.ppermute(value, 'shard', [(2 * a + y, 2 * b + y) for a, b in pairs fo...  24.1 us
  transfers between devices with their start and end apart: 68, of which 28 were waited for; matrix products, arithmetic and copies ran while one was open for 13% of the time, Pallas kernels for 39%

profile of v4, /device:TPU:0, one launch (start us, length us, event | category | flops | bytes accessed | tf_op | source)
XLA Modules:
  0.0 569.0 jit_solution(14197636521875313924)
XLA Ops:
  41.4 13.6 %collective-permute-done.4 = bf16[2,64,1792]{2,1,0:T(8,128)(2,1)S(1)} collective-permute-done((bf16[2,64,1792]{2,1,0:T(8,128)(2,1)S(1)}, bf16[2,64,1792]{2,1,0:T(8,128)(2,1)S(1)}, u32[]{:S(2)}, u32[]{:S(2)}) %collective-permute-start.4) | collective-permute-done | bytes 458784 | tf_op jit(solution)/shard_map/ppermute | solution.py:358
  56.5 16.5 %collective-permute-done.5 = bf16[2,64,1792]{2,1,0:T(8,128)(2,1)S(1)} collective-permute-done((bf16[2,64,1792]{2,1,0:T(8,128)(2,1)S(1)}, bf16[2,64,1792]{2,1,0:T(8,128)(2,1)S(1)}, u32[]{:S(2)}, u32[]{:S(2)}) %collective-permute-start.5) | collective-permute-done | bytes 458784 | tf_op jit(solution)/shard_map/ppermute | solution.py:358
  96.2 10.2 %collective-permute-done.10 = bf16[256,2048]{1,0:T(8,128)(2,1)} collective-permute-done((bf16[256,2048]{1,0:T(8,128)(2,1)}, bf16[256,2048]{1,0:T(8,128)(2,1)}, u32[]{:S(2)}, u32[]{:S(2)}) %collective-permute-start.10) | collective-permute-done | bytes 1048608 | tf_op jit(solution)/shard_map/ppermute | solution.py:362
  122.2 13.0 %shard_map.266 = (bf16[2048,1024]{1,0:T(8,128)(2,1)}, bf16[2048,768]{1,0:T(8,128)(2,1)}, bf16[2048,1024]{1,0:T(8,128)(2,1)}, bf16[2048,768]{1,0:T(8,128)(2,1)}, f32[1,1792]{1,0:T(1,128)}) custom-call(s32[2]{0:T(128)} %copy-done.2, bf16[8,64,1792]{2,1,0:T(8,128)(2,1)} %bitcast.159, bf16[8,64,1792]{2,1,0:T(8,128)(2,1)} %collective-permute-done.16.p1_ref, ...), custom_call_target="tpu_custom_call" | custom-call | flops 1048576 | bytes 1048576 | tf_op jit(solution)/shard_map/pallas_call | solution.py:637
  154.9 18.5 %shard_map.270 = (bf16[2048,1024]{1,0:T(8,128)(2,1)}, bf16[2048,1024]{1,0:T(8,128)(2,1)}, bf16[2048,768]{1,0:T(8,128)(2,1)}) custom-call(bf16[2048,2048]{1,0:T(8,128)(2,1)} %shard_map.269.normed_ref.refs_1_, bf16[2048,1024]{1,0:T(8,128)(2,1)} %get-tuple-element.239.up_ref.w_one_ref, bf16[2048,768]{1,0:T(8,128)(2,1)} %get-tuple-element.240.qkv_w_ref.w_two_ref, ...), custom_call_target="tpu_custom_call" | custom-call | flops 1048576 | bytes 1048576 | tf_op jit(solution)/shard_map/pallas_call | solution.py:813
  180.4 9.3 %shard_map.272 = (bf16[2048,1024]{1,0:T(8,128)(2,1)}, bf16[2048,1024]{1,0:T(8,128)(2,1)}, bf16[2048,768]{1,0:T(8,128)(2,1)}) custom-call(bf16[2048,2048]{1,0:T(8,128)(2,1)} %shard_map.271.normed_ref, bf16[2048,1024]{1,0:T(8,128)(2,1)} %get-tuple-element.239.up_ref.w_one_ref, ...), custom_call_target="tpu_custom_call", output_to_operand_aliasing={{0}: (4, {}), {1}: (5, {}), {2}: (6, {})} | custom-call | flops 1048576 | bytes 1048576 | tf_op jit(solution)/shard_map/pallas_call | solution.py:813
  189.7 8.8 %shard_map.273 = (bf16[8,256,256]{2,1,0:T(8,128)(2,1)}, bf16[8,256,256]{2,1,0:T(8,128)(2,1)}, bf16[8,256,256]{2,1,0:T(8,128)(2,1)}) custom-call(s32[17]{0:T(128)} %pad_add_fusion.1.seq_ref, bf16[8,256,768]{2,1,0:T(8,128)(2,1)} %bitcast.135, f32[8,256,128]{2,1,0:T(8,128)} %get-tuple-element.511.cos_ref, f32[8,256,128]{2,1,0:T(8,128)} %get-tuple-element.512.sin_ref), custom_call_target="tpu_custom_call" | custom-call | flops 1048576 | bytes 1048576 | tf_op jit(solution)/shard_map/pallas_call | solution.py:526
  203.9 10.8 %shard_map.275 = (bf16[256,2048]{1,0:T(8,128)(2,1)}, bf16[256,2048]{1,0:T(8,128)(2,1)}, bf16[256,2048]{1,0:T(8,128)(2,1)}, bf16[256,2048]{1,0:T(8,128)(2,1)}) custom-call(bf16[2048,1024]{1,0:T(8,128)(2,1)} %get-tuple-element.256.one_a_ref.one_b_ref.act_ref, bf16[2048,1024]{1,0:T(8,128)(2,1)} %get-tuple-element.256.one_a_ref.one_b_ref.act_ref, ...), custom_call_target="tpu_custom_call" | custom-call | flops 1048576 | bytes 1048576 | tf_op jit(solution)/shard_map/pallas_call | solution.py:856
  214.7 10.8 %shard_map.274 = (bf16[256,2048]{1,0:T(8,128)(2,1)}, bf16[256,2048]{1,0:T(8,128)(2,1)}, bf16[256,2048]{1,0:T(8,128)(2,1)}, bf16[256,2048]{1,0:T(8,128)(2,1)}) custom-call(bf16[2048,1024]{1,0:T(8,128)(2,1)} %get-tuple-element.256.one_a_ref.one_b_ref.act_ref, bf16[2048,1024]{1,0:T(8,128)(2,1)} %get-tuple-element.256.one_a_ref.one_b_ref.act_ref, ...), custom_call_target="tpu_custom_call" | custom-call | flops 1048576 | bytes 1048576 | tf_op jit(solution)/shard_map/pallas_call | solution.py:856
  229.9 11.9 %shard_map.276 = (bf16[2048,1024]{1,0:T(8,128)(2,1)}, bf16[2048,256]{1,0:T(8,128)(2,1)}, f32[1,1024]{1,0:T(1,128)}) custom-call(bf16[256,2048]{1,0:T(8,128)(2,1)} %bitcast.150, bf16[256,2048]{1,0:T(8,128)(2,1)} %collective-permute-done.18.refs_1_, bf16[256,2048]{1,0:T(8,128)(2,1)} %collective-permute-done.12.refs_2_, bf16[256,2048]{1,0:T(8,128)(2,1)} %copy-done.15, ...), custom_call_target="tpu_custom_call" | custom-call | flops 1048576 | bytes 1048576 | tf_op jit(solution)/shard_map/pallas_call | solution.py:909
  241.8 8.8 %shard_map.277 = (bf16[2048,1024]{1,0:T(8,128)(2,1)}, bf16[2048,256]{1,0:T(8,128)(2,1)}, f32[1,1024]{1,0:T(1,128)}) custom-call(bf16[256,2048]{1,0:T(8,128)(2,1)} %copy-done.9, bf16[256,2048]{1,0:T(8,128)(2,1)} %copy-done.10, bf16[1024,2048]{1,0:T(8,128)(2,1)} %refs_2_.3, bf16[256,2048]{1,0:T(8,128)(2,1)} %refs_3_.3, ...), custom_call_target="tpu_custom_call", output_to_operand_aliasing={{0}: (5, {}), {1}: (6, {})} | custom-call | flops 1048576 | bytes 1048576 | tf_op jit(solution)/shard_map/pallas_call | solution.py:909
  262.1 16.3 %shard_map.279 = (bf16[1024,1024]{1,0:T(8,128)(2,1)}, bf16[1024,1024]{1,0:T(8,128)(2,1)}, f32[1,2048]{1,0:T(1,128)}, f32[1,2048]{1,0:T(1,128)}) custom-call(s32[1]{0:T(128)} %bitcast.18.core_ref, bf16[2048,2048]{1,0:T(8,128)(2,1)} %shard_map.271.normed_ref, bf16[2048,1024]{1,0:T(8,128)(2,1)} %get-tuple-element.345.right_ref.one_a_ref.one_b_ref, ...), custom_call_target="tpu_custom_call" | custom-call | flops 1048576 | bytes 1048576 | tf_op jit(solution)/shard_map/pallas_call | solution.py:983
  287.1 13.2 %shard_map.280 = (bf16[8,256,768]{2,1,0:T(8,128)(2,1)}, f32[1,768]{1,0:T(1,128)}) custom-call(s32[17]{0:T(128)} %pad_add_fusion.1.seq_ref, bf16[8,256,768]{2,1,0:T(8,128)(2,1)} %bitcast.136, bf16[8,256,256]{2,1,0:T(8,128)(2,1)} %bitcast.156, f32[8,256,128]{2,1,0:T(8,128)} %get-tuple-element.511.cos_ref, f32[8,256,128]{2,1,0:T(8,128)} %get-tuple-element.512.sin_ref, ...), custom_call_target="tpu_custom_call" | custom-call | flops 1048576 | bytes 1048576 | tf_op jit(solution)/shard_map/pallas_call | solution.py:543
  301.1 12.9 %shard_map.281 = (bf16[1024,768]{1,0:T(8,128)(2,1)}, bf16[1024,768]{1,0:T(8,128)(2,1)}, f32[1,2048]{1,0:T(1,128)}, f32[1,2048]{1,0:T(1,128)}) custom-call(s32[1]{0:T(128)} %bitcast.18.core_ref, bf16[2048,2048]{1,0:T(8,128)(2,1)} %shard_map.271.normed_ref, bf16[2048,768]{1,0:T(8,128)(2,1)} %bitcast.130, bf16[2048,768]{1,0:T(8,128)(2,1)} %get-tuple-element.300.weight_ref, ...), custom_call_target="tpu_custom_call" | custom-call | flops 1048576 | bytes 1048576 | tf_op jit(solution)/shard_map/pallas_call | solution.py:983
  332.9 12.9 %shard_map.282 = (bf16[256,2048]{1,0:T(8,128)(2,1)}, bf16[256,2048]{1,0:T(8,128)(2,1)}, bf16[256,2048]{1,0:T(8,128)(2,1)}, bf16[256,2048]{1,0:T(8,128)(2,1)}) custom-call(bf16[2048,1024]{1,0:T(8,128)(2,1)} %get-tuple-element.345.right_ref.one_a_ref.one_b_ref, bf16[2048,1024]{1,0:T(8,128)(2,1)} %get-tuple-element.345.right_ref.one_a_ref.one_b_ref, ...), custom_call_target="tpu_custom_call" | custom-call | flops 1048576 | bytes 1048576 | tf_op jit(solution)/shard_map/pallas_call | solution.py:856
  366.7 19.8 %shard_map.283 = (bf16[1280,1024]{1,0:T(8,128)(2,1)}, bf16[1280,1024]{1,0:T(8,128)(2,1)}) custom-call(s32[1]{0:T(128)} %bitcast.18.core_ref, bf16[2048,1024]{1,0:T(8,128)(2,1)} %get-tuple-element.256.one_a_ref.one_b_ref.act_ref, bf16[2048,256]{1,0:T(8,128)(2,1)} %bitcast.149, bf16[256,2048]{1,0:T(8,128)(2,1)} %bitcast.151, ...), custom_call_target="tpu_custom_call" | custom-call | flops 1048576 | bytes 1048576 | tf_op jit(solution)/shard_map/pallas_call | solution.py:1045
  399.3 12.8 %shard_map.284 = (bf16[256,2048]{1,0:T(8,128)(2,1)}, bf16[256,2048]{1,0:T(8,128)(2,1)}, bf16[256,2048]{1,0:T(8,128)(2,1)}, bf16[256,2048]{1,0:T(8,128)(2,1)}) custom-call(bf16[2048,1024]{1,0:T(8,128)(2,1)} %get-tuple-element.345.right_ref.one_a_ref.one_b_ref, bf16[2048,1024]{1,0:T(8,128)(2,1)} %get-tuple-element.345.right_ref.one_a_ref.one_b_ref, ...), custom_call_target="tpu_custom_call" | custom-call | flops 1048576 | bytes 1048576 | tf_op jit(solution)/shard_map/pallas_call | solution.py:856
  415.4 11.6 %collective-permute-done.44 = bf16[4,64,768]{2,1,0:T(8,128)(2,1)} collective-permute-done((bf16[4,64,768]{2,1,0:T(8,128)(2,1)}, bf16[4,64,768]{2,1,0:T(8,128)(2,1)}, u32[]{:S(2)}, u32[]{:S(2)}) %collective-permute-start.44) | collective-permute-done | bytes 393248 | tf_op jit(solution)/shard_map/ppermute | solution.py:358
  441.5 13.2 %collective-permute-done.48 = bf16[256,2048]{1,0:T(8,128)(2,1)S(1)} collective-permute-done((bf16[256,2048]{1,0:T(8,128)(2,1)S(1)}, bf16[256,2048]{1,0:T(8,128)(2,1)S(1)}, u32[]{:S(2)}, u32[]{:S(2)}) %collective-permute-start.48) | collective-permute-done | bytes 1048608 | tf_op jit(solution)/shard_map/ppermute | solution.py:358
  457.7 9.9 %collective-permute-done.46 = bf16[2,2,64,768]{3,2,1,0:T(8,128)(2,1)S(1)} collective-permute-done((bf16[2,2,64,768]{3,2,1,0:T(8,128)(2,1)S(1)}, bf16[2,2,64,768]{3,2,1,0:T(8,128)(2,1)S(1)}, u32[]{:S(2)}, u32[]{:S(2)}) %collective-permute-start.46) | collective-permute-done | bytes 393248 | tf_op jit(solution)/shard_map/ppermute | solution.py:358
  479.0 10.5 %collective-permute-done.53 = bf16[256,2048]{1,0:T(8,128)(2,1)S(1)} collective-permute-done((bf16[256,2048]{1,0:T(8,128)(2,1)S(1)}, bf16[256,2048]{1,0:T(8,128)(2,1)S(1)}, u32[]{:S(2)}, u32[]{:S(2)}) %collective-permute-start.53) | collective-permute-done | bytes 1048608 | tf_op jit(solution)/shard_map/ppermute | solution.py:358
  489.8 9.8 %collective-permute-done.50 = bf16[256,2048]{1,0:T(8,128)(2,1)S(1)} collective-permute-done((bf16[256,2048]{1,0:T(8,128)(2,1)S(1)}, bf16[256,2048]{1,0:T(8,128)(2,1)S(1)}, u32[]{:S(2)}, u32[]{:S(2)}) %collective-permute-start.50) | collective-permute-done | bytes 1048608 | tf_op jit(solution)/shard_map/ppermute | solution.py:362
  513.3 9.8 %collective-permute-done.58 = bf16[256,2048]{1,0:T(8,128)(2,1)S(1)} collective-permute-done((bf16[256,2048]{1,0:T(8,128)(2,1)S(1)}, bf16[256,2048]{1,0:T(8,128)(2,1)S(1)}, u32[]{:S(2)}, u32[]{:S(2)}) %collective-permute-start.58) | collective-permute-done | bytes 1048608 | tf_op jit(solution)/shard_map/ppermute | solution.py:358
  523.5 9.6 %collective-permute-done.54 = bf16[256,2048]{1,0:T(8,128)(2,1)S(1)} collective-permute-done((bf16[256,2048]{1,0:T(8,128)(2,1)S(1)}, bf16[256,2048]{1,0:T(8,128)(2,1)S(1)}, u32[]{:S(2)}, u32[]{:S(2)}) %collective-permute-start.54) | collective-permute-done | bytes 1048608 | tf_op jit(solution)/shard_map/ppermute | solution.py:358
  (337 shorter events, 272.2 us)
Async XLA Ops:
  0.6 33.1 %collective-permute-start = (bf16[256,2048]{1,0:T(8,128)(2,1)}, bf16[256,2048]{1,0:T(8,128)(2,1)}, u32[]{:S(2)}, u32[]{:S(2)}) collective-permute-start(bf16[256,2048]{1,0:T(8,128)(2,1)} %bitcast.137), channel_id=1, source_target_pairs={{0,2},{1,3},{2,0},{3,1},{4,6},{5,7},{6,4},{7,5},{8,10},{9,11},{10,... | collective-permute-start | bytes 3145736 | tf_op jit(solution)/shard_map/ppermute | solution.py:358
  3.7 30.0 %collective-permute-start.1 = (bf16[256,2048]{1,0:T(8,128)(2,1)}, bf16[256,2048]{1,0:T(8,128)(2,1)}, u32[]{:S(2)}, u32[]{:S(2)}) collective-permute-start(bf16[256,2048]{1,0:T(8,128)(2,1)} %bitcast.138), channel_id=1, source_target_pairs={{2,4},{3,5},{4,2},{5,3},{10,12},{11,13},{12,10},{13,11},{18,20},{1... | collective-permute-start | bytes 3145736 | tf_op jit(solution)/shard_map/ppermute | solution.py:362
  33.8 40.5 %collective-permute-start.7 = (bf16[256,2048]{1,0:T(8,128)(2,1)S(1)}, bf16[256,2048]{1,0:T(8,128)(2,1)S(1)}, u32[]{:S(2)}, u32[]{:S(2)}) collective-permute-start(bf16[256,2048]{1,0:T(8,128)(2,1)S(1)} %bitcast.140), channel_id=1, source_target_pairs={{0,1},{1,0},{2,3},{3,2},{4,5},{5,4},{6,7},{7,6},{8,9},{9,8},{10,11... | collective-permute-start | bytes 3145736 | tf_op jit(solution)/shard_map/ppermute | solution.py:358
  35.3 44.7 %collective-permute-start.3 = (bf16[256,2048]{1,0:T(8,128)(2,1)}, bf16[256,2048]{1,0:T(8,128)(2,1)S(1)}, u32[]{:S(2)}, u32[]{:S(2)}) collective-permute-start(bf16[256,2048]{1,0:T(8,128)(2,1)} %collective-permute-done.refs_1_), channel_id=1, source_target_pairs={{0,1},{1,0},{2,3},{3,2},{4,5},{5,4},{6,7},{7,6},{8,9},{9,8},{10,11... | collective-permute-start | bytes 3145736 | tf_op jit(solution)/shard_map/ppermute | solution.py:358
  39.0 34.0 %collective-permute-start.5 = (bf16[2,64,1792]{2,1,0:T(8,128)(2,1)S(1)}, bf16[2,64,1792]{2,1,0:T(8,128)(2,1)S(1)}, u32[]{:S(2)}, u32[]{:S(2)}) collective-permute-start(bf16[2,64,1792]{2,1,0:T(8,128)(2,1)S(1)} %get-tuple-element.218), channel_id=1, source_target_pairs={{0,4},{1,5},{2,6},{3,7},{4,0},{5,1},{6,2},{7,3},{8,12},{9,13},{10,... | collective-permute-start | bytes 1376264 | tf_op jit(solution)/shard_map/ppermute | solution.py:358
  39.0 34.0 %collective-permute-start.6 = (bf16[2,64,1792]{2,1,0:T(8,128)(2,1)S(1)}, bf16[2,64,1792]{2,1,0:T(8,128)(2,1)S(1)}, u32[]{:S(2)}, u32[]{:S(2)}) collective-permute-start(bf16[2,64,1792]{2,1,0:T(8,128)(2,1)S(1)} %get-tuple-element.219), channel_id=1, source_target_pairs={{0,6},{1,7},{2,4},{3,5},{4,2},{5,3},{6,0},{7,1},{8,14},{9,15},{10,... | collective-permute-start | bytes 1376264 | tf_op jit(solution)/shard_map/ppermute | solution.py:358
  80.0 30.1 %collective-permute-start.11 = (bf16[3,2,64,1792]{3,2,1,0:T(8,128)(2,1)}, bf16[3,2,64,1792]{3,2,1,0:T(8,128)(2,1)}, u32[]{:S(2)}, u32[]{:S(2)}) collective-permute-start(bf16[3,2,64,1792]{3,2,1,0:T(8,128)(2,1)} %pad_maximum_fusion.3), channel_id=1, source_target_pairs={{0,16},{8,24},{16,0},{24,8},{1,17},{9,25},{17,1},{25,9},{2,18},{10... | collective-permute-start | bytes 4128776 | tf_op jit(solution)/shard_map/ppermute | solution.py:358
  87.5 34.7 %collective-permute-start.16 = (bf16[8,64,1792]{2,1,0:T(8,128)(2,1)S(1)}, bf16[8,64,1792]{2,1,0:T(8,128)(2,1)}, u32[]{:S(2)}, u32[]{:S(2)}) collective-permute-start(bf16[8,64,1792]{2,1,0:T(8,128)(2,1)S(1)} %bitcast.158), channel_id=1, source_target_pairs={{0,8},{8,0},{16,24},{24,16},{1,9},{9,1},{17,25},{25,17},{2,10},{10... | collective-permute-start | bytes 5505032 | tf_op jit(solution)/shard_map/ppermute | solution.py:358
  150.8 47.7 %collective-permute-start.21 = (bf16[256,2048]{1,0:T(8,128)(2,1)}, bf16[256,2048]{1,0:T(8,128)(2,1)}, u32[]{:S(2)}, u32[]{:S(2)}) collective-permute-start(bf16[256,2048]{1,0:T(8,128)(2,1)} %collective-permute-done.14), channel_id=1, source_target_pairs={{2,0},{3,1},{4,6},{5,7},{10,8},{11,9},{12,14},{13,15},{18,16},{19,... | collective-permute-start | bytes 3145736 | tf_op jit(solution)/shard_map/ppermute | solution.py:362
  278.8 39.9 %collective-permute-start.27 = (bf16[1024,1024]{1,0:T(8,128)(2,1)}, bf16[1024,1024]{1,0:T(8,128)(2,1)S(1)}, u32[]{:S(2)}, u32[]{:S(2)}) collective-permute-start(bf16[1024,1024]{1,0:T(8,128)(2,1)} %get-tuple-element.294), channel_id=1, source_target_pairs={{0,8},{8,0},{16,24},{24,16},{1,9},{9,1},{17,25},{25,17},{2,10},{10... | collective-permute-start | bytes 6291464 | tf_op jit(solution)/shard_map/ppermute | solution.py:358
  278.9 37.9 %collective-permute-start.29 = (bf16[256,2048]{1,0:T(8,128)(2,1)}, bf16[256,2048]{1,0:T(8,128)(2,1)}, u32[]{:S(2)}, u32[]{:S(2)}) collective-permute-start(bf16[256,2048]{1,0:T(8,128)(2,1)} %get-tuple-element.304), channel_id=1, source_target_pairs={{0,1},{1,0},{2,3},{3,2},{4,5},{5,4},{6,7},{7,6},{8,9},{9,8},{10,11... | collective-permute-start | bytes 3145736 | tf_op jit(solution)/shard_map/ppermute | solution.py:358
  280.0 40.9 %collective-permute-start.28 = (bf16[256,2048]{1,0:T(8,128)(2,1)S(1)}, bf16[256,2048]{1,0:T(8,128)(2,1)}, u32[]{:S(2)}, u32[]{:S(2)}) collective-permute-start(bf16[256,2048]{1,0:T(8,128)(2,1)S(1)} %add_convert_fusion.16), channel_id=1, source_target_pairs={{0,2},{1,3},{6,4},{7,5},{8,10},{9,11},{14,12},{15,13},{16,18},{17,... | collective-permute-start | bytes 3145736 | tf_op jit(solution)/shard_map/ppermute | solution.py:362
  355.0 31.4 %collective-permute-start.39 = (bf16[4,64,1024]{2,1,0:T(8,128)(2,1)}, bf16[4,64,1024]{2,1,0:T(8,128)(2,1)S(1)}, u32[]{:S(2)}, u32[]{:S(2)}) collective-permute-start(bf16[4,64,1024]{2,1,0:T(8,128)(2,1)} %get-tuple-element.333), channel_id=1, source_target_pairs={{0,1},{1,0},{2,3},{3,2},{4,5},{5,4},{6,7},{7,6},{8,9},{9,8},{10,11... | collective-permute-start | bytes 1572872 | tf_op jit(solution)/shard_map/ppermute | solution.py:358
  356.1 35.0 %collective-permute-start.38 = (bf16[256,2048]{1,0:T(8,128)(2,1)}, bf16[256,2048]{1,0:T(8,128)(2,1)}, u32[]{:S(2)}, u32[]{:S(2)}) collective-permute-start(bf16[256,2048]{1,0:T(8,128)(2,1)} %get-tuple-element.332), channel_id=1, source_target_pairs={{0,1},{1,0},{2,3},{3,2},{4,5},{5,4},{6,7},{7,6},{8,9},{9,8},{10,11... | collective-permute-start | bytes 3145736 | tf_op jit(solution)/shard_map/ppermute | solution.py:358
  357.0 29.5 %collective-permute-start.37 = (bf16[8,64,768]{2,1,0:T(8,128)(2,1)}, bf16[8,64,768]{2,1,0:T(8,128)(2,1)}, u32[]{:S(2)}, u32[]{:S(2)}) collective-permute-start(bf16[8,64,768]{2,1,0:T(8,128)(2,1)} %get-tuple-element.328), channel_id=1, source_target_pairs={{0,16},{8,24},{16,0},{24,8},{1,17},{9,25},{17,1},{25,9},{2,18},{10... | collective-permute-start | bytes 2359304 | tf_op jit(solution)/shard_map/ppermute | solution.py:358
  360.2 32.4 %collective-permute-start.36 = (bf16[256,2048]{1,0:T(8,128)(2,1)}, bf16[256,2048]{1,0:T(8,128)(2,1)}, u32[]{:S(2)}, u32[]{:S(2)}) collective-permute-start(bf16[256,2048]{1,0:T(8,128)(2,1)} %add_convert_fusion.10), channel_id=1, source_target_pairs={{2,4},{3,5},{4,2},{5,3},{10,12},{11,13},{12,10},{13,11},{18,20},{1... | collective-permute-start | bytes 3145736 | tf_op jit(solution)/shard_map/ppermute | solution.py:362
  392.6 37.3 %collective-permute-start.41 = (bf16[1280,1024]{1,0:T(8,128)(2,1)}, bf16[1280,1024]{1,0:T(8,128)(2,1)}, u32[]{:S(2)}, u32[]{:S(2)}) collective-permute-start(bf16[1280,1024]{1,0:T(8,128)(2,1)} %get-tuple-element.343), channel_id=1, source_target_pairs={{0,8},{8,0},{16,24},{24,16},{1,9},{9,1},{17,25},{25,17},{2,10},{10... | collective-permute-start | bytes 7864328 | tf_op jit(solution)/shard_map/ppermute | solution.py:358
  392.7 35.6 %collective-permute-start.43 = (bf16[256,2048]{1,0:T(8,128)(2,1)}, bf16[256,2048]{1,0:T(8,128)(2,1)}, u32[]{:S(2)}, u32[]{:S(2)}) collective-permute-start(bf16[256,2048]{1,0:T(8,128)(2,1)} %get-tuple-element.347), channel_id=1, source_target_pairs={{0,1},{1,0},{2,3},{3,2},{4,5},{5,4},{6,7},{7,6},{8,9},{9,8},{10,11... | collective-permute-start | bytes 3145736 | tf_op jit(solution)/shard_map/ppermute | solution.py:358
  394.1 35.8 %collective-permute-start.42 = (f32[24576]{0:T(1024)}, f32[24576]{0:T(1024)}, u32[]{:S(2)}, u32[]{:S(2)}) collective-permute-start(f32[24576]{0:T(1024)} %constant_dynamic-update-slice_fusion), channel_id=1, source_target_pairs={{0,16},{8,24},{16,0},{24,8},{1,17},{9,25},{17,1},{25,9},{2,18},{10... | collective-permute-start | bytes 294920 | tf_op jit(solution)/shard_map/ppermute | solution.py:358
  394.7 32.3 %collective-permute-start.44 = (bf16[4,64,768]{2,1,0:T(8,128)(2,1)}, bf16[4,64,768]{2,1,0:T(8,128)(2,1)}, u32[]{:S(2)}, u32[]{:S(2)}) collective-permute-start(bf16[4,64,768]{2,1,0:T(8,128)(2,1)} %get-tuple-element.349), channel_id=1, source_target_pairs={{0,1},{1,0},{2,3},{3,2},{4,5},{5,4},{6,7},{7,6},{8,9},{9,8},{10,11... | collective-permute-start | bytes 1179656 | tf_op jit(solution)/shard_map/ppermute | solution.py:358
  396.6 33.4 %collective-permute-start.40 = (bf16[2,2,64,1024]{3,2,1,0:T(8,128)(2,1)}, bf16[2,2,64,1024]{3,2,1,0:T(8,128)(2,1)}, u32[]{:S(2)}, u32[]{:S(2)}) collective-permute-start(bf16[2,2,64,1024]{3,2,1,0:T(8,128)(2,1)} %pad_maximum_fusion.6), channel_id=1, source_target_pairs={{0,4},{1,5},{2,6},{3,7},{4,0},{5,1},{6,2},{7,3},{8,12},{9,13},{10,... | collective-permute-start | bytes 1572872 | tf_op jit(solution)/shard_map/ppermute | solution.py:358
  431.1 36.4 %collective-permute-start.45 = (bf16[256,2048]{1,0:T(8,128)(2,1)S(1)}, bf16[256,2048]{1,0:T(8,128)(2,1)S(1)}, u32[]{:S(2)}, u32[]{:S(2)}) collective-permute-start(bf16[256,2048]{1,0:T(8,128)(2,1)S(1)} %add_convert_fusion.9), channel_id=1, source_target_pairs={{0,2},{1,3},{6,4},{7,5},{8,10},{9,11},{14,12},{15,13},{16,18},{17,... | collective-permute-start | bytes 3145736 | tf_op jit(solution)/shard_map/ppermute | solution.py:362
  438.6 61.0 %collective-permute-start.52 = (bf16[1280,1024]{1,0:T(8,128)(2,1)S(1)}, bf16[1280,1024]{1,0:T(8,128)(2,1)S(1)}, u32[]{:S(2)}, u32[]{:S(2)}) collective-permute-start(bf16[1280,1024]{1,0:T(8,128)(2,1)S(1)} %add_convert_fusion.1), channel_id=1, source_target_pairs={{0,16},{8,24},{16,0},{24,8},{1,17},{9,25},{17,1},{25,9},{2,18},{10... | collective-permute-start | bytes 7864328 | tf_op jit(solution)/shard_map/ppermute | solution.py:358
  469.8 29.8 %collective-permute-start.50 = (bf16[256,2048]{1,0:T(8,128)(2,1)S(1)}, bf16[256,2048]{1,0:T(8,128)(2,1)S(1)}, u32[]{:S(2)}, u32[]{:S(2)}) collective-permute-start(bf16[256,2048]{1,0:T(8,128)(2,1)S(1)} %add_convert_fusion.7), channel_id=1, source_target_pairs={{0,2},{1,3},{6,4},{7,5},{8,10},{9,11},{14,12},{15,13},{16,18},{17,... | collective-permute-start | bytes 3145736 | tf_op jit(solution)/shard_map/ppermute | solution.py:362
  (90 other events, 1320.9 us)

commit v5 on v4

--- a/solution.py
+++ b/solution.py
@@ -839,7 +839,7 @@
 
 def combine(one, two, w_one, w_two, rows, side, right_dim):
     width = w_one.shape[1 - right_dim]
-    lanes = 256
+    lanes = 512
 
     def weight_spec(weight):
         if right_dim:

time: 580 us -> 575 us (level)
  waiting for transfers between devices: 159 us -> 165 us
  transfers between devices with their start and end apart: 68 -> 68, of which waited for: 28 -> 29; matrix products, arithmetic and copies ran while one was open for 13% -> 13% of each run, Pallas kernels for 39% -> 39%
where the time goes in v5:
time: 575 us; the launch traced here: 565 us
  Pallas kernels  219 us (38%)
  waiting for transfers between devices  165 us (29%)
  starting transfers between devices  95.5 us (17%)
  other arithmetic  58.8 us (10%)
  local copies, waits for them, and re-layouts  25.1 us (4%)
    ppermute x52, waiting for transfers between devices, flip(): return lax.ppermute(value, axis, [(i, i ^ bit) for i in range(size)])  138 us
    ppermute x52, starting transfers between devices, flip(): return lax.ppermute(value, axis, [(i, i ^ bit) for i in range(size)])  61.5 us
    pallas_call x4, Pallas kernels, combine(): pl.pallas_call(functools.partial(combine_kernel, right_dim=right_dim), ou...  41.8 us
    ppermute x16, starting transfers between devices, send(): lax.ppermute(value, 'shard', [(2 * a + y, 2 * b + y) for a, b in pairs fo...  34 us
    pallas_call x3, Pallas kernels, pull(): pl.pallas_call(functools.partial(pull_kernel, count=count), out_shape=(ja...  29.4 us
    pallas_call x2, Pallas kernels, moments_of(): pl.pallas_call(functools.partial(moments_kernel, quarter=quarter, norm=no...  29.2 us
    pallas_call x2, Pallas kernels, project(): pl.pallas_call(project_kernel, out_shape=tuple((jax.ShapeDtypeStruct((cou...  27.9 us
    ppermute x16, waiting for transfers between devices, send(): lax.ppermute(value, 'shard', [(2 * a + y, 2 * b + y) for a, b in pairs fo...  26.6 us
  transfers between devices with their start and end apart: 68, of which 29 were waited for; matrix products, arithmetic and copies ran while one was open for 13% of the time, Pallas kernels for 39%

profile of v5, /device:TPU:0, one launch (start us, length us, event | category | flops | bytes accessed | tf_op | source)
XLA Modules:
  0.0 565.2 jit_solution(13666256156281372674)
XLA Ops:
  41.4 13.6 %collective-permute-done.4 = bf16[2,64,1792]{2,1,0:T(8,128)(2,1)S(1)} collective-permute-done((bf16[2,64,1792]{2,1,0:T(8,128)(2,1)S(1)}, bf16[2,64,1792]{2,1,0:T(8,128)(2,1)S(1)}, u32[]{:S(2)}, u32[]{:S(2)}) %collective-permute-start.4) | collective-permute-done | bytes 458784 | tf_op jit(solution)/shard_map/ppermute | solution.py:358
  56.5 16.5 %collective-permute-done.5 = bf16[2,64,1792]{2,1,0:T(8,128)(2,1)S(1)} collective-permute-done((bf16[2,64,1792]{2,1,0:T(8,128)(2,1)S(1)}, bf16[2,64,1792]{2,1,0:T(8,128)(2,1)S(1)}, u32[]{:S(2)}, u32[]{:S(2)}) %collective-permute-start.5) | collective-permute-done | bytes 458784 | tf_op jit(solution)/shard_map/ppermute | solution.py:358
  96.2 10.2 %collective-permute-done.10 = bf16[256,2048]{1,0:T(8,128)(2,1)} collective-permute-done((bf16[256,2048]{1,0:T(8,128)(2,1)}, bf16[256,2048]{1,0:T(8,128)(2,1)}, u32[]{:S(2)}, u32[]{:S(2)}) %collective-permute-start.10) | collective-permute-done | bytes 1048608 | tf_op jit(solution)/shard_map/ppermute | solution.py:362
  122.2 13.0 %shard_map.266 = (bf16[2048,1024]{1,0:T(8,128)(2,1)}, bf16[2048,768]{1,0:T(8,128)(2,1)}, bf16[2048,1024]{1,0:T(8,128)(2,1)}, bf16[2048,768]{1,0:T(8,128)(2,1)}, f32[1,1792]{1,0:T(1,128)}) custom-call(s32[2]{0:T(128)} %copy-done.2, bf16[8,64,1792]{2,1,0:T(8,128)(2,1)} %bitcast.159, bf16[8,64,1792]{2,1,0:T(8,128)(2,1)} %collective-permute-done.16.p1_ref, ...), custom_call_target="tpu_custom_call" | custom-call | flops 1048576 | bytes 1048576 | tf_op jit(solution)/shard_map/pallas_call | solution.py:637
  154.8 18.5 %shard_map.270 = (bf16[2048,1024]{1,0:T(8,128)(2,1)}, bf16[2048,1024]{1,0:T(8,128)(2,1)}, bf16[2048,768]{1,0:T(8,128)(2,1)}) custom-call(bf16[2048,2048]{1,0:T(8,128)(2,1)} %shard_map.269.normed_ref.refs_1_, bf16[2048,1024]{1,0:T(8,128)(2,1)} %get-tuple-element.239.up_ref.w_one_ref, bf16[2048,768]{1,0:T(8,128)(2,1)} %get-tuple-element.240.qkv_w_ref.w_two_ref, ...), custom_call_target="tpu_custom_call" | custom-call | flops 1048576 | bytes 1048576 | tf_op jit(solution)/shard_map/pallas_call | solution.py:813
  180.4 9.3 %shard_map.272 = (bf16[2048,1024]{1,0:T(8,128)(2,1)}, bf16[2048,1024]{1,0:T(8,128)(2,1)}, bf16[2048,768]{1,0:T(8,128)(2,1)}) custom-call(bf16[2048,2048]{1,0:T(8,128)(2,1)} %shard_map.271.normed_ref, bf16[2048,1024]{1,0:T(8,128)(2,1)} %get-tuple-element.239.up_ref.w_one_ref, ...), custom_call_target="tpu_custom_call", output_to_operand_aliasing={{0}: (4, {}), {1}: (5, {}), {2}: (6, {})} | custom-call | flops 1048576 | bytes 1048576 | tf_op jit(solution)/shard_map/pallas_call | solution.py:813
  189.7 8.8 %shard_map.273 = (bf16[8,256,256]{2,1,0:T(8,128)(2,1)}, bf16[8,256,256]{2,1,0:T(8,128)(2,1)}, bf16[8,256,256]{2,1,0:T(8,128)(2,1)}) custom-call(s32[17]{0:T(128)} %pad_add_fusion.1.seq_ref, bf16[8,256,768]{2,1,0:T(8,128)(2,1)} %bitcast.135, f32[8,256,128]{2,1,0:T(8,128)} %get-tuple-element.511.cos_ref, f32[8,256,128]{2,1,0:T(8,128)} %get-tuple-element.512.sin_ref), custom_call_target="tpu_custom_call" | custom-call | flops 1048576 | bytes 1048576 | tf_op jit(solution)/shard_map/pallas_call | solution.py:526
  203.7 9.1 %shard_map.275 = (bf16[256,2048]{1,0:T(8,128)(2,1)}, bf16[256,2048]{1,0:T(8,128)(2,1)}, bf16[256,2048]{1,0:T(8,128)(2,1)}, bf16[256,2048]{1,0:T(8,128)(2,1)}) custom-call(bf16[2048,1024]{1,0:T(8,128)(2,1)} %get-tuple-element.256.one_a_ref.one_b_ref.act_ref, bf16[2048,1024]{1,0:T(8,128)(2,1)} %get-tuple-element.256.one_a_ref.one_b_ref.act_ref, ...), custom_call_target="tpu_custom_call" | custom-call | flops 1048576 | bytes 1048576 | tf_op jit(solution)/shard_map/pallas_call | solution.py:856
  212.7 9.1 %shard_map.274 = (bf16[256,2048]{1,0:T(8,128)(2,1)}, bf16[256,2048]{1,0:T(8,128)(2,1)}, bf16[256,2048]{1,0:T(8,128)(2,1)}, bf16[256,2048]{1,0:T(8,128)(2,1)}) custom-call(bf16[2048,1024]{1,0:T(8,128)(2,1)} %get-tuple-element.256.one_a_ref.one_b_ref.act_ref, bf16[2048,1024]{1,0:T(8,128)(2,1)} %get-tuple-element.256.one_a_ref.one_b_ref.act_ref, ...), custom_call_target="tpu_custom_call" | custom-call | flops 1048576 | bytes 1048576 | tf_op jit(solution)/shard_map/pallas_call | solution.py:856
  229.8 11.9 %shard_map.276 = (bf16[2048,1024]{1,0:T(8,128)(2,1)}, bf16[2048,256]{1,0:T(8,128)(2,1)}, f32[1,1024]{1,0:T(1,128)}) custom-call(bf16[256,2048]{1,0:T(8,128)(2,1)} %bitcast.150, bf16[256,2048]{1,0:T(8,128)(2,1)} %collective-permute-done.18.refs_1_, bf16[256,2048]{1,0:T(8,128)(2,1)} %collective-permute-done.12.refs_2_, bf16[256,2048]{1,0:T(8,128)(2,1)} %copy-done.15, ...), custom_call_target="tpu_custom_call" | custom-call | flops 1048576 | bytes 1048576 | tf_op jit(solution)/shard_map/pallas_call | solution.py:909
  241.8 8.8 %shard_map.277 = (bf16[2048,1024]{1,0:T(8,128)(2,1)}, bf16[2048,256]{1,0:T(8,128)(2,1)}, f32[1,1024]{1,0:T(1,128)}) custom-call(bf16[256,2048]{1,0:T(8,128)(2,1)} %copy-done.9, bf16[256,2048]{1,0:T(8,128)(2,1)} %copy-done.10, bf16[1024,2048]{1,0:T(8,128)(2,1)} %refs_2_.3, bf16[256,2048]{1,0:T(8,128)(2,1)} %refs_3_.3, ...), custom_call_target="tpu_custom_call", output_to_operand_aliasing={{0}: (5, {}), {1}: (6, {})} | custom-call | flops 1048576 | bytes 1048576 | tf_op jit(solution)/shard_map/pallas_call | solution.py:909
  262.1 16.3 %shard_map.279 = (bf16[1024,1024]{1,0:T(8,128)(2,1)}, bf16[1024,1024]{1,0:T(8,128)(2,1)}, f32[1,2048]{1,0:T(1,128)}, f32[1,2048]{1,0:T(1,128)}) custom-call(s32[1]{0:T(128)} %bitcast.18.core_ref, bf16[2048,2048]{1,0:T(8,128)(2,1)} %shard_map.271.normed_ref, bf16[2048,1024]{1,0:T(8,128)(2,1)} %get-tuple-element.345.right_ref.one_a_ref.one_b_ref, ...), custom_call_target="tpu_custom_call" | custom-call | flops 1048576 | bytes 1048576 | tf_op jit(solution)/shard_map/pallas_call | solution.py:983
  283.5 13.2 %shard_map.280 = (bf16[8,256,768]{2,1,0:T(8,128)(2,1)}, f32[1,768]{1,0:T(1,128)}) custom-call(s32[17]{0:T(128)} %pad_add_fusion.1.seq_ref, bf16[8,256,768]{2,1,0:T(8,128)(2,1)} %bitcast.136, bf16[8,256,256]{2,1,0:T(8,128)(2,1)} %bitcast.156, f32[8,256,128]{2,1,0:T(8,128)} %get-tuple-element.511.cos_ref, f32[8,256,128]{2,1,0:T(8,128)} %get-tuple-element.512.sin_ref, ...), custom_call_target="tpu_custom_call" | custom-call | flops 1048576 | bytes 1048576 | tf_op jit(solution)/shard_map/pallas_call | solution.py:543
  297.5 12.9 %shard_map.281 = (bf16[1024,768]{1,0:T(8,128)(2,1)}, bf16[1024,768]{1,0:T(8,128)(2,1)}, f32[1,2048]{1,0:T(1,128)}, f32[1,2048]{1,0:T(1,128)}) custom-call(s32[1]{0:T(128)} %bitcast.18.core_ref, bf16[2048,2048]{1,0:T(8,128)(2,1)} %shard_map.271.normed_ref, bf16[2048,768]{1,0:T(8,128)(2,1)} %bitcast.130, bf16[2048,768]{1,0:T(8,128)(2,1)} %get-tuple-element.300.weight_ref, ...), custom_call_target="tpu_custom_call" | custom-call | flops 1048576 | bytes 1048576 | tf_op jit(solution)/shard_map/pallas_call | solution.py:983
  329.2 11.8 %shard_map.282 = (bf16[256,2048]{1,0:T(8,128)(2,1)}, bf16[256,2048]{1,0:T(8,128)(2,1)}, bf16[256,2048]{1,0:T(8,128)(2,1)}, bf16[256,2048]{1,0:T(8,128)(2,1)}) custom-call(bf16[2048,1024]{1,0:T(8,128)(2,1)} %get-tuple-element.345.right_ref.one_a_ref.one_b_ref, bf16[2048,1024]{1,0:T(8,128)(2,1)} %get-tuple-element.345.right_ref.one_a_ref.one_b_ref, ...), custom_call_target="tpu_custom_call" | custom-call | flops 1048576 | bytes 1048576 | tf_op jit(solution)/shard_map/pallas_call | solution.py:856
  363.1 19.8 %shard_map.283 = (bf16[1280,1024]{1,0:T(8,128)(2,1)}, bf16[1280,1024]{1,0:T(8,128)(2,1)}) custom-call(s32[1]{0:T(128)} %bitcast.18.core_ref, bf16[2048,1024]{1,0:T(8,128)(2,1)} %get-tuple-element.256.one_a_ref.one_b_ref.act_ref, bf16[2048,256]{1,0:T(8,128)(2,1)} %bitcast.149, bf16[256,2048]{1,0:T(8,128)(2,1)} %bitcast.151, ...), custom_call_target="tpu_custom_call" | custom-call | flops 1048576 | bytes 1048576 | tf_op jit(solution)/shard_map/pallas_call | solution.py:1045
  395.7 11.8 %shard_map.284 = (bf16[256,2048]{1,0:T(8,128)(2,1)}, bf16[256,2048]{1,0:T(8,128)(2,1)}, bf16[256,2048]{1,0:T(8,128)(2,1)}, bf16[256,2048]{1,0:T(8,128)(2,1)}) custom-call(bf16[2048,1024]{1,0:T(8,128)(2,1)} %get-tuple-element.345.right_ref.one_a_ref.one_b_ref, bf16[2048,1024]{1,0:T(8,128)(2,1)} %get-tuple-element.345.right_ref.one_a_ref.one_b_ref, ...), custom_call_target="tpu_custom_call" | custom-call | flops 1048576 | bytes 1048576 | tf_op jit(solution)/shard_map/pallas_call | solution.py:856
  410.7 12.6 %collective-permute-done.44 = bf16[4,64,768]{2,1,0:T(8,128)(2,1)} collective-permute-done((bf16[4,64,768]{2,1,0:T(8,128)(2,1)}, bf16[4,64,768]{2,1,0:T(8,128)(2,1)}, u32[]{:S(2)}, u32[]{:S(2)}) %collective-permute-start.44) | collective-permute-done | bytes 393248 | tf_op jit(solution)/shard_map/ppermute | solution.py:358
  437.8 13.3 %collective-permute-done.48 = bf16[256,2048]{1,0:T(8,128)(2,1)S(1)} collective-permute-done((bf16[256,2048]{1,0:T(8,128)(2,1)S(1)}, bf16[256,2048]{1,0:T(8,128)(2,1)S(1)}, u32[]{:S(2)}, u32[]{:S(2)}) %collective-permute-start.48) | collective-permute-done | bytes 1048608 | tf_op jit(solution)/shard_map/ppermute | solution.py:358
  454.0 9.8 %collective-permute-done.46 = bf16[2,2,64,768]{3,2,1,0:T(8,128)(2,1)S(1)} collective-permute-done((bf16[2,2,64,768]{3,2,1,0:T(8,128)(2,1)S(1)}, bf16[2,2,64,768]{3,2,1,0:T(8,128)(2,1)S(1)}, u32[]{:S(2)}, u32[]{:S(2)}) %collective-permute-start.46) | collective-permute-done | bytes 393248 | tf_op jit(solution)/shard_map/ppermute | solution.py:358
  475.2 10.5 %collective-permute-done.53 = bf16[256,2048]{1,0:T(8,128)(2,1)S(1)} collective-permute-done((bf16[256,2048]{1,0:T(8,128)(2,1)S(1)}, bf16[256,2048]{1,0:T(8,128)(2,1)S(1)}, u32[]{:S(2)}, u32[]{:S(2)}) %collective-permute-start.53) | collective-permute-done | bytes 1048608 | tf_op jit(solution)/shard_map/ppermute | solution.py:358
  486.0 9.8 %collective-permute-done.50 = bf16[256,2048]{1,0:T(8,128)(2,1)S(1)} collective-permute-done((bf16[256,2048]{1,0:T(8,128)(2,1)S(1)}, bf16[256,2048]{1,0:T(8,128)(2,1)S(1)}, u32[]{:S(2)}, u32[]{:S(2)}) %collective-permute-start.50) | collective-permute-done | bytes 1048608 | tf_op jit(solution)/shard_map/ppermute | solution.py:362
  509.7 9.7 %collective-permute-done.58 = bf16[256,2048]{1,0:T(8,128)(2,1)S(1)} collective-permute-done((bf16[256,2048]{1,0:T(8,128)(2,1)S(1)}, bf16[256,2048]{1,0:T(8,128)(2,1)S(1)}, u32[]{:S(2)}, u32[]{:S(2)}) %collective-permute-start.58) | collective-permute-done | bytes 1048608 | tf_op jit(solution)/shard_map/ppermute | solution.py:358
  519.7 9.7 %collective-permute-done.54 = bf16[256,2048]{1,0:T(8,128)(2,1)S(1)} collective-permute-done((bf16[256,2048]{1,0:T(8,128)(2,1)S(1)}, bf16[256,2048]{1,0:T(8,128)(2,1)S(1)}, u32[]{:S(2)}, u32[]{:S(2)}) %collective-permute-start.54) | collective-permute-done | bytes 1048608 | tf_op jit(solution)/shard_map/ppermute | solution.py:358
  (337 shorter events, 273.2 us)
Async XLA Ops:
  0.6 33.1 %collective-permute-start = (bf16[256,2048]{1,0:T(8,128)(2,1)}, bf16[256,2048]{1,0:T(8,128)(2,1)}, u32[]{:S(2)}, u32[]{:S(2)}) collective-permute-start(bf16[256,2048]{1,0:T(8,128)(2,1)} %bitcast.137), channel_id=1, source_target_pairs={{0,2},{1,3},{2,0},{3,1},{4,6},{5,7},{6,4},{7,5},{8,10},{9,11},{10,... | collective-permute-start | bytes 3145736 | tf_op jit(solution)/shard_map/ppermute | solution.py:358
  3.7 30.0 %collective-permute-start.1 = (bf16[256,2048]{1,0:T(8,128)(2,1)}, bf16[256,2048]{1,0:T(8,128)(2,1)}, u32[]{:S(2)}, u32[]{:S(2)}) collective-permute-start(bf16[256,2048]{1,0:T(8,128)(2,1)} %bitcast.138), channel_id=1, source_target_pairs={{2,4},{3,5},{4,2},{5,3},{10,12},{11,13},{12,10},{13,11},{18,20},{1... | collective-permute-start | bytes 3145736 | tf_op jit(solution)/shard_map/ppermute | solution.py:362
  33.8 40.5 %collective-permute-start.7 = (bf16[256,2048]{1,0:T(8,128)(2,1)S(1)}, bf16[256,2048]{1,0:T(8,128)(2,1)S(1)}, u32[]{:S(2)}, u32[]{:S(2)}) collective-permute-start(bf16[256,2048]{1,0:T(8,128)(2,1)S(1)} %bitcast.140), channel_id=1, source_target_pairs={{0,1},{1,0},{2,3},{3,2},{4,5},{5,4},{6,7},{7,6},{8,9},{9,8},{10,11... | collective-permute-start | bytes 3145736 | tf_op jit(solution)/shard_map/ppermute | solution.py:358
  35.3 44.7 %collective-permute-start.3 = (bf16[256,2048]{1,0:T(8,128)(2,1)}, bf16[256,2048]{1,0:T(8,128)(2,1)S(1)}, u32[]{:S(2)}, u32[]{:S(2)}) collective-permute-start(bf16[256,2048]{1,0:T(8,128)(2,1)} %collective-permute-done.refs_1_), channel_id=1, source_target_pairs={{0,1},{1,0},{2,3},{3,2},{4,5},{5,4},{6,7},{7,6},{8,9},{9,8},{10,11... | collective-permute-start | bytes 3145736 | tf_op jit(solution)/shard_map/ppermute | solution.py:358
  39.0 34.0 %collective-permute-start.5 = (bf16[2,64,1792]{2,1,0:T(8,128)(2,1)S(1)}, bf16[2,64,1792]{2,1,0:T(8,128)(2,1)S(1)}, u32[]{:S(2)}, u32[]{:S(2)}) collective-permute-start(bf16[2,64,1792]{2,1,0:T(8,128)(2,1)S(1)} %get-tuple-element.218), channel_id=1, source_target_pairs={{0,4},{1,5},{2,6},{3,7},{4,0},{5,1},{6,2},{7,3},{8,12},{9,13},{10,... | collective-permute-start | bytes 1376264 | tf_op jit(solution)/shard_map/ppermute | solution.py:358
  39.0 34.0 %collective-permute-start.6 = (bf16[2,64,1792]{2,1,0:T(8,128)(2,1)S(1)}, bf16[2,64,1792]{2,1,0:T(8,128)(2,1)S(1)}, u32[]{:S(2)}, u32[]{:S(2)}) collective-permute-start(bf16[2,64,1792]{2,1,0:T(8,128)(2,1)S(1)} %get-tuple-element.219), channel_id=1, source_target_pairs={{0,6},{1,7},{2,4},{3,5},{4,2},{5,3},{6,0},{7,1},{8,14},{9,15},{10,... | collective-permute-start | bytes 1376264 | tf_op jit(solution)/shard_map/ppermute | solution.py:358
  80.0 30.1 %collective-permute-start.11 = (bf16[3,2,64,1792]{3,2,1,0:T(8,128)(2,1)}, bf16[3,2,64,1792]{3,2,1,0:T(8,128)(2,1)}, u32[]{:S(2)}, u32[]{:S(2)}) collective-permute-start(bf16[3,2,64,1792]{3,2,1,0:T(8,128)(2,1)} %pad_maximum_fusion.3), channel_id=1, source_target_pairs={{0,16},{8,24},{16,0},{24,8},{1,17},{9,25},{17,1},{25,9},{2,18},{10... | collective-permute-start | bytes 4128776 | tf_op jit(solution)/shard_map/ppermute | solution.py:358
  87.5 34.7 %collective-permute-start.16 = (bf16[8,64,1792]{2,1,0:T(8,128)(2,1)S(1)}, bf16[8,64,1792]{2,1,0:T(8,128)(2,1)}, u32[]{:S(2)}, u32[]{:S(2)}) collective-permute-start(bf16[8,64,1792]{2,1,0:T(8,128)(2,1)S(1)} %bitcast.158), channel_id=1, source_target_pairs={{0,8},{8,0},{16,24},{24,16},{1,9},{9,1},{17,25},{25,17},{2,10},{10... | collective-permute-start | bytes 5505032 | tf_op jit(solution)/shard_map/ppermute | solution.py:358
  150.8 47.7 %collective-permute-start.21 = (bf16[256,2048]{1,0:T(8,128)(2,1)}, bf16[256,2048]{1,0:T(8,128)(2,1)}, u32[]{:S(2)}, u32[]{:S(2)}) collective-permute-start(bf16[256,2048]{1,0:T(8,128)(2,1)} %collective-permute-done.14), channel_id=1, source_target_pairs={{2,0},{3,1},{4,6},{5,7},{10,8},{11,9},{12,14},{13,15},{18,16},{19,... | collective-permute-start | bytes 3145736 | tf_op jit(solution)/shard_map/ppermute | solution.py:362
  278.8 36.3 %collective-permute-start.27 = (bf16[1024,1024]{1,0:T(8,128)(2,1)}, bf16[1024,1024]{1,0:T(8,128)(2,1)S(1)}, u32[]{:S(2)}, u32[]{:S(2)}) collective-permute-start(bf16[1024,1024]{1,0:T(8,128)(2,1)} %get-tuple-element.294), channel_id=1, source_target_pairs={{0,8},{8,0},{16,24},{24,16},{1,9},{9,1},{17,25},{25,17},{2,10},{10... | collective-permute-start | bytes 6291464 | tf_op jit(solution)/shard_map/ppermute | solution.py:358
  278.9 34.3 %collective-permute-start.29 = (bf16[256,2048]{1,0:T(8,128)(2,1)}, bf16[256,2048]{1,0:T(8,128)(2,1)}, u32[]{:S(2)}, u32[]{:S(2)}) collective-permute-start(bf16[256,2048]{1,0:T(8,128)(2,1)} %get-tuple-element.304), channel_id=1, source_target_pairs={{0,1},{1,0},{2,3},{3,2},{4,5},{5,4},{6,7},{7,6},{8,9},{9,8},{10,11... | collective-permute-start | bytes 3145736 | tf_op jit(solution)/shard_map/ppermute | solution.py:358
  280.0 37.4 %collective-permute-start.28 = (bf16[256,2048]{1,0:T(8,128)(2,1)S(1)}, bf16[256,2048]{1,0:T(8,128)(2,1)}, u32[]{:S(2)}, u32[]{:S(2)}) collective-permute-start(bf16[256,2048]{1,0:T(8,128)(2,1)S(1)} %add_convert_fusion.16), channel_id=1, source_target_pairs={{0,2},{1,3},{6,4},{7,5},{8,10},{9,11},{14,12},{15,13},{16,18},{17,... | collective-permute-start | bytes 3145736 | tf_op jit(solution)/shard_map/ppermute | solution.py:362
  351.4 31.5 %collective-permute-start.39 = (bf16[4,64,1024]{2,1,0:T(8,128)(2,1)}, bf16[4,64,1024]{2,1,0:T(8,128)(2,1)S(1)}, u32[]{:S(2)}, u32[]{:S(2)}) collective-permute-start(bf16[4,64,1024]{2,1,0:T(8,128)(2,1)} %get-tuple-element.333), channel_id=1, source_target_pairs={{0,1},{1,0},{2,3},{3,2},{4,5},{5,4},{6,7},{7,6},{8,9},{9,8},{10,11... | collective-permute-start | bytes 1572872 | tf_op jit(solution)/shard_map/ppermute | solution.py:358
  352.3 35.1 %collective-permute-start.38 = (bf16[256,2048]{1,0:T(8,128)(2,1)}, bf16[256,2048]{1,0:T(8,128)(2,1)}, u32[]{:S(2)}, u32[]{:S(2)}) collective-permute-start(bf16[256,2048]{1,0:T(8,128)(2,1)} %get-tuple-element.332), channel_id=1, source_target_pairs={{0,1},{1,0},{2,3},{3,2},{4,5},{5,4},{6,7},{7,6},{8,9},{9,8},{10,11... | collective-permute-start | bytes 3145736 | tf_op jit(solution)/shard_map/ppermute | solution.py:358
  353.4 29.6 %collective-permute-start.37 = (bf16[8,64,768]{2,1,0:T(8,128)(2,1)}, bf16[8,64,768]{2,1,0:T(8,128)(2,1)}, u32[]{:S(2)}, u32[]{:S(2)}) collective-permute-start(bf16[8,64,768]{2,1,0:T(8,128)(2,1)} %get-tuple-element.328), channel_id=1, source_target_pairs={{0,16},{8,24},{16,0},{24,8},{1,17},{9,25},{17,1},{25,9},{2,18},{10... | collective-permute-start | bytes 2359304 | tf_op jit(solution)/shard_map/ppermute | solution.py:358
  356.6 32.4 %collective-permute-start.36 = (bf16[256,2048]{1,0:T(8,128)(2,1)}, bf16[256,2048]{1,0:T(8,128)(2,1)}, u32[]{:S(2)}, u32[]{:S(2)}) collective-permute-start(bf16[256,2048]{1,0:T(8,128)(2,1)} %add_convert_fusion.10), channel_id=1, source_target_pairs={{2,4},{3,5},{4,2},{5,3},{10,12},{11,13},{12,10},{13,11},{18,20},{1... | collective-permute-start | bytes 3145736 | tf_op jit(solution)/shard_map/ppermute | solution.py:362
  389.0 37.3 %collective-permute-start.41 = (bf16[1280,1024]{1,0:T(8,128)(2,1)}, bf16[1280,1024]{1,0:T(8,128)(2,1)}, u32[]{:S(2)}, u32[]{:S(2)}) collective-permute-start(bf16[1280,1024]{1,0:T(8,128)(2,1)} %get-tuple-element.343), channel_id=1, source_target_pairs={{0,8},{8,0},{16,24},{24,16},{1,9},{9,1},{17,25},{25,17},{2,10},{10... | collective-permute-start | bytes 7864328 | tf_op jit(solution)/shard_map/ppermute | solution.py:358
  389.1 35.6 %collective-permute-start.43 = (bf16[256,2048]{1,0:T(8,128)(2,1)}, bf16[256,2048]{1,0:T(8,128)(2,1)}, u32[]{:S(2)}, u32[]{:S(2)}) collective-permute-start(bf16[256,2048]{1,0:T(8,128)(2,1)} %get-tuple-element.347), channel_id=1, source_target_pairs={{0,1},{1,0},{2,3},{3,2},{4,5},{5,4},{6,7},{7,6},{8,9},{9,8},{10,11... | collective-permute-start | bytes 3145736 | tf_op jit(solution)/shard_map/ppermute | solution.py:358
  390.3 36.0 %collective-permute-start.42 = (f32[24576]{0:T(1024)}, f32[24576]{0:T(1024)}, u32[]{:S(2)}, u32[]{:S(2)}) collective-permute-start(f32[24576]{0:T(1024)} %constant_dynamic-update-slice_fusion), channel_id=1, source_target_pairs={{0,16},{8,24},{16,0},{24,8},{1,17},{9,25},{17,1},{25,9},{2,18},{10... | collective-permute-start | bytes 294920 | tf_op jit(solution)/shard_map/ppermute | solution.py:358
  391.0 32.4 %collective-permute-start.44 = (bf16[4,64,768]{2,1,0:T(8,128)(2,1)}, bf16[4,64,768]{2,1,0:T(8,128)(2,1)}, u32[]{:S(2)}, u32[]{:S(2)}) collective-permute-start(bf16[4,64,768]{2,1,0:T(8,128)(2,1)} %get-tuple-element.349), channel_id=1, source_target_pairs={{0,1},{1,0},{2,3},{3,2},{4,5},{5,4},{6,7},{7,6},{8,9},{9,8},{10,11... | collective-permute-start | bytes 1179656 | tf_op jit(solution)/shard_map/ppermute | solution.py:358
  393.0 33.3 %collective-permute-start.40 = (bf16[2,2,64,1024]{3,2,1,0:T(8,128)(2,1)}, bf16[2,2,64,1024]{3,2,1,0:T(8,128)(2,1)}, u32[]{:S(2)}, u32[]{:S(2)}) collective-permute-start(bf16[2,2,64,1024]{3,2,1,0:T(8,128)(2,1)} %pad_maximum_fusion.6), channel_id=1, source_target_pairs={{0,4},{1,5},{2,6},{3,7},{4,0},{5,1},{6,2},{7,3},{8,12},{9,13},{10,... | collective-permute-start | bytes 1572872 | tf_op jit(solution)/shard_map/ppermute | solution.py:358
  427.4 36.4 %collective-permute-start.45 = (bf16[256,2048]{1,0:T(8,128)(2,1)S(1)}, bf16[256,2048]{1,0:T(8,128)(2,1)S(1)}, u32[]{:S(2)}, u32[]{:S(2)}) collective-permute-start(bf16[256,2048]{1,0:T(8,128)(2,1)S(1)} %add_convert_fusion.9), channel_id=1, source_target_pairs={{0,2},{1,3},{6,4},{7,5},{8,10},{9,11},{14,12},{15,13},{16,18},{17,... | collective-permute-start | bytes 3145736 | tf_op jit(solution)/shard_map/ppermute | solution.py:362
  434.8 61.0 %collective-permute-start.52 = (bf16[1280,1024]{1,0:T(8,128)(2,1)S(1)}, bf16[1280,1024]{1,0:T(8,128)(2,1)S(1)}, u32[]{:S(2)}, u32[]{:S(2)}) collective-permute-start(bf16[1280,1024]{1,0:T(8,128)(2,1)S(1)} %add_convert_fusion.1), channel_id=1, source_target_pairs={{0,16},{8,24},{16,0},{24,8},{1,17},{9,25},{17,1},{25,9},{2,18},{10... | collective-permute-start | bytes 7864328 | tf_op jit(solution)/shard_map/ppermute | solution.py:358
  466.1 29.7 %collective-permute-start.50 = (bf16[256,2048]{1,0:T(8,128)(2,1)S(1)}, bf16[256,2048]{1,0:T(8,128)(2,1)S(1)}, u32[]{:S(2)}, u32[]{:S(2)}) collective-permute-start(bf16[256,2048]{1,0:T(8,128)(2,1)S(1)} %add_convert_fusion.7), channel_id=1, source_target_pairs={{0,2},{1,3},{6,4},{7,5},{8,10},{9,11},{14,12},{15,13},{16,18},{17,... | collective-permute-start | bytes 3145736 | tf_op jit(solution)/shard_map/ppermute | solution.py:362
  (90 other events, 1320.2 us)

commit v6 on v5

--- a/solution.py
+++ b/solution.py
@@ -1392,14 +1392,14 @@
     up_grad = place_grads(me, rep, (up_part, up_c[0], up_beside, up_c[1]), 1)
     down_grad, dense_grad = place_halves(my_core, half, other, hidden)
     qkv_c = flip(qkv_part, "rep", 1)
+    (small,) = hold((small,), (up_c, qkv_c, other))
+    one, two, three = [flip(small, "shard", bit) for bit in (2, 4, 6)]
+    small = (small + one) + (two + three)
     input_grad, up_grad, down_grad, qkv_beside, qkv_c, small = hold(
         (input_grad, up_grad, down_grad, qkv_beside, qkv_c, small), ()
     )
     qkv_beside_c = flip(qkv_beside, "rep", 1)
-    one, two, three = [flip(small, "shard", bit) for bit in (2, 4, 6)]
     qkv_grad = place_grads(me, rep, (qkv_part, qkv_c, qkv_beside, qkv_beside_c), 3)
-    small, one, two, three = hold((small, one, two, three), (qkv_grad,))
-    small = (small + one) + (two + three)
     vectors = small[: 5 * width].reshape(5, width)
     slots = small[5 * width :].reshape(HEADS, wide)
     b_up_grad = slots[:, :hidden].reshape(-1)

time: 575 us -> 570 us (level)
    unnamed x102 -> x108, local copies, waits for them, and re-layouts: 15.1 us -> 12.2 us
  transfers between devices with their start and end apart: 68 -> 68, of which waited for: 29 -> 24; matrix products, arithmetic and copies ran while one was open for 13% -> 13% of each run, Pallas kernels for 39% -> 38%
where the time goes in v6:
time: 570 us; the launch traced here: 560 us
  Pallas kernels  219 us (38%)
  waiting for transfers between devices  165 us (29%)
  starting transfers between devices  92.3 us (16%)
  other arithmetic  59.7 us (10%)
  local copies, waits for them, and re-layouts  21.6 us (4%)
    ppermute x52, waiting for transfers between devices, flip(): return lax.ppermute(value, axis, [(i, i ^ bit) for i in range(size)])  140 us
    ppermute x52, starting transfers between devices, flip(): return lax.ppermute(value, axis, [(i, i ^ bit) for i in range(size)])  60.1 us
    pallas_call x4, Pallas kernels, combine(): pl.pallas_call(functools.partial(combine_kernel, right_dim=right_dim), ou...  41.7 us
    ppermute x16, starting transfers between devices, send(): lax.ppermute(value, 'shard', [(2 * a + y, 2 * b + y) for a, b in pairs fo...  32.2 us
    pallas_call x3, Pallas kernels, pull(): pl.pallas_call(functools.partial(pull_kernel, count=count), out_shape=(ja...  29.4 us
    pallas_call x2, Pallas kernels, moments_of(): pl.pallas_call(functools.partial(moments_kernel, quarter=quarter, norm=no...  29.2 us
    pallas_call x2, Pallas kernels, project(): pl.pallas_call(project_kernel, out_shape=tuple((jax.ShapeDtypeStruct((cou...  27.8 us
    ppermute x16, waiting for transfers between devices, send(): lax.ppermute(value, 'shard', [(2 * a + y, 2 * b + y) for a, b in pairs fo...  25.1 us
  transfers between devices with their start and end apart: 68, of which 24 were waited for; matrix products, arithmetic and copies ran while one was open for 13% of the time, Pallas kernels for 38%

profile of v6, /device:TPU:0, one launch (start us, length us, event | category | flops | bytes accessed | tf_op | source)
XLA Modules:
  0.0 559.7 jit_solution(7479458522413471363)
XLA Ops:
  41.4 13.6 %collective-permute-done.4 = bf16[2,64,1792]{2,1,0:T(8,128)(2,1)S(1)} collective-permute-done((bf16[2,64,1792]{2,1,0:T(8,128)(2,1)S(1)}, bf16[2,64,1792]{2,1,0:T(8,128)(2,1)S(1)}, u32[]{:S(2)}, u32[]{:S(2)}) %collective-permute-start.4) | collective-permute-done | bytes 458784 | tf_op jit(solution)/shard_map/ppermute | solution.py:358
  56.5 16.5 %collective-permute-done.5 = bf16[2,64,1792]{2,1,0:T(8,128)(2,1)S(1)} collective-permute-done((bf16[2,64,1792]{2,1,0:T(8,128)(2,1)S(1)}, bf16[2,64,1792]{2,1,0:T(8,128)(2,1)S(1)}, u32[]{:S(2)}, u32[]{:S(2)}) %collective-permute-start.5) | collective-permute-done | bytes 458784 | tf_op jit(solution)/shard_map/ppermute | solution.py:358
  87.8 8.8 %shard_map.265.refs_1_ = bf16[2048,2048]{1,0:T(8,128)(2,1)} custom-call(bf16[256,2048]{1,0:T(8,128)(2,1)} %bitcast.139, bf16[256,2048]{1,0:T(8,128)(2,1)} %collective-permute-done.refs_1_, bf16[256,2048]{1,0:T(8,128)(2,1)} %copy-done.24, bf16[256,2048]{1,0:T(8,128)(2,1)} %copy-done.25), custom_call_target="tpu_custom_call" | custom-call | flops 1048576 | bytes 1048576 | tf_op jit(solution)/shard_map/pallas_call | solution.py:762
  96.5 9.9 %collective-permute-done.10 = bf16[256,2048]{1,0:T(8,128)(2,1)} collective-permute-done((bf16[256,2048]{1,0:T(8,128)(2,1)}, bf16[256,2048]{1,0:T(8,128)(2,1)}, u32[]{:S(2)}, u32[]{:S(2)}) %collective-permute-start.10) | collective-permute-done | bytes 1048608 | tf_op jit(solution)/shard_map/ppermute | solution.py:362
  122.3 13.0 %shard_map.266 = (bf16[2048,1024]{1,0:T(8,128)(2,1)}, bf16[2048,768]{1,0:T(8,128)(2,1)}, bf16[2048,1024]{1,0:T(8,128)(2,1)}, bf16[2048,768]{1,0:T(8,128)(2,1)}, f32[1,1792]{1,0:T(1,128)}) custom-call(s32[2]{0:T(128)} %copy-done.2, bf16[8,64,1792]{2,1,0:T(8,128)(2,1)} %bitcast.159, bf16[8,64,1792]{2,1,0:T(8,128)(2,1)} %collective-permute-done.16.p1_ref, ...), custom_call_target="tpu_custom_call" | custom-call | flops 1048576 | bytes 1048576 | tf_op jit(solution)/shard_map/pallas_call | solution.py:637
  154.8 18.5 %shard_map.270 = (bf16[2048,1024]{1,0:T(8,128)(2,1)}, bf16[2048,1024]{1,0:T(8,128)(2,1)}, bf16[2048,768]{1,0:T(8,128)(2,1)}) custom-call(bf16[2048,2048]{1,0:T(8,128)(2,1)} %shard_map.269.normed_ref.refs_1_, bf16[2048,1024]{1,0:T(8,128)(2,1)} %get-tuple-element.236.up_ref.w_one_ref, bf16[2048,768]{1,0:T(8,128)(2,1)} %get-tuple-element.237.qkv_w_ref.w_two_ref, ...), custom_call_target="tpu_custom_call" | custom-call | flops 1048576 | bytes 1048576 | tf_op jit(solution)/shard_map/pallas_call | solution.py:813
  180.3 9.3 %shard_map.272 = (bf16[2048,1024]{1,0:T(8,128)(2,1)}, bf16[2048,1024]{1,0:T(8,128)(2,1)}, bf16[2048,768]{1,0:T(8,128)(2,1)}) custom-call(bf16[2048,2048]{1,0:T(8,128)(2,1)} %shard_map.271.normed_ref, bf16[2048,1024]{1,0:T(8,128)(2,1)} %get-tuple-element.236.up_ref.w_one_ref, ...), custom_call_target="tpu_custom_call", output_to_operand_aliasing={{0}: (4, {}), {1}: (5, {}), {2}: (6, {})} | custom-call | flops 1048576 | bytes 1048576 | tf_op jit(solution)/shard_map/pallas_call | solution.py:813
  203.4 9.1 %shard_map.275 = (bf16[256,2048]{1,0:T(8,128)(2,1)}, bf16[256,2048]{1,0:T(8,128)(2,1)}, bf16[256,2048]{1,0:T(8,128)(2,1)}, bf16[256,2048]{1,0:T(8,128)(2,1)}) custom-call(bf16[2048,1024]{1,0:T(8,128)(2,1)} %get-tuple-element.253.one_a_ref.one_b_ref.act_ref, bf16[2048,1024]{1,0:T(8,128)(2,1)} %get-tuple-element.253.one_a_ref.one_b_ref.act_ref, ...), custom_call_target="tpu_custom_call" | custom-call | flops 1048576 | bytes 1048576 | tf_op jit(solution)/shard_map/pallas_call | solution.py:856
  212.4 9.1 %shard_map.274 = (bf16[256,2048]{1,0:T(8,128)(2,1)}, bf16[256,2048]{1,0:T(8,128)(2,1)}, bf16[256,2048]{1,0:T(8,128)(2,1)}, bf16[256,2048]{1,0:T(8,128)(2,1)}) custom-call(bf16[2048,1024]{1,0:T(8,128)(2,1)} %get-tuple-element.253.one_a_ref.one_b_ref.act_ref, bf16[2048,1024]{1,0:T(8,128)(2,1)} %get-tuple-element.253.one_a_ref.one_b_ref.act_ref, ...), custom_call_target="tpu_custom_call" | custom-call | flops 1048576 | bytes 1048576 | tf_op jit(solution)/shard_map/pallas_call | solution.py:856
  230.0 11.9 %shard_map.276 = (bf16[2048,1024]{1,0:T(8,128)(2,1)}, bf16[2048,256]{1,0:T(8,128)(2,1)}, f32[1,1024]{1,0:T(1,128)}) custom-call(bf16[256,2048]{1,0:T(8,128)(2,1)} %bitcast.150, bf16[256,2048]{1,0:T(8,128)(2,1)} %copy-done.15, bf16[256,2048]{1,0:T(8,128)(2,1)} %collective-permute-done.12.refs_2_, bf16[256,2048]{1,0:T(8,128)(2,1)} %copy-done.16, ...), custom_call_target="tpu_custom_call" | custom-call | flops 1048576 | bytes 1048576 | tf_op jit(solution)/shard_map/pallas_call | solution.py:909
  241.9 8.8 %shard_map.277 = (bf16[2048,1024]{1,0:T(8,128)(2,1)}, bf16[2048,256]{1,0:T(8,128)(2,1)}, f32[1,1024]{1,0:T(1,128)}) custom-call(bf16[256,2048]{1,0:T(8,128)(2,1)} %copy-done.9, bf16[256,2048]{1,0:T(8,128)(2,1)} %copy-done.10, bf16[1024,2048]{1,0:T(8,128)(2,1)} %refs_2_.3, bf16[256,2048]{1,0:T(8,128)(2,1)} %refs_3_.3, ...), custom_call_target="tpu_custom_call", output_to_operand_aliasing={{0}: (5, {}), {1}: (6, {})} | custom-call | flops 1048576 | bytes 1048576 | tf_op jit(solution)/shard_map/pallas_call | solution.py:909
  262.5 16.3 %shard_map.279 = (bf16[1024,1024]{1,0:T(8,128)(2,1)}, bf16[1024,1024]{1,0:T(8,128)(2,1)}, f32[1,2048]{1,0:T(1,128)}, f32[1,2048]{1,0:T(1,128)}) custom-call(s32[1]{0:T(128)} %bitcast.18.core_ref, bf16[2048,2048]{1,0:T(8,128)(2,1)} %shard_map.271.normed_ref, bf16[2048,1024]{1,0:T(8,128)(2,1)} %get-tuple-element.342.right_ref.one_a_ref.one_b_ref, ...), custom_call_target="tpu_custom_call" | custom-call | flops 1048576 | bytes 1048576 | tf_op jit(solution)/shard_map/pallas_call | solution.py:983
  283.6 13.2 %shard_map.280 = (bf16[8,256,768]{2,1,0:T(8,128)(2,1)}, f32[1,768]{1,0:T(1,128)}) custom-call(s32[17]{0:T(128)} %pad_add_fusion.1.seq_ref, bf16[8,256,768]{2,1,0:T(8,128)(2,1)} %bitcast.136, bf16[8,256,256]{2,1,0:T(8,128)(2,1)} %bitcast.156, f32[8,256,128]{2,1,0:T(8,128)} %get-tuple-element.505.cos_ref, f32[8,256,128]{2,1,0:T(8,128)} %get-tuple-element.506.sin_ref, ...), custom_call_target="tpu_custom_call" | custom-call | flops 1048576 | bytes 1048576 | tf_op jit(solution)/shard_map/pallas_call | solution.py:543
  297.6 12.9 %shard_map.281 = (bf16[1024,768]{1,0:T(8,128)(2,1)}, bf16[1024,768]{1,0:T(8,128)(2,1)}, f32[1,2048]{1,0:T(1,128)}, f32[1,2048]{1,0:T(1,128)}) custom-call(s32[1]{0:T(128)} %bitcast.18.core_ref, bf16[2048,2048]{1,0:T(8,128)(2,1)} %shard_map.271.normed_ref, bf16[2048,768]{1,0:T(8,128)(2,1)} %bitcast.130, bf16[2048,768]{1,0:T(8,128)(2,1)} %get-tuple-element.297.weight_ref, ...), custom_call_target="tpu_custom_call" | custom-call | flops 1048576 | bytes 1048576 | tf_op jit(solution)/shard_map/pallas_call | solution.py:983
  325.2 11.8 %shard_map.282 = (bf16[256,2048]{1,0:T(8,128)(2,1)}, bf16[256,2048]{1,0:T(8,128)(2,1)}, bf16[256,2048]{1,0:T(8,128)(2,1)}, bf16[256,2048]{1,0:T(8,128)(2,1)}) custom-call(bf16[2048,1024]{1,0:T(8,128)(2,1)} %get-tuple-element.342.right_ref.one_a_ref.one_b_ref, bf16[2048,1024]{1,0:T(8,128)(2,1)} %get-tuple-element.342.right_ref.one_a_ref.one_b_ref, ...), custom_call_target="tpu_custom_call" | custom-call | flops 1048576 | bytes 1048576 | tf_op jit(solution)/shard_map/pallas_call | solution.py:856
  359.7 19.8 %shard_map.283 = (bf16[1280,1024]{1,0:T(8,128)(2,1)}, bf16[1280,1024]{1,0:T(8,128)(2,1)}) custom-call(s32[1]{0:T(128)} %bitcast.18.core_ref, bf16[2048,1024]{1,0:T(8,128)(2,1)} %get-tuple-element.253.one_a_ref.one_b_ref.act_ref, bf16[2048,256]{1,0:T(8,128)(2,1)} %bitcast.149, bf16[256,2048]{1,0:T(8,128)(2,1)} %bitcast.151, bf16[256,2048]{1,0:T(8,128)(2,1)} %copy-done.15, ...), custom_call_target="tpu_custom_call" | custom-call | flops 1048576 | bytes 1048576 | tf_op jit(solution)/shard_map/pallas_call | solution.py:1045
  392.3 11.8 %shard_map.284 = (bf16[256,2048]{1,0:T(8,128)(2,1)}, bf16[256,2048]{1,0:T(8,128)(2,1)}, bf16[256,2048]{1,0:T(8,128)(2,1)}, bf16[256,2048]{1,0:T(8,128)(2,1)}) custom-call(bf16[2048,1024]{1,0:T(8,128)(2,1)} %get-tuple-element.342.right_ref.one_a_ref.one_b_ref, bf16[2048,1024]{1,0:T(8,128)(2,1)} %get-tuple-element.342.right_ref.one_a_ref.one_b_ref, ...), custom_call_target="tpu_custom_call" | custom-call | flops 1048576 | bytes 1048576 | tf_op jit(solution)/shard_map/pallas_call | solution.py:856
  407.3 13.3 %collective-permute-done.44 = bf16[4,64,768]{2,1,0:T(8,128)(2,1)} collective-permute-done((bf16[4,64,768]{2,1,0:T(8,128)(2,1)}, bf16[4,64,768]{2,1,0:T(8,128)(2,1)}, u32[]{:S(2)}, u32[]{:S(2)}) %collective-permute-start.44) | collective-permute-done | bytes 393248 | tf_op jit(solution)/shard_map/ppermute | solution.py:358
  433.0 15.3 %collective-permute-done.48 = bf16[256,2048]{1,0:T(8,128)(2,1)S(1)} collective-permute-done((bf16[256,2048]{1,0:T(8,128)(2,1)S(1)}, bf16[256,2048]{1,0:T(8,128)(2,1)S(1)}, u32[]{:S(2)}, u32[]{:S(2)}) %collective-permute-start.48) | collective-permute-done | bytes 1048608 | tf_op jit(solution)/shard_map/ppermute | solution.py:358
  450.0 9.8 %collective-permute-done.46 = bf16[2,2,64,768]{3,2,1,0:T(8,128)(2,1)S(1)} collective-permute-done((bf16[2,2,64,768]{3,2,1,0:T(8,128)(2,1)S(1)}, bf16[2,2,64,768]{3,2,1,0:T(8,128)(2,1)S(1)}, u32[]{:S(2)}, u32[]{:S(2)}) %collective-permute-start.46) | collective-permute-done | bytes 393248 | tf_op jit(solution)/shard_map/ppermute | solution.py:358
  471.3 10.4 %collective-permute-done.53 = bf16[256,2048]{1,0:T(8,128)(2,1)S(1)} collective-permute-done((bf16[256,2048]{1,0:T(8,128)(2,1)S(1)}, bf16[256,2048]{1,0:T(8,128)(2,1)S(1)}, u32[]{:S(2)}, u32[]{:S(2)}) %collective-permute-start.53) | collective-permute-done | bytes 1048608 | tf_op jit(solution)/shard_map/ppermute | solution.py:358
  482.1 9.8 %collective-permute-done.50 = bf16[256,2048]{1,0:T(8,128)(2,1)S(1)} collective-permute-done((bf16[256,2048]{1,0:T(8,128)(2,1)S(1)}, bf16[256,2048]{1,0:T(8,128)(2,1)S(1)}, u32[]{:S(2)}, u32[]{:S(2)}) %collective-permute-start.50) | collective-permute-done | bytes 1048608 | tf_op jit(solution)/shard_map/ppermute | solution.py:362
  505.7 9.7 %collective-permute-done.58 = bf16[256,2048]{1,0:T(8,128)(2,1)S(1)} collective-permute-done((bf16[256,2048]{1,0:T(8,128)(2,1)S(1)}, bf16[256,2048]{1,0:T(8,128)(2,1)S(1)}, u32[]{:S(2)}, u32[]{:S(2)}) %collective-permute-start.58) | collective-permute-done | bytes 1048608 | tf_op jit(solution)/shard_map/ppermute | solution.py:358
  515.8 9.6 %collective-permute-done.54 = bf16[256,2048]{1,0:T(8,128)(2,1)S(1)} collective-permute-done((bf16[256,2048]{1,0:T(8,128)(2,1)S(1)}, bf16[256,2048]{1,0:T(8,128)(2,1)S(1)}, u32[]{:S(2)}, u32[]{:S(2)}) %collective-permute-start.54) | collective-permute-done | bytes 1048608 | tf_op jit(solution)/shard_map/ppermute | solution.py:358
  (343 shorter events, 265.1 us)
Async XLA Ops:
  0.6 33.2 %collective-permute-start = (bf16[256,2048]{1,0:T(8,128)(2,1)}, bf16[256,2048]{1,0:T(8,128)(2,1)}, u32[]{:S(2)}, u32[]{:S(2)}) collective-permute-start(bf16[256,2048]{1,0:T(8,128)(2,1)} %bitcast.137), channel_id=1, source_target_pairs={{0,2},{1,3},{2,0},{3,1},{4,6},{5,7},{6,4},{7,5},{8,10},{9,11},{10,... | collective-permute-start | bytes 3145736 | tf_op jit(solution)/shard_map/ppermute | solution.py:358
  3.7 30.1 %collective-permute-start.1 = (bf16[256,2048]{1,0:T(8,128)(2,1)}, bf16[256,2048]{1,0:T(8,128)(2,1)}, u32[]{:S(2)}, u32[]{:S(2)}) collective-permute-start(bf16[256,2048]{1,0:T(8,128)(2,1)} %bitcast.138), channel_id=1, source_target_pairs={{2,4},{3,5},{4,2},{5,3},{10,12},{11,13},{12,10},{13,11},{18,20},{1... | collective-permute-start | bytes 3145736 | tf_op jit(solution)/shard_map/ppermute | solution.py:362
  33.9 40.4 %collective-permute-start.7 = (bf16[256,2048]{1,0:T(8,128)(2,1)S(1)}, bf16[256,2048]{1,0:T(8,128)(2,1)S(1)}, u32[]{:S(2)}, u32[]{:S(2)}) collective-permute-start(bf16[256,2048]{1,0:T(8,128)(2,1)S(1)} %bitcast.140), channel_id=1, source_target_pairs={{0,1},{1,0},{2,3},{3,2},{4,5},{5,4},{6,7},{7,6},{8,9},{9,8},{10,11... | collective-permute-start | bytes 3145736 | tf_op jit(solution)/shard_map/ppermute | solution.py:358
  35.5 44.7 %collective-permute-start.3 = (bf16[256,2048]{1,0:T(8,128)(2,1)}, bf16[256,2048]{1,0:T(8,128)(2,1)S(1)}, u32[]{:S(2)}, u32[]{:S(2)}) collective-permute-start(bf16[256,2048]{1,0:T(8,128)(2,1)} %collective-permute-done.refs_1_), channel_id=1, source_target_pairs={{0,1},{1,0},{2,3},{3,2},{4,5},{5,4},{6,7},{7,6},{8,9},{9,8},{10,11... | collective-permute-start | bytes 3145736 | tf_op jit(solution)/shard_map/ppermute | solution.py:358
  39.0 34.0 %collective-permute-start.5 = (bf16[2,64,1792]{2,1,0:T(8,128)(2,1)S(1)}, bf16[2,64,1792]{2,1,0:T(8,128)(2,1)S(1)}, u32[]{:S(2)}, u32[]{:S(2)}) collective-permute-start(bf16[2,64,1792]{2,1,0:T(8,128)(2,1)S(1)} %get-tuple-element.215), channel_id=1, source_target_pairs={{0,4},{1,5},{2,6},{3,7},{4,0},{5,1},{6,2},{7,3},{8,12},{9,13},{10,... | collective-permute-start | bytes 1376264 | tf_op jit(solution)/shard_map/ppermute | solution.py:358
  39.0 34.0 %collective-permute-start.6 = (bf16[2,64,1792]{2,1,0:T(8,128)(2,1)S(1)}, bf16[2,64,1792]{2,1,0:T(8,128)(2,1)S(1)}, u32[]{:S(2)}, u32[]{:S(2)}) collective-permute-start(bf16[2,64,1792]{2,1,0:T(8,128)(2,1)S(1)} %get-tuple-element.216), channel_id=1, source_target_pairs={{0,6},{1,7},{2,4},{3,5},{4,2},{5,3},{6,0},{7,1},{8,14},{9,15},{10,... | collective-permute-start | bytes 1376264 | tf_op jit(solution)/shard_map/ppermute | solution.py:358
  80.1 30.1 %collective-permute-start.11 = (bf16[3,2,64,1792]{3,2,1,0:T(8,128)(2,1)}, bf16[3,2,64,1792]{3,2,1,0:T(8,128)(2,1)}, u32[]{:S(2)}, u32[]{:S(2)}) collective-permute-start(bf16[3,2,64,1792]{3,2,1,0:T(8,128)(2,1)} %pad_maximum_fusion.3), channel_id=1, source_target_pairs={{0,16},{8,24},{16,0},{24,8},{1,17},{9,25},{17,1},{25,9},{2,18},{10... | collective-permute-start | bytes 4128776 | tf_op jit(solution)/shard_map/ppermute | solution.py:358
  87.7 34.7 %collective-permute-start.16 = (bf16[8,64,1792]{2,1,0:T(8,128)(2,1)S(1)}, bf16[8,64,1792]{2,1,0:T(8,128)(2,1)}, u32[]{:S(2)}, u32[]{:S(2)}) collective-permute-start(bf16[8,64,1792]{2,1,0:T(8,128)(2,1)S(1)} %bitcast.158), channel_id=1, source_target_pairs={{0,8},{8,0},{16,24},{24,16},{1,9},{9,1},{17,25},{25,17},{2,10},{10... | collective-permute-start | bytes 5505032 | tf_op jit(solution)/shard_map/ppermute | solution.py:358
  150.7 47.6 %collective-permute-start.21 = (bf16[256,2048]{1,0:T(8,128)(2,1)}, bf16[256,2048]{1,0:T(8,128)(2,1)}, u32[]{:S(2)}, u32[]{:S(2)}) collective-permute-start(bf16[256,2048]{1,0:T(8,128)(2,1)} %collective-permute-done.14), channel_id=1, source_target_pairs={{2,0},{3,1},{4,6},{5,7},{10,8},{11,9},{12,14},{13,15},{18,16},{19,... | collective-permute-start | bytes 3145736 | tf_op jit(solution)/shard_map/ppermute | solution.py:362
  279.2 34.8 %collective-permute-start.27 = (bf16[1024,1024]{1,0:T(8,128)(2,1)}, bf16[1024,1024]{1,0:T(8,128)(2,1)S(1)}, u32[]{:S(2)}, u32[]{:S(2)}) collective-permute-start(bf16[1024,1024]{1,0:T(8,128)(2,1)} %get-tuple-element.291), channel_id=1, source_target_pairs={{0,8},{8,0},{16,24},{24,16},{1,9},{9,1},{17,25},{25,17},{2,10},{10... | collective-permute-start | bytes 6291464 | tf_op jit(solution)/shard_map/ppermute | solution.py:358
  279.2 32.8 %collective-permute-start.29 = (bf16[256,2048]{1,0:T(8,128)(2,1)}, bf16[256,2048]{1,0:T(8,128)(2,1)}, u32[]{:S(2)}, u32[]{:S(2)}) collective-permute-start(bf16[256,2048]{1,0:T(8,128)(2,1)} %get-tuple-element.301), channel_id=1, source_target_pairs={{0,1},{1,0},{2,3},{3,2},{4,5},{5,4},{6,7},{7,6},{8,9},{9,8},{10,11... | collective-permute-start | bytes 3145736 | tf_op jit(solution)/shard_map/ppermute | solution.py:358
  280.3 36.0 %collective-permute-start.28 = (bf16[256,2048]{1,0:T(8,128)(2,1)S(1)}, bf16[256,2048]{1,0:T(8,128)(2,1)}, u32[]{:S(2)}, u32[]{:S(2)}) collective-permute-start(bf16[256,2048]{1,0:T(8,128)(2,1)S(1)} %add_convert_fusion.16), channel_id=1, source_target_pairs={{0,2},{1,3},{6,4},{7,5},{8,10},{9,11},{14,12},{15,13},{16,18},{17,... | collective-permute-start | bytes 3145736 | tf_op jit(solution)/shard_map/ppermute | solution.py:362
  348.8 30.6 %collective-permute-start.39 = (bf16[4,64,1024]{2,1,0:T(8,128)(2,1)}, bf16[4,64,1024]{2,1,0:T(8,128)(2,1)}, u32[]{:S(2)}, u32[]{:S(2)}) collective-permute-start(bf16[4,64,1024]{2,1,0:T(8,128)(2,1)} %get-tuple-element.330), channel_id=1, source_target_pairs={{0,1},{1,0},{2,3},{3,2},{4,5},{5,4},{6,7},{7,6},{8,9},{9,8},{10,11... | collective-permute-start | bytes 1572872 | tf_op jit(solution)/shard_map/ppermute | solution.py:358
  349.8 34.8 %collective-permute-start.38 = (bf16[256,2048]{1,0:T(8,128)(2,1)}, bf16[256,2048]{1,0:T(8,128)(2,1)}, u32[]{:S(2)}, u32[]{:S(2)}) collective-permute-start(bf16[256,2048]{1,0:T(8,128)(2,1)} %get-tuple-element.329), channel_id=1, source_target_pairs={{0,1},{1,0},{2,3},{3,2},{4,5},{5,4},{6,7},{7,6},{8,9},{9,8},{10,11... | collective-permute-start | bytes 3145736 | tf_op jit(solution)/shard_map/ppermute | solution.py:358
  350.9 30.5 %collective-permute-start.37 = (bf16[8,64,768]{2,1,0:T(8,128)(2,1)}, bf16[8,64,768]{2,1,0:T(8,128)(2,1)}, u32[]{:S(2)}, u32[]{:S(2)}) collective-permute-start(bf16[8,64,768]{2,1,0:T(8,128)(2,1)} %get-tuple-element.325), channel_id=1, source_target_pairs={{0,16},{8,24},{16,0},{24,8},{1,17},{9,25},{17,1},{25,9},{2,18},{10... | collective-permute-start | bytes 2359304 | tf_op jit(solution)/shard_map/ppermute | solution.py:358
  355.0 31.2 %collective-permute-start.36 = (bf16[256,2048]{1,0:T(8,128)(2,1)}, bf16[256,2048]{1,0:T(8,128)(2,1)}, u32[]{:S(2)}, u32[]{:S(2)}) collective-permute-start(bf16[256,2048]{1,0:T(8,128)(2,1)} %add_convert_fusion.10), channel_id=1, source_target_pairs={{2,4},{3,5},{4,2},{5,3},{10,12},{11,13},{12,10},{13,11},{18,20},{1... | collective-permute-start | bytes 3145736 | tf_op jit(solution)/shard_map/ppermute | solution.py:362
  386.2 37.3 %collective-permute-start.41 = (bf16[1280,1024]{1,0:T(8,128)(2,1)}, bf16[1280,1024]{1,0:T(8,128)(2,1)}, u32[]{:S(2)}, u32[]{:S(2)}) collective-permute-start(bf16[1280,1024]{1,0:T(8,128)(2,1)} %get-tuple-element.340), channel_id=1, source_target_pairs={{0,8},{8,0},{16,24},{24,16},{1,9},{9,1},{17,25},{25,17},{2,10},{10... | collective-permute-start | bytes 7864328 | tf_op jit(solution)/shard_map/ppermute | solution.py:358
  386.3 35.6 %collective-permute-start.43 = (bf16[256,2048]{1,0:T(8,128)(2,1)}, bf16[256,2048]{1,0:T(8,128)(2,1)}, u32[]{:S(2)}, u32[]{:S(2)}) collective-permute-start(bf16[256,2048]{1,0:T(8,128)(2,1)} %get-tuple-element.344), channel_id=1, source_target_pairs={{0,1},{1,0},{2,3},{3,2},{4,5},{5,4},{6,7},{7,6},{8,9},{9,8},{10,11... | collective-permute-start | bytes 3145736 | tf_op jit(solution)/shard_map/ppermute | solution.py:358
  387.6 36.0 %collective-permute-start.42 = (f32[24576]{0:T(1024)S(1)}, f32[24576]{0:T(1024)S(1)}, u32[]{:S(2)}, u32[]{:S(2)}) collective-permute-start(f32[24576]{0:T(1024)S(1)} %constant_dynamic-update-slice_fusion), channel_id=1, source_target_pairs={{0,16},{8,24},{16,0},{24,8},{1,17},{9,25},{17,1},{25,9},{2,18},{10... | collective-permute-start | bytes 294920 | tf_op jit(solution)/shard_map/ppermute | solution.py:358
  389.2 31.4 %collective-permute-start.44 = (bf16[4,64,768]{2,1,0:T(8,128)(2,1)}, bf16[4,64,768]{2,1,0:T(8,128)(2,1)}, u32[]{:S(2)}, u32[]{:S(2)}) collective-permute-start(bf16[4,64,768]{2,1,0:T(8,128)(2,1)} %get-tuple-element.346), channel_id=1, source_target_pairs={{0,1},{1,0},{2,3},{3,2},{4,5},{5,4},{6,7},{7,6},{8,9},{9,8},{10,11... | collective-permute-start | bytes 1179656 | tf_op jit(solution)/shard_map/ppermute | solution.py:358
  391.1 32.4 %collective-permute-start.40 = (bf16[2,2,64,1024]{3,2,1,0:T(8,128)(2,1)}, bf16[2,2,64,1024]{3,2,1,0:T(8,128)(2,1)}, u32[]{:S(2)}, u32[]{:S(2)}) collective-permute-start(bf16[2,2,64,1024]{3,2,1,0:T(8,128)(2,1)} %pad_maximum_fusion.6), channel_id=1, source_target_pairs={{0,4},{1,5},{2,6},{3,7},{4,0},{5,1},{6,2},{7,3},{8,12},{9,13},{10,... | collective-permute-start | bytes 1572872 | tf_op jit(solution)/shard_map/ppermute | solution.py:358
  424.6 35.2 %collective-permute-start.45 = (bf16[256,2048]{1,0:T(8,128)(2,1)S(1)}, bf16[256,2048]{1,0:T(8,128)(2,1)S(1)}, u32[]{:S(2)}, u32[]{:S(2)}) collective-permute-start(bf16[256,2048]{1,0:T(8,128)(2,1)S(1)} %add_convert_fusion.9), channel_id=1, source_target_pairs={{0,2},{1,3},{6,4},{7,5},{8,10},{9,11},{14,12},{15,13},{16,18},{17,... | collective-permute-start | bytes 3145736 | tf_op jit(solution)/shard_map/ppermute | solution.py:362
  430.9 61.0 %collective-permute-start.52 = (bf16[1280,1024]{1,0:T(8,128)(2,1)S(1)}, bf16[1280,1024]{1,0:T(8,128)(2,1)S(1)}, u32[]{:S(2)}, u32[]{:S(2)}) collective-permute-start(bf16[1280,1024]{1,0:T(8,128)(2,1)S(1)} %add_convert_fusion.1), channel_id=1, source_target_pairs={{0,16},{8,24},{16,0},{24,8},{1,17},{9,25},{17,1},{25,9},{2,18},{10... | collective-permute-start | bytes 7864328 | tf_op jit(solution)/shard_map/ppermute | solution.py:358
  462.1 29.8 %collective-permute-start.50 = (bf16[256,2048]{1,0:T(8,128)(2,1)S(1)}, bf16[256,2048]{1,0:T(8,128)(2,1)S(1)}, u32[]{:S(2)}, u32[]{:S(2)}) collective-permute-start(bf16[256,2048]{1,0:T(8,128)(2,1)S(1)} %add_convert_fusion.7), channel_id=1, source_target_pairs={{0,2},{1,3},{6,4},{7,5},{8,10},{9,11},{14,12},{15,13},{16,18},{17,... | collective-permute-start | bytes 3145736 | tf_op jit(solution)/shard_map/ppermute | solution.py:362
  (93 other events, 1379.8 us)

commit v7 on v6

--- a/solution.py
+++ b/solution.py
@@ -899,7 +899,7 @@
     hidden, head = w_down.shape[0], w_dense.shape[0]
     tokens = HEADS * rows
     count = len(blocks)
-    lanes = 256
+    lanes = 512
     steps = hidden // lanes
 
     def at(i):

time: 570 us -> 569 us (level)
  transfers between devices with their start and end apart: 68 -> 68, of which waited for: 24 -> 25; matrix products, arithmetic and copies ran while one was open for 13% -> 13% of each run, Pallas kernels for 38% -> 38%
where the time goes in v7:
time: 569 us; the launch traced here: 560 us
  Pallas kernels  218 us (38%)
  waiting for transfers between devices  165 us (29%)
  starting transfers between devices  92.4 us (16%)
  other arithmetic  59.7 us (10%)
  local copies, waits for them, and re-layouts  21.6 us (4%)
    ppermute x52, waiting for transfers between devices, flip(): return lax.ppermute(value, axis, [(i, i ^ bit) for i in range(size)])  140 us
    ppermute x52, starting transfers between devices, flip(): return lax.ppermute(value, axis, [(i, i ^ bit) for i in range(size)])  60.2 us
    pallas_call x4, Pallas kernels, combine(): pl.pallas_call(functools.partial(combine_kernel, right_dim=right_dim), ou...  41.7 us
    ppermute x16, starting transfers between devices, send(): lax.ppermute(value, 'shard', [(2 * a + y, 2 * b + y) for a, b in pairs fo...  32.2 us
    pallas_call x2, Pallas kernels, moments_of(): pl.pallas_call(functools.partial(moments_kernel, quarter=quarter, norm=no...  29.2 us
    pallas_call x3, Pallas kernels, pull(): pl.pallas_call(functools.partial(pull_kernel, count=count), out_shape=(ja...  28.5 us
    pallas_call x2, Pallas kernels, project(): pl.pallas_call(project_kernel, out_shape=tuple((jax.ShapeDtypeStruct((cou...  27.8 us
    ppermute x16, waiting for transfers between devices, send(): lax.ppermute(value, 'shard', [(2 * a + y, 2 * b + y) for a, b in pairs fo...  25.1 us
  transfers between devices with their start and end apart: 68, of which 25 were waited for; matrix products, arithmetic and copies ran while one was open for 13% of the time, Pallas kernels for 38%

profile of v7, /device:TPU:0, one launch (start us, length us, event | category | flops | bytes accessed | tf_op | source)
XLA Modules:
  0.0 559.5 jit_solution(4650362029906119164)
XLA Ops:
  41.4 13.6 %collective-permute-done.4 = bf16[2,64,1792]{2,1,0:T(8,128)(2,1)S(1)} collective-permute-done((bf16[2,64,1792]{2,1,0:T(8,128)(2,1)S(1)}, bf16[2,64,1792]{2,1,0:T(8,128)(2,1)S(1)}, u32[]{:S(2)}, u32[]{:S(2)}) %collective-permute-start.4) | collective-permute-done | bytes 458784 | tf_op jit(solution)/shard_map/ppermute | solution.py:358
  56.5 16.5 %collective-permute-done.5 = bf16[2,64,1792]{2,1,0:T(8,128)(2,1)S(1)} collective-permute-done((bf16[2,64,1792]{2,1,0:T(8,128)(2,1)S(1)}, bf16[2,64,1792]{2,1,0:T(8,128)(2,1)S(1)}, u32[]{:S(2)}, u32[]{:S(2)}) %collective-permute-start.5) | collective-permute-done | bytes 458784 | tf_op jit(solution)/shard_map/ppermute | solution.py:358
  87.8 8.8 %shard_map.265.refs_1_ = bf16[2048,2048]{1,0:T(8,128)(2,1)} custom-call(bf16[256,2048]{1,0:T(8,128)(2,1)} %bitcast.139, bf16[256,2048]{1,0:T(8,128)(2,1)} %collective-permute-done.refs_1_, bf16[256,2048]{1,0:T(8,128)(2,1)} %copy-done.24, bf16[256,2048]{1,0:T(8,128)(2,1)} %copy-done.25), custom_call_target="tpu_custom_call" | custom-call | flops 1048576 | bytes 1048576 | tf_op jit(solution)/shard_map/pallas_call | solution.py:762
  96.5 9.9 %collective-permute-done.10 = bf16[256,2048]{1,0:T(8,128)(2,1)} collective-permute-done((bf16[256,2048]{1,0:T(8,128)(2,1)}, bf16[256,2048]{1,0:T(8,128)(2,1)}, u32[]{:S(2)}, u32[]{:S(2)}) %collective-permute-start.10) | collective-permute-done | bytes 1048608 | tf_op jit(solution)/shard_map/ppermute | solution.py:362
  122.3 13.0 %shard_map.266 = (bf16[2048,1024]{1,0:T(8,128)(2,1)}, bf16[2048,768]{1,0:T(8,128)(2,1)}, bf16[2048,1024]{1,0:T(8,128)(2,1)}, bf16[2048,768]{1,0:T(8,128)(2,1)}, f32[1,1792]{1,0:T(1,128)}) custom-call(s32[2]{0:T(128)} %copy-done.2, bf16[8,64,1792]{2,1,0:T(8,128)(2,1)} %bitcast.159, bf16[8,64,1792]{2,1,0:T(8,128)(2,1)} %collective-permute-done.16.p1_ref, ...), custom_call_target="tpu_custom_call" | custom-call | flops 1048576 | bytes 1048576 | tf_op jit(solution)/shard_map/pallas_call | solution.py:637
  154.8 18.5 %shard_map.270 = (bf16[2048,1024]{1,0:T(8,128)(2,1)}, bf16[2048,1024]{1,0:T(8,128)(2,1)}, bf16[2048,768]{1,0:T(8,128)(2,1)}) custom-call(bf16[2048,2048]{1,0:T(8,128)(2,1)} %shard_map.269.normed_ref.refs_1_, bf16[2048,1024]{1,0:T(8,128)(2,1)} %get-tuple-element.236.up_ref.w_one_ref, bf16[2048,768]{1,0:T(8,128)(2,1)} %get-tuple-element.237.qkv_w_ref.w_two_ref, ...), custom_call_target="tpu_custom_call" | custom-call | flops 1048576 | bytes 1048576 | tf_op jit(solution)/shard_map/pallas_call | solution.py:813
  180.3 9.3 %shard_map.272 = (bf16[2048,1024]{1,0:T(8,128)(2,1)}, bf16[2048,1024]{1,0:T(8,128)(2,1)}, bf16[2048,768]{1,0:T(8,128)(2,1)}) custom-call(bf16[2048,2048]{1,0:T(8,128)(2,1)} %shard_map.271.normed_ref, bf16[2048,1024]{1,0:T(8,128)(2,1)} %get-tuple-element.236.up_ref.w_one_ref, ...), custom_call_target="tpu_custom_call", output_to_operand_aliasing={{0}: (4, {}), {1}: (5, {}), {2}: (6, {})} | custom-call | flops 1048576 | bytes 1048576 | tf_op jit(solution)/shard_map/pallas_call | solution.py:813
  189.6 8.8 %shard_map.273 = (bf16[8,256,256]{2,1,0:T(8,128)(2,1)}, bf16[8,256,256]{2,1,0:T(8,128)(2,1)}, bf16[8,256,256]{2,1,0:T(8,128)(2,1)}) custom-call(s32[17]{0:T(128)} %pad_add_fusion.1.seq_ref, bf16[8,256,768]{2,1,0:T(8,128)(2,1)} %bitcast.135, f32[8,256,128]{2,1,0:T(8,128)} %get-tuple-element.505.cos_ref, f32[8,256,128]{2,1,0:T(8,128)} %get-tuple-element.506.sin_ref), custom_call_target="tpu_custom_call" | custom-call | flops 1048576 | bytes 1048576 | tf_op jit(solution)/shard_map/pallas_call | solution.py:526
  203.4 9.1 %shard_map.275 = (bf16[256,2048]{1,0:T(8,128)(2,1)}, bf16[256,2048]{1,0:T(8,128)(2,1)}, bf16[256,2048]{1,0:T(8,128)(2,1)}, bf16[256,2048]{1,0:T(8,128)(2,1)}) custom-call(bf16[2048,1024]{1,0:T(8,128)(2,1)} %get-tuple-element.253.one_a_ref.one_b_ref.act_ref, bf16[2048,1024]{1,0:T(8,128)(2,1)} %get-tuple-element.253.one_a_ref.one_b_ref.act_ref, ...), custom_call_target="tpu_custom_call" | custom-call | flops 1048576 | bytes 1048576 | tf_op jit(solution)/shard_map/pallas_call | solution.py:856
  212.4 9.1 %shard_map.274 = (bf16[256,2048]{1,0:T(8,128)(2,1)}, bf16[256,2048]{1,0:T(8,128)(2,1)}, bf16[256,2048]{1,0:T(8,128)(2,1)}, bf16[256,2048]{1,0:T(8,128)(2,1)}) custom-call(bf16[2048,1024]{1,0:T(8,128)(2,1)} %get-tuple-element.253.one_a_ref.one_b_ref.act_ref, bf16[2048,1024]{1,0:T(8,128)(2,1)} %get-tuple-element.253.one_a_ref.one_b_ref.act_ref, ...), custom_call_target="tpu_custom_call" | custom-call | flops 1048576 | bytes 1048576 | tf_op jit(solution)/shard_map/pallas_call | solution.py:856
  230.0 12.1 %shard_map.276 = (bf16[2048,1024]{1,0:T(8,128)(2,1)}, bf16[2048,256]{1,0:T(8,128)(2,1)}, f32[1,1024]{1,0:T(1,128)}) custom-call(bf16[256,2048]{1,0:T(8,128)(2,1)} %bitcast.150, bf16[256,2048]{1,0:T(8,128)(2,1)} %copy-done.15, bf16[256,2048]{1,0:T(8,128)(2,1)} %collective-permute-done.12.refs_2_, bf16[256,2048]{1,0:T(8,128)(2,1)} %copy-done.16, ...), custom_call_target="tpu_custom_call" | custom-call | flops 1048576 | bytes 1048576 | tf_op jit(solution)/shard_map/pallas_call | solution.py:909
  262.3 16.3 %shard_map.279 = (bf16[1024,1024]{1,0:T(8,128)(2,1)}, bf16[1024,1024]{1,0:T(8,128)(2,1)}, f32[1,2048]{1,0:T(1,128)}, f32[1,2048]{1,0:T(1,128)}) custom-call(s32[1]{0:T(128)} %bitcast.18.core_ref, bf16[2048,2048]{1,0:T(8,128)(2,1)} %shard_map.271.normed_ref, bf16[2048,1024]{1,0:T(8,128)(2,1)} %get-tuple-element.342.right_ref.one_a_ref.one_b_ref, ...), custom_call_target="tpu_custom_call" | custom-call | flops 1048576 | bytes 1048576 | tf_op jit(solution)/shard_map/pallas_call | solution.py:983
  283.4 13.2 %shard_map.280 = (bf16[8,256,768]{2,1,0:T(8,128)(2,1)}, f32[1,768]{1,0:T(1,128)}) custom-call(s32[17]{0:T(128)} %pad_add_fusion.1.seq_ref, bf16[8,256,768]{2,1,0:T(8,128)(2,1)} %bitcast.136, bf16[8,256,256]{2,1,0:T(8,128)(2,1)} %bitcast.156, f32[8,256,128]{2,1,0:T(8,128)} %get-tuple-element.505.cos_ref, f32[8,256,128]{2,1,0:T(8,128)} %get-tuple-element.506.sin_ref, ...), custom_call_target="tpu_custom_call" | custom-call | flops 1048576 | bytes 1048576 | tf_op jit(solution)/shard_map/pallas_call | solution.py:543
  297.5 12.9 %shard_map.281 = (bf16[1024,768]{1,0:T(8,128)(2,1)}, bf16[1024,768]{1,0:T(8,128)(2,1)}, f32[1,2048]{1,0:T(1,128)}, f32[1,2048]{1,0:T(1,128)}) custom-call(s32[1]{0:T(128)} %bitcast.18.core_ref, bf16[2048,2048]{1,0:T(8,128)(2,1)} %shard_map.271.normed_ref, bf16[2048,768]{1,0:T(8,128)(2,1)} %bitcast.130, bf16[2048,768]{1,0:T(8,128)(2,1)} %get-tuple-element.297.weight_ref, ...), custom_call_target="tpu_custom_call" | custom-call | flops 1048576 | bytes 1048576 | tf_op jit(solution)/shard_map/pallas_call | solution.py:983
  325.1 11.8 %shard_map.282 = (bf16[256,2048]{1,0:T(8,128)(2,1)}, bf16[256,2048]{1,0:T(8,128)(2,1)}, bf16[256,2048]{1,0:T(8,128)(2,1)}, bf16[256,2048]{1,0:T(8,128)(2,1)}) custom-call(bf16[2048,1024]{1,0:T(8,128)(2,1)} %get-tuple-element.342.right_ref.one_a_ref.one_b_ref, bf16[2048,1024]{1,0:T(8,128)(2,1)} %get-tuple-element.342.right_ref.one_a_ref.one_b_ref, ...), custom_call_target="tpu_custom_call" | custom-call | flops 1048576 | bytes 1048576 | tf_op jit(solution)/shard_map/pallas_call | solution.py:856
  359.5 19.8 %shard_map.283 = (bf16[1280,1024]{1,0:T(8,128)(2,1)}, bf16[1280,1024]{1,0:T(8,128)(2,1)}) custom-call(s32[1]{0:T(128)} %bitcast.18.core_ref, bf16[2048,1024]{1,0:T(8,128)(2,1)} %get-tuple-element.253.one_a_ref.one_b_ref.act_ref, bf16[2048,256]{1,0:T(8,128)(2,1)} %bitcast.149, bf16[256,2048]{1,0:T(8,128)(2,1)} %bitcast.151, bf16[256,2048]{1,0:T(8,128)(2,1)} %copy-done.15, ...), custom_call_target="tpu_custom_call" | custom-call | flops 1048576 | bytes 1048576 | tf_op jit(solution)/shard_map/pallas_call | solution.py:1045
  392.1 11.8 %shard_map.284 = (bf16[256,2048]{1,0:T(8,128)(2,1)}, bf16[256,2048]{1,0:T(8,128)(2,1)}, bf16[256,2048]{1,0:T(8,128)(2,1)}, bf16[256,2048]{1,0:T(8,128)(2,1)}) custom-call(bf16[2048,1024]{1,0:T(8,128)(2,1)} %get-tuple-element.342.right_ref.one_a_ref.one_b_ref, bf16[2048,1024]{1,0:T(8,128)(2,1)} %get-tuple-element.342.right_ref.one_a_ref.one_b_ref, ...), custom_call_target="tpu_custom_call" | custom-call | flops 1048576 | bytes 1048576 | tf_op jit(solution)/shard_map/pallas_call | solution.py:856
  407.1 13.3 %collective-permute-done.44 = bf16[4,64,768]{2,1,0:T(8,128)(2,1)} collective-permute-done((bf16[4,64,768]{2,1,0:T(8,128)(2,1)}, bf16[4,64,768]{2,1,0:T(8,128)(2,1)}, u32[]{:S(2)}, u32[]{:S(2)}) %collective-permute-start.44) | collective-permute-done | bytes 393248 | tf_op jit(solution)/shard_map/ppermute | solution.py:358
  432.9 15.3 %collective-permute-done.48 = bf16[256,2048]{1,0:T(8,128)(2,1)S(1)} collective-permute-done((bf16[256,2048]{1,0:T(8,128)(2,1)S(1)}, bf16[256,2048]{1,0:T(8,128)(2,1)S(1)}, u32[]{:S(2)}, u32[]{:S(2)}) %collective-permute-start.48) | collective-permute-done | bytes 1048608 | tf_op jit(solution)/shard_map/ppermute | solution.py:358
  449.9 9.8 %collective-permute-done.46 = bf16[2,2,64,768]{3,2,1,0:T(8,128)(2,1)S(1)} collective-permute-done((bf16[2,2,64,768]{3,2,1,0:T(8,128)(2,1)S(1)}, bf16[2,2,64,768]{3,2,1,0:T(8,128)(2,1)S(1)}, u32[]{:S(2)}, u32[]{:S(2)}) %collective-permute-start.46) | collective-permute-done | bytes 393248 | tf_op jit(solution)/shard_map/ppermute | solution.py:358
  471.1 10.4 %collective-permute-done.53 = bf16[256,2048]{1,0:T(8,128)(2,1)S(1)} collective-permute-done((bf16[256,2048]{1,0:T(8,128)(2,1)S(1)}, bf16[256,2048]{1,0:T(8,128)(2,1)S(1)}, u32[]{:S(2)}, u32[]{:S(2)}) %collective-permute-start.53) | collective-permute-done | bytes 1048608 | tf_op jit(solution)/shard_map/ppermute | solution.py:358
  482.0 9.8 %collective-permute-done.50 = bf16[256,2048]{1,0:T(8,128)(2,1)S(1)} collective-permute-done((bf16[256,2048]{1,0:T(8,128)(2,1)S(1)}, bf16[256,2048]{1,0:T(8,128)(2,1)S(1)}, u32[]{:S(2)}, u32[]{:S(2)}) %collective-permute-start.50) | collective-permute-done | bytes 1048608 | tf_op jit(solution)/shard_map/ppermute | solution.py:362
  505.5 9.8 %collective-permute-done.58 = bf16[256,2048]{1,0:T(8,128)(2,1)S(1)} collective-permute-done((bf16[256,2048]{1,0:T(8,128)(2,1)S(1)}, bf16[256,2048]{1,0:T(8,128)(2,1)S(1)}, u32[]{:S(2)}, u32[]{:S(2)}) %collective-permute-start.58) | collective-permute-done | bytes 1048608 | tf_op jit(solution)/shard_map/ppermute | solution.py:358
  515.7 9.6 %collective-permute-done.54 = bf16[256,2048]{1,0:T(8,128)(2,1)S(1)} collective-permute-done((bf16[256,2048]{1,0:T(8,128)(2,1)S(1)}, bf16[256,2048]{1,0:T(8,128)(2,1)S(1)}, u32[]{:S(2)}, u32[]{:S(2)}) %collective-permute-start.54) | collective-permute-done | bytes 1048608 | tf_op jit(solution)/shard_map/ppermute | solution.py:358
  (343 shorter events, 264.9 us)
Async XLA Ops:
  0.6 33.2 %collective-permute-start = (bf16[256,2048]{1,0:T(8,128)(2,1)}, bf16[256,2048]{1,0:T(8,128)(2,1)}, u32[]{:S(2)}, u32[]{:S(2)}) collective-permute-start(bf16[256,2048]{1,0:T(8,128)(2,1)} %bitcast.137), channel_id=1, source_target_pairs={{0,2},{1,3},{2,0},{3,1},{4,6},{5,7},{6,4},{7,5},{8,10},{9,11},{10,... | collective-permute-start | bytes 3145736 | tf_op jit(solution)/shard_map/ppermute | solution.py:358
  3.7 30.1 %collective-permute-start.1 = (bf16[256,2048]{1,0:T(8,128)(2,1)}, bf16[256,2048]{1,0:T(8,128)(2,1)}, u32[]{:S(2)}, u32[]{:S(2)}) collective-permute-start(bf16[256,2048]{1,0:T(8,128)(2,1)} %bitcast.138), channel_id=1, source_target_pairs={{2,4},{3,5},{4,2},{5,3},{10,12},{11,13},{12,10},{13,11},{18,20},{1... | collective-permute-start | bytes 3145736 | tf_op jit(solution)/shard_map/ppermute | solution.py:362
  33.9 40.4 %collective-permute-start.7 = (bf16[256,2048]{1,0:T(8,128)(2,1)S(1)}, bf16[256,2048]{1,0:T(8,128)(2,1)S(1)}, u32[]{:S(2)}, u32[]{:S(2)}) collective-permute-start(bf16[256,2048]{1,0:T(8,128)(2,1)S(1)} %bitcast.140), channel_id=1, source_target_pairs={{0,1},{1,0},{2,3},{3,2},{4,5},{5,4},{6,7},{7,6},{8,9},{9,8},{10,11... | collective-permute-start | bytes 3145736 | tf_op jit(solution)/shard_map/ppermute | solution.py:358
  35.5 44.7 %collective-permute-start.3 = (bf16[256,2048]{1,0:T(8,128)(2,1)}, bf16[256,2048]{1,0:T(8,128)(2,1)S(1)}, u32[]{:S(2)}, u32[]{:S(2)}) collective-permute-start(bf16[256,2048]{1,0:T(8,128)(2,1)} %collective-permute-done.refs_1_), channel_id=1, source_target_pairs={{0,1},{1,0},{2,3},{3,2},{4,5},{5,4},{6,7},{7,6},{8,9},{9,8},{10,11... | collective-permute-start | bytes 3145736 | tf_op jit(solution)/shard_map/ppermute | solution.py:358
  39.0 34.0 %collective-permute-start.5 = (bf16[2,64,1792]{2,1,0:T(8,128)(2,1)S(1)}, bf16[2,64,1792]{2,1,0:T(8,128)(2,1)S(1)}, u32[]{:S(2)}, u32[]{:S(2)}) collective-permute-start(bf16[2,64,1792]{2,1,0:T(8,128)(2,1)S(1)} %get-tuple-element.215), channel_id=1, source_target_pairs={{0,4},{1,5},{2,6},{3,7},{4,0},{5,1},{6,2},{7,3},{8,12},{9,13},{10,... | collective-permute-start | bytes 1376264 | tf_op jit(solution)/shard_map/ppermute | solution.py:358
  39.0 34.0 %collective-permute-start.6 = (bf16[2,64,1792]{2,1,0:T(8,128)(2,1)S(1)}, bf16[2,64,1792]{2,1,0:T(8,128)(2,1)S(1)}, u32[]{:S(2)}, u32[]{:S(2)}) collective-permute-start(bf16[2,64,1792]{2,1,0:T(8,128)(2,1)S(1)} %get-tuple-element.216), channel_id=1, source_target_pairs={{0,6},{1,7},{2,4},{3,5},{4,2},{5,3},{6,0},{7,1},{8,14},{9,15},{10,... | collective-permute-start | bytes 1376264 | tf_op jit(solution)/shard_map/ppermute | solution.py:358
  80.1 30.1 %collective-permute-start.11 = (bf16[3,2,64,1792]{3,2,1,0:T(8,128)(2,1)}, bf16[3,2,64,1792]{3,2,1,0:T(8,128)(2,1)}, u32[]{:S(2)}, u32[]{:S(2)}) collective-permute-start(bf16[3,2,64,1792]{3,2,1,0:T(8,128)(2,1)} %pad_maximum_fusion.3), channel_id=1, source_target_pairs={{0,16},{8,24},{16,0},{24,8},{1,17},{9,25},{17,1},{25,9},{2,18},{10... | collective-permute-start | bytes 4128776 | tf_op jit(solution)/shard_map/ppermute | solution.py:358
  87.7 34.7 %collective-permute-start.16 = (bf16[8,64,1792]{2,1,0:T(8,128)(2,1)S(1)}, bf16[8,64,1792]{2,1,0:T(8,128)(2,1)}, u32[]{:S(2)}, u32[]{:S(2)}) collective-permute-start(bf16[8,64,1792]{2,1,0:T(8,128)(2,1)S(1)} %bitcast.158), channel_id=1, source_target_pairs={{0,8},{8,0},{16,24},{24,16},{1,9},{9,1},{17,25},{25,17},{2,10},{10... | collective-permute-start | bytes 5505032 | tf_op jit(solution)/shard_map/ppermute | solution.py:358
  150.7 47.6 %collective-permute-start.21 = (bf16[256,2048]{1,0:T(8,128)(2,1)}, bf16[256,2048]{1,0:T(8,128)(2,1)}, u32[]{:S(2)}, u32[]{:S(2)}) collective-permute-start(bf16[256,2048]{1,0:T(8,128)(2,1)} %collective-permute-done.14), channel_id=1, source_target_pairs={{2,0},{3,1},{4,6},{5,7},{10,8},{11,9},{12,14},{13,15},{18,16},{19,... | collective-permute-start | bytes 3145736 | tf_op jit(solution)/shard_map/ppermute | solution.py:362
  279.0 34.8 %collective-permute-start.27 = (bf16[1024,1024]{1,0:T(8,128)(2,1)}, bf16[1024,1024]{1,0:T(8,128)(2,1)S(1)}, u32[]{:S(2)}, u32[]{:S(2)}) collective-permute-start(bf16[1024,1024]{1,0:T(8,128)(2,1)} %get-tuple-element.291), channel_id=1, source_target_pairs={{0,8},{8,0},{16,24},{24,16},{1,9},{9,1},{17,25},{25,17},{2,10},{10... | collective-permute-start | bytes 6291464 | tf_op jit(solution)/shard_map/ppermute | solution.py:358
  279.1 32.8 %collective-permute-start.29 = (bf16[256,2048]{1,0:T(8,128)(2,1)}, bf16[256,2048]{1,0:T(8,128)(2,1)}, u32[]{:S(2)}, u32[]{:S(2)}) collective-permute-start(bf16[256,2048]{1,0:T(8,128)(2,1)} %get-tuple-element.301), channel_id=1, source_target_pairs={{0,1},{1,0},{2,3},{3,2},{4,5},{5,4},{6,7},{7,6},{8,9},{9,8},{10,11... | collective-permute-start | bytes 3145736 | tf_op jit(solution)/shard_map/ppermute | solution.py:358
  280.1 35.9 %collective-permute-start.28 = (bf16[256,2048]{1,0:T(8,128)(2,1)S(1)}, bf16[256,2048]{1,0:T(8,128)(2,1)}, u32[]{:S(2)}, u32[]{:S(2)}) collective-permute-start(bf16[256,2048]{1,0:T(8,128)(2,1)S(1)} %add_convert_fusion.16), channel_id=1, source_target_pairs={{0,2},{1,3},{6,4},{7,5},{8,10},{9,11},{14,12},{15,13},{16,18},{17,... | collective-permute-start | bytes 3145736 | tf_op jit(solution)/shard_map/ppermute | solution.py:362
  348.7 30.6 %collective-permute-start.39 = (bf16[4,64,1024]{2,1,0:T(8,128)(2,1)}, bf16[4,64,1024]{2,1,0:T(8,128)(2,1)}, u32[]{:S(2)}, u32[]{:S(2)}) collective-permute-start(bf16[4,64,1024]{2,1,0:T(8,128)(2,1)} %get-tuple-element.330), channel_id=1, source_target_pairs={{0,1},{1,0},{2,3},{3,2},{4,5},{5,4},{6,7},{7,6},{8,9},{9,8},{10,11... | collective-permute-start | bytes 1572872 | tf_op jit(solution)/shard_map/ppermute | solution.py:358
  349.7 34.8 %collective-permute-start.38 = (bf16[256,2048]{1,0:T(8,128)(2,1)}, bf16[256,2048]{1,0:T(8,128)(2,1)}, u32[]{:S(2)}, u32[]{:S(2)}) collective-permute-start(bf16[256,2048]{1,0:T(8,128)(2,1)} %get-tuple-element.329), channel_id=1, source_target_pairs={{0,1},{1,0},{2,3},{3,2},{4,5},{5,4},{6,7},{7,6},{8,9},{9,8},{10,11... | collective-permute-start | bytes 3145736 | tf_op jit(solution)/shard_map/ppermute | solution.py:358
  350.7 30.5 %collective-permute-start.37 = (bf16[8,64,768]{2,1,0:T(8,128)(2,1)}, bf16[8,64,768]{2,1,0:T(8,128)(2,1)}, u32[]{:S(2)}, u32[]{:S(2)}) collective-permute-start(bf16[8,64,768]{2,1,0:T(8,128)(2,1)} %get-tuple-element.325), channel_id=1, source_target_pairs={{0,16},{8,24},{16,0},{24,8},{1,17},{9,25},{17,1},{25,9},{2,18},{10... | collective-permute-start | bytes 2359304 | tf_op jit(solution)/shard_map/ppermute | solution.py:358
  354.9 31.2 %collective-permute-start.36 = (bf16[256,2048]{1,0:T(8,128)(2,1)}, bf16[256,2048]{1,0:T(8,128)(2,1)}, u32[]{:S(2)}, u32[]{:S(2)}) collective-permute-start(bf16[256,2048]{1,0:T(8,128)(2,1)} %add_convert_fusion.10), channel_id=1, source_target_pairs={{2,4},{3,5},{4,2},{5,3},{10,12},{11,13},{12,10},{13,11},{18,20},{1... | collective-permute-start | bytes 3145736 | tf_op jit(solution)/shard_map/ppermute | solution.py:362
  386.0 37.3 %collective-permute-start.41 = (bf16[1280,1024]{1,0:T(8,128)(2,1)}, bf16[1280,1024]{1,0:T(8,128)(2,1)}, u32[]{:S(2)}, u32[]{:S(2)}) collective-permute-start(bf16[1280,1024]{1,0:T(8,128)(2,1)} %get-tuple-element.340), channel_id=1, source_target_pairs={{0,8},{8,0},{16,24},{24,16},{1,9},{9,1},{17,25},{25,17},{2,10},{10... | collective-permute-start | bytes 7864328 | tf_op jit(solution)/shard_map/ppermute | solution.py:358
  386.1 35.6 %collective-permute-start.43 = (bf16[256,2048]{1,0:T(8,128)(2,1)}, bf16[256,2048]{1,0:T(8,128)(2,1)}, u32[]{:S(2)}, u32[]{:S(2)}) collective-permute-start(bf16[256,2048]{1,0:T(8,128)(2,1)} %get-tuple-element.344), channel_id=1, source_target_pairs={{0,1},{1,0},{2,3},{3,2},{4,5},{5,4},{6,7},{7,6},{8,9},{9,8},{10,11... | collective-permute-start | bytes 3145736 | tf_op jit(solution)/shard_map/ppermute | solution.py:358
  387.4 36.0 %collective-permute-start.42 = (f32[24576]{0:T(1024)S(1)}, f32[24576]{0:T(1024)S(1)}, u32[]{:S(2)}, u32[]{:S(2)}) collective-permute-start(f32[24576]{0:T(1024)S(1)} %constant_dynamic-update-slice_fusion), channel_id=1, source_target_pairs={{0,16},{8,24},{16,0},{24,8},{1,17},{9,25},{17,1},{25,9},{2,18},{10... | collective-permute-start | bytes 294920 | tf_op jit(solution)/shard_map/ppermute | solution.py:358
  389.0 31.4 %collective-permute-start.44 = (bf16[4,64,768]{2,1,0:T(8,128)(2,1)}, bf16[4,64,768]{2,1,0:T(8,128)(2,1)}, u32[]{:S(2)}, u32[]{:S(2)}) collective-permute-start(bf16[4,64,768]{2,1,0:T(8,128)(2,1)} %get-tuple-element.346), channel_id=1, source_target_pairs={{0,1},{1,0},{2,3},{3,2},{4,5},{5,4},{6,7},{7,6},{8,9},{9,8},{10,11... | collective-permute-start | bytes 1179656 | tf_op jit(solution)/shard_map/ppermute | solution.py:358
  391.0 32.4 %collective-permute-start.40 = (bf16[2,2,64,1024]{3,2,1,0:T(8,128)(2,1)}, bf16[2,2,64,1024]{3,2,1,0:T(8,128)(2,1)}, u32[]{:S(2)}, u32[]{:S(2)}) collective-permute-start(bf16[2,2,64,1024]{3,2,1,0:T(8,128)(2,1)} %pad_maximum_fusion.6), channel_id=1, source_target_pairs={{0,4},{1,5},{2,6},{3,7},{4,0},{5,1},{6,2},{7,3},{8,12},{9,13},{10,... | collective-permute-start | bytes 1572872 | tf_op jit(solution)/shard_map/ppermute | solution.py:358
  424.5 35.2 %collective-permute-start.45 = (bf16[256,2048]{1,0:T(8,128)(2,1)S(1)}, bf16[256,2048]{1,0:T(8,128)(2,1)S(1)}, u32[]{:S(2)}, u32[]{:S(2)}) collective-permute-start(bf16[256,2048]{1,0:T(8,128)(2,1)S(1)} %add_convert_fusion.9), channel_id=1, source_target_pairs={{0,2},{1,3},{6,4},{7,5},{8,10},{9,11},{14,12},{15,13},{16,18},{17,... | collective-permute-start | bytes 3145736 | tf_op jit(solution)/shard_map/ppermute | solution.py:362
  430.7 61.0 %collective-permute-start.52 = (bf16[1280,1024]{1,0:T(8,128)(2,1)S(1)}, bf16[1280,1024]{1,0:T(8,128)(2,1)S(1)}, u32[]{:S(2)}, u32[]{:S(2)}) collective-permute-start(bf16[1280,1024]{1,0:T(8,128)(2,1)S(1)} %add_convert_fusion.1), channel_id=1, source_target_pairs={{0,16},{8,24},{16,0},{24,8},{1,17},{9,25},{17,1},{25,9},{2,18},{10... | collective-permute-start | bytes 7864328 | tf_op jit(solution)/shard_map/ppermute | solution.py:358
  461.9 29.8 %collective-permute-start.50 = (bf16[256,2048]{1,0:T(8,128)(2,1)S(1)}, bf16[256,2048]{1,0:T(8,128)(2,1)S(1)}, u32[]{:S(2)}, u32[]{:S(2)}) collective-permute-start(bf16[256,2048]{1,0:T(8,128)(2,1)S(1)} %add_convert_fusion.7), channel_id=1, source_target_pairs={{0,2},{1,3},{6,4},{7,5},{8,10},{9,11},{14,12},{15,13},{16,18},{17,... | collective-permute-start | bytes 3145736 | tf_op jit(solution)/shard_map/ppermute | solution.py:362
  (93 other events, 1379.1 us)
